TPU v7x, 32 devices: a whole 2x2x4 slice. The times are simulated.
32 devices in a mesh: fsdp: 4 (over y, core), tile: 8 (over z, x).
Axes of the slice: x: 2, y: 2, z: 4, core: 2. Of those that a mesh axis runs over, the one named last changes fastest.
Arguments:
- tiles: bfloat16 [4, 2048, 768], P('fsdp', 'tile')
- nbr_tiles: int32 [4, 512, 4], P('fsdp', 'tile'), may hold values from 0 to 2047, as said below
- nbr_mask: int32 [4, 512, 4], P('fsdp', 'tile'), may hold values 0 or 1
- tile_count: int32 [4], P('fsdp'), may hold values from 1024 to 2048, as said below
- w_query: bfloat16 [768, 768], P('fsdp'), may hold values from -0.21875 to 0.21875
- w_key: bfloat16 [768, 768], P('fsdp'), may hold values from -0.21875 to 0.21875
- w_value: bfloat16 [768, 768], P('fsdp'), may hold values from -0.21875 to 0.21875
- w_out: bfloat16 [768, 768], P('fsdp'), may hold values from -0.875 to 0.875
- key_gain: float32 [768], replicated, may hold values from 0.1 to 1.9
Outputs:
- attended: bfloat16 [4, 2048, 768], P('fsdp', 'tile')
Inputs may be any that keep to these rules, and one draw needn't show every extreme that they name: `nbr_tiles`: the slots of region r hold tiles with indices from (r // 64 - 1) * 256 to (r // 64 + 2) * 256 - 1, within the group. `tile_count`: some group has all 2048 tiles live.
All inputs are finite; a program needn't handle non-finite values. No bound on the sum of `nbr_mask` on one device may be relied on, other than what follows from the above.
Results may differ from a plain program's by a relative error of at most 0.008.
The roundings to bfloat16 on the way count: a program that leaves them out, or rounds other values in their place, can miss the bound.
Values may be sent and summed in bfloat16 or wider, within the bound.
No kernel may reach another device: no remote copies, remote signals or barrier semaphores. Data moves between devices by JAX's collectives and lax.ppermute only.
A program may use at most 64 MiB of HBM per device.

v0:
```python
import jax
import jax.numpy as jnp
from jax import lax
from jax.sharding import PartitionSpec as P

HEADS = 16
NB = 4
REGIONS_PER_KEY = 8
KEY_DILATION = 2


def padded_2(cells, sides, width):
    for axis, dim in sides:
        count = lax.axis_size(axis)
        ends = count - 1
        head = lax.slice_in_dim(cells, 0, width, axis=dim)
        tail = lax.slice_in_dim(cells, cells.shape[dim] - width, cells.shape[dim], axis=dim)
        cells = jnp.concatenate(
            [
                lax.ppermute(tail, axis, [(i, (i + 1) % count) for i in range(ends)]),
                cells,
                lax.ppermute(head, axis, [((i + 1) % count, i) for i in range(ends)]),
            ],
            axis=dim,
        )
    return cells


def project_all(sources, w_query, w_key, w_value):
    pieces = (
        lax.all_gather(w_query, "fsdp", axis=0, tiled=True),
        lax.all_gather(w_key, "fsdp", axis=0, tiled=True),
        lax.all_gather(w_value, "fsdp", axis=0, tiled=True),
    )
    sums = tuple(
        (
            jnp.dot(src, key_segment, preferred_element_type=jnp.float32)
            for src, key_segment in zip(sources, pieces)
        )
    )
    return tuple((s.astype(jnp.bfloat16) for s in sums))


def by_parity(key_segment, head_list, window_width):
    region_number = key_segment.shape[0]
    split_point = key_segment.reshape(
        region_number // KEY_DILATION,
        KEY_DILATION,
        head_list // KEY_DILATION,
        KEY_DILATION,
        window_width,
    )
    selected_keys = jnp.stack(
        [
            split_point[:, inner_position, :, inner_position, :]
            for inner_position in range(KEY_DILATION)
        ],
        axis=2,
    )
    return selected_keys.reshape(region_number // KEY_DILATION, head_list, window_width)


def attend_block(state, key_piece, value_piece, query_heads, key_count_total):
    top, total, accum = state
    head_list = query_heads.shape[1]
    window_width = query_heads.shape[2]
    region_number = key_piece.shape[0]
    key_heads = by_parity(key_piece, head_list, window_width)
    value_heads = by_parity(value_piece, head_list, window_width)
    score = jnp.einsum(
        "qhd,khd->hqk", query_heads, key_heads, preferred_element_type=jnp.float32
    ) / jnp.sqrt(jnp.float32(window_width))
    pair_position = jnp.arange(region_number // KEY_DILATION, dtype=jnp.int32)
    head_position = jnp.arange(head_list, dtype=jnp.int32)
    key_position = KEY_DILATION * pair_position[None, :] + (head_position % KEY_DILATION)[:, None]
    valid_mask = key_position * 4 * REGIONS_PER_KEY < key_count_total
    score = jnp.where(valid_mask[:, None, :], score, -jnp.inf)
    new_top = jnp.maximum(top, jnp.max(score, axis=2))
    expo = jnp.exp(score - new_top[:, :, None])
    total = jnp.sum(expo, axis=2)
    accum = jnp.einsum(
        "hqk,khd->hqd", expo.astype(jnp.bfloat16), value_heads, preferred_element_type=jnp.float32
    )
    return (new_top, total, accum)


def body(tiles, nbr_tiles, nbr_mask, tile_count, w_query, w_key, w_value, w_out, key_gain):
    own_tiles = tiles[0]
    tile_rows, window_width = own_tiles.shape
    head_list = HEADS
    head_size = window_width // head_list
    device = lax.axis_index("tile")
    region_count = nbr_tiles.shape[1]
    key_rows = region_count // REGIONS_PER_KEY
    padded = padded_2(tiles, (("tile", 1),), tile_rows)[0]
    local_index = nbr_tiles[0] - (device - 1) * tile_rows
    rows = (
        jnp.take(padded, local_index.reshape(-1), axis=0)
        .reshape(region_count, NB, window_width)
        .astype(jnp.float32)
    )
    mask_f = nbr_mask[0].astype(jnp.float32)
    denom = jnp.maximum(jnp.sum(mask_f, axis=1), 1.0)
    region = jnp.sum(rows * mask_f[:, :, None], axis=1) / denom[:, None]
    pooled = jnp.mean(region.reshape(key_rows, REGIONS_PER_KEY, window_width), axis=1)
    normed = (
        pooled
        * lax.rsqrt(jnp.mean(pooled * pooled, axis=1, keepdims=True) + 1e-06)
        * key_gain[None, :]
    ).astype(jnp.bfloat16)
    key_count_total = tile_count[0]
    blank = (
        jnp.full((head_list, tile_rows), -1e30, jnp.float32),
        jnp.zeros((head_list, tile_rows), jnp.float32),
        jnp.zeros((head_list, tile_rows, head_size), jnp.float32),
    )
    query, keys, values = project_all((own_tiles, normed, normed), w_query, w_key, w_value)
    query_heads = query.reshape(tile_rows, head_list, head_size)
    top, total, accum = attend_block(
        blank,
        lax.all_gather(keys, "tile", axis=0, tiled=True),
        lax.all_gather(values, "tile", axis=0, tiled=True),
        query_heads,
        key_count_total,
    )
    context = accum / total[:, :, None]
    context = (
        jnp.transpose(context, (1, 0, 2)).reshape(tile_rows, window_width).astype(jnp.bfloat16)
    )
    attended = jnp.dot(
        context,
        lax.all_gather(w_out, "fsdp", axis=0, tiled=True),
        preferred_element_type=jnp.float32,
    )
    return attended.astype(jnp.bfloat16)[None]


def solution(mesh):
    placed = (
        P("fsdp", "tile", None),
        P("fsdp", "tile", None),
        P("fsdp", "tile", None),
        P("fsdp"),
        P("fsdp", None),
        P("fsdp", None),
        P("fsdp", None),
        P("fsdp", None),
        P(),
    )
    return jax.shard_map(
        body, mesh=mesh, in_specs=placed, out_specs=P("fsdp", "tile", None), check_vma=False
    )
```

profile of v0, /device:TPU:0, one launch (start us, length us, event | category | flops | bytes accessed | tf_op | source)
XLA Modules:
  0.0 112.5 jit_solution(6760142922323926561)
XLA Ops:
  6.5 0.0 copy-start
  6.5 0.0 copy-start.2
  6.5 0.0 copy-start.3
  6.5 0.0 all-gather.7.cloned.1.call-start
  6.5 0.7 all-gather.7.cloned.1.call-update
  7.3 0.0 all-gather.5.cloned.1.call-start
  7.3 0.7 all-gather.5.cloned.1.call-update
  8.0 0.0 all-gather.9.cloned.1.call-start
  8.1 0.7 all-gather.9.cloned.1.call-update
  8.7 0.0 all-gather.11.cloned.1.call-start
  8.8 4.9 %collective-permute-start = (bf16[1,256,768]{2,1,0:T(8,128)(2,1)}, bf16[1,256,768]{2,1,0:T(8,128)(2,1)S(1)}, u32[]{:S(2)}, u32[]{:S(2)}) collective-permute-start(bf16[1,256,768]{2,1,0:T(8,128)(2,1)} %param.9), channel_id=1, source_target_pairs={{0,1},{1,2},{2,3},{3,4},{4,5},{5,6},{6,7},{8,9},{9,10},{10,11},{11... | collective-permute-start | bytes 1179656 | tf_op jit(solution)/shard_map/ppermute | solution.py:20
  13.7 1.3 %collective-permute-start.1 = (bf16[1,256,768]{2,1,0:T(8,128)(2,1)}, bf16[1,256,768]{2,1,0:T(8,128)(2,1)S(1)}, u32[]{:S(2)}, u32[]{:S(2)}) collective-permute-start(bf16[1,256,768]{2,1,0:T(8,128)(2,1)} %param.9), channel_id=1, source_target_pairs={{1,0},{2,1},{3,2},{4,3},{5,4},{6,5},{7,6},{9,8},{10,9},{11,10},{12... | collective-permute-start | bytes 1179656 | tf_op jit(solution)/shard_map/ppermute | solution.py:22
  15.0 0.0 all-gather.11.cloned.1.call-update
  15.0 0.0 copy-done.2
  15.0 0.0 copy-done.3
  15.1 0.1 copy.29
  15.2 0.1 sub.38
  15.3 0.1 copy.28
  15.4 0.1 copy.30
  15.5 0.1 max.15
  16.3 0.1 multiply_compare_fusion
  16.3 14.4 %collective-permute-done = bf16[1,256,768]{2,1,0:T(8,128)(2,1)S(1)} collective-permute-done((bf16[1,256,768]{2,1,0:T(8,128)(2,1)}, bf16[1,256,768]{2,1,0:T(8,128)(2,1)S(1)}, u32[]{:S(2)}, u32[]{:S(2)}) %collective-permute-start) | collective-permute-done | bytes 393248 | tf_op jit(solution)/shard_map/ppermute | solution.py:20
  30.8 0.0 collective-permute-done.1
  30.8 0.0 copy-done
  30.8 0.1 maximum_bitcast_fusion
  30.9 1.2 %gather_fusion = bf16[256,768]{1,0:T(8,128)(2,1)S(1)} fusion(bf16[768,768]{1,0:T(8,128)(2,1)S(1)} %maximum_bitcast_fusion, s32[1024]{0:T(1024)S(1)} %pad_clamp_fusion), kind=kCustom, calls=%fused_computation | custom fusion | bytes 787456 | tf_op jit(solution)/shard_map/jit(_take)/gather | solution.py:98
  32.0 0.0 copy-start.1
  32.1 0.1 gather.7
  32.2 0.6 multiply_reduce_fusion
  32.8 0.1 fusion.9
  32.9 0.1 multiply_reduce_fusion.1
  33.1 0.0 all-gather.7.cloned.1.call-done
  33.1 0.0 copy-done.1
  33.1 1.6 %convolution_convert_fusion.3 = bf16[8,768]{1,0:T(8,128)(2,1)S(1)} fusion(bf16[768,768]{1,0:T(8,128)(2,1)} %all-gather.7.cloned.1.call-done, f32[8,768]{1,0:T(8,128)S(1)} %fusion.9, f32[768]{0:T(1024)S(1)} %copy-done.1, f32[8]{0:T(128)S(1)} %rsqrt_multiply_fusion), kind=kOutput, calls=%fused_computation.11 | convolution fusion | flops 9461760 | bytes 1219616 | tf_op jit(solution)/shard_map/dot_general | solution.py:37
  34.7 32.6 %all_gather.20 = bf16[64,768]{1,0:T(8,128)(2,1)S(1)} all-gather(bf16[8,768]{1,0:T(8,128)(2,1)S(1)} %convolution_convert_fusion.3), channel_id=1, replica_groups=mesh['fsdp'=4,'tile'=8] {'tile'}, dimensions={0}, use_global_device_ids=true | all-gather | bytes 110592 | tf_op jit(solution)/shard_map/all_gather | solution.py:121
  67.3 0.3 reshape.127
  67.6 0.2 fusion.10
  67.9 0.0 all-gather.5.cloned.1.call-done
  67.9 1.8 %convolution_convert_fusion.1 = bf16[256,768]{1,0:T(8,128)(2,1)S(1)} fusion(bf16[768,768]{1,0:T(8,128)(2,1)} %all-gather.5.cloned.1.call-done, bf16[1,256,768]{2,1,0:T(8,128)(2,1)S(1)} %copy-done), kind=kOutput, calls=%fused_computation.5 | convolution fusion | flops 302186496 | bytes 1966080 | tf_op jit(solution)/shard_map/dot_general | solution.py:37
  69.8 0.2 copy.27
  69.9 0.0 all-gather.9.cloned.1.call-done
  70.0 1.6 %convolution_convert_fusion.2 = bf16[8,768]{1,0:T(8,128)(2,1)S(1)} fusion(bf16[768,768]{1,0:T(8,128)(2,1)} %all-gather.9.cloned.1.call-done, f32[8,768]{1,0:T(8,128)S(1)} %fusion.9, f32[768]{0:T(1024)S(1)} %copy-done.1, f32[8]{0:T(128)S(1)} %rsqrt_multiply_fusion), kind=kOutput, calls=%fused_computation.10 | convolution fusion | flops 9461760 | bytes 1219616 | tf_op jit(solution)/shard_map/dot_general | solution.py:37
  71.6 30.5 %all_gather.22 = bf16[64,768]{1,0:T(8,128)(2,1)S(1)} all-gather(bf16[8,768]{1,0:T(8,128)(2,1)S(1)} %convolution_convert_fusion.2), channel_id=1, replica_groups=mesh['fsdp'=4,'tile'=8] {'tile'}, dimensions={0}, use_global_device_ids=true | all-gather | bytes 110592 | tf_op jit(solution)/shard_map/all_gather | solution.py:122
  102.1 0.3 reshape.129
  102.4 0.2 fusion.11
  102.8 0.2 fusion.12
  103.0 0.1 fusion.4
  103.1 0.3 fusion.1
  103.4 0.0 all-gather.11.cloned.1.call-done
  103.5 2.5 %fusion.3 = bf16[1,256,768]{2,1,0:T(8,128)(2,1)} fusion(bf16[256,768]{0,1:T(8,128)(2,1)S(1)} %bitcast.49, bf16[768,768]{1,0:T(8,128)(2,1)} %all-gather.11.cloned.1.call-done), kind=kOutput, calls=%fused_computation.8 | convolution fusion | flops 302186496 | bytes 1966080 | tf_op jit(solution)/shard_map/dot_general | solution.py:130
  (16 shorter events, 0.2 us)
Async XLA Ops:
  6.5 24.2 %copy-start = (bf16[1,256,768]{2,1,0:T(8,128)(2,1)S(1)}, bf16[1,256,768]{2,1,0:T(8,128)(2,1)}, u32[]{:S(2)}) copy-start(bf16[1,256,768]{2,1,0:T(8,128)(2,1)} %param.9) | copy-start | bytes 1179652
  6.5 8.5 %copy-start.2 = (s32[1,64,4]{1,2,0:T(4,128)S(1)}, s32[1,64,4]{1,2,0:T(4,128)}, u32[]{:S(2)}) copy-start(s32[1,64,4]{1,2,0:T(4,128)} %param.11) | copy-start | bytes 3076
  6.5 8.5 %copy-start.3 = (s32[1,64,4]{1,2,0:T(4,128)S(1)}, s32[1,64,4]{1,2,0:T(4,128)}, u32[]{:S(2)}) copy-start(s32[1,64,4]{1,2,0:T(4,128)} %param.10) | copy-start | bytes 3076
  6.5 26.6 %all-gather.7.cloned.1.call-start = ((), (), s32[]{:S(2)}) async-start(), calls=%async_computation.1 | async-start | bytes 1474560 | tf_op jit(solution)/shard_map/all_gather | solution.py:32
  7.3 60.7 %all-gather.5.cloned.1.call-start = ((), (), s32[]{:S(2)}) async-start(), calls=%async_computation | async-start | bytes 1474560 | tf_op jit(solution)/shard_map/all_gather | solution.py:31
  8.0 61.9 %all-gather.9.cloned.1.call-start = ((), (), s32[]{:S(2)}) async-start(), calls=%async_computation.2 | async-start | bytes 1474560 | tf_op jit(solution)/shard_map/all_gather | solution.py:33
  8.7 94.7 %all-gather.11.cloned.1.call-start = ((), (), s32[]{:S(2)}) async-start(), calls=%async_computation.3 | async-start | bytes 1474560 | tf_op jit(solution)/shard_map/all_gather | solution.py:132
  8.8 22.0 %collective-permute-start = (bf16[1,256,768]{2,1,0:T(8,128)(2,1)}, bf16[1,256,768]{2,1,0:T(8,128)(2,1)S(1)}, u32[]{:S(2)}, u32[]{:S(2)}) collective-permute-start(bf16[1,256,768]{2,1,0:T(8,128)(2,1)} %param.9), channel_id=1, source_target_pairs={{0,1},{1,2},{2,3},{3,4},{4,5},{5,6},{6,7},{8,9},{9,10},{10,11},{11... | collective-permute-start | bytes 1179656 | tf_op jit(solution)/shard_map/ppermute | solution.py:20
  13.7 17.1 %collective-permute-start.1 = (bf16[1,256,768]{2,1,0:T(8,128)(2,1)}, bf16[1,256,768]{2,1,0:T(8,128)(2,1)S(1)}, u32[]{:S(2)}, u32[]{:S(2)}) collective-permute-start(bf16[1,256,768]{2,1,0:T(8,128)(2,1)} %param.9), channel_id=1, source_target_pairs={{1,0},{2,1},{3,2},{4,3},{5,4},{6,5},{7,6},{9,8},{10,9},{11,10},{12... | collective-permute-start | bytes 1179656 | tf_op jit(solution)/shard_map/ppermute | solution.py:22
  32.0 1.1 copy-start.1
Sparse Core Ops, SparseCore 0:
  8.9 20.1 all-gather.6
  30.7 17.5 all-gather.4
  49.8 17.4 all-gather.8
  68.7 17.4 all-gather.10
where the time goes:
time: 113 us
  blocking collectives  63.2 us (56%)
  waiting for transfers between devices  16.6 us (15%)
  between operations  14.1 us (12%)
  matrix products  7.99 us (7%)
  starting transfers between devices  6.27 us (6%)
  local copies, waits for them, and re-layouts  3.12 us (3%)
  other arithmetic  1.28 us (1%)
    all_gather x1, blocking collectives, body(): lax.all_gather(keys, 'tile', axis=0, tiled=True)  32.6 us
    all_gather x1, blocking collectives, body(): lax.all_gather(values, 'tile', axis=0, tiled=True)  30.5 us
    ppermute x1, waiting for transfers between devices, padded_2(): lax.ppermute(tail, axis, [(i, (i + 1) % count) for i in range(ends)])  14.4 us
    dot_general x3, matrix products, project_all(): jnp.dot(src, key_segment, preferred_element_type=jnp.float32)  4.92 us
    ppermute x1, starting transfers between devices, padded_2(): lax.ppermute(tail, axis, [(i, (i + 1) % count) for i in range(ends)])  4.87 us
    dot_general x1, matrix products, body(): jnp.dot(context, lax.all_gather(w_out, 'fsdp', axis=0, tiled=True), prefe...  2.52 us
  transfers between devices with their start and end apart: 6, of which 1 were waited for; matrix products, arithmetic and copies ran while one was open for 9% of the time, Pallas kernels for 0%

commit v1 on v0

v1 whole, which is shorter than its diff:
```python
import functools

import jax
import jax.numpy as jnp
from jax import lax
from jax.experimental import pallas as pl
from jax.experimental.pallas import tpu as pltpu
from jax.sharding import PartitionSpec as P

HEADS = 16
NB = 4
REGIONS_PER_KEY = 8
KEY_DILATION = 2
LANE_GROUPS = 2
F32 = jnp.float32
BF16 = jnp.bfloat16


def vmem():
    return pl.BlockSpec(memory_space=pltpu.VMEM)


def smem():
    return pl.BlockSpec(memory_space=pltpu.SMEM)


def anywhere():
    return pl.BlockSpec(memory_space=pl.ANY)


def over(left, right, left_dim, right_dim, precision=None):
    return lax.dot_general(
        left,
        right,
        (((left_dim,), (right_dim,)), ((), ())),
        precision=precision,
        preferred_element_type=F32,
    )


def pool_kernel(place, slots, tiles, left, own, right):
    count, width = tiles.shape[0], slots.shape[1]
    keys = width // REGIONS_PER_KEY
    row = lax.broadcasted_iota(jnp.int32, (count, width), 0) + place[0] * count + 1
    hits = jnp.zeros((count, width), F32)
    live = jnp.zeros((1, width), F32)
    for s in range(NB):
        slot = slots[s : s + 1, :]
        hits += (slot == row).astype(F32)
        live += (slot > 0).astype(F32)
    sums = over(hits.astype(BF16), tiles[...], 0, 0)
    share = 1.0 / (jnp.maximum(live, 1.0) * REGIONS_PER_KEY)
    key = lax.broadcasted_iota(jnp.int32, (keys, width), 0)
    region = lax.broadcasted_iota(jnp.int32, (keys, width), 1)
    chosen = jnp.where(region // REGIONS_PER_KEY == key, share, 0.0)
    pooled = over(chosen, sums, 1, 0, lax.Precision.HIGHEST)
    part = keys // 3
    left[...] = pooled[:part]
    own[...] = pooled[part : 2 * part]
    right[...] = pooled[2 * part :]


def norm_kernel(own, first, second, gain, normed):
    pooled = own[...] + first[...] + second[...]
    scale = lax.rsqrt(jnp.mean(pooled * pooled, axis=1, keepdims=True) + 1e-06)
    normed[...] = (pooled * scale * gain[...]).astype(BF16)


def collect(copies, sem):
    started = []
    for n, (src, dst) in enumerate(copies):
        copy = pltpu.make_async_copy(src, dst, sem.at[n])
        copy.start()
        started.append(copy)
    return started


def rows_of(fsdp, me, own, sibling, other, far, held):
    rows = own.shape[0]
    chips = fsdp // 2
    chip, core = me // 2, me % 2

    def at(index):
        return held.at[pl.ds(pl.multiple_of(index * rows, rows), rows)]

    pieces = [(own, at(me)), (sibling, at(2 * chip + 1 - core))]
    for j in range(1, chips):
        source = lax.rem(chip - j + chips, chips)
        pieces.append((other.at[j - 1], at(2 * source + core)))
        pieces.append((far.at[j - 1], at(2 * source + 1 - core)))
    return pieces


def sorted_rows(normed):
    keys = normed.shape[0]
    half = keys // KEY_DILATION
    row = lax.broadcasted_iota(jnp.int32, (keys, keys), 0)
    column = lax.broadcasted_iota(jnp.int32, (keys, keys), 1)
    wanted = KEY_DILATION * (row % half) + row // half
    return over((column == wanted).astype(BF16), normed, 1, 0).astype(BF16)


def spread(rows, group, wide):
    half = rows.shape[0] // KEY_DILATION
    heads = HEADS // LANE_GROUPS
    size = wide // heads
    part = rows[:, group * wide : (group + 1) * wide].astype(F32)
    lane = lax.broadcasted_iota(jnp.int32, (half, wide), 1)
    out = []
    for head in range(heads):
        parity = head % KEY_DILATION
        mine = (lane >= head * size) & (lane < (head + 1) * size)
        out.append(jnp.where(mine, part[parity * half : (parity + 1) * half], 0.0))
    return jnp.concatenate(out, axis=0).astype(BF16)


def attend_scores(
    fsdp, block, place, normed, tiles, wk, wq, sibling, near, far, weights, totals, wk_held, wq_held, sem
):
    tile, me, count, pair = place[0], place[1], place[2], place[3]
    pieces = rows_of(fsdp, me, wk, sibling.at[0], near.at[pair], far.at[pair], wk_held)
    pieces += rows_of(fsdp, me, wq, sibling.at[1], near.at[1 - pair], far.at[1 - pair], wq_held)
    started = collect(pieces, sem)
    ordered = sorted_rows(normed[...])
    for copy in started:
        copy.wait()
    keys = over(ordered, wk_held[...], 1, 0).astype(BF16)
    query = over(tiles[...], wq_held[...], 1, 0).astype(BF16)
    half = keys.shape[0] // KEY_DILATION
    heads = HEADS // LANE_GROUPS
    wide = keys.shape[1] // LANE_GROUPS
    rows = tiles.shape[0]
    size = wide // heads
    row = lax.broadcasted_iota(jnp.int32, (half, 1), 0)
    per = block // KEY_DILATION
    first = (tile ^ (row // per)) * block + KEY_DILATION * (row % per)
    valid = [(first + parity) * (4 * REGIONS_PER_KEY) < count for parity in range(KEY_DILATION)]
    hidden = jnp.concatenate(
        [jnp.where(valid[head % KEY_DILATION], 0.0, -jnp.inf) for head in range(heads)], axis=0
    )
    for group in range(LANE_GROUPS):
        score = over(spread(keys, group, wide), query[:, group * wide : (group + 1) * wide], 1, 1)
        score = (score * (1.0 / size**0.5) + hidden).reshape(heads, half, rows)
        expo = jnp.exp(score - jnp.max(score, axis=1, keepdims=True))
        totals[group * heads : (group + 1) * heads, :] = jnp.sum(expo, axis=1)
        weights[group * heads * half : (group + 1) * heads * half, :] = expo.reshape(
            heads * half, rows
        ).astype(BF16)


def attend_values(
    fsdp, place, normed, weights, totals, wv, wo, sibling, near, far, out, wv_held, wo_held, sem
):
    me, pair = place[1], place[3]
    pieces = rows_of(fsdp, me, wv, sibling.at[2], near.at[pair], far.at[pair], wv_held)
    pieces += rows_of(fsdp, me, wo, sibling.at[3], near.at[1 - pair], far.at[1 - pair], wo_held)
    started = collect(pieces, sem)
    ordered = sorted_rows(normed[...])
    for copy in started:
        copy.wait()
    values = over(ordered, wv_held[...], 1, 0).astype(BF16)
    half = values.shape[0] // KEY_DILATION
    heads = HEADS // LANE_GROUPS
    wide = values.shape[1] // LANE_GROUPS
    rows = weights.shape[1]
    size = wide // heads
    total = None
    for group in range(LANE_GROUPS):
        part = weights[group * heads * half : (group + 1) * heads * half, :]
        context = over(spread(values, group, wide), part, 0, 0).reshape(heads, size, rows)
        share = 1.0 / totals[group * heads : (group + 1) * heads, :]
        context = (context * share[:, None, :]).reshape(wide, rows).astype(BF16)
        term = over(context, wo_held[group * wide : (group + 1) * wide, :], 0, 0)
        total = term if total is None else total + term
    out[...] = total.astype(BF16)


def swap(array, axis, offset):
    count = lax.axis_size(axis)
    return lax.ppermute(array, axis, [(i, i ^ offset) for i in range(count)])


def gather_rows(rows, axis):
    count = lax.axis_size(axis)
    held = 1
    digits = [1] + [2] * 16
    for digit in digits:
        if held >= count:
            break
        width = min(1 << digit, count // held)
        parts = [rows] + [swap(rows, axis, held * d) for d in range(1, width)]
        rows = jnp.concatenate(parts, axis=0)
        held *= width
    return rows


def chip_shift(array, axis, step):
    count = lax.axis_size(axis)
    return lax.ppermute(array, axis, [(i, (i + 2 * step) % count) for i in range(count)])


def fetch(first, second, pair):
    chips = lax.axis_size("fsdp") // 2
    mine = jnp.where(pair == 0, first, second)
    near = jnp.stack([chip_shift(mine, "fsdp", j) for j in range(1, chips)])
    both = jnp.stack([near, swap(near, "tile", 1)])
    return both, swap(both, "fsdp", 1)


def body(tiles, nbr_tiles, nbr_mask, tile_count, w_query, w_key, w_value, w_out, key_gain):
    own_tiles = tiles[0]
    rows, width = own_tiles.shape
    tile = lax.axis_index("tile")
    me = lax.axis_index("fsdp")
    tile_devices = lax.axis_size("tile")
    fsdp = lax.axis_size("fsdp")
    regions = nbr_tiles.shape[1]
    block = regions // REGIONS_PER_KEY
    place = jnp.stack([tile, me, tile_count[0], tile % 2]).astype(jnp.int32)

    forward = [(i, i + 1) for i in range(tile_devices - 1)]
    backward = [(i + 1, i) for i in range(tile_devices - 1)]
    slots = jnp.where(nbr_mask[0] > 0, nbr_tiles[0] + 1, 0).T
    slots_all = jnp.concatenate(
        [lax.ppermute(slots, "tile", forward), slots, lax.ppermute(slots, "tile", backward)], axis=1
    )
    part = jax.ShapeDtypeStruct((block, width), F32)
    left, own, right = pl.pallas_call(
        pool_kernel,
        out_shape=(part, part, part),
        in_specs=[smem(), vmem(), vmem()],
        out_specs=(vmem(), vmem(), vmem()),
        name="pool",
    )(place, slots_all, own_tiles)
    normed = pl.pallas_call(
        norm_kernel,
        out_shape=jax.ShapeDtypeStruct((block, width), BF16),
        in_specs=[vmem()] * 4,
        out_specs=vmem(),
        name="norm",
    )(
        own,
        lax.ppermute(right, "tile", forward),
        lax.ppermute(left, "tile", backward),
        key_gain[None, :],
    )
    normed = gather_rows(normed, "tile")
    keys = normed.shape[0]

    sibling = swap(jnp.stack([w_key, w_query, w_value, w_out]), "fsdp", 1)
    near1, far1 = fetch(w_key, w_query, tile % 2)
    near2, far2 = fetch(w_value, w_out, tile % 2)

    held = pltpu.VMEM((width, width), BF16)
    scratch = [held, held, pltpu.SemaphoreType.DMA((2 * fsdp,))]
    limit = pltpu.CompilerParams(vmem_limit_bytes=40 * 1024 * 1024)
    weights, totals = pl.pallas_call(
        functools.partial(attend_scores, fsdp, block),
        out_shape=(
            jax.ShapeDtypeStruct((HEADS * keys // KEY_DILATION, rows), BF16),
            jax.ShapeDtypeStruct((HEADS, rows), F32),
        ),
        in_specs=[smem(), vmem(), vmem()] + [anywhere()] * 5,
        out_specs=(vmem(), vmem()),
        scratch_shapes=scratch,
        compiler_params=limit,
        name="scores",
    )(place, normed, own_tiles, w_key, w_query, sibling, near1, far1)
    attended = pl.pallas_call(
        functools.partial(attend_values, fsdp),
        out_shape=jax.ShapeDtypeStruct((rows, width), BF16),
        in_specs=[smem()] + [vmem()] * 3 + [anywhere()] * 5,
        out_specs=vmem(),
        scratch_shapes=scratch,
        compiler_params=limit,
        name="values",
    )(place, normed, weights, totals, w_value, w_out, sibling, near2, far2)
    return attended[None]


def solution(mesh):
    placed = (
        P("fsdp", "tile", None),
        P("fsdp", "tile", None),
        P("fsdp", "tile", None),
        P("fsdp"),
        P("fsdp", None),
        P("fsdp", None),
        P("fsdp", None),
        P("fsdp", None),
        P(),
    )
    return jax.shard_map(
        body, mesh=mesh, in_specs=placed, out_specs=P("fsdp", "tile", None), check_vma=False
    )
```

time: 113 us -> 54.9 us (0.49)
  blocking collectives: 63.2 us -> 0 us
  starting transfers between devices: 6.27 us -> 25.7 us
  between operations: 14.1 us -> 0.84 us
  Pallas kernels: 0 us -> 9.46 us
  matrix products: 7.99 us -> 0 us
  waiting for transfers between devices: 16.6 us -> 11.3 us
  other arithmetic: 1.28 us -> 6.51 us
  local copies, waits for them, and re-layouts: 3.12 us -> 0.63 us
    all_gather x2 -> x0, blocking collectives: 63.2 us -> none  [the longest x1 32.6 us: body(): lax.all_gather(keys, 'tile', axis=0, tiled=True)]
    ppermute x2 -> x15, starting transfers between devices: 6.16 us -> 25.7 us  [the longest x9 12.7 us: swap(): return lax.ppermute(array, axis, [(i, i ^ offset) for i in range(count)])]
    pallas_call x0 -> x4, Pallas kernels: none -> 9.46 us  [the longest x1 3.36 us: body(): pl.pallas_call(functools.partial(attend_values, fsdp), out_shape=jax.Shap...]
    dot_general x6 -> x0, matrix products: 7.99 us -> none  [the longest x3 4.92 us: project_all(): jnp.dot(src, key_segment, preferred_element_type=jnp.float32)]
    ppermute x2 -> x15, waiting for transfers between devices: 14.4 us -> 11.3 us  [the longest x9 4.76 us: swap(): return lax.ppermute(array, axis, [(i, i ^ offset) for i in range(count)])]
    another operation x3 -> x4, other arithmetic: 0.06 us -> 3.03 us  [the longest x2 2.27 us: fetch(): both = jnp.stack([near, swap(near, 'tile', 1)])]
    select_n x2, other arithmetic: 0.01 us -> 2.8 us  [fetch(): mine = jnp.where(pair == 0, first, second)]
    unnamed x4 -> x0, waiting for transfers between devices: 2.1 us -> none
  transfers between devices with their start and end apart: 6 -> 15, of which waited for: 1 -> 6; matrix products, arithmetic and copies ran while one was open for 9% -> 11% of each run, Pallas kernels for 0% -> 11%
where the time goes in v1:
time: 54.9 us; the launch traced here: 54.5 us
  starting transfers between devices  25.7 us (47%)
  waiting for transfers between devices  11.3 us (21%)
  Pallas kernels  9.46 us (17%)
  other arithmetic  6.51 us (12%)
  between operations  0.84 us (2%)
  local copies, waits for them, and re-layouts  0.63 us (1%)
    ppermute x9, starting transfers between devices, swap(): return lax.ppermute(array, axis, [(i, i ^ offset) for i in range(count)])  12.7 us
    ppermute x9, waiting for transfers between devices, swap(): return lax.ppermute(array, axis, [(i, i ^ offset) for i in range(count)])  4.76 us
    ppermute x1, starting transfers between devices, body(): lax.ppermute(slots, 'tile', forward)  4.55 us
    ppermute x1, waiting for transfers between devices, body(): lax.ppermute(left, 'tile', backward)  4.27 us
    pallas_call x1, Pallas kernels, body(): pl.pallas_call(functools.partial(attend_values, fsdp), out_shape=jax.Shap...  3.36 us
    ppermute x2, starting transfers between devices, chip_shift(): lax.ppermute(array, axis, [(i, (i + 2 * step) % count) for i in range(cou...  3.07 us
    ppermute x1, starting transfers between devices, body(): lax.ppermute(right, 'tile', forward)  2.82 us
    select_n x2, other arithmetic, fetch(): mine = jnp.where(pair == 0, first, second)  2.8 us
  transfers between devices with their start and end apart: 15, of which 6 were waited for; matrix products, arithmetic and copies ran while one was open for 11% of the time, Pallas kernels for 11%

profile of v1, /device:TPU:0, one launch (start us, length us, event | category | flops | bytes accessed | tf_op | source)
XLA Modules:
  0.0 54.5 jit_solution(3838596936041051458)
XLA Ops:
  0.0 0.0 copy-start
  0.0 0.0 copy-start.1
  0.0 0.0 copy-start.2
  0.0 0.0 copy-start.3
  0.0 0.0 copy-start.8
  0.0 0.0 copy-start.9
  0.0 1.1 %broadcast_select_fusion.1 = bf16[192,768]{1,0:T(8,128)(2,1)S(1)} fusion(bf16[192,768]{1,0:T(8,128)(2,1)} %wk.1, bf16[192,768]{1,0:T(8,128)(2,1)} %wq.1, pred[]{:T(512)S(6)} %eq.8), kind=kLoop, calls=%fused_computation.4 | loop fusion | flops 147456 | bytes 884737 | tf_op jit(solution)/shard_map/jit(_where)/select_n | solution.py:204
  1.1 3.0 %collective-permute-start.9 = (bf16[192,768]{1,0:T(8,128)(2,1)S(1)}, bf16[192,768]{1,0:T(8,128)(2,1)}, u32[]{:S(2)}, u32[]{:S(2)}) collective-permute-start(bf16[192,768]{1,0:T(8,128)(2,1)S(1)} %broadcast_select_fusion.1), channel_id=1, source_target_pairs={{0,16},{8,24},{16,0},{24,8},{1,17},{9,25},{17,1},{25,9},{2,18},{10... | collective-permute-start | bytes 884744 | tf_op jit(solution)/shard_map/ppermute | solution.py:199
  4.2 1.7 %broadcast_select_fusion = bf16[192,768]{1,0:T(8,128)(2,1)} fusion(bf16[192,768]{1,0:T(8,128)(2,1)} %wv.1, bf16[192,768]{1,0:T(8,128)(2,1)} %wo.1, pred[]{:T(512)S(6)} %eq.8), kind=kLoop, calls=%fused_computation.3 | loop fusion | flops 147456 | bytes 884737 | tf_op jit(solution)/shard_map/jit(_where)/select_n | solution.py:204
  5.9 0.0 collective-permute-start.12
  5.9 0.0 copy-done.8
  5.9 0.0 copy-done.9
  5.9 1.3 %collective-permute-start.1 = (s32[4,64]{1,0:T(4,128)S(1)}, s32[4,64]{1,0:T(4,128)S(1)}, u32[]{:S(2)}, u32[]{:S(2)}) collective-permute-start(s32[4,64]{1,0:T(4,128)S(1)} %select_bitcast_fusion), channel_id=1, source_target_pairs={{1,0},{2,1},{3,2},{4,3},{5,4},{6,5},{7,6},{9,8},{10,9},{11,10},{12... | collective-permute-start | bytes 3080 | tf_op jit(solution)/shard_map/ppermute | solution.py:225
  7.2 4.5 %collective-permute-start = (s32[4,64]{1,0:T(4,128)S(1)}, s32[4,64]{1,0:T(4,128)S(1)}, u32[]{:S(2)}, u32[]{:S(2)}) collective-permute-start(s32[4,64]{1,0:T(4,128)S(1)} %select_bitcast_fusion), channel_id=1, source_target_pairs={{0,1},{1,2},{2,3},{3,4},{4,5},{5,6},{6,7},{8,9},{9,10},{10,11},{11... | collective-permute-start | bytes 3080 | tf_op jit(solution)/shard_map/ppermute | solution.py:225
  11.8 0.3 collective-permute-done.9
  12.1 2.6 %collective-permute-start.10 = (bf16[1,192,768]{2,1,0:T(8,128)(2,1)}, bf16[1,192,768]{2,1,0:T(8,128)(2,1)}, u32[]{:S(2)}, u32[]{:S(2)}) collective-permute-start(bf16[1,192,768]{2,1,0:T(8,128)(2,1)} %bitcast.12), channel_id=1, source_target_pairs={{0,1},{1,0},{2,3},{3,2},{4,5},{5,4},{6,7},{7,6},{8,9},{9,8},{10,11... | collective-permute-start | bytes 884744 | tf_op jit(solution)/shard_map/ppermute | solution.py:180
  14.7 0.0 copy-done
  14.7 0.0 copy-done.1
  14.7 0.0 copy-done.2
  14.7 0.0 copy-done.3
  14.7 0.0 copy-start.7
  14.8 0.2 pad_maximum_fusion
  14.9 0.1 collective-permute-start.8
  15.6 2.0 %collective-permute-done.12 = bf16[192,768]{1,0:T(8,128)(2,1)} collective-permute-done((bf16[192,768]{1,0:T(8,128)(2,1)}, bf16[192,768]{1,0:T(8,128)(2,1)}, u32[]{:S(2)}, u32[]{:S(2)}) %collective-permute-start.12) | collective-permute-done | bytes 294944 | tf_op jit(solution)/shard_map/ppermute | solution.py:199
  17.6 1.7 %collective-permute-start.13 = (bf16[1,192,768]{2,1,0:T(8,128)(2,1)}, bf16[1,192,768]{2,1,0:T(8,128)(2,1)}, u32[]{:S(2)}, u32[]{:S(2)}) collective-permute-start(bf16[1,192,768]{2,1,0:T(8,128)(2,1)} %bitcast.15), channel_id=1, source_target_pairs={{0,1},{1,0},{2,3},{3,2},{4,5},{5,4},{6,7},{7,6},{8,9},{9,8},{10,11... | collective-permute-start | bytes 884744 | tf_op jit(solution)/shard_map/ppermute | solution.py:180
  19.3 0.6 %pad_add_fusion.1.place = s32[4]{0:T(128)} fusion(s32[1]{0:T(128)} %bitcast.2, s32[1]{0:T(128)S(6)} %copy.14, s32[1]{0:T(128)} %bitcast.1, s32[1]{0:T(128)} %bitcast), kind=kLoop, calls=%fused_computation.13 | loop fusion | flops 12 | bytes 32 | tf_op jit(solution)/shard_map/stack | solution.py:219
  19.9 0.0 collective-permute-done.1
  19.9 0.0 collective-permute-done
  19.9 0.7 %pad_add_fusion.slots = s32[4,192]{1,0:T(4,128)} fusion(s32[4,64]{1,0:T(4,128)S(1)} %collective-permute-done.1, s32[4,64]{1,0:T(4,128)S(1)} %select_bitcast_fusion, s32[4,64]{1,0:T(4,128)S(1)} %collective-permute-done), kind=kLoop, calls=%fused_computation.11 | loop fusion | flops 1536 | bytes 6144 | tf_op jit(solution)/shard_map/concatenate | solution.py:224
  20.6 2.3 %pool.1 = (f32[8,768]{1,0:T(8,128)}, f32[8,768]{1,0:T(8,128)}, f32[8,768]{1,0:T(8,128)}) custom-call(s32[4]{0:T(128)} %pad_add_fusion.1.place, s32[4,192]{1,0:T(4,128)} %pad_add_fusion.slots, bf16[256,768]{1,0:T(8,128)(2,1)} %bitcast.23), custom_call_target="tpu_custom_call" | custom-call | tf_op jit(solution)/shard_map/pool/pallas_call | solution.py:228
  22.9 2.8 %collective-permute-start.2 = (f32[8,768]{1,0:T(8,128)}, f32[8,768]{1,0:T(8,128)}, u32[]{:S(2)}, u32[]{:S(2)}) collective-permute-start(f32[8,768]{1,0:T(8,128)} %get-tuple-element.11), channel_id=1, source_target_pairs={{0,1},{1,2},{2,3},{3,4},{4,5},{5,6},{6,7},{8,9},{9,10},{10,11},{11... | collective-permute-start | bytes 73736 | tf_op jit(solution)/shard_map/ppermute | solution.py:243
  25.8 1.3 %collective-permute-start.3 = (f32[8,768]{1,0:T(8,128)}, f32[8,768]{1,0:T(8,128)}, u32[]{:S(2)}, u32[]{:S(2)}) collective-permute-start(f32[8,768]{1,0:T(8,128)} %get-tuple-element.12), channel_id=1, source_target_pairs={{1,0},{2,1},{3,2},{4,3},{5,4},{6,5},{7,6},{9,8},{10,9},{11,10},{12... | collective-permute-start | bytes 73736 | tf_op jit(solution)/shard_map/ppermute | solution.py:244
  27.1 0.0 copy-done.7
  27.1 0.6 %broadcast_in_dim.8.gain = f32[1,768]{1,0:T(1,128)} reshape(f32[768]{0:T(1024)S(1)} %copy-done.7) | data formatting | bytes 6144 | tf_op jit(solution)/shard_map/broadcast_in_dim | solution.py:245
  27.6 0.0 collective-permute-done.2.first
  27.6 4.3 %collective-permute-done.3.second = f32[8,768]{1,0:T(8,128)} collective-permute-done((f32[8,768]{1,0:T(8,128)}, f32[8,768]{1,0:T(8,128)}, u32[]{:S(2)}, u32[]{:S(2)}) %collective-permute-start.3) | collective-permute-done | bytes 24608 | tf_op jit(solution)/shard_map/ppermute | solution.py:244
  31.9 1.5 %norm.1 = bf16[8,768]{1,0:T(8,128)(2,1)} custom-call(f32[8,768]{1,0:T(8,128)} %get-tuple-element.10.own, f32[8,768]{1,0:T(8,128)} %collective-permute-done.2.first, f32[8,768]{1,0:T(8,128)} %collective-permute-done.3.second, f32[1,768]{1,0:T(1,128)} %broadcast_in_dim.8.gain), custom_call_target="tpu_custom_call" | custom-call | tf_op jit(solution)/shard_map/norm/pallas_call | solution.py:235
  33.4 2.9 %collective-permute-start.4 = (bf16[8,768]{1,0:T(8,128)(2,1)}, bf16[8,768]{1,0:T(8,128)(2,1)S(1)}, u32[]{:S(2)}, u32[]{:S(2)}) collective-permute-start(bf16[8,768]{1,0:T(8,128)(2,1)} %norm.1), channel_id=1, source_target_pairs={{0,1},{1,0},{2,3},{3,2},{4,5},{5,4},{6,7},{7,6},{8,9},{9,8},{10,11... | collective-permute-start | bytes 36872 | tf_op jit(solution)/shard_map/ppermute | solution.py:180
  36.3 0.0 collective-permute-done.10
  36.3 0.0 copy-start.6
  36.3 0.0 copy-start.4
  36.3 0.0 copy-start.5
  36.3 1.2 %pad_maximum_fusion.1.near = bf16[2,1,192,768]{3,2,1,0:T(8,128)(2,1)S(1)} fusion(bf16[1,1,192,768]{3,2,1,0:T(8,128)(2,1)} %bitcast.13, bf16[1,1,192,768]{3,2,1,0:T(8,128)(2,1)} %bitcast.11), kind=kLoop, calls=%fused_computation.1 | loop fusion | flops 294912 | bytes 1179648 | tf_op jit(solution)/shard_map/stack | solution.py:206
  37.5 0.1 collective-permute-start.11
  37.6 0.0 collective-permute-done.13
  37.6 1.1 %pad_maximum_fusion.2.near = bf16[2,1,192,768]{3,2,1,0:T(8,128)(2,1)S(1)} fusion(bf16[1,1,192,768]{3,2,1,0:T(8,128)(2,1)} %bitcast.16, bf16[1,1,192,768]{3,2,1,0:T(8,128)(2,1)} %bitcast.14), kind=kLoop, calls=%fused_computation.2 | loop fusion | flops 294912 | bytes 1179648 | tf_op jit(solution)/shard_map/stack | solution.py:206
  38.7 0.6 %collective-permute-start.14 = (bf16[2,1,192,768]{3,2,1,0:T(8,128)(2,1)S(1)}, bf16[2,1,192,768]{3,2,1,0:T(8,128)(2,1)S(1)}, u32[]{:S(2)}, u32[]{:S(2)}) collective-permute-start(bf16[2,1,192,768]{3,2,1,0:T(8,128)(2,1)S(1)} %pad_maximum_fusion.2.near), channel_id=1, source_target_pairs={{0,8},{8,0},{16,24},{24,16},{1,9},{9,1},{17,25},{25,17},{2,10},{10... | collective-permute-start | bytes 1769480 | tf_op jit(solution)/shard_map/ppermute | solution.py:180
  39.2 0.0 copy-done.6
  39.2 0.0 collective-permute-done.4
  39.3 1.6 %collective-permute-start.5 = (bf16[16,768]{1,0:T(8,128)(2,1)S(1)}, bf16[16,768]{1,0:T(8,128)(2,1)S(1)}, u32[]{:S(2)}, u32[]{:S(2)}) collective-permute-start(bf16[16,768]{1,0:T(8,128)(2,1)S(1)} %pad_maximum_fusion.3), channel_id=1, source_target_pairs={{0,2},{1,3},{2,0},{3,1},{4,6},{5,7},{6,4},{7,5},{8,10},{9,11},{10,... | collective-permute-start | bytes 73736 | tf_op jit(solution)/shard_map/ppermute | solution.py:180
  40.9 1.1 %collective-permute-start.6 = (bf16[16,768]{1,0:T(8,128)(2,1)S(1)}, bf16[16,768]{1,0:T(8,128)(2,1)S(1)}, u32[]{:S(2)}, u32[]{:S(2)}) collective-permute-start(bf16[16,768]{1,0:T(8,128)(2,1)S(1)} %pad_maximum_fusion.3), channel_id=1, source_target_pairs={{0,4},{1,5},{2,6},{3,7},{4,0},{5,1},{6,2},{7,3},{8,12},{9,13},{10,... | collective-permute-start | bytes 73736 | tf_op jit(solution)/shard_map/ppermute | solution.py:180
  42.0 1.2 %collective-permute-done.5 = bf16[16,768]{1,0:T(8,128)(2,1)S(1)} collective-permute-done((bf16[16,768]{1,0:T(8,128)(2,1)S(1)}, bf16[16,768]{1,0:T(8,128)(2,1)S(1)}, u32[]{:S(2)}, u32[]{:S(2)}) %collective-permute-start.5) | collective-permute-done | bytes 24608 | tf_op jit(solution)/shard_map/ppermute | solution.py:180
  43.1 2.0 %collective-permute-start.7 = (bf16[16,768]{1,0:T(8,128)(2,1)S(1)}, bf16[16,768]{1,0:T(8,128)(2,1)S(1)}, u32[]{:S(2)}, u32[]{:S(2)}) collective-permute-start(bf16[16,768]{1,0:T(8,128)(2,1)S(1)} %pad_maximum_fusion.3), channel_id=1, source_target_pairs={{0,6},{1,7},{2,4},{3,5},{4,2},{5,3},{6,0},{7,1},{8,14},{9,15},{10,... | collective-permute-start | bytes 73736 | tf_op jit(solution)/shard_map/ppermute | solution.py:180
  45.2 0.7 %collective-permute-done.6 = bf16[16,768]{1,0:T(8,128)(2,1)S(1)} collective-permute-done((bf16[16,768]{1,0:T(8,128)(2,1)S(1)}, bf16[16,768]{1,0:T(8,128)(2,1)S(1)}, u32[]{:S(2)}, u32[]{:S(2)}) %collective-permute-start.6) | collective-permute-done | bytes 24608 | tf_op jit(solution)/shard_map/ppermute | solution.py:180
  45.9 2.9 %collective-permute-done.7 = bf16[16,768]{1,0:T(8,128)(2,1)S(1)} collective-permute-done((bf16[16,768]{1,0:T(8,128)(2,1)S(1)}, bf16[16,768]{1,0:T(8,128)(2,1)S(1)}, u32[]{:S(2)}, u32[]{:S(2)}) %collective-permute-start.7) | collective-permute-done | bytes 24608 | tf_op jit(solution)/shard_map/ppermute | solution.py:180
  48.8 0.0 collective-permute-done.8.sibling
  48.8 0.0 collective-permute-done.11.far
  48.8 0.0 copy-done.4
  48.8 0.0 copy-done.5
  48.8 2.3 %scores.1 = (bf16[512,256]{1,0:T(8,128)(2,1)S(1)}, f32[16,256]{1,0:T(8,128)S(1)}) custom-call(s32[4]{0:T(128)S(1)} %copy-done.5, bf16[64,768]{1,0:T(8,128)(2,1)S(1)} %constant_dynamic-update-slice_fusion.normed, bf16[256,768]{1,0:T(8,128)(2,1)S(1)} %bitcast.24, bf16[192,768]{1,0:T(8,128)(2,1)S(1)} %copy-done, bf16[192,768]{1,0:T(8,128)(2,1)S(1)} %copy-done.1, ...), custom_call_target="tpu_custom_call" | custom-call | tf_op jit(solution)/shard_map/scores/pallas_call | solution.py:257
  51.1 0.0 collective-permute-done.14.far
  51.1 3.4 %values.1 = bf16[256,768]{1,0:T(8,128)(2,1)} custom-call(s32[4]{0:T(128)S(1)} %copy-done.5, bf16[64,768]{1,0:T(8,128)(2,1)S(1)} %constant_dynamic-update-slice_fusion.normed, bf16[512,256]{1,0:T(8,128)(2,1)S(1)} %get-tuple-element.13.weights, f32[16,256]{1,0:T(8,128)S(1)} %get-tuple-element.14.totals, bf16[192,768]{1,0:T(8,128)(2,1)S(1)} %copy-done.3, ...), custom_call_target="tpu_custom_call" | custom-call | tf_op jit(solution)/shard_map/values/pallas_call | solution.py:269
  (7 shorter events, 0.0 us)
Async XLA Ops:
  0.0 14.7 %copy-start = (bf16[192,768]{1,0:T(8,128)(2,1)S(1)}, bf16[192,768]{1,0:T(8,128)(2,1)}, u32[]{:S(2)}) copy-start(bf16[192,768]{1,0:T(8,128)(2,1)} %wk.1) | copy-start | bytes 884740
  0.0 14.7 %copy-start.1 = (bf16[192,768]{1,0:T(8,128)(2,1)S(1)}, bf16[192,768]{1,0:T(8,128)(2,1)}, u32[]{:S(2)}) copy-start(bf16[192,768]{1,0:T(8,128)(2,1)} %wq.1) | copy-start | bytes 884740
  0.0 14.7 %copy-start.2 = (bf16[192,768]{1,0:T(8,128)(2,1)S(1)}, bf16[192,768]{1,0:T(8,128)(2,1)}, u32[]{:S(2)}) copy-start(bf16[192,768]{1,0:T(8,128)(2,1)} %wo.1) | copy-start | bytes 884740
  0.0 14.7 %copy-start.3 = (bf16[192,768]{1,0:T(8,128)(2,1)S(1)}, bf16[192,768]{1,0:T(8,128)(2,1)}, u32[]{:S(2)}) copy-start(bf16[192,768]{1,0:T(8,128)(2,1)} %wv.1) | copy-start | bytes 884740
  0.0 5.9 %copy-start.8 = (s32[1,64,4]{1,2,0:T(4,128)S(1)}, s32[1,64,4]{1,2,0:T(4,128)}, u32[]{:S(2)}) copy-start(s32[1,64,4]{1,2,0:T(4,128)} %param.10) | copy-start | bytes 3076
  0.0 5.9 %copy-start.9 = (s32[1,64,4]{1,2,0:T(4,128)S(1)}, s32[1,64,4]{1,2,0:T(4,128)}, u32[]{:S(2)}) copy-start(s32[1,64,4]{1,2,0:T(4,128)} %param.11) | copy-start | bytes 3076
  1.1 11.0 %collective-permute-start.9 = (bf16[192,768]{1,0:T(8,128)(2,1)S(1)}, bf16[192,768]{1,0:T(8,128)(2,1)}, u32[]{:S(2)}, u32[]{:S(2)}) collective-permute-start(bf16[192,768]{1,0:T(8,128)(2,1)S(1)} %broadcast_select_fusion.1), channel_id=1, source_target_pairs={{0,16},{8,24},{16,0},{24,8},{1,17},{9,25},{17,1},{25,9},{2,18},{10... | collective-permute-start | bytes 884744 | tf_op jit(solution)/shard_map/ppermute | solution.py:199
  5.9 11.7 %collective-permute-start.12 = (bf16[192,768]{1,0:T(8,128)(2,1)}, bf16[192,768]{1,0:T(8,128)(2,1)}, u32[]{:S(2)}, u32[]{:S(2)}) collective-permute-start(bf16[192,768]{1,0:T(8,128)(2,1)} %broadcast_select_fusion), channel_id=1, source_target_pairs={{0,16},{8,24},{16,0},{24,8},{1,17},{9,25},{17,1},{25,9},{2,18},{10... | collective-permute-start | bytes 884744 | tf_op jit(solution)/shard_map/ppermute | solution.py:199
  5.9 14.0 %collective-permute-start.1 = (s32[4,64]{1,0:T(4,128)S(1)}, s32[4,64]{1,0:T(4,128)S(1)}, u32[]{:S(2)}, u32[]{:S(2)}) collective-permute-start(s32[4,64]{1,0:T(4,128)S(1)} %select_bitcast_fusion), channel_id=1, source_target_pairs={{1,0},{2,1},{3,2},{4,3},{5,4},{6,5},{7,6},{9,8},{10,9},{11,10},{12... | collective-permute-start | bytes 3080 | tf_op jit(solution)/shard_map/ppermute | solution.py:225
  7.2 12.7 %collective-permute-start = (s32[4,64]{1,0:T(4,128)S(1)}, s32[4,64]{1,0:T(4,128)S(1)}, u32[]{:S(2)}, u32[]{:S(2)}) collective-permute-start(s32[4,64]{1,0:T(4,128)S(1)} %select_bitcast_fusion), channel_id=1, source_target_pairs={{0,1},{1,2},{2,3},{3,4},{4,5},{5,6},{6,7},{8,9},{9,10},{10,11},{11... | collective-permute-start | bytes 3080 | tf_op jit(solution)/shard_map/ppermute | solution.py:225
  12.1 24.2 %collective-permute-start.10 = (bf16[1,192,768]{2,1,0:T(8,128)(2,1)}, bf16[1,192,768]{2,1,0:T(8,128)(2,1)}, u32[]{:S(2)}, u32[]{:S(2)}) collective-permute-start(bf16[1,192,768]{2,1,0:T(8,128)(2,1)} %bitcast.12), channel_id=1, source_target_pairs={{0,1},{1,0},{2,3},{3,2},{4,5},{5,4},{6,7},{7,6},{8,9},{9,8},{10,11... | collective-permute-start | bytes 884744 | tf_op jit(solution)/shard_map/ppermute | solution.py:180
  14.7 12.3 %copy-start.7 = (f32[768]{0:T(1024)S(1)}, f32[768]{0:T(1024)}, u32[]{:S(2)}) copy-start(f32[768]{0:T(1024)} %param.17) | copy-start | bytes 9220
  14.9 33.9 %collective-permute-start.8 = (bf16[4,192,768]{2,1,0:T(8,128)(2,1)S(1)}, bf16[4,192,768]{2,1,0:T(8,128)(2,1)S(1)}, u32[]{:S(2)}, u32[]{:S(2)}) collective-permute-start(bf16[4,192,768]{2,1,0:T(8,128)(2,1)S(1)} %pad_maximum_fusion), channel_id=1, source_target_pairs={{0,8},{8,0},{16,24},{24,16},{1,9},{9,1},{17,25},{25,17},{2,10},{10... | collective-permute-start | bytes 3538952 | tf_op jit(solution)/shard_map/ppermute | solution.py:180
  17.6 19.9 %collective-permute-start.13 = (bf16[1,192,768]{2,1,0:T(8,128)(2,1)}, bf16[1,192,768]{2,1,0:T(8,128)(2,1)}, u32[]{:S(2)}, u32[]{:S(2)}) collective-permute-start(bf16[1,192,768]{2,1,0:T(8,128)(2,1)} %bitcast.15), channel_id=1, source_target_pairs={{0,1},{1,0},{2,3},{3,2},{4,5},{5,4},{6,7},{7,6},{8,9},{9,8},{10,11... | collective-permute-start | bytes 884744 | tf_op jit(solution)/shard_map/ppermute | solution.py:180
  22.9 4.7 %collective-permute-start.2 = (f32[8,768]{1,0:T(8,128)}, f32[8,768]{1,0:T(8,128)}, u32[]{:S(2)}, u32[]{:S(2)}) collective-permute-start(f32[8,768]{1,0:T(8,128)} %get-tuple-element.11), channel_id=1, source_target_pairs={{0,1},{1,2},{2,3},{3,4},{4,5},{5,6},{6,7},{8,9},{9,10},{10,11},{11... | collective-permute-start | bytes 73736 | tf_op jit(solution)/shard_map/ppermute | solution.py:243
  25.8 6.2 %collective-permute-start.3 = (f32[8,768]{1,0:T(8,128)}, f32[8,768]{1,0:T(8,128)}, u32[]{:S(2)}, u32[]{:S(2)}) collective-permute-start(f32[8,768]{1,0:T(8,128)} %get-tuple-element.12), channel_id=1, source_target_pairs={{1,0},{2,1},{3,2},{4,3},{5,4},{6,5},{7,6},{9,8},{10,9},{11,10},{12... | collective-permute-start | bytes 73736 | tf_op jit(solution)/shard_map/ppermute | solution.py:244
  33.4 5.8 %collective-permute-start.4 = (bf16[8,768]{1,0:T(8,128)(2,1)}, bf16[8,768]{1,0:T(8,128)(2,1)S(1)}, u32[]{:S(2)}, u32[]{:S(2)}) collective-permute-start(bf16[8,768]{1,0:T(8,128)(2,1)} %norm.1), channel_id=1, source_target_pairs={{0,1},{1,0},{2,3},{3,2},{4,5},{5,4},{6,7},{7,6},{8,9},{9,8},{10,11... | collective-permute-start | bytes 36872 | tf_op jit(solution)/shard_map/ppermute | solution.py:180
  36.3 2.9 %copy-start.6 = (bf16[8,768]{1,0:T(8,128)(2,1)S(1)}, bf16[8,768]{1,0:T(8,128)(2,1)}, u32[]{:S(2)}) copy-start(bf16[8,768]{1,0:T(8,128)(2,1)} %norm.1) | copy-start | bytes 36868
  36.3 12.5 %copy-start.4 = (bf16[1,256,768]{2,1,0:T(8,128)(2,1)S(1)}, bf16[1,256,768]{2,1,0:T(8,128)(2,1)}, u32[]{:S(2)}) copy-start(bf16[1,256,768]{2,1,0:T(8,128)(2,1)} %param.9) | copy-start | bytes 1179652
  36.3 12.5 %copy-start.5 = (s32[4]{0:T(128)S(1)}, s32[4]{0:T(128)}, u32[]{:S(2)}) copy-start(s32[4]{0:T(128)} %pad_add_fusion.1.place) | copy-start | bytes 52
  37.5 11.3 %collective-permute-start.11 = (bf16[2,1,192,768]{3,2,1,0:T(8,128)(2,1)S(1)}, bf16[2,1,192,768]{3,2,1,0:T(8,128)(2,1)S(1)}, u32[]{:S(2)}, u32[]{:S(2)}) collective-permute-start(bf16[2,1,192,768]{3,2,1,0:T(8,128)(2,1)S(1)} %pad_maximum_fusion.1.near), channel_id=1, source_target_pairs={{0,8},{8,0},{16,24},{24,16},{1,9},{9,1},{17,25},{25,17},{2,10},{10... | collective-permute-start | bytes 1769480 | tf_op jit(solution)/shard_map/ppermute | solution.py:180
  38.7 12.4 %collective-permute-start.14 = (bf16[2,1,192,768]{3,2,1,0:T(8,128)(2,1)S(1)}, bf16[2,1,192,768]{3,2,1,0:T(8,128)(2,1)S(1)}, u32[]{:S(2)}, u32[]{:S(2)}) collective-permute-start(bf16[2,1,192,768]{3,2,1,0:T(8,128)(2,1)S(1)} %pad_maximum_fusion.2.near), channel_id=1, source_target_pairs={{0,8},{8,0},{16,24},{24,16},{1,9},{9,1},{17,25},{25,17},{2,10},{10... | collective-permute-start | bytes 1769480 | tf_op jit(solution)/shard_map/ppermute | solution.py:180
  39.3 3.9 %collective-permute-start.5 = (bf16[16,768]{1,0:T(8,128)(2,1)S(1)}, bf16[16,768]{1,0:T(8,128)(2,1)S(1)}, u32[]{:S(2)}, u32[]{:S(2)}) collective-permute-start(bf16[16,768]{1,0:T(8,128)(2,1)S(1)} %pad_maximum_fusion.3), channel_id=1, source_target_pairs={{0,2},{1,3},{2,0},{3,1},{4,6},{5,7},{6,4},{7,5},{8,10},{9,11},{10,... | collective-permute-start | bytes 73736 | tf_op jit(solution)/shard_map/ppermute | solution.py:180
  40.9 5.0 %collective-permute-start.6 = (bf16[16,768]{1,0:T(8,128)(2,1)S(1)}, bf16[16,768]{1,0:T(8,128)(2,1)S(1)}, u32[]{:S(2)}, u32[]{:S(2)}) collective-permute-start(bf16[16,768]{1,0:T(8,128)(2,1)S(1)} %pad_maximum_fusion.3), channel_id=1, source_target_pairs={{0,4},{1,5},{2,6},{3,7},{4,0},{5,1},{6,2},{7,3},{8,12},{9,13},{10,... | collective-permute-start | bytes 73736 | tf_op jit(solution)/shard_map/ppermute | solution.py:180
  43.1 5.6 %collective-permute-start.7 = (bf16[16,768]{1,0:T(8,128)(2,1)S(1)}, bf16[16,768]{1,0:T(8,128)(2,1)S(1)}, u32[]{:S(2)}, u32[]{:S(2)}) collective-permute-start(bf16[16,768]{1,0:T(8,128)(2,1)S(1)} %pad_maximum_fusion.3), channel_id=1, source_target_pairs={{0,6},{1,7},{2,4},{3,5},{4,2},{5,3},{6,0},{7,1},{8,14},{9,15},{10,... | collective-permute-start | bytes 73736 | tf_op jit(solution)/shard_map/ppermute | solution.py:180

commit v2 on v1

v2 whole, which is shorter than its diff:
```python
import functools

import jax
import jax.numpy as jnp
from jax import lax
from jax.experimental import pallas as pl
from jax.experimental.pallas import tpu as pltpu
from jax.sharding import PartitionSpec as P

HEADS = 16
NB = 4
REGIONS_PER_KEY = 8
KEY_DILATION = 2
LANE_GROUPS = 2
F32 = jnp.float32
BF16 = jnp.bfloat16


def vmem():
    return pl.BlockSpec(memory_space=pltpu.VMEM)


def smem():
    return pl.BlockSpec(memory_space=pltpu.SMEM)


def anywhere():
    return pl.BlockSpec(memory_space=pl.ANY)


def over(left, right, left_dim, right_dim, precision=None):
    return lax.dot_general(
        left,
        right,
        (((left_dim,), (right_dim,)), ((), ())),
        precision=precision,
        preferred_element_type=F32,
    )


def pool_kernel(before, here, after, tiles, left, own, right):
    count = tiles.shape[0]
    regions = here.shape[0]
    base = lax.axis_index("tile") * count + 1
    row = lax.broadcasted_iota(jnp.int32, (regions, count), 1) + base
    hits, shares = [], []
    for slots in (before, here, after):
        hit = jnp.zeros((regions, count), F32)
        live = jnp.zeros((regions, 1), F32)
        for s in range(NB):
            slot = slots[:, s : s + 1]
            hit += (slot == row).astype(F32)
            live += (slot > 0).astype(F32)
        hits.append(hit.astype(BF16))
        shares.append(1.0 / (jnp.maximum(live, 1.0) * REGIONS_PER_KEY))
    sums = over(jnp.concatenate(hits, axis=0), tiles[...], 1, 0)
    sums = sums * jnp.concatenate(shares, axis=0)
    pooled = jnp.sum(sums.reshape(-1, REGIONS_PER_KEY, sums.shape[1]), axis=1)
    part = regions // REGIONS_PER_KEY
    left[...] = pooled[:part]
    own[...] = pooled[part : 2 * part]
    right[...] = pooled[2 * part :]


def collect(copies, sem):
    started = []
    for n, (src, dst) in enumerate(copies):
        copy = pltpu.make_async_copy(src, dst, sem.at[n])
        copy.start()
        started.append(copy)
    return started


def piece_rows(fsdp, rows):
    me = lax.axis_index("fsdp")
    chips = fsdp // 2
    chip, core = me // 2, me % 2
    owners = [me, 2 * chip + 1 - core]
    for j in range(1, chips):
        source = lax.rem(chip - j + chips, chips)
        owners += [2 * source + core, 2 * source + 1 - core]
    return [pl.multiple_of(owner * rows, rows) for owner in owners]


def sorted_rows(normed):
    keys = normed.shape[0]
    half = keys // KEY_DILATION
    row = lax.broadcasted_iota(jnp.int32, (keys, keys), 0)
    column = lax.broadcasted_iota(jnp.int32, (keys, keys), 1)
    wanted = KEY_DILATION * (row % half) + row // half
    return over((column == wanted).astype(BF16), normed, 1, 0).astype(BF16)


def spread(rows, group, wide):
    half = rows.shape[0] // KEY_DILATION
    heads = HEADS // LANE_GROUPS
    size = wide // heads
    part = rows[:, group * wide : (group + 1) * wide].astype(F32)
    lane = lax.broadcasted_iota(jnp.int32, (half, wide), 1)
    out = []
    for head in range(heads):
        parity = head % KEY_DILATION
        mine = (lane >= head * size) & (lane < (head + 1) * size)
        out.append(jnp.where(mine, part[parity * half : (parity + 1) * half], 0.0))
    return jnp.concatenate(out, axis=0).astype(BF16)


def attend_kernel(fsdp, block, *refs):
    count, normed, tiles = refs[:3]
    pieces = refs[3 : 3 + 3 * fsdp]
    out, held, sem = refs[3 + 3 * fsdp :]
    shard = pieces[0].shape[0]
    begins = piece_rows(fsdp, shard)
    copies = [
        (pieces[w * fsdp + i], held.at[w, pl.ds(begins[i], shard)])
        for w in range(3)
        for i in range(fsdp)
    ]
    started = collect(copies, sem)
    ordered = sorted_rows(normed[...])
    for copy in started:
        copy.wait()
    query = over(tiles[...], held[0], 1, 0).astype(BF16)
    keys = over(ordered, held[1], 1, 0).astype(BF16)
    values = over(ordered, held[2], 1, 0).astype(BF16)
    half = keys.shape[0] // KEY_DILATION
    heads = HEADS // LANE_GROUPS
    wide = keys.shape[1] // LANE_GROUPS
    rows = tiles.shape[0]
    size = wide // heads
    row = lax.broadcasted_iota(jnp.int32, (half, 1), 0)
    valid = [
        (KEY_DILATION * row + parity) * (4 * REGIONS_PER_KEY) < count[0]
        for parity in range(KEY_DILATION)
    ]
    hidden = jnp.concatenate(
        [jnp.where(valid[head % KEY_DILATION], 0.0, -jnp.inf) for head in range(heads)], axis=0
    )
    for group in range(LANE_GROUPS):
        lanes = slice(group * wide, (group + 1) * wide)
        score = over(spread(keys, group, wide), query[:, lanes], 1, 1)
        score = (score * (1.0 / size**0.5) + hidden).reshape(heads, half, rows)
        expo = jnp.exp(score - jnp.max(score, axis=1, keepdims=True))
        share = 1.0 / jnp.sum(expo, axis=1, keepdims=True)
        weight = expo.reshape(heads * half, rows).astype(BF16)
        context = over(spread(values, group, wide), weight, 0, 0).reshape(heads, size, rows)
        out[lanes, :] = (context * share).reshape(wide, rows).astype(BF16)


def project_kernel(fsdp, first, count, last, *refs):
    context = refs[0]
    before = None if first == 0 else refs[1]
    pieces = refs[-1 - count : -1]
    out = refs[-1]
    shard = pieces[0].shape[0]
    begins = piece_rows(fsdp, shard)
    total = None if before is None else before[...]
    for i, piece in enumerate(pieces):
        part = over(context[pl.ds(begins[first + i], shard), :], piece[...], 0, 0)
        total = part if total is None else total + part
    out[...] = total.astype(out.dtype)


def swap(array, axis, offset):
    count = lax.axis_size(axis)
    return lax.ppermute(array, axis, [(i, i ^ offset) for i in range(count)])


def chip_shift(array, axis, step):
    count = lax.axis_size(axis)
    return lax.ppermute(array, axis, [(i, (i + 2 * step) % count) for i in range(count)])


def gather_weight(weight):
    chips = lax.axis_size("fsdp") // 2
    pieces = [weight, swap(weight, "fsdp", 1)]
    for j in range(1, chips):
        near = chip_shift(weight, "fsdp", j)
        pieces += [near, swap(near, "fsdp", 1)]
    return pieces


def body(tiles, nbr_tiles, nbr_mask, tile_count, w_query, w_key, w_value, w_out, key_gain):
    own_tiles = tiles[0]
    rows, width = own_tiles.shape
    tile_devices = lax.axis_size("tile")
    fsdp = lax.axis_size("fsdp")
    regions = nbr_tiles.shape[1]
    block = regions // REGIONS_PER_KEY

    forward = [(i, i + 1) for i in range(tile_devices - 1)]
    backward = [(i + 1, i) for i in range(tile_devices - 1)]
    slots = jnp.where(nbr_mask[0] > 0, nbr_tiles[0] + 1, 0)
    before = lax.ppermute(slots, "tile", forward)
    after = lax.ppermute(slots, "tile", backward)
    part = jax.ShapeDtypeStruct((block, width), F32)
    left, own, right = pl.pallas_call(
        pool_kernel,
        out_shape=(part, part, part),
        in_specs=[vmem()] * 4,
        out_specs=(vmem(), vmem(), vmem()),
        name="pool",
    )(before, slots, after, own_tiles)
    pooled = (
        own + lax.ppermute(right, "tile", forward) + lax.ppermute(left, "tile", backward)
    )
    scale = lax.rsqrt(jnp.mean(pooled * pooled, axis=1, keepdims=True) + 1e-06)
    normed = (pooled * scale * key_gain[None, :]).astype(BF16)
    normed = lax.all_to_all(
        jnp.tile(normed, (tile_devices, 1)), "tile", split_axis=0, concat_axis=0, tiled=True
    )

    keys = gather_weight(w_key)
    values = gather_weight(w_value)
    queries = gather_weight(w_query)
    outs = gather_weight(w_out)

    limit = pltpu.CompilerParams(vmem_limit_bytes=40 * 1024 * 1024)
    context = pl.pallas_call(
        functools.partial(attend_kernel, fsdp, block),
        out_shape=jax.ShapeDtypeStruct((width, rows), BF16),
        in_specs=[smem(), vmem(), vmem()] + [anywhere()] * (3 * fsdp),
        out_specs=vmem(),
        scratch_shapes=[
            pltpu.VMEM((3, width, width), BF16),
            pltpu.SemaphoreType.DMA((3 * fsdp,)),
        ],
        compiler_params=limit,
        name="attend",
    )(tile_count, normed, own_tiles, *queries, *keys, *values)
    partial = pl.pallas_call(
        functools.partial(project_kernel, fsdp, 0, 2, False),
        out_shape=jax.ShapeDtypeStruct((rows, width), F32),
        in_specs=[vmem()] * 3,
        out_specs=vmem(),
        compiler_params=limit,
        name="project_near",
    )(context, *outs[:2])
    attended = pl.pallas_call(
        functools.partial(project_kernel, fsdp, 2, fsdp - 2, True),
        out_shape=jax.ShapeDtypeStruct((rows, width), BF16),
        in_specs=[vmem()] * fsdp,
        out_specs=vmem(),
        compiler_params=limit,
        name="project_far",
    )(context, partial, *outs[2:])
    return attended[None]


def solution(mesh):
    placed = (
        P("fsdp", "tile", None),
        P("fsdp", "tile", None),
        P("fsdp", "tile", None),
        P("fsdp"),
        P("fsdp", None),
        P("fsdp", None),
        P("fsdp", None),
        P("fsdp", None),
        P(),
    )
    return jax.shard_map(
        body, mesh=mesh, in_specs=placed, out_specs=P("fsdp", "tile", None), check_vma=False
    )
```

time: 54.9 us -> 68.1 us (1.24)
  waiting for transfers between devices: 11.3 us -> 26.2 us
  other arithmetic: 6.51 us -> 2.37 us
  local copies, waits for them, and re-layouts: 0.63 us -> 2.46 us
  starting transfers between devices: 25.7 us -> 26.4 us
    ppermute x9 -> x8, starting transfers between devices: 12.7 us -> 1.12 us  [swap(): return lax.ppermute(array, axis, [(i, i ^ offset) for i in range(count)])]
    ppermute x2 -> x4, waiting for transfers between devices: 2.31 us -> 12.9 us  [chip_shift(): lax.ppermute(array, axis, [(i, (i + 2 * step) % count) for i in range(cou...]
    all_to_all x0 -> x1, starting transfers between devices: none -> 8.61 us  [body(): lax.all_to_all(jnp.tile(normed, (tile_devices, 1)), 'tile', split_axis=0,...]
    all_to_all x0 -> x1, waiting for transfers between devices: none -> 6.52 us  [body(): lax.all_to_all(jnp.tile(normed, (tile_devices, 1)), 'tile', split_axis=0,...]
    ppermute x9 -> x8, waiting for transfers between devices: 4.76 us -> 0.02 us  [swap(): return lax.ppermute(array, axis, [(i, i ^ offset) for i in range(count)])]
    another operation x4 -> x0, other arithmetic: 3.03 us -> none  [the longest x2 2.27 us: fetch(): both = jnp.stack([near, swap(near, 'tile', 1)])]
    select_n x2 -> x1, other arithmetic: 2.8 us -> 0.01 us  [body(): slots = jnp.where(nbr_mask[0] > 0, nbr_tiles[0] + 1, 0)]
    ppermute x2 -> x4, starting transfers between devices: 3.07 us -> 5.11 us  [chip_shift(): lax.ppermute(array, axis, [(i, (i + 2 * step) % count) for i in range(cou...]
  transfers between devices with their start and end apart: 15 -> 17, of which waited for: 6 -> 7; matrix products, arithmetic and copies ran while one was open for 11% -> 5% of each run, Pallas kernels for 11% -> 10%
where the time goes in v2:
time: 68.1 us; the launch traced here: 67.5 us
  starting transfers between devices  26.4 us (39%)
  waiting for transfers between devices  26.2 us (38%)
  Pallas kernels  9.22 us (14%)
  local copies, waits for them, and re-layouts  2.46 us (4%)
  other arithmetic  2.37 us (3%)
  between operations  0.83 us (1%)
    ppermute x4, waiting for transfers between devices, chip_shift(): lax.ppermute(array, axis, [(i, (i + 2 * step) % count) for i in range(cou...  12.9 us
    all_to_all x1, starting transfers between devices, body(): lax.all_to_all(jnp.tile(normed, (tile_devices, 1)), 'tile', split_axis=0,...  8.61 us
    all_to_all x1, waiting for transfers between devices, body(): lax.all_to_all(jnp.tile(normed, (tile_devices, 1)), 'tile', split_axis=0,...  6.52 us
    ppermute x4, starting transfers between devices, chip_shift(): lax.ppermute(array, axis, [(i, (i + 2 * step) % count) for i in range(cou...  5.11 us
    ppermute x1, waiting for transfers between devices, body(): lax.ppermute(left, 'tile', backward)  4.92 us
    ppermute x1, starting transfers between devices, body(): before = lax.ppermute(slots, 'tile', forward)  4.55 us
    ppermute x1, starting transfers between devices, body(): lax.ppermute(right, 'tile', forward)  4.41 us
    pallas_call x1, Pallas kernels, body(): pl.pallas_call(functools.partial(attend_kernel, fsdp, block), out_shape=j...  3.4 us
  transfers between devices with their start and end apart: 17, of which 7 were waited for; matrix products, arithmetic and copies ran while one was open for 5% of the time, Pallas kernels for 10%

profile of v2, /device:TPU:0, one launch (start us, length us, event | category | flops | bytes accessed | tf_op | source)
XLA Modules:
  0.0 67.5 jit_solution(6082318861779314795)
XLA Ops:
  0.0 0.0 copy-start.9
  0.0 0.5 collective-permute-start.4
  0.5 2.6 %collective-permute-start.5 = (bf16[192,768]{1,0:T(8,128)(2,1)}, bf16[192,768]{1,0:T(8,128)(2,1)S(1)}, u32[]{:S(2)}, u32[]{:S(2)}) collective-permute-start(bf16[192,768]{1,0:T(8,128)(2,1)} %refs_3_.1), channel_id=1, source_target_pairs={{0,16},{8,24},{16,0},{24,8},{1,17},{9,25},{17,1},{25,9},{2,18},{10... | collective-permute-start | bytes 884744 | tf_op jit(solution)/shard_map/ppermute | solution.py:171
  3.0 0.7 %broadcast_add_fusion = s32[1,64,4]{1,2,0:T(4,128)S(1)} fusion(s32[1,64,4]{1,2,0:T(4,128)} %param.10), kind=kLoop, calls=%fused_computation.5 | loop fusion | flops 256 | bytes 2048 | tf_op jit(solution)/shard_map/add | solution.py:193
  3.7 0.0 copy-done.9
  3.7 0.1 copy.15
  3.8 0.0 copy-start.2
  3.9 0.1 copy.16
  3.9 0.0 copy-start.8
  4.0 0.0 copy-start.5
  4.0 1.3 %collective-permute-start.1 = (s32[64,4]{1,0:T(8,128)S(1)}, s32[64,4]{1,0:T(8,128)S(1)}, u32[]{:S(2)}, u32[]{:S(2)}) collective-permute-start(s32[64,4]{1,0:T(8,128)S(1)} %select_bitcast_fusion.here), channel_id=1, source_target_pairs={{1,0},{2,1},{3,2},{4,3},{5,4},{6,5},{7,6},{9,8},{10,9},{11,10},{12... | collective-permute-start | bytes 3080 | tf_op jit(solution)/shard_map/ppermute | solution.py:195
  5.3 4.5 %collective-permute-start = (s32[64,4]{1,0:T(8,128)S(1)}, s32[64,4]{1,0:T(8,128)S(1)}, u32[]{:S(2)}, u32[]{:S(2)}) collective-permute-start(s32[64,4]{1,0:T(8,128)S(1)} %select_bitcast_fusion.here), channel_id=1, source_target_pairs={{0,1},{1,2},{2,3},{3,4},{4,5},{5,6},{6,7},{8,9},{9,10},{10,11},{11... | collective-permute-start | bytes 3080 | tf_op jit(solution)/shard_map/ppermute | solution.py:194
  9.8 0.0 collective-permute-done.1.after
  9.8 0.0 copy-start.6
  9.8 1.6 %collective-permute-done.before = s32[64,4]{1,0:T(8,128)S(1)} collective-permute-done((s32[64,4]{1,0:T(8,128)S(1)}, s32[64,4]{1,0:T(8,128)S(1)}, u32[]{:S(2)}, u32[]{:S(2)}) %collective-permute-start) | collective-permute-done | bytes 1056 | tf_op jit(solution)/shard_map/ppermute | solution.py:194
  11.4 0.0 copy-start.7
  11.4 0.0 copy-done.5
  11.4 0.0 copy-done.6
  11.4 0.6 copy-done.7
  12.0 0.0 copy-start
  12.0 2.2 %pool.1 = (f32[8,768]{1,0:T(8,128)}, f32[8,768]{1,0:T(8,128)}, f32[8,768]{1,0:T(8,128)}) custom-call(s32[64,4]{1,0:T(8,128)} %copy-done.7, s32[64,4]{1,0:T(8,128)} %copy-done.5, s32[64,4]{1,0:T(8,128)} %copy-done.6, bf16[256,768]{1,0:T(8,128)(2,1)} %bitcast.5), custom_call_target="tpu_custom_call" | custom-call | tf_op jit(solution)/shard_map/pool/pallas_call | solution.py:197
  14.3 0.0 copy-start.1
  14.3 4.4 %collective-permute-start.2 = (f32[8,768]{1,0:T(8,128)}, f32[8,768]{1,0:T(8,128)S(1)}, u32[]{:S(2)}, u32[]{:S(2)}) collective-permute-start(f32[8,768]{1,0:T(8,128)} %get-tuple-element.9), channel_id=1, source_target_pairs={{0,1},{1,2},{2,3},{3,4},{4,5},{5,6},{6,7},{8,9},{9,10},{10,11},{11... | collective-permute-start | bytes 73736 | tf_op jit(solution)/shard_map/ppermute | solution.py:205
  18.7 1.3 %collective-permute-start.3 = (f32[8,768]{1,0:T(8,128)}, f32[8,768]{1,0:T(8,128)S(1)}, u32[]{:S(2)}, u32[]{:S(2)}) collective-permute-start(f32[8,768]{1,0:T(8,128)} %get-tuple-element.10), channel_id=1, source_target_pairs={{1,0},{2,1},{3,2},{4,3},{5,4},{6,5},{7,6},{9,8},{10,9},{11,10},{12... | collective-permute-start | bytes 73736 | tf_op jit(solution)/shard_map/ppermute | solution.py:205
  20.0 0.0 copy-done.2
  20.0 0.1 collective-permute-start.7
  20.1 0.3 collective-permute-done.2
  20.4 0.5 collective-permute-start.8
  20.9 4.9 %collective-permute-done.3 = f32[8,768]{1,0:T(8,128)S(1)} collective-permute-done((f32[8,768]{1,0:T(8,128)}, f32[8,768]{1,0:T(8,128)S(1)}, u32[]{:S(2)}, u32[]{:S(2)}) %collective-permute-start.3) | collective-permute-done | bytes 24608 | tf_op jit(solution)/shard_map/ppermute | solution.py:205
  25.8 0.0 collective-permute-start.10
  25.8 0.0 collective-permute-done.4.refs_4_
  25.8 0.5 collective-permute-start.11
  26.3 0.0 collective-permute-done.5.refs_5_
  26.3 1.5 %collective-permute-start.14 = (bf16[192,768]{1,0:T(8,128)(2,1)}, bf16[192,768]{1,0:T(8,128)(2,1)}, u32[]{:S(2)}, u32[]{:S(2)}) collective-permute-start(bf16[192,768]{1,0:T(8,128)(2,1)} %refs_1_.1), channel_id=1, source_target_pairs={{0,16},{8,24},{16,0},{24,8},{1,17},{9,25},{17,1},{25,9},{2,18},{10... | collective-permute-start | bytes 884744 | tf_op jit(solution)/shard_map/ppermute | solution.py:171
  27.9 0.9 %multiply_reduce_fusion = f32[8]{0:T(128)S(1)} fusion(f32[8,768]{1,0:T(8,128)S(1)} %collective-permute-done.3, f32[8,768]{1,0:T(8,128)} %get-tuple-element.8, f32[8,768]{1,0:T(8,128)S(1)} %collective-permute-done.2), kind=kLoop, calls=%fused_computation.2 | loop fusion | flops 24568 | bytes 73760 | tf_op jit(solution)/shard_map/reduce_sum | solution.py:207
  28.7 0.0 collective-permute-done.7.refs_8_
  28.7 0.1 collective-permute-start.13
  28.8 1.0 %collective-permute-done.8.refs_9_ = bf16[192,768]{1,0:T(8,128)(2,1)S(1)} collective-permute-done((bf16[192,768]{1,0:T(8,128)(2,1)S(1)}, bf16[192,768]{1,0:T(8,128)(2,1)S(1)}, u32[]{:S(2)}, u32[]{:S(2)}) %collective-permute-start.8) | collective-permute-done | bytes 294944 | tf_op jit(solution)/shard_map/ppermute | solution.py:171
  29.8 0.0 collective-permute-start.6
  29.8 0.0 collective-permute-done.10.refs_12_
  29.8 0.5 collective-permute-start.9
  30.3 5.8 %collective-permute-done.11.refs_13_ = bf16[192,768]{1,0:T(8,128)(2,1)S(1)} collective-permute-done((bf16[192,768]{1,0:T(8,128)(2,1)}, bf16[192,768]{1,0:T(8,128)(2,1)S(1)}, u32[]{:S(2)}, u32[]{:S(2)}) %collective-permute-start.11) | collective-permute-done | bytes 294944 | tf_op jit(solution)/shard_map/ppermute | solution.py:171
  36.1 0.0 collective-permute-start.12
  36.1 6.1 %collective-permute-done.14.refs_2_ = bf16[192,768]{1,0:T(8,128)(2,1)} collective-permute-done((bf16[192,768]{1,0:T(8,128)(2,1)}, bf16[192,768]{1,0:T(8,128)(2,1)}, u32[]{:S(2)}, u32[]{:S(2)}) %collective-permute-start.14) | collective-permute-done | bytes 294944 | tf_op jit(solution)/shard_map/ppermute | solution.py:171
  42.2 0.0 collective-permute-start.15
  42.2 0.0 copy-done.8
  42.2 0.8 %multiply_convert_fusion = bf16[8,768]{1,0:T(8,128)(2,1)S(1)} fusion(f32[768]{0:T(1024)S(1)} %copy-done.8, f32[8]{0:T(128)S(1)} %add_rsqrt_fusion, f32[8,768]{1,0:T(8,128)S(1)} %collective-permute-done.3, f32[8,768]{1,0:T(8,128)} %get-tuple-element.8, f32[8,768]{1,0:T(8,128)S(1)} %collective-permute-done.2), kind=kLoop, calls=%fused_computation.1 | loop fusion | flops 30720 | bytes 89120 | tf_op jit(solution)/shard_map/convert_element_type | solution.py:208
  43.0 0.6 tile.2
  43.7 8.6 %all-to-all-start = ((bf16[8,8,768]{2,1,0:T(8,128)(2,1)}), bf16[8,8,768]{2,1,0:T(8,128)(2,1)S(1)}, u32[]{:S(2)}, u32[]{:S(2)}) async-start(bf16[8,8,768]{2,1,0:T(8,128)(2,1)} %tile.2), calls=%async_computation | async-start | bytes 196608 | tf_op jit(solution)/shard_map/all_to_all | solution.py:209
  53.0 6.5 %all-to-all-done = bf16[8,8,768]{2,1,0:T(8,128)(2,1)S(1)} async-done(((bf16[8,8,768]{2,1,0:T(8,128)(2,1)}), bf16[8,8,768]{2,1,0:T(8,128)(2,1)S(1)}, u32[]{:S(2)}, u32[]{:S(2)}) %all-to-all-start) | async-done | bytes 98336 | tf_op jit(solution)/shard_map/all_to_all | solution.py:209
  59.5 0.0 collective-permute-done.6.refs_6_
  59.5 0.0 collective-permute-done.9.refs_10_
  59.5 0.0 collective-permute-done.12.refs_14_
  59.5 0.0 copy-done
  59.5 0.0 copy-done.1
  59.5 0.0 copy-start.3
  59.5 1.0 %copy-done.3 = bf16[192,768]{1,0:T(8,128)(2,1)S(1)} copy-done((bf16[192,768]{1,0:T(8,128)(2,1)S(1)}, bf16[192,768]{1,0:T(8,128)(2,1)}, u32[]{:S(2)}) %copy-start.3) | copy-done | bytes 294936
  60.5 0.0 copy-start.4
  60.5 3.4 %attend.1.refs_0_ = bf16[768,256]{1,0:T(8,128)(2,1)S(1)} custom-call(s32[1]{0:T(128)S(6)} %copy.17.refs_0_, bf16[64,768]{1,0:T(8,128)(2,1)S(1)} %bitcast.7, bf16[256,768]{1,0:T(8,128)(2,1)S(1)} %bitcast.6, bf16[192,768]{1,0:T(8,128)(2,1)S(1)} %copy-done.1, bf16[192,768]{1,0:T(8,128)(2,1)S(1)} %collective-permute-done.4.refs_4_, ...), custom_call_target="tpu_custom_call" | custom-call | tf_op jit(solution)/shard_map/attend/pallas_call | solution.py:219
  63.9 0.0 collective-permute-done.13.refs_2_
  63.9 0.0 copy-done.4
  63.9 1.4 %project_near.1.refs_1_ = f32[256,768]{1,0:T(8,128)S(1)} custom-call(bf16[768,256]{1,0:T(8,128)(2,1)S(1)} %attend.1.refs_0_, bf16[192,768]{1,0:T(8,128)(2,1)S(1)} %copy-done.4, bf16[192,768]{1,0:T(8,128)(2,1)} %collective-permute-done.13.refs_2_), custom_call_target="tpu_custom_call" | custom-call | tf_op jit(solution)/shard_map/project_near/pallas_call | solution.py:231
  65.3 0.0 collective-permute-done.15.refs_3_
  65.3 2.2 %project_far.1 = bf16[256,768]{1,0:T(8,128)(2,1)} custom-call(bf16[768,256]{1,0:T(8,128)(2,1)S(1)} %attend.1.refs_0_, f32[256,768]{1,0:T(8,128)S(1)} %project_near.1.refs_1_, bf16[192,768]{1,0:T(8,128)(2,1)} %collective-permute-done.14.refs_2_, bf16[192,768]{1,0:T(8,128)(2,1)} %collective-permute-done.15.refs_3_), custom_call_target="tpu_custom_call" | custom-call | tf_op jit(solution)/shard_map/project_far/pallas_call | solution.py:239
  (3 shorter events, 0.0 us)
Async XLA Ops:
  0.0 3.7 %copy-start.9 = (s32[1,64,4]{1,2,0:T(4,128)S(1)}, s32[1,64,4]{1,2,0:T(4,128)}, u32[]{:S(2)}) copy-start(s32[1,64,4]{1,2,0:T(4,128)} %param.11) | copy-start | bytes 3076
  0.0 25.8 %collective-permute-start.4 = (bf16[192,768]{1,0:T(8,128)(2,1)}, bf16[192,768]{1,0:T(8,128)(2,1)S(1)}, u32[]{:S(2)}, u32[]{:S(2)}) collective-permute-start(bf16[192,768]{1,0:T(8,128)(2,1)} %refs_3_.1), channel_id=1, source_target_pairs={{0,8},{8,0},{16,24},{24,16},{1,9},{9,1},{17,25},{25,17},{2,10},{10... | collective-permute-start | bytes 884744 | tf_op jit(solution)/shard_map/ppermute | solution.py:166
  0.5 25.9 %collective-permute-start.5 = (bf16[192,768]{1,0:T(8,128)(2,1)}, bf16[192,768]{1,0:T(8,128)(2,1)S(1)}, u32[]{:S(2)}, u32[]{:S(2)}) collective-permute-start(bf16[192,768]{1,0:T(8,128)(2,1)} %refs_3_.1), channel_id=1, source_target_pairs={{0,16},{8,24},{16,0},{24,8},{1,17},{9,25},{17,1},{25,9},{2,18},{10... | collective-permute-start | bytes 884744 | tf_op jit(solution)/shard_map/ppermute | solution.py:171
  3.8 16.1 %copy-start.2 = (bf16[192,768]{1,0:T(8,128)(2,1)S(1)}, bf16[192,768]{1,0:T(8,128)(2,1)}, u32[]{:S(2)}) copy-start(bf16[192,768]{1,0:T(8,128)(2,1)} %refs_7_.1) | copy-start | bytes 884740
  3.9 38.3 %copy-start.8 = (f32[768]{0:T(1024)S(1)}, f32[768]{0:T(1024)}, u32[]{:S(2)}) copy-start(f32[768]{0:T(1024)} %param.17) | copy-start | bytes 9220
  4.0 7.4 %copy-start.5 = (s32[64,4]{1,0:T(8,128)}, s32[64,4]{1,0:T(8,128)S(1)}, u32[]{:S(2)}) copy-start(s32[64,4]{1,0:T(8,128)S(1)} %select_bitcast_fusion.here) | copy-start | bytes 3076
  4.0 5.9 %collective-permute-start.1 = (s32[64,4]{1,0:T(8,128)S(1)}, s32[64,4]{1,0:T(8,128)S(1)}, u32[]{:S(2)}, u32[]{:S(2)}) collective-permute-start(s32[64,4]{1,0:T(8,128)S(1)} %select_bitcast_fusion.here), channel_id=1, source_target_pairs={{1,0},{2,1},{3,2},{4,3},{5,4},{6,5},{7,6},{9,8},{10,9},{11,10},{12... | collective-permute-start | bytes 3080 | tf_op jit(solution)/shard_map/ppermute | solution.py:195
  5.3 6.1 %collective-permute-start = (s32[64,4]{1,0:T(8,128)S(1)}, s32[64,4]{1,0:T(8,128)S(1)}, u32[]{:S(2)}, u32[]{:S(2)}) collective-permute-start(s32[64,4]{1,0:T(8,128)S(1)} %select_bitcast_fusion.here), channel_id=1, source_target_pairs={{0,1},{1,2},{2,3},{3,4},{4,5},{5,6},{6,7},{8,9},{9,10},{10,11},{11... | collective-permute-start | bytes 3080 | tf_op jit(solution)/shard_map/ppermute | solution.py:194
  9.8 1.6 %copy-start.6 = (s32[64,4]{1,0:T(8,128)}, s32[64,4]{1,0:T(8,128)S(1)}, u32[]{:S(2)}) copy-start(s32[64,4]{1,0:T(8,128)S(1)} %collective-permute-done.1.after) | copy-start | bytes 3076
  11.4 0.6 copy-start.7
  12.0 47.5 %copy-start = (bf16[1,256,768]{2,1,0:T(8,128)(2,1)S(1)}, bf16[1,256,768]{2,1,0:T(8,128)(2,1)}, u32[]{:S(2)}) copy-start(bf16[1,256,768]{2,1,0:T(8,128)(2,1)} %param.9) | copy-start | bytes 1179652
  14.3 45.2 %copy-start.1 = (bf16[192,768]{1,0:T(8,128)(2,1)S(1)}, bf16[192,768]{1,0:T(8,128)(2,1)}, u32[]{:S(2)}) copy-start(bf16[192,768]{1,0:T(8,128)(2,1)} %refs_3_.1) | copy-start | bytes 884740
  14.3 6.1 %collective-permute-start.2 = (f32[8,768]{1,0:T(8,128)}, f32[8,768]{1,0:T(8,128)S(1)}, u32[]{:S(2)}, u32[]{:S(2)}) collective-permute-start(f32[8,768]{1,0:T(8,128)} %get-tuple-element.9), channel_id=1, source_target_pairs={{0,1},{1,2},{2,3},{3,4},{4,5},{5,6},{6,7},{8,9},{9,10},{10,11},{11... | collective-permute-start | bytes 73736 | tf_op jit(solution)/shard_map/ppermute | solution.py:205
  18.7 7.1 %collective-permute-start.3 = (f32[8,768]{1,0:T(8,128)}, f32[8,768]{1,0:T(8,128)S(1)}, u32[]{:S(2)}, u32[]{:S(2)}) collective-permute-start(f32[8,768]{1,0:T(8,128)} %get-tuple-element.10), channel_id=1, source_target_pairs={{1,0},{2,1},{3,2},{4,3},{5,4},{6,5},{7,6},{9,8},{10,9},{11,10},{12... | collective-permute-start | bytes 73736 | tf_op jit(solution)/shard_map/ppermute | solution.py:205
  20.0 8.7 %collective-permute-start.7 = (bf16[192,768]{1,0:T(8,128)(2,1)S(1)}, bf16[192,768]{1,0:T(8,128)(2,1)S(1)}, u32[]{:S(2)}, u32[]{:S(2)}) collective-permute-start(bf16[192,768]{1,0:T(8,128)(2,1)S(1)} %copy-done.2), channel_id=1, source_target_pairs={{0,8},{8,0},{16,24},{24,16},{1,9},{9,1},{17,25},{25,17},{2,10},{10... | collective-permute-start | bytes 884744 | tf_op jit(solution)/shard_map/ppermute | solution.py:166
  20.4 9.4 %collective-permute-start.8 = (bf16[192,768]{1,0:T(8,128)(2,1)S(1)}, bf16[192,768]{1,0:T(8,128)(2,1)S(1)}, u32[]{:S(2)}, u32[]{:S(2)}) collective-permute-start(bf16[192,768]{1,0:T(8,128)(2,1)S(1)} %copy-done.2), channel_id=1, source_target_pairs={{0,16},{8,24},{16,0},{24,8},{1,17},{9,25},{17,1},{25,9},{2,18},{10... | collective-permute-start | bytes 884744 | tf_op jit(solution)/shard_map/ppermute | solution.py:171
  25.8 4.0 %collective-permute-start.10 = (bf16[192,768]{1,0:T(8,128)(2,1)}, bf16[192,768]{1,0:T(8,128)(2,1)S(1)}, u32[]{:S(2)}, u32[]{:S(2)}) collective-permute-start(bf16[192,768]{1,0:T(8,128)(2,1)} %refs_11_.1), channel_id=1, source_target_pairs={{0,8},{8,0},{16,24},{24,16},{1,9},{9,1},{17,25},{25,17},{2,10},{10... | collective-permute-start | bytes 884744 | tf_op jit(solution)/shard_map/ppermute | solution.py:166
  25.8 10.3 %collective-permute-start.11 = (bf16[192,768]{1,0:T(8,128)(2,1)}, bf16[192,768]{1,0:T(8,128)(2,1)S(1)}, u32[]{:S(2)}, u32[]{:S(2)}) collective-permute-start(bf16[192,768]{1,0:T(8,128)(2,1)} %refs_11_.1), channel_id=1, source_target_pairs={{0,16},{8,24},{16,0},{24,8},{1,17},{9,25},{17,1},{25,9},{2,18},{10... | collective-permute-start | bytes 884744 | tf_op jit(solution)/shard_map/ppermute | solution.py:171
  26.3 15.9 %collective-permute-start.14 = (bf16[192,768]{1,0:T(8,128)(2,1)}, bf16[192,768]{1,0:T(8,128)(2,1)}, u32[]{:S(2)}, u32[]{:S(2)}) collective-permute-start(bf16[192,768]{1,0:T(8,128)(2,1)} %refs_1_.1), channel_id=1, source_target_pairs={{0,16},{8,24},{16,0},{24,8},{1,17},{9,25},{17,1},{25,9},{2,18},{10... | collective-permute-start | bytes 884744 | tf_op jit(solution)/shard_map/ppermute | solution.py:171
  28.7 35.2 %collective-permute-start.13 = (bf16[192,768]{1,0:T(8,128)(2,1)}, bf16[192,768]{1,0:T(8,128)(2,1)}, u32[]{:S(2)}, u32[]{:S(2)}) collective-permute-start(bf16[192,768]{1,0:T(8,128)(2,1)} %refs_1_.1), channel_id=1, source_target_pairs={{0,8},{8,0},{16,24},{24,16},{1,9},{9,1},{17,25},{25,17},{2,10},{10... | collective-permute-start | bytes 884744 | tf_op jit(solution)/shard_map/ppermute | solution.py:166
  29.8 29.7 %collective-permute-start.6 = (bf16[192,768]{1,0:T(8,128)(2,1)S(1)}, bf16[192,768]{1,0:T(8,128)(2,1)S(1)}, u32[]{:S(2)}, u32[]{:S(2)}) collective-permute-start(bf16[192,768]{1,0:T(8,128)(2,1)S(1)} %collective-permute-done.5.refs_5_), channel_id=1, source_target_pairs={{0,8},{8,0},{16,24},{24,16},{1,9},{9,1},{17,25},{25,17},{2,10},{10... | collective-permute-start | bytes 884744 | tf_op jit(solution)/shard_map/ppermute | solution.py:166
  29.8 29.7 %collective-permute-start.9 = (bf16[192,768]{1,0:T(8,128)(2,1)S(1)}, bf16[192,768]{1,0:T(8,128)(2,1)S(1)}, u32[]{:S(2)}, u32[]{:S(2)}) collective-permute-start(bf16[192,768]{1,0:T(8,128)(2,1)S(1)} %collective-permute-done.8.refs_9_), channel_id=1, source_target_pairs={{0,8},{8,0},{16,24},{24,16},{1,9},{9,1},{17,25},{25,17},{2,10},{10... | collective-permute-start | bytes 884744 | tf_op jit(solution)/shard_map/ppermute | solution.py:166
  36.1 23.4 %collective-permute-start.12 = (bf16[192,768]{1,0:T(8,128)(2,1)S(1)}, bf16[192,768]{1,0:T(8,128)(2,1)}, u32[]{:S(2)}, u32[]{:S(2)}) collective-permute-start(bf16[192,768]{1,0:T(8,128)(2,1)S(1)} %collective-permute-done.11.refs_13_), channel_id=1, source_target_pairs={{0,8},{8,0},{16,24},{24,16},{1,9},{9,1},{17,25},{25,17},{2,10},{10... | collective-permute-start | bytes 884744 | tf_op jit(solution)/shard_map/ppermute | solution.py:166
  42.2 23.1 %collective-permute-start.15 = (bf16[192,768]{1,0:T(8,128)(2,1)}, bf16[192,768]{1,0:T(8,128)(2,1)}, u32[]{:S(2)}, u32[]{:S(2)}) collective-permute-start(bf16[192,768]{1,0:T(8,128)(2,1)} %collective-permute-done.14.refs_2_), channel_id=1, source_target_pairs={{0,8},{8,0},{16,24},{24,16},{1,9},{9,1},{17,25},{25,17},{2,10},{10... | collective-permute-start | bytes 884744 | tf_op jit(solution)/shard_map/ppermute | solution.py:166
  43.7 15.8 %all-to-all-start = ((bf16[8,8,768]{2,1,0:T(8,128)(2,1)}), bf16[8,8,768]{2,1,0:T(8,128)(2,1)S(1)}, u32[]{:S(2)}, u32[]{:S(2)}) async-start(bf16[8,8,768]{2,1,0:T(8,128)(2,1)} %tile.2), calls=%async_computation | async-start | bytes 196608 | tf_op jit(solution)/shard_map/all_to_all | solution.py:209
  59.5 1.0 %copy-start.3 = (bf16[192,768]{1,0:T(8,128)(2,1)S(1)}, bf16[192,768]{1,0:T(8,128)(2,1)}, u32[]{:S(2)}) copy-start(bf16[192,768]{1,0:T(8,128)(2,1)} %refs_11_.1) | copy-start | bytes 884740
  60.5 3.4 %copy-start.4 = (bf16[192,768]{1,0:T(8,128)(2,1)S(1)}, bf16[192,768]{1,0:T(8,128)(2,1)}, u32[]{:S(2)}) copy-start(bf16[192,768]{1,0:T(8,128)(2,1)} %refs_1_.1) | copy-start | bytes 884740

commit v3 on v2

v3 whole, which is shorter than its diff:
```python
import functools

import jax
import jax.numpy as jnp
from jax import lax
from jax.experimental import pallas as pl
from jax.experimental.pallas import tpu as pltpu
from jax.sharding import PartitionSpec as P

HEADS = 16
NB = 4
REGIONS_PER_KEY = 8
KEY_DILATION = 2
LANE_GROUPS = 2
F32 = jnp.float32
BF16 = jnp.bfloat16


def vmem():
    return pl.BlockSpec(memory_space=pltpu.VMEM)


def smem():
    return pl.BlockSpec(memory_space=pltpu.SMEM)


def anywhere():
    return pl.BlockSpec(memory_space=pl.ANY)


def over(left, right, left_dim, right_dim, precision=None):
    return lax.dot_general(
        left,
        right,
        (((left_dim,), (right_dim,)), ((), ())),
        precision=precision,
        preferred_element_type=F32,
    )


def pool_kernel(here, mate, other, tiles, out):
    count = tiles.shape[0]
    regions = here.shape[0]
    base = lax.axis_index("tile") * count + 1
    row = lax.broadcasted_iota(jnp.int32, (regions, count), 1) + base
    hits, shares = [], []
    for slots in (here, mate, other):
        hit = jnp.zeros((regions, count), F32)
        live = jnp.zeros((regions, 1), F32)
        for s in range(NB):
            slot = slots[:, s : s + 1]
            hit += (slot == row).astype(F32)
            live += (slot > 0).astype(F32)
        hits.append(hit.astype(BF16))
        shares.append(1.0 / (jnp.maximum(live, 1.0) * REGIONS_PER_KEY))
    sums = over(jnp.concatenate(hits, axis=0), tiles[...], 1, 0)
    sums = sums * jnp.concatenate(shares, axis=0)
    out[...] = jnp.sum(sums.reshape(-1, REGIONS_PER_KEY, sums.shape[1]), axis=1)


def pair_kernel(mine, theirs, out):
    block = mine.shape[0] // 3
    first = mine[:block] + theirs[block : 2 * block]
    second = mine[block : 2 * block] + theirs[:block]
    inner = jnp.concatenate([first, second], axis=0)
    high = inner.astype(BF16)
    out[: 2 * block, :] = high
    out[2 * block : 4 * block, :] = (inner - high.astype(F32)).astype(BF16)
    outer = jnp.concatenate([mine[2 * block :], theirs[2 * block :]], axis=0)
    out[4 * block :, :] = outer.astype(BF16)


def collect(copies, sem):
    started = []
    for n, (src, dst) in enumerate(copies):
        copy = pltpu.make_async_copy(src, dst, sem.at[n])
        copy.start()
        started.append(copy)
    return started


def sorted_rows(normed):
    keys = normed.shape[0]
    half = keys // KEY_DILATION
    row = lax.broadcasted_iota(jnp.int32, (keys, keys), 0)
    column = lax.broadcasted_iota(jnp.int32, (keys, keys), 1)
    wanted = KEY_DILATION * (row % half) + row // half
    return over((column == wanted).astype(BF16), normed, 1, 0).astype(BF16)


def spread(rows, group, wide):
    half = rows.shape[0] // KEY_DILATION
    heads = HEADS // LANE_GROUPS
    size = wide // heads
    part = rows[:, group * wide : (group + 1) * wide].astype(F32)
    lane = lax.broadcasted_iota(jnp.int32, (half, wide), 1)
    out = []
    for head in range(heads):
        parity = head % KEY_DILATION
        mine = (lane >= head * size) & (lane < (head + 1) * size)
        out.append(jnp.where(mine, part[parity * half : (parity + 1) * half], 0.0))
    return jnp.concatenate(out, axis=0).astype(BF16)


def attend_kernel(fsdp, block, *refs):
    count, sums, gain, tiles = refs[:4]
    own, mate = refs[4:8], refs[8]
    near, far = refs[9:12], refs[12:15]
    out, held, pooled, sem = refs[15:]
    shard = mate.shape[1]
    chips = fsdp // 2
    half_width = held.shape[2] // 2
    device = lax.axis_index("tile")
    me = lax.axis_index("fsdp")
    chip, core = me // 2, me % 2
    cut = device % 2

    def at(weight, owner, side=None):
        rows = pl.ds(pl.multiple_of(owner * shard, shard), shard)
        if side is None:
            return held.at[weight, rows]
        columns = pl.ds(pl.multiple_of(side * half_width, half_width), half_width)
        return held.at[weight, rows, columns]

    copies = []
    for weight in range(4):
        copies.append((own[weight], at(weight, me)))
        copies.append((mate.at[weight], at(weight, 2 * chip + 1 - core)))
        for j in range(1, chips):
            source = 2 * lax.rem(chip - j + chips, chips)
            for pieces, owner in ((near, source + core), (far, source + 1 - core)):
                whole, mine, theirs = pieces
                if weight < 2:
                    copies.append((whole.at[j - 1, weight], at(weight, owner)))
                else:
                    copies.append((mine.at[j - 1, weight - 2], at(weight, owner, cut)))
                    copies.append((theirs.at[j - 1, weight - 2], at(weight, owner, 1 - cut)))
    started = collect(copies, sem)
    counts = [fsdp, fsdp, 2 + 4 * (chips - 1), 2 + 4 * (chips - 1)]

    def arrive(weight):
        begin = sum(counts[:weight])
        for copy in started[begin : begin + counts[weight]]:
            copy.wait()

    pooled[...] = jnp.zeros_like(pooled)
    pairs = sums.shape[0] // (6 * block)
    for s in range(pairs):
        even = device ^ (2 * s)
        odd = even ^ 1
        blocks = [even, odd, even, odd, even - 1 + 2 * (even % 2), odd - 1 + 2 * (odd % 2)]
        for i, index in enumerate(blocks):
            begin = (6 * s + i) * block
            rows = pl.ds(pl.multiple_of((index + 1) * block, block), block)
            pooled[rows, :] += sums[begin : begin + block, :].astype(F32)
    mean = pooled[block : (2 * pairs + 1) * block, :]
    scale = lax.rsqrt(jnp.mean(mean * mean, axis=1, keepdims=True) + 1e-06)
    normed = (mean * scale * gain[...]).astype(BF16)
    ordered = sorted_rows(normed)
    arrive(0)
    query = over(tiles[...], held[0], 1, 0).astype(BF16)
    arrive(1)
    keys = over(ordered, held[1], 1, 0).astype(BF16)
    arrive(2)
    values = over(ordered, held[2], 1, 0).astype(BF16)
    half = keys.shape[0] // KEY_DILATION
    heads = HEADS // LANE_GROUPS
    wide = keys.shape[1] // LANE_GROUPS
    rows = tiles.shape[0]
    size = wide // heads
    row = lax.broadcasted_iota(jnp.int32, (half, 1), 0)
    valid = [
        (KEY_DILATION * row + parity) * (4 * REGIONS_PER_KEY) < count[0]
        for parity in range(KEY_DILATION)
    ]
    hidden = jnp.concatenate(
        [jnp.where(valid[head % KEY_DILATION], 0.0, -jnp.inf) for head in range(heads)], axis=0
    )
    contexts = []
    for group in range(LANE_GROUPS):
        lanes = slice(group * wide, (group + 1) * wide)
        score = over(spread(keys, group, wide), query[:, lanes], 1, 1)
        score = (score * (1.0 / size**0.5) + hidden).reshape(heads, half, rows)
        expo = jnp.exp(score - jnp.max(score, axis=1, keepdims=True))
        share = 1.0 / jnp.sum(expo, axis=1, keepdims=True)
        weight = expo.reshape(heads * half, rows).astype(BF16)
        context = over(spread(values, group, wide), weight, 0, 0).reshape(heads, size, rows)
        contexts.append((context * share).reshape(wide, rows).astype(BF16))
    arrive(3)
    context = jnp.concatenate(contexts, axis=0)
    out[...] = over(context, held[3], 0, 0).astype(out.dtype)


def swap(array, axis, offset):
    count = lax.axis_size(axis)
    return lax.ppermute(array, axis, [(i, i ^ offset) for i in range(count)])


def chip_shift(array, axis, step):
    count = lax.axis_size(axis)
    return lax.ppermute(array, axis, [(i, (i + 2 * step) % count) for i in range(count)])


def stack_kernel(w_query, w_key, w_value, w_out, halves, pair, whole, sem):
    cut = lax.axis_index("tile") % 2
    width = halves.shape[2]
    columns = pl.ds(pl.multiple_of(cut * width, width), width)
    copies = [(w.at[:, columns], halves.at[n]) for n, w in enumerate((w_value, w_out))]
    copies += [(w, pair.at[n]) for n, w in enumerate((w_query, w_key))]
    copies += [(w, whole.at[n]) for n, w in enumerate((w_query, w_key, w_value, w_out))]
    for copy in collect(copies, sem):
        copy.wait()


def behind(array, *others):
    return lax.optimization_barrier((array,) + others)[0]


def from_chips(weight):
    chips = lax.axis_size("fsdp") // 2
    return jnp.stack([chip_shift(weight, "fsdp", j) for j in range(1, chips)])


def gather_pairs(rows, axis):
    pairs = lax.axis_size(axis) // 2
    held = 1
    while held < pairs:
        width = min(4, pairs // held)
        parts = [rows] + [swap(rows, axis, 2 * held * d) for d in range(1, width)]
        rows = jnp.concatenate(parts, axis=0)
        held *= width
    return rows


def local_call(kernel, out_shape, in_specs, name, scratch=()):
    return pl.pallas_call(
        kernel,
        out_shape=out_shape,
        in_specs=in_specs,
        out_specs=vmem(),
        scratch_shapes=list(scratch),
        compiler_params=pltpu.CompilerParams(vmem_limit_bytes=40 * 1024 * 1024),
        cost_estimate=pl.CostEstimate(flops=1000, bytes_accessed=1000, transcendentals=0),
        name=name,
    )


def body(tiles, nbr_tiles, nbr_mask, tile_count, w_query, w_key, w_value, w_out, key_gain):
    own_tiles = tiles[0]
    rows, width = own_tiles.shape
    tile_devices = lax.axis_size("tile")
    fsdp = lax.axis_size("fsdp")
    regions = nbr_tiles.shape[1]
    block = regions // REGIONS_PER_KEY

    shard = w_query.shape[0]
    halves, first_two, whole = pl.pallas_call(
        stack_kernel,
        out_shape=(
            jax.ShapeDtypeStruct((2, shard, width // 2), BF16),
            jax.ShapeDtypeStruct((2, shard, width), BF16),
            jax.ShapeDtypeStruct((4, shard, width), BF16),
        ),
        in_specs=[anywhere()] * 4,
        out_specs=(vmem(), vmem(), vmem()),
        scratch_shapes=[pltpu.SemaphoreType.DMA((8,))],
        name="stack",
    )(w_query, w_key, w_value, w_out)
    near_halves = from_chips(halves)
    near_two = from_chips(first_two)
    mate_whole = swap(whole, "fsdp", 1)

    slots = jnp.where(nbr_mask[0] > 0, nbr_tiles[0] + 1, 0)
    mate = swap(slots, "tile", 1)
    inner = [(i, i + 1) for i in range(1, tile_devices - 1, 2)]
    other = lax.ppermute(slots, "tile", inner + [(b, a) for a, b in inner])
    mine = local_call(
        pool_kernel,
        jax.ShapeDtypeStruct((3 * block, width), F32),
        [vmem()] * 4,
        "pool",
    )(slots, mate, other, behind(own_tiles, mate_whole))
    pair = local_call(
        pair_kernel,
        jax.ShapeDtypeStruct((6 * block, width), BF16),
        [vmem()] * 2,
        "pair",
    )(mine, swap(mine, "tile", 1))
    near_halves = behind(near_halves, pair)
    other_halves = swap(near_halves, "tile", 1)
    far_halves = swap(near_halves, "fsdp", 1)
    sums = gather_pairs(pair, "tile")
    near_two = behind(near_two, sums)
    other_halves = behind(other_halves, sums)
    far_two = swap(near_two, "fsdp", 1)
    far_other = swap(other_halves, "fsdp", 1)
    chips = fsdp // 2
    attended = local_call(
        functools.partial(attend_kernel, fsdp, block),
        jax.ShapeDtypeStruct((rows, width), BF16),
        [smem()] + [vmem()] * 3 + [anywhere()] * 11,
        "attend",
        [
            pltpu.VMEM((4, width, width), BF16),
            pltpu.VMEM(((tile_devices + 2) * block, width), F32),
            pltpu.SemaphoreType.DMA((2 * fsdp + 2 * (2 + 4 * (chips - 1)),)),
        ],
    )(
        tile_count,
        sums,
        key_gain[None, :],
        own_tiles,
        *(w_query, w_key, w_value, w_out),
        mate_whole,
        *(near_two, near_halves, other_halves),
        *(far_two, far_halves, far_other),
    )
    return attended[None]


def solution(mesh):
    placed = (
        P("fsdp", "tile", None),
        P("fsdp", "tile", None),
        P("fsdp", "tile", None),
        P("fsdp"),
        P("fsdp", None),
        P("fsdp", None),
        P("fsdp", None),
        P("fsdp", None),
        P(),
    )
    return jax.shard_map(
        body, mesh=mesh, in_specs=placed, out_specs=P("fsdp", "tile", None), check_vma=False
    )
```

time: 68.1 us -> 37.1 us (0.54)
  waiting for transfers between devices: 26.2 us -> 9.65 us
  starting transfers between devices: 26.4 us -> 17.8 us
  other arithmetic: 2.37 us -> 0.04 us
  local copies, waits for them, and re-layouts: 2.46 us -> 0.25 us
  Pallas kernels: 9.22 us -> 8.47 us
    ppermute x8 -> x10, starting transfers between devices: 1.12 us -> 14.4 us  [swap(): return lax.ppermute(array, axis, [(i, i ^ offset) for i in range(count)])]
    ppermute x4 -> x2, waiting for transfers between devices: 12.9 us -> 0.01 us  [chip_shift(): lax.ppermute(array, axis, [(i, (i + 2 * step) % count) for i in range(cou...]
    ppermute x4 -> x1, starting transfers between devices: 11.5 us -> 0.66 us  [body(): other = lax.ppermute(slots, 'tile', inner + [(b, a) for a, b in inner])]
    ppermute x8 -> x10, waiting for transfers between devices: 0.02 us -> 9.64 us  [swap(): return lax.ppermute(array, axis, [(i, i ^ offset) for i in range(count)])]
    all_to_all x1 -> x0, starting transfers between devices: 8.61 us -> none  [body(): lax.all_to_all(jnp.tile(normed, (tile_devices, 1)), 'tile', split_axis=0,...]
    ppermute x4 -> x1, waiting for transfers between devices: 6.8 us -> 0.01 us  [body(): other = lax.ppermute(slots, 'tile', inner + [(b, a) for a, b in inner])]
    all_to_all x1 -> x0, waiting for transfers between devices: 6.52 us -> none  [body(): lax.all_to_all(jnp.tile(normed, (tile_devices, 1)), 'tile', split_axis=0,...]
    ppermute x4 -> x2, starting transfers between devices: 5.11 us -> 2.69 us  [chip_shift(): lax.ppermute(array, axis, [(i, (i + 2 * step) % count) for i in range(cou...]
  transfers between devices with their start and end apart: 17 -> 13, of which waited for: 7 -> 5; matrix products, arithmetic and copies ran while one was open for 5% -> 1% of each run, Pallas kernels for 10% -> 1%
where the time goes in v3:
time: 37.1 us; the launch traced here: 37 us
  starting transfers between devices  17.8 us (48%)
  waiting for transfers between devices  9.65 us (26%)
  Pallas kernels  8.47 us (23%)
  between operations  0.79 us (2%)
    ppermute x10, starting transfers between devices, swap(): return lax.ppermute(array, axis, [(i, i ^ offset) for i in range(count)])  14.4 us
    ppermute x10, waiting for transfers between devices, swap(): return lax.ppermute(array, axis, [(i, i ^ offset) for i in range(count)])  9.64 us
    pallas_call x1, Pallas kernels, body(): local_call(functools.partial(attend_kernel, fsdp, block), jax.ShapeDtypeS...  4.91 us
    pallas_call x1, Pallas kernels, body(): pl.pallas_call(stack_kernel, out_shape=(jax.ShapeDtypeStruct((2, shard, w...  3.07 us
    ppermute x2, starting transfers between devices, chip_shift(): lax.ppermute(array, axis, [(i, (i + 2 * step) % count) for i in range(cou...  2.69 us
  transfers between devices with their start and end apart: 13, of which 5 were waited for; matrix products, arithmetic and copies ran while one was open for 1% of the time, Pallas kernels for 1%

profile of v3, /device:TPU:0, one launch (start us, length us, event | category | flops | bytes accessed | tf_op | source)
XLA Modules:
  0.0 37.0 jit_solution(13801291381656638631)
XLA Ops:
  0.0 0.0 copy-start.3
  0.0 0.0 copy-start.2
  0.0 0.0 copy-start.1
  0.0 0.0 copy-start.7
  0.0 0.0 copy-start.6
  0.0 0.0 copy-start
  0.0 0.0 copy-start.4
  0.0 0.0 copy-start.5
  0.0 3.1 %stack.9 = (bf16[2,192,384]{2,1,0:T(8,128)(2,1)}, bf16[2,192,768]{2,1,0:T(8,128)(2,1)}, bf16[4,192,768]{2,1,0:T(8,128)(2,1)}) custom-call(bf16[192,768]{1,0:T(8,128)(2,1)} %refs_4_.1, bf16[192,768]{1,0:T(8,128)(2,1)} %refs_5_.1, bf16[192,768]{1,0:T(8,128)(2,1)} %refs_6_.1, bf16[192,768]{1,0:T(8,128)(2,1)} %refs_7_.1), custom_call_target="tpu_custom_call" | custom-call | tf_op jit(solution)/shard_map/stack/pallas_call | solution.py:257
  3.1 0.5 %collective-permute-start.2 = (bf16[4,192,768]{2,1,0:T(8,128)(2,1)}, bf16[4,192,768]{2,1,0:T(8,128)(2,1)S(1)}, u32[]{:S(2)}, u32[]{:S(2)}) collective-permute-start(bf16[4,192,768]{2,1,0:T(8,128)(2,1)} %get-tuple-element.12), channel_id=1, source_target_pairs={{0,8},{8,0},{16,24},{24,16},{1,9},{9,1},{17,25},{25,17},{2,10},{10... | collective-permute-start | bytes 3538952 | tf_op jit(solution)/shard_map/ppermute | solution.py:196
  3.7 2.6 %collective-permute-start.8 = (bf16[2,192,384]{2,1,0:T(8,128)(2,1)}, bf16[2,192,384]{2,1,0:T(8,128)(2,1)}, u32[]{:S(2)}, u32[]{:S(2)}) collective-permute-start(bf16[2,192,384]{2,1,0:T(8,128)(2,1)} %get-tuple-element.16), channel_id=1, source_target_pairs={{0,16},{8,24},{16,0},{24,8},{1,17},{9,25},{17,1},{25,9},{2,18},{10... | collective-permute-start | bytes 884744 | tf_op jit(solution)/shard_map/ppermute | solution.py:201
  6.2 0.1 collective-permute-start.7
  6.3 0.0 copy-done.7
  6.3 0.0 copy-done.6
  6.4 0.1 copy.15
  6.5 0.1 copy.16
  6.6 0.7 %collective-permute-start.1 = (s32[64,4]{1,0:T(8,128)S(1)}, s32[64,4]{1,0:T(8,128)S(1)}, u32[]{:S(2)}, u32[]{:S(2)}) collective-permute-start(s32[64,4]{1,0:T(8,128)S(1)} %select_bitcast_fusion.here), channel_id=1, source_target_pairs={{1,2},{3,4},{5,6},{2,1},{4,3},{6,5},{9,10},{11,12},{13,14},{10,9},... | collective-permute-start | bytes 3080 | tf_op jit(solution)/shard_map/ppermute | solution.py:276
  7.2 4.8 %collective-permute-start = (s32[64,4]{1,0:T(8,128)S(1)}, s32[64,4]{1,0:T(8,128)S(1)}, u32[]{:S(2)}, u32[]{:S(2)}) collective-permute-start(s32[64,4]{1,0:T(8,128)S(1)} %select_bitcast_fusion.here), channel_id=1, source_target_pairs={{0,1},{1,0},{2,3},{3,2},{4,5},{5,4},{6,7},{7,6},{8,9},{9,8},{10,11... | collective-permute-start | bytes 3080 | tf_op jit(solution)/shard_map/ppermute | solution.py:196
  12.0 0.0 collective-permute-done.2.refs_8_
  12.0 0.0 collective-permute-done.1.other
  12.0 1.9 %collective-permute-done.mate = s32[64,4]{1,0:T(8,128)S(1)} collective-permute-done((s32[64,4]{1,0:T(8,128)S(1)}, s32[64,4]{1,0:T(8,128)S(1)}, u32[]{:S(2)}, u32[]{:S(2)}) %collective-permute-start) | collective-permute-done | bytes 1056 | tf_op jit(solution)/shard_map/ppermute | solution.py:196
  13.9 0.0 copy-done
  13.9 0.5 %pool.1.mine = f32[24,768]{1,0:T(8,128)S(1)} custom-call(s32[64,4]{1,0:T(8,128)S(1)} %select_bitcast_fusion.here, s32[64,4]{1,0:T(8,128)S(1)} %collective-permute-done.mate, s32[64,4]{1,0:T(8,128)S(1)} %collective-permute-done.1.other, bf16[256,768]{1,0:T(8,128)(2,1)S(1)} %bitcast.6), custom_call_target="tpu_custom_call" | custom-call | flops 1000 | bytes 1000 | tf_op jit(solution)/shard_map/pool/pallas_call | solution.py:277
  14.4 2.1 %collective-permute-start.3 = (f32[24,768]{1,0:T(8,128)S(1)}, f32[24,768]{1,0:T(8,128)S(1)}, u32[]{:S(2)}, u32[]{:S(2)}) collective-permute-start(f32[24,768]{1,0:T(8,128)S(1)} %pool.1.mine), channel_id=1, source_target_pairs={{0,1},{1,0},{2,3},{3,2},{4,5},{5,4},{6,7},{7,6},{8,9},{9,8},{10,11... | collective-permute-start | bytes 221192 | tf_op jit(solution)/shard_map/ppermute | solution.py:196
  16.5 2.3 %collective-permute-done.3.theirs = f32[24,768]{1,0:T(8,128)S(1)} collective-permute-done((f32[24,768]{1,0:T(8,128)S(1)}, f32[24,768]{1,0:T(8,128)S(1)}, u32[]{:S(2)}, u32[]{:S(2)}) %collective-permute-start.3) | collective-permute-done | bytes 73760 | tf_op jit(solution)/shard_map/ppermute | solution.py:196
  18.8 4.0 %collective-permute-start.6 = (bf16[48,768]{1,0:T(8,128)(2,1)S(1)}, bf16[48,768]{1,0:T(8,128)(2,1)S(1)}, u32[]{:S(2)}, u32[]{:S(2)}) collective-permute-start(bf16[48,768]{1,0:T(8,128)(2,1)S(1)} %pair.1), channel_id=1, source_target_pairs={{0,6},{1,7},{2,4},{3,5},{4,2},{5,3},{6,0},{7,1},{8,14},{9,15},{10,... | collective-permute-start | bytes 221192 | tf_op jit(solution)/shard_map/ppermute | solution.py:196
  22.9 0.0 collective-permute-start.5
  22.9 0.6 %collective-permute-start.4 = (bf16[48,768]{1,0:T(8,128)(2,1)S(1)}, bf16[48,768]{1,0:T(8,128)(2,1)S(1)}, u32[]{:S(2)}, u32[]{:S(2)}) collective-permute-start(bf16[48,768]{1,0:T(8,128)(2,1)S(1)} %pair.1), channel_id=1, source_target_pairs={{0,2},{1,3},{2,0},{3,1},{4,6},{5,7},{6,4},{7,5},{8,10},{9,11},{10,... | collective-permute-start | bytes 221192 | tf_op jit(solution)/shard_map/ppermute | solution.py:196
  23.5 0.0 collective-permute-done.8
  23.5 1.8 %collective-permute-start.9 = (bf16[1,2,192,384]{3,2,1,0:T(8,128)(2,1)}, bf16[1,2,192,384]{3,2,1,0:T(8,128)(2,1)S(1)}, u32[]{:S(2)}, u32[]{:S(2)}) collective-permute-start(bf16[1,2,192,384]{3,2,1,0:T(8,128)(2,1)} %bitcast.3.refs_10_), channel_id=1, source_target_pairs={{0,1},{1,0},{2,3},{3,2},{4,5},{5,4},{6,7},{7,6},{8,9},{9,8},{10,11... | collective-permute-start | bytes 884744 | tf_op jit(solution)/shard_map/ppermute | solution.py:196
  25.3 0.0 collective-permute-done.6
  25.3 2.8 %collective-permute-done.5 = bf16[48,768]{1,0:T(8,128)(2,1)S(1)} collective-permute-done((bf16[48,768]{1,0:T(8,128)(2,1)S(1)}, bf16[48,768]{1,0:T(8,128)(2,1)S(1)}, u32[]{:S(2)}, u32[]{:S(2)}) %collective-permute-start.5) | collective-permute-done | bytes 73760 | tf_op jit(solution)/shard_map/ppermute | solution.py:196
  28.1 0.0 collective-permute-done.4
  28.1 0.0 collective-permute-done.7
  28.2 0.1 collective-permute-start.10
  28.2 0.5 %collective-permute-start.11 = (bf16[1,2,192,384]{3,2,1,0:T(8,128)(2,1)}, bf16[1,2,192,384]{3,2,1,0:T(8,128)(2,1)S(1)}, u32[]{:S(2)}, u32[]{:S(2)}) collective-permute-start(bf16[1,2,192,384]{3,2,1,0:T(8,128)(2,1)} %bitcast.3.refs_10_), channel_id=1, source_target_pairs={{0,8},{8,0},{16,24},{24,16},{1,9},{9,1},{17,25},{25,17},{2,10},{10... | collective-permute-start | bytes 884744 | tf_op jit(solution)/shard_map/ppermute | solution.py:196
  28.7 1.7 %collective-permute-done.9.refs_11_ = bf16[1,2,192,384]{3,2,1,0:T(8,128)(2,1)S(1)} collective-permute-done((bf16[1,2,192,384]{3,2,1,0:T(8,128)(2,1)}, bf16[1,2,192,384]{3,2,1,0:T(8,128)(2,1)S(1)}, u32[]{:S(2)}, u32[]{:S(2)}) %collective-permute-start.9) | collective-permute-done | bytes 294944 | tf_op jit(solution)/shard_map/ppermute | solution.py:196
  30.4 0.0 collective-permute-start.12
  31.1 0.0 copy-done.5
  31.1 0.0 collective-permute-done.11.refs_13_
  31.1 0.9 %collective-permute-done.12.refs_14_ = bf16[1,2,192,384]{3,2,1,0:T(8,128)(2,1)S(1)} collective-permute-done((bf16[1,2,192,384]{3,2,1,0:T(8,128)(2,1)S(1)}, bf16[1,2,192,384]{3,2,1,0:T(8,128)(2,1)S(1)}, u32[]{:S(2)}, u32[]{:S(2)}) %collective-permute-start.12) | collective-permute-done | bytes 294944 | tf_op jit(solution)/shard_map/ppermute | solution.py:196
  32.0 0.0 collective-permute-done.10.refs_12_
  32.0 0.0 copy-done.3
  32.0 0.0 copy-done.2
  32.0 0.0 copy-done.1
  32.0 0.0 copy-done.4
  32.1 4.9 %attend.1 = bf16[256,768]{1,0:T(8,128)(2,1)} custom-call(s32[1]{0:T(128)S(6)} %copy.17.refs_0_, bf16[192,768]{1,0:T(8,128)(2,1)S(1)} %pad_maximum_fusion.refs_1_, f32[1,768]{1,0:T(1,128)S(1)} %broadcast_in_dim.8.refs_2_, bf16[256,768]{1,0:T(8,128)(2,1)S(1)} %bitcast.7, bf16[192,768]{1,0:T(8,128)(2,1)S(1)} %copy-done.1, bf16[192,768]{1,0:T(8,128)(2,1)S(1)} %copy-done.2, ...), custom_call_target="tpu_custom_call" | custom-call | flops 1000 | bytes 1000 | tf_op jit(solution)/shard_map/attend/pallas_call | solution.py:298
  (6 shorter events, 0.1 us)
Async XLA Ops:
  0.0 32.0 %copy-start.3 = (bf16[192,768]{1,0:T(8,128)(2,1)S(1)}, bf16[192,768]{1,0:T(8,128)(2,1)}, u32[]{:S(2)}) copy-start(bf16[192,768]{1,0:T(8,128)(2,1)} %refs_6_.1) | copy-start | bytes 884740
  0.0 32.0 %copy-start.2 = (bf16[192,768]{1,0:T(8,128)(2,1)S(1)}, bf16[192,768]{1,0:T(8,128)(2,1)}, u32[]{:S(2)}) copy-start(bf16[192,768]{1,0:T(8,128)(2,1)} %refs_5_.1) | copy-start | bytes 884740
  0.0 32.0 %copy-start.1 = (bf16[192,768]{1,0:T(8,128)(2,1)S(1)}, bf16[192,768]{1,0:T(8,128)(2,1)}, u32[]{:S(2)}) copy-start(bf16[192,768]{1,0:T(8,128)(2,1)} %refs_4_.1) | copy-start | bytes 884740
  0.0 6.3 %copy-start.7 = (s32[1,64,4]{1,2,0:T(4,128)S(1)}, s32[1,64,4]{1,2,0:T(4,128)}, u32[]{:S(2)}) copy-start(s32[1,64,4]{1,2,0:T(4,128)} %param.10) | copy-start | bytes 3076
  0.0 6.3 %copy-start.6 = (s32[1,64,4]{1,2,0:T(4,128)S(1)}, s32[1,64,4]{1,2,0:T(4,128)}, u32[]{:S(2)}) copy-start(s32[1,64,4]{1,2,0:T(4,128)} %param.11) | copy-start | bytes 3076
  0.0 13.9 %copy-start = (bf16[1,256,768]{2,1,0:T(8,128)(2,1)S(1)}, bf16[1,256,768]{2,1,0:T(8,128)(2,1)}, u32[]{:S(2)}) copy-start(bf16[1,256,768]{2,1,0:T(8,128)(2,1)} %param.9) | copy-start | bytes 1179652
  0.0 32.0 %copy-start.4 = (bf16[192,768]{1,0:T(8,128)(2,1)S(1)}, bf16[192,768]{1,0:T(8,128)(2,1)}, u32[]{:S(2)}) copy-start(bf16[192,768]{1,0:T(8,128)(2,1)} %refs_7_.1) | copy-start | bytes 884740
  0.0 31.1 %copy-start.5 = (f32[768]{0:T(1024)S(1)}, f32[768]{0:T(1024)}, u32[]{:S(2)}) copy-start(f32[768]{0:T(1024)} %param.17) | copy-start | bytes 9220
  3.1 8.9 %collective-permute-start.2 = (bf16[4,192,768]{2,1,0:T(8,128)(2,1)}, bf16[4,192,768]{2,1,0:T(8,128)(2,1)S(1)}, u32[]{:S(2)}, u32[]{:S(2)}) collective-permute-start(bf16[4,192,768]{2,1,0:T(8,128)(2,1)} %get-tuple-element.12), channel_id=1, source_target_pairs={{0,8},{8,0},{16,24},{24,16},{1,9},{9,1},{17,25},{25,17},{2,10},{10... | collective-permute-start | bytes 3538952 | tf_op jit(solution)/shard_map/ppermute | solution.py:196
  3.7 19.9 %collective-permute-start.8 = (bf16[2,192,384]{2,1,0:T(8,128)(2,1)}, bf16[2,192,384]{2,1,0:T(8,128)(2,1)}, u32[]{:S(2)}, u32[]{:S(2)}) collective-permute-start(bf16[2,192,384]{2,1,0:T(8,128)(2,1)} %get-tuple-element.16), channel_id=1, source_target_pairs={{0,16},{8,24},{16,0},{24,8},{1,17},{9,25},{17,1},{25,9},{2,18},{10... | collective-permute-start | bytes 884744 | tf_op jit(solution)/shard_map/ppermute | solution.py:201
  6.2 21.9 %collective-permute-start.7 = (bf16[2,192,768]{2,1,0:T(8,128)(2,1)}, bf16[2,192,768]{2,1,0:T(8,128)(2,1)S(1)}, u32[]{:S(2)}, u32[]{:S(2)}) collective-permute-start(bf16[2,192,768]{2,1,0:T(8,128)(2,1)} %get-tuple-element.14), channel_id=1, source_target_pairs={{0,16},{8,24},{16,0},{24,8},{1,17},{9,25},{17,1},{25,9},{2,18},{10... | collective-permute-start | bytes 1769480 | tf_op jit(solution)/shard_map/ppermute | solution.py:201
  6.6 5.4 %collective-permute-start.1 = (s32[64,4]{1,0:T(8,128)S(1)}, s32[64,4]{1,0:T(8,128)S(1)}, u32[]{:S(2)}, u32[]{:S(2)}) collective-permute-start(s32[64,4]{1,0:T(8,128)S(1)} %select_bitcast_fusion.here), channel_id=1, source_target_pairs={{1,2},{3,4},{5,6},{2,1},{4,3},{6,5},{9,10},{11,12},{13,14},{10,9},... | collective-permute-start | bytes 3080 | tf_op jit(solution)/shard_map/ppermute | solution.py:276
  7.2 6.7 %collective-permute-start = (s32[64,4]{1,0:T(8,128)S(1)}, s32[64,4]{1,0:T(8,128)S(1)}, u32[]{:S(2)}, u32[]{:S(2)}) collective-permute-start(s32[64,4]{1,0:T(8,128)S(1)} %select_bitcast_fusion.here), channel_id=1, source_target_pairs={{0,1},{1,0},{2,3},{3,2},{4,5},{5,4},{6,7},{7,6},{8,9},{9,8},{10,11... | collective-permute-start | bytes 3080 | tf_op jit(solution)/shard_map/ppermute | solution.py:196
  14.4 4.4 %collective-permute-start.3 = (f32[24,768]{1,0:T(8,128)S(1)}, f32[24,768]{1,0:T(8,128)S(1)}, u32[]{:S(2)}, u32[]{:S(2)}) collective-permute-start(f32[24,768]{1,0:T(8,128)S(1)} %pool.1.mine), channel_id=1, source_target_pairs={{0,1},{1,0},{2,3},{3,2},{4,5},{5,4},{6,7},{7,6},{8,9},{9,8},{10,11... | collective-permute-start | bytes 221192 | tf_op jit(solution)/shard_map/ppermute | solution.py:196
  18.8 6.5 %collective-permute-start.6 = (bf16[48,768]{1,0:T(8,128)(2,1)S(1)}, bf16[48,768]{1,0:T(8,128)(2,1)S(1)}, u32[]{:S(2)}, u32[]{:S(2)}) collective-permute-start(bf16[48,768]{1,0:T(8,128)(2,1)S(1)} %pair.1), channel_id=1, source_target_pairs={{0,6},{1,7},{2,4},{3,5},{4,2},{5,3},{6,0},{7,1},{8,14},{9,15},{10,... | collective-permute-start | bytes 221192 | tf_op jit(solution)/shard_map/ppermute | solution.py:196
  22.9 5.3 %collective-permute-start.5 = (bf16[48,768]{1,0:T(8,128)(2,1)S(1)}, bf16[48,768]{1,0:T(8,128)(2,1)S(1)}, u32[]{:S(2)}, u32[]{:S(2)}) collective-permute-start(bf16[48,768]{1,0:T(8,128)(2,1)S(1)} %pair.1), channel_id=1, source_target_pairs={{0,4},{1,5},{2,6},{3,7},{4,0},{5,1},{6,2},{7,3},{8,12},{9,13},{10,... | collective-permute-start | bytes 221192 | tf_op jit(solution)/shard_map/ppermute | solution.py:196
  22.9 5.3 %collective-permute-start.4 = (bf16[48,768]{1,0:T(8,128)(2,1)S(1)}, bf16[48,768]{1,0:T(8,128)(2,1)S(1)}, u32[]{:S(2)}, u32[]{:S(2)}) collective-permute-start(bf16[48,768]{1,0:T(8,128)(2,1)S(1)} %pair.1), channel_id=1, source_target_pairs={{0,2},{1,3},{2,0},{3,1},{4,6},{5,7},{6,4},{7,5},{8,10},{9,11},{10,... | collective-permute-start | bytes 221192 | tf_op jit(solution)/shard_map/ppermute | solution.py:196
  23.5 6.9 %collective-permute-start.9 = (bf16[1,2,192,384]{3,2,1,0:T(8,128)(2,1)}, bf16[1,2,192,384]{3,2,1,0:T(8,128)(2,1)S(1)}, u32[]{:S(2)}, u32[]{:S(2)}) collective-permute-start(bf16[1,2,192,384]{3,2,1,0:T(8,128)(2,1)} %bitcast.3.refs_10_), channel_id=1, source_target_pairs={{0,1},{1,0},{2,3},{3,2},{4,5},{5,4},{6,7},{7,6},{8,9},{9,8},{10,11... | collective-permute-start | bytes 884744 | tf_op jit(solution)/shard_map/ppermute | solution.py:196
  28.2 3.9 %collective-permute-start.10 = (bf16[1,2,192,768]{3,2,1,0:T(8,128)(2,1)S(1)}, bf16[1,2,192,768]{3,2,1,0:T(8,128)(2,1)S(1)}, u32[]{:S(2)}, u32[]{:S(2)}) collective-permute-start(bf16[1,2,192,768]{3,2,1,0:T(8,128)(2,1)S(1)} %bitcast.8), channel_id=1, source_target_pairs={{0,8},{8,0},{16,24},{24,16},{1,9},{9,1},{17,25},{25,17},{2,10},{10... | collective-permute-start | bytes 1769480 | tf_op jit(solution)/shard_map/ppermute | solution.py:196
  28.2 2.9 %collective-permute-start.11 = (bf16[1,2,192,384]{3,2,1,0:T(8,128)(2,1)}, bf16[1,2,192,384]{3,2,1,0:T(8,128)(2,1)S(1)}, u32[]{:S(2)}, u32[]{:S(2)}) collective-permute-start(bf16[1,2,192,384]{3,2,1,0:T(8,128)(2,1)} %bitcast.3.refs_10_), channel_id=1, source_target_pairs={{0,8},{8,0},{16,24},{24,16},{1,9},{9,1},{17,25},{25,17},{2,10},{10... | collective-permute-start | bytes 884744 | tf_op jit(solution)/shard_map/ppermute | solution.py:196
  30.4 1.6 %collective-permute-start.12 = (bf16[1,2,192,384]{3,2,1,0:T(8,128)(2,1)S(1)}, bf16[1,2,192,384]{3,2,1,0:T(8,128)(2,1)S(1)}, u32[]{:S(2)}, u32[]{:S(2)}) collective-permute-start(bf16[1,2,192,384]{3,2,1,0:T(8,128)(2,1)S(1)} %collective-permute-done.9.refs_11_), channel_id=1, source_target_pairs={{0,8},{8,0},{16,24},{24,16},{1,9},{9,1},{17,25},{25,17},{2,10},{10... | collective-permute-start | bytes 884744 | tf_op jit(solution)/shard_map/ppermute | solution.py:196

commit v4 on v3

--- a/solution.py
+++ b/solution.py
@@ -102,45 +102,68 @@
     return jnp.concatenate(out, axis=0).astype(BF16)
 
 
-def attend_kernel(fsdp, block, *refs):
-    count, sums, gain, tiles = refs[:4]
-    own, mate = refs[4:8], refs[8]
-    near, far = refs[9:12], refs[12:15]
-    out, held, pooled, sem = refs[15:]
-    shard = mate.shape[1]
+def place_rows(fsdp, shard, held):
+    half_width = held.shape[2] // 2
     chips = fsdp // 2
-    half_width = held.shape[2] // 2
-    device = lax.axis_index("tile")
     me = lax.axis_index("fsdp")
+    cut = lax.axis_index("tile") % 2
     chip, core = me // 2, me % 2
-    cut = device % 2
-
-    def at(weight, owner, side=None):
+
+    def at(weight, owner, side):
         rows = pl.ds(pl.multiple_of(owner * shard, shard), shard)
         if side is None:
             return held.at[weight, rows]
         columns = pl.ds(pl.multiple_of(side * half_width, half_width), half_width)
         return held.at[weight, rows, columns]
 
-    copies = []
-    for weight in range(4):
-        copies.append((own[weight], at(weight, me)))
-        copies.append((mate.at[weight], at(weight, 2 * chip + 1 - core)))
+    def own(weight, piece, mate):
+        return [(piece, at(weight, me, None)), (mate, at(weight, 2 * chip + 1 - core, None))]
+
+    def others(weight, near, far, side=None):
+        copies = []
         for j in range(1, chips):
             source = 2 * lax.rem(chip - j + chips, chips)
-            for pieces, owner in ((near, source + core), (far, source + 1 - core)):
-                whole, mine, theirs = pieces
-                if weight < 2:
-                    copies.append((whole.at[j - 1, weight], at(weight, owner)))
-                else:
-                    copies.append((mine.at[j - 1, weight - 2], at(weight, owner, cut)))
-                    copies.append((theirs.at[j - 1, weight - 2], at(weight, owner, 1 - cut)))
+            columns = None if side is None else (cut if side == 0 else 1 - cut)
+            copies.append((near(j - 1), at(weight, source + core, columns)))
+            copies.append((far(j - 1), at(weight, source + 1 - core, columns)))
+        return copies
+
+    return own, others
+
+
+def query_kernel(fsdp, tiles, piece, mate, near, far, out, held, sem):
+    own, others = place_rows(fsdp, piece.shape[0], held)
+    copies = own(0, piece, mate) + others(0, lambda j: near.at[j], lambda j: far.at[j])
+    for copy in collect(copies, sem):
+        copy.wait()
+    out[...] = over(tiles[...], held[0], 1, 0).astype(BF16)
+
+
+def attend_kernel(fsdp, block, *refs):
+    count, sums, gain, query = refs[:4]
+    pieces, mates = refs[4:7], refs[7:10]
+    near, far = refs[10:13], refs[13:16]
+    out, held, pooled, sem = refs[16:]
+    device = lax.axis_index("tile")
+    own, others = place_rows(fsdp, pieces[0].shape[0], held)
+    copies, ends = [], []
+    for weight in (1, 2, 0):
+        copies += own(weight, pieces[weight], mates[weight])
+        if weight == 0:
+            copies += others(0, lambda j: near[0].at[j], lambda j: far[0].at[j])
+        else:
+            for side in range(2):
+                copies += others(
+                    weight,
+                    lambda j: near[1 + side].at[j, weight - 1],
+                    lambda j: far[1 + side].at[j, weight - 1],
+                    side,
+                )
+        ends.append(len(copies))
     started = collect(copies, sem)
-    counts = [fsdp, fsdp, 2 + 4 * (chips - 1), 2 + 4 * (chips - 1)]
-
-    def arrive(weight):
-        begin = sum(counts[:weight])
-        for copy in started[begin : begin + counts[weight]]:
+
+    def arrive(begin, end):
+        for copy in started[begin:end]:
             copy.wait()
 
     pooled[...] = jnp.zeros_like(pooled)
@@ -157,16 +180,14 @@
     scale = lax.rsqrt(jnp.mean(mean * mean, axis=1, keepdims=True) + 1e-06)
     normed = (mean * scale * gain[...]).astype(BF16)
     ordered = sorted_rows(normed)
-    arrive(0)
-    query = over(tiles[...], held[0], 1, 0).astype(BF16)
-    arrive(1)
-    keys = over(ordered, held[1], 1, 0).astype(BF16)
-    arrive(2)
-    values = over(ordered, held[2], 1, 0).astype(BF16)
+    arrive(0, ends[0])
+    values = over(ordered, held[1], 1, 0).astype(BF16)
+    arrive(ends[1], ends[2])
+    keys = over(ordered, held[0], 1, 0).astype(BF16)
     half = keys.shape[0] // KEY_DILATION
     heads = HEADS // LANE_GROUPS
     wide = keys.shape[1] // LANE_GROUPS
-    rows = tiles.shape[0]
+    rows = query.shape[0]
     size = wide // heads
     row = lax.broadcasted_iota(jnp.int32, (half, 1), 0)
     valid = [
@@ -186,9 +207,9 @@
         weight = expo.reshape(heads * half, rows).astype(BF16)
         context = over(spread(values, group, wide), weight, 0, 0).reshape(heads, size, rows)
         contexts.append((context * share).reshape(wide, rows).astype(BF16))
-    arrive(3)
+    arrive(ends[0], ends[1])
     context = jnp.concatenate(contexts, axis=0)
-    out[...] = over(context, held[3], 0, 0).astype(out.dtype)
+    out[...] = over(context, held[2], 0, 0).astype(out.dtype)
 
 
 def swap(array, axis, offset):
@@ -201,13 +222,11 @@
     return lax.ppermute(array, axis, [(i, (i + 2 * step) % count) for i in range(count)])
 
 
-def stack_kernel(w_query, w_key, w_value, w_out, halves, pair, whole, sem):
+def halves_kernel(w_value, w_out, halves, sem):
     cut = lax.axis_index("tile") % 2
     width = halves.shape[2]
     columns = pl.ds(pl.multiple_of(cut * width, width), width)
     copies = [(w.at[:, columns], halves.at[n]) for n, w in enumerate((w_value, w_out))]
-    copies += [(w, pair.at[n]) for n, w in enumerate((w_query, w_key))]
-    copies += [(w, whole.at[n]) for n, w in enumerate((w_query, w_key, w_value, w_out))]
     for copy in collect(copies, sem):
         copy.wait()
 
@@ -254,66 +273,67 @@
     block = regions // REGIONS_PER_KEY
 
     shard = w_query.shape[0]
-    halves, first_two, whole = pl.pallas_call(
-        stack_kernel,
-        out_shape=(
-            jax.ShapeDtypeStruct((2, shard, width // 2), BF16),
-            jax.ShapeDtypeStruct((2, shard, width), BF16),
-            jax.ShapeDtypeStruct((4, shard, width), BF16),
-        ),
-        in_specs=[anywhere()] * 4,
-        out_specs=(vmem(), vmem(), vmem()),
-        scratch_shapes=[pltpu.SemaphoreType.DMA((8,))],
-        name="stack",
-    )(w_query, w_key, w_value, w_out)
+    halves = pl.pallas_call(
+        halves_kernel,
+        out_shape=jax.ShapeDtypeStruct((2, shard, width // 2), BF16),
+        in_specs=[anywhere()] * 2,
+        out_specs=vmem(),
+        scratch_shapes=[pltpu.SemaphoreType.DMA((2,))],
+        name="halves",
+    )(w_value, w_out)
     near_halves = from_chips(halves)
-    near_two = from_chips(first_two)
-    mate_whole = swap(whole, "fsdp", 1)
 
     slots = jnp.where(nbr_mask[0] > 0, nbr_tiles[0] + 1, 0)
     mate = swap(slots, "tile", 1)
     inner = [(i, i + 1) for i in range(1, tile_devices - 1, 2)]
     other = lax.ppermute(slots, "tile", inner + [(b, a) for a, b in inner])
+    near_query = from_chips(behind(w_query, slots))
+    near_key = from_chips(behind(w_key, slots))
     mine = local_call(
         pool_kernel,
         jax.ShapeDtypeStruct((3 * block, width), F32),
         [vmem()] * 4,
         "pool",
-    )(slots, mate, other, behind(own_tiles, mate_whole))
+    )(slots, mate, other, own_tiles)
+    mates = [swap(behind(w, mine), "fsdp", 1) for w in (w_query, w_key, w_value, w_out)]
     pair = local_call(
         pair_kernel,
         jax.ShapeDtypeStruct((6 * block, width), BF16),
         [vmem()] * 2,
         "pair",
-    )(mine, swap(mine, "tile", 1))
+    )(mine, behind(swap(mine, "tile", 1), near_halves, *mates))
     near_halves = behind(near_halves, pair)
     other_halves = swap(near_halves, "tile", 1)
     far_halves = swap(near_halves, "fsdp", 1)
-    sums = gather_pairs(pair, "tile")
-    near_two = behind(near_two, sums)
+    near_query = behind(near_query, pair)
+    query = local_call(
+        functools.partial(query_kernel, fsdp),
+        jax.ShapeDtypeStruct((rows, width), BF16),
+        [vmem()] + [anywhere()] * 4,
+        "query",
+        [pltpu.VMEM((1, width, width), BF16), pltpu.SemaphoreType.DMA((fsdp,))],
+    )(own_tiles, w_query, mates[0], near_query, swap(near_query, "fsdp", 1))
+    sums = behind(gather_pairs(pair, "tile"), query, near_key)
     other_halves = behind(other_halves, sums)
-    far_two = swap(near_two, "fsdp", 1)
-    far_other = swap(other_halves, "fsdp", 1)
-    chips = fsdp // 2
     attended = local_call(
         functools.partial(attend_kernel, fsdp, block),
         jax.ShapeDtypeStruct((rows, width), BF16),
-        [smem()] + [vmem()] * 3 + [anywhere()] * 11,
+        [smem()] + [vmem()] * 3 + [anywhere()] * 12,
         "attend",
         [
-            pltpu.VMEM((4, width, width), BF16),
+            pltpu.VMEM((3, width, width), BF16),
             pltpu.VMEM(((tile_devices + 2) * block, width), F32),
-            pltpu.SemaphoreType.DMA((2 * fsdp + 2 * (2 + 4 * (chips - 1)),)),
+            pltpu.SemaphoreType.DMA((5 * fsdp,)),
         ],
     )(
         tile_count,
         sums,
         key_gain[None, :],
-        own_tiles,
-        *(w_query, w_key, w_value, w_out),
-        mate_whole,
-        *(near_two, near_halves, other_halves),
-        *(far_two, far_halves, far_other),
+        query,
+        *(w_key, w_value, w_out),
+        *mates[1:],
+        *(near_key, near_halves, other_halves),
+        *(swap(near_key, "fsdp", 1), far_halves, swap(other_halves, "fsdp", 1)),
     )
     return attended[None]
 

time: 37.1 us -> 46.8 us (1.26)
  waiting for transfers between devices: 9.65 us -> 18 us
  starting transfers between devices: 17.8 us -> 20 us
  Pallas kernels: 8.47 us -> 6.91 us
  other arithmetic: 0.04 us -> 0.71 us
    ppermute x2 -> x3, waiting for transfers between devices: 0.01 us -> 8.81 us  [chip_shift(): lax.ppermute(array, axis, [(i, (i + 2 * step) % count) for i in range(cou...]
    ppermute x2 -> x3, starting transfers between devices: 2.69 us -> 5.14 us  [chip_shift(): lax.ppermute(array, axis, [(i, (i + 2 * step) % count) for i in range(cou...]
    pallas_call x1, Pallas kernels: 4.91 us -> 3.82 us  [body(): local_call(functools.partial(attend_kernel, fsdp, block), jax.ShapeDtypeS...]
    add x1, other arithmetic: 0.01 us -> 0.68 us  [body(): slots = jnp.where(nbr_mask[0] > 0, nbr_tiles[0] + 1, 0)]
    ppermute x10 -> x14, waiting for transfers between devices: 9.64 us -> 9.15 us  [swap(): return lax.ppermute(array, axis, [(i, i ^ offset) for i in range(count)])]
    pallas_call x1 -> x2, Pallas kernels: 3.07 us -> 2.6 us  [the longest x1 1.8 us: body(): pl.pallas_call(halves_kernel, out_shape=jax.ShapeDtypeStruct((2, shard, w...]
    ppermute x10 -> x14, starting transfers between devices: 14.4 us -> 14.1 us  [swap(): return lax.ppermute(array, axis, [(i, i ^ offset) for i in range(count)])]
  transfers between devices with their start and end apart: 13 -> 18, of which waited for: 5 -> 7; matrix products, arithmetic and copies ran while one was open for 1% -> 2% of each run, Pallas kernels for 1% -> 3%
where the time goes in v4:
time: 46.8 us; the launch traced here: 46.6 us
  starting transfers between devices  20 us (43%)
  waiting for transfers between devices  18 us (38%)
  Pallas kernels  6.91 us (15%)
  between operations  0.81 us (2%)
  other arithmetic  0.71 us (2%)
    ppermute x14, starting transfers between devices, swap(): return lax.ppermute(array, axis, [(i, i ^ offset) for i in range(count)])  14.1 us
    ppermute x14, waiting for transfers between devices, swap(): return lax.ppermute(array, axis, [(i, i ^ offset) for i in range(count)])  9.15 us
    ppermute x3, waiting for transfers between devices, chip_shift(): lax.ppermute(array, axis, [(i, (i + 2 * step) % count) for i in range(cou...  8.81 us
    ppermute x3, starting transfers between devices, chip_shift(): lax.ppermute(array, axis, [(i, (i + 2 * step) % count) for i in range(cou...  5.14 us
    pallas_call x1, Pallas kernels, body(): local_call(functools.partial(attend_kernel, fsdp, block), jax.ShapeDtypeS...  3.82 us
    pallas_call x1, Pallas kernels, body(): pl.pallas_call(halves_kernel, out_shape=jax.ShapeDtypeStruct((2, shard, w...  1.8 us
  transfers between devices with their start and end apart: 18, of which 7 were waited for; matrix products, arithmetic and copies ran while one was open for 2% of the time, Pallas kernels for 3%

profile of v4, /device:TPU:0, one launch (start us, length us, event | category | flops | bytes accessed | tf_op | source)
XLA Modules:
  0.0 46.6 jit_solution(14783015521367188350)
XLA Ops:
  0.0 0.0 copy-start.6
  0.0 0.0 copy-start
  0.0 0.0 copy-start.4
  0.0 0.0 copy-start.3
  0.0 1.8 %halves.1 = bf16[2,192,384]{2,1,0:T(8,128)(2,1)} custom-call(bf16[192,768]{1,0:T(8,128)(2,1)} %refs_5_.1, bf16[192,768]{1,0:T(8,128)(2,1)} %refs_6_.1), custom_call_target="tpu_custom_call" | custom-call | tf_op jit(solution)/shard_map/halves/pallas_call | solution.py:276
  1.8 3.0 %collective-permute-start.3 = (bf16[2,192,384]{2,1,0:T(8,128)(2,1)}, bf16[2,192,384]{2,1,0:T(8,128)(2,1)S(1)}, u32[]{:S(2)}, u32[]{:S(2)}) collective-permute-start(bf16[2,192,384]{2,1,0:T(8,128)(2,1)} %halves.1), channel_id=1, source_target_pairs={{0,16},{8,24},{16,0},{24,8},{1,17},{9,25},{17,1},{25,9},{2,18},{10... | collective-permute-start | bytes 884744 | tf_op jit(solution)/shard_map/ppermute | solution.py:222
  4.9 0.0 copy-done.6
  4.9 0.7 %broadcast_add_fusion = s32[1,64,4]{1,2,0:T(4,128)S(1)} fusion(s32[1,64,4]{1,2,0:T(4,128)} %param.10), kind=kLoop, calls=%fused_computation.3 | loop fusion | flops 256 | bytes 2048 | tf_op jit(solution)/shard_map/add | solution.py:286
  5.6 0.1 copy.15
  5.7 0.1 copy.16
  5.8 0.0 copy-start.2
  5.8 0.0 copy-start.1
  5.8 0.8 %collective-permute-start.1 = (s32[64,4]{1,0:T(8,128)S(1)}, s32[64,4]{1,0:T(8,128)S(1)}, u32[]{:S(2)}, u32[]{:S(2)}) collective-permute-start(s32[64,4]{1,0:T(8,128)S(1)} %select_bitcast_fusion.here), channel_id=1, source_target_pairs={{1,2},{3,4},{5,6},{2,1},{4,3},{6,5},{9,10},{11,12},{13,14},{10,9},... | collective-permute-start | bytes 3080 | tf_op jit(solution)/shard_map/ppermute | solution.py:289
  6.6 4.3 %collective-permute-start = (s32[64,4]{1,0:T(8,128)S(1)}, s32[64,4]{1,0:T(8,128)S(1)}, u32[]{:S(2)}, u32[]{:S(2)}) collective-permute-start(s32[64,4]{1,0:T(8,128)S(1)} %select_bitcast_fusion.here), channel_id=1, source_target_pairs={{0,1},{1,0},{2,3},{3,2},{4,5},{5,4},{6,7},{7,6},{8,9},{9,8},{10,11... | collective-permute-start | bytes 3080 | tf_op jit(solution)/shard_map/ppermute | solution.py:217
  10.9 0.0 collective-permute-done.1.other
  11.0 1.9 %collective-permute-done.mate = s32[64,4]{1,0:T(8,128)S(1)} collective-permute-done((s32[64,4]{1,0:T(8,128)S(1)}, s32[64,4]{1,0:T(8,128)S(1)}, u32[]{:S(2)}, u32[]{:S(2)}) %collective-permute-start) | collective-permute-done | bytes 1056 | tf_op jit(solution)/shard_map/ppermute | solution.py:217
  12.8 0.0 copy-done
  12.8 0.5 %pool.1.mine = f32[24,768]{1,0:T(8,128)S(1)} custom-call(s32[64,4]{1,0:T(8,128)S(1)} %select_bitcast_fusion.here, s32[64,4]{1,0:T(8,128)S(1)} %collective-permute-done.mate, s32[64,4]{1,0:T(8,128)S(1)} %collective-permute-done.1.other, bf16[256,768]{1,0:T(8,128)(2,1)S(1)} %bitcast.7), custom_call_target="tpu_custom_call" | custom-call | flops 1000 | bytes 1000 | tf_op jit(solution)/shard_map/pool/pallas_call | solution.py:292
  13.3 0.0 copy-done.4
  13.3 0.1 collective-permute-start.4
  13.4 2.1 %collective-permute-start.2 = (f32[24,768]{1,0:T(8,128)S(1)}, f32[24,768]{1,0:T(8,128)S(1)}, u32[]{:S(2)}, u32[]{:S(2)}) collective-permute-start(f32[24,768]{1,0:T(8,128)S(1)} %pool.1.mine), channel_id=1, source_target_pairs={{0,1},{1,0},{2,3},{3,2},{4,5},{5,4},{6,7},{7,6},{8,9},{9,8},{10,11... | collective-permute-start | bytes 221192 | tf_op jit(solution)/shard_map/ppermute | solution.py:217
  15.5 0.0 copy-done.3
  15.5 0.2 collective-permute-start.5
  15.7 0.0 copy-done.1
  15.7 0.3 collective-permute-start.6
  16.0 2.3 %collective-permute-done.2.theirs = f32[24,768]{1,0:T(8,128)S(1)} collective-permute-done((f32[24,768]{1,0:T(8,128)S(1)}, f32[24,768]{1,0:T(8,128)S(1)}, u32[]{:S(2)}, u32[]{:S(2)}) %collective-permute-start.2) | collective-permute-done | bytes 73760 | tf_op jit(solution)/shard_map/ppermute | solution.py:217
  18.4 0.0 copy-done.2
  18.4 0.0 collective-permute-start.7
  18.4 0.0 collective-permute-done.3
  18.4 0.6 %collective-permute-start.11 = (bf16[192,768]{1,0:T(8,128)(2,1)S(1)}, bf16[192,768]{1,0:T(8,128)(2,1)S(1)}, u32[]{:S(2)}, u32[]{:S(2)}) collective-permute-start(bf16[192,768]{1,0:T(8,128)(2,1)S(1)} %copy-done.4), channel_id=1, source_target_pairs={{0,16},{8,24},{16,0},{24,8},{1,17},{9,25},{17,1},{25,9},{2,18},{10... | collective-permute-start | bytes 884744 | tf_op jit(solution)/shard_map/ppermute | solution.py:222
  19.0 0.0 collective-permute-done.4.mate
  19.0 1.5 %collective-permute-start.13 = (bf16[192,768]{1,0:T(8,128)(2,1)S(1)}, bf16[192,768]{1,0:T(8,128)(2,1)S(1)}, u32[]{:S(2)}, u32[]{:S(2)}) collective-permute-start(bf16[192,768]{1,0:T(8,128)(2,1)S(1)} %copy-done.3), channel_id=1, source_target_pairs={{0,16},{8,24},{16,0},{24,8},{1,17},{9,25},{17,1},{25,9},{2,18},{10... | collective-permute-start | bytes 884744 | tf_op jit(solution)/shard_map/ppermute | solution.py:222
  20.5 0.0 collective-permute-done.5.refs_7_
  20.5 0.0 collective-permute-done.6.refs_8_
  20.5 0.0 collective-permute-done.7.refs_9_
  20.5 7.7 %collective-permute-done.11 = bf16[192,768]{1,0:T(8,128)(2,1)S(1)} collective-permute-done((bf16[192,768]{1,0:T(8,128)(2,1)S(1)}, bf16[192,768]{1,0:T(8,128)(2,1)S(1)}, u32[]{:S(2)}, u32[]{:S(2)}) %collective-permute-start.11) | collective-permute-done | bytes 294944 | tf_op jit(solution)/shard_map/ppermute | solution.py:222
  28.3 0.0 collective-permute-start.12
  28.3 1.8 %collective-permute-start.14 = (bf16[1,2,192,384]{3,2,1,0:T(8,128)(2,1)S(1)}, bf16[1,2,192,384]{3,2,1,0:T(8,128)(2,1)S(1)}, u32[]{:S(2)}, u32[]{:S(2)}) collective-permute-start(bf16[1,2,192,384]{3,2,1,0:T(8,128)(2,1)S(1)} %bitcast.9), channel_id=1, source_target_pairs={{0,1},{1,0},{2,3},{3,2},{4,5},{5,4},{6,7},{7,6},{8,9},{9,8},{10,11... | collective-permute-start | bytes 884744 | tf_op jit(solution)/shard_map/ppermute | solution.py:217
  30.0 2.2 %collective-permute-start.10 = (bf16[48,768]{1,0:T(8,128)(2,1)S(1)}, bf16[48,768]{1,0:T(8,128)(2,1)S(1)}, u32[]{:S(2)}, u32[]{:S(2)}) collective-permute-start(bf16[48,768]{1,0:T(8,128)(2,1)S(1)} %pair.1), channel_id=1, source_target_pairs={{0,6},{1,7},{2,4},{3,5},{4,2},{5,3},{6,0},{7,1},{8,14},{9,15},{10,... | collective-permute-start | bytes 221192 | tf_op jit(solution)/shard_map/ppermute | solution.py:217
  32.2 0.8 %collective-permute-start.9 = (bf16[48,768]{1,0:T(8,128)(2,1)S(1)}, bf16[48,768]{1,0:T(8,128)(2,1)S(1)}, u32[]{:S(2)}, u32[]{:S(2)}) collective-permute-start(bf16[48,768]{1,0:T(8,128)(2,1)S(1)} %pair.1), channel_id=1, source_target_pairs={{0,4},{1,5},{2,6},{3,7},{4,0},{5,1},{6,2},{7,3},{8,12},{9,13},{10,... | collective-permute-start | bytes 221192 | tf_op jit(solution)/shard_map/ppermute | solution.py:217
  33.1 1.1 %collective-permute-done.13 = bf16[192,768]{1,0:T(8,128)(2,1)S(1)} collective-permute-done((bf16[192,768]{1,0:T(8,128)(2,1)S(1)}, bf16[192,768]{1,0:T(8,128)(2,1)S(1)}, u32[]{:S(2)}, u32[]{:S(2)}) %collective-permute-start.13) | collective-permute-done | bytes 294944 | tf_op jit(solution)/shard_map/ppermute | solution.py:222
  34.1 1.7 %collective-permute-start.8 = (bf16[48,768]{1,0:T(8,128)(2,1)S(1)}, bf16[48,768]{1,0:T(8,128)(2,1)S(1)}, u32[]{:S(2)}, u32[]{:S(2)}) collective-permute-start(bf16[48,768]{1,0:T(8,128)(2,1)S(1)} %pair.1), channel_id=1, source_target_pairs={{0,2},{1,3},{2,0},{3,1},{4,6},{5,7},{6,4},{7,5},{8,10},{9,11},{10,... | collective-permute-start | bytes 221192 | tf_op jit(solution)/shard_map/ppermute | solution.py:217
  35.8 0.8 %collective-permute-done.10 = bf16[48,768]{1,0:T(8,128)(2,1)S(1)} collective-permute-done((bf16[48,768]{1,0:T(8,128)(2,1)S(1)}, bf16[48,768]{1,0:T(8,128)(2,1)S(1)}, u32[]{:S(2)}, u32[]{:S(2)}) %collective-permute-start.10) | collective-permute-done | bytes 73760 | tf_op jit(solution)/shard_map/ppermute | solution.py:217
  36.6 0.0 collective-permute-start.15
  36.6 3.6 %collective-permute-done.9 = bf16[48,768]{1,0:T(8,128)(2,1)S(1)} collective-permute-done((bf16[48,768]{1,0:T(8,128)(2,1)S(1)}, bf16[48,768]{1,0:T(8,128)(2,1)S(1)}, u32[]{:S(2)}, u32[]{:S(2)}) %collective-permute-start.9) | collective-permute-done | bytes 73760 | tf_op jit(solution)/shard_map/ppermute | solution.py:217
  40.2 0.0 collective-permute-start.16
  40.2 0.0 collective-permute-done.8
  40.2 0.0 collective-permute-done.12.far
  40.2 0.0 copy-start.5
  40.2 0.8 %query.1.refs_3_ = bf16[256,768]{1,0:T(8,128)(2,1)S(1)} custom-call(bf16[256,768]{1,0:T(8,128)(2,1)S(1)} %bitcast.8, bf16[192,768]{1,0:T(8,128)(2,1)S(1)} %copy-done.4, bf16[192,768]{1,0:T(8,128)(2,1)S(1)} %collective-permute-done.4.mate, bf16[1,192,768]{2,1,0:T(8,128)(2,1)S(1)} %bitcast.15, bf16[1,192,768]{2,1,0:T(8,128)(2,1)S(1)} %collective-permute-done.12.far), custom_call_target="tpu_custom_call" | custom-call | flops 1000 | bytes 1000 | tf_op jit(solution)/shard_map/query/pallas_call | solution.py:309
  41.0 0.0 collective-permute-done.14.refs_12_
  41.0 0.6 %collective-permute-start.17 = (bf16[1,2,192,384]{3,2,1,0:T(8,128)(2,1)S(1)}, bf16[1,2,192,384]{3,2,1,0:T(8,128)(2,1)S(1)}, u32[]{:S(2)}, u32[]{:S(2)}) collective-permute-start(bf16[1,2,192,384]{3,2,1,0:T(8,128)(2,1)S(1)} %collective-permute-done.14.refs_12_), channel_id=1, source_target_pairs={{0,8},{8,0},{16,24},{24,16},{1,9},{9,1},{17,25},{25,17},{2,10},{10... | collective-permute-start | bytes 884744 | tf_op jit(solution)/shard_map/ppermute | solution.py:217
  42.3 0.0 copy-done.5
  42.3 0.0 collective-permute-done.15.refs_13_
  42.3 0.0 collective-permute-done.16.refs_14_
  42.3 0.5 %collective-permute-done.17.refs_15_ = bf16[1,2,192,384]{3,2,1,0:T(8,128)(2,1)S(1)} collective-permute-done((bf16[1,2,192,384]{3,2,1,0:T(8,128)(2,1)S(1)}, bf16[1,2,192,384]{3,2,1,0:T(8,128)(2,1)S(1)}, u32[]{:S(2)}, u32[]{:S(2)}) %collective-permute-start.17) | collective-permute-done | bytes 294944 | tf_op jit(solution)/shard_map/ppermute | solution.py:217
  42.8 3.8 %attend.1 = bf16[256,768]{1,0:T(8,128)(2,1)} custom-call(s32[1]{0:T(128)S(6)} %copy.17.refs_0_, bf16[192,768]{1,0:T(8,128)(2,1)S(1)} %pad_maximum_fusion.refs_1_, f32[1,768]{1,0:T(1,128)S(1)} %broadcast_in_dim.8.refs_2_, bf16[256,768]{1,0:T(8,128)(2,1)S(1)} %query.1.refs_3_, bf16[192,768]{1,0:T(8,128)(2,1)S(1)} %copy-done.3, bf16[192,768]{1,0:T(8,128)(2,1)S(1)} %copy-done.1, ...), custom_call_target="tpu_custom_call" | custom-call | flops 1000 | bytes 1000 | tf_op jit(solution)/shard_map/attend/pallas_call | solution.py:318
  (5 shorter events, 0.1 us)
Async XLA Ops:
  0.0 4.9 %copy-start.6 = (s32[1,64,4]{1,2,0:T(4,128)S(1)}, s32[1,64,4]{1,2,0:T(4,128)}, u32[]{:S(2)}) copy-start(s32[1,64,4]{1,2,0:T(4,128)} %param.11) | copy-start | bytes 3076
  0.0 12.8 %copy-start = (bf16[1,256,768]{2,1,0:T(8,128)(2,1)S(1)}, bf16[1,256,768]{2,1,0:T(8,128)(2,1)}, u32[]{:S(2)}) copy-start(bf16[1,256,768]{2,1,0:T(8,128)(2,1)} %param.9) | copy-start | bytes 1179652
  0.0 13.3 %copy-start.4 = (bf16[192,768]{1,0:T(8,128)(2,1)S(1)}, bf16[192,768]{1,0:T(8,128)(2,1)}, u32[]{:S(2)}) copy-start(bf16[192,768]{1,0:T(8,128)(2,1)} %piece.1) | copy-start | bytes 884740
  0.0 15.5 %copy-start.3 = (bf16[192,768]{1,0:T(8,128)(2,1)S(1)}, bf16[192,768]{1,0:T(8,128)(2,1)}, u32[]{:S(2)}) copy-start(bf16[192,768]{1,0:T(8,128)(2,1)} %refs_4_.1) | copy-start | bytes 884740
  1.8 16.6 %collective-permute-start.3 = (bf16[2,192,384]{2,1,0:T(8,128)(2,1)}, bf16[2,192,384]{2,1,0:T(8,128)(2,1)S(1)}, u32[]{:S(2)}, u32[]{:S(2)}) collective-permute-start(bf16[2,192,384]{2,1,0:T(8,128)(2,1)} %halves.1), channel_id=1, source_target_pairs={{0,16},{8,24},{16,0},{24,8},{1,17},{9,25},{17,1},{25,9},{2,18},{10... | collective-permute-start | bytes 884744 | tf_op jit(solution)/shard_map/ppermute | solution.py:222
  5.8 12.6 %copy-start.2 = (bf16[192,768]{1,0:T(8,128)(2,1)S(1)}, bf16[192,768]{1,0:T(8,128)(2,1)}, u32[]{:S(2)}) copy-start(bf16[192,768]{1,0:T(8,128)(2,1)} %refs_6_.1) | copy-start | bytes 884740
  5.8 9.9 %copy-start.1 = (bf16[192,768]{1,0:T(8,128)(2,1)S(1)}, bf16[192,768]{1,0:T(8,128)(2,1)}, u32[]{:S(2)}) copy-start(bf16[192,768]{1,0:T(8,128)(2,1)} %refs_5_.1) | copy-start | bytes 884740
  5.8 5.2 %collective-permute-start.1 = (s32[64,4]{1,0:T(8,128)S(1)}, s32[64,4]{1,0:T(8,128)S(1)}, u32[]{:S(2)}, u32[]{:S(2)}) collective-permute-start(s32[64,4]{1,0:T(8,128)S(1)} %select_bitcast_fusion.here), channel_id=1, source_target_pairs={{1,2},{3,4},{5,6},{2,1},{4,3},{6,5},{9,10},{11,12},{13,14},{10,9},... | collective-permute-start | bytes 3080 | tf_op jit(solution)/shard_map/ppermute | solution.py:289
  6.6 6.2 %collective-permute-start = (s32[64,4]{1,0:T(8,128)S(1)}, s32[64,4]{1,0:T(8,128)S(1)}, u32[]{:S(2)}, u32[]{:S(2)}) collective-permute-start(s32[64,4]{1,0:T(8,128)S(1)} %select_bitcast_fusion.here), channel_id=1, source_target_pairs={{0,1},{1,0},{2,3},{3,2},{4,5},{5,4},{6,7},{7,6},{8,9},{9,8},{10,11... | collective-permute-start | bytes 3080 | tf_op jit(solution)/shard_map/ppermute | solution.py:217
  13.3 5.6 %collective-permute-start.4 = (bf16[192,768]{1,0:T(8,128)(2,1)S(1)}, bf16[192,768]{1,0:T(8,128)(2,1)S(1)}, u32[]{:S(2)}, u32[]{:S(2)}) collective-permute-start(bf16[192,768]{1,0:T(8,128)(2,1)S(1)} %copy-done.4), channel_id=1, source_target_pairs={{0,8},{8,0},{16,24},{24,16},{1,9},{9,1},{17,25},{25,17},{2,10},{10... | collective-permute-start | bytes 884744 | tf_op jit(solution)/shard_map/ppermute | solution.py:217
  13.4 4.9 %collective-permute-start.2 = (f32[24,768]{1,0:T(8,128)S(1)}, f32[24,768]{1,0:T(8,128)S(1)}, u32[]{:S(2)}, u32[]{:S(2)}) collective-permute-start(f32[24,768]{1,0:T(8,128)S(1)} %pool.1.mine), channel_id=1, source_target_pairs={{0,1},{1,0},{2,3},{3,2},{4,5},{5,4},{6,7},{7,6},{8,9},{9,8},{10,11... | collective-permute-start | bytes 221192 | tf_op jit(solution)/shard_map/ppermute | solution.py:217
  15.5 5.0 %collective-permute-start.5 = (bf16[192,768]{1,0:T(8,128)(2,1)S(1)}, bf16[192,768]{1,0:T(8,128)(2,1)S(1)}, u32[]{:S(2)}, u32[]{:S(2)}) collective-permute-start(bf16[192,768]{1,0:T(8,128)(2,1)S(1)} %copy-done.3), channel_id=1, source_target_pairs={{0,8},{8,0},{16,24},{24,16},{1,9},{9,1},{17,25},{25,17},{2,10},{10... | collective-permute-start | bytes 884744 | tf_op jit(solution)/shard_map/ppermute | solution.py:217
  15.7 4.8 %collective-permute-start.6 = (bf16[192,768]{1,0:T(8,128)(2,1)S(1)}, bf16[192,768]{1,0:T(8,128)(2,1)S(1)}, u32[]{:S(2)}, u32[]{:S(2)}) collective-permute-start(bf16[192,768]{1,0:T(8,128)(2,1)S(1)} %copy-done.1), channel_id=1, source_target_pairs={{0,8},{8,0},{16,24},{24,16},{1,9},{9,1},{17,25},{25,17},{2,10},{10... | collective-permute-start | bytes 884744 | tf_op jit(solution)/shard_map/ppermute | solution.py:217
  18.4 2.1 %collective-permute-start.7 = (bf16[192,768]{1,0:T(8,128)(2,1)S(1)}, bf16[192,768]{1,0:T(8,128)(2,1)S(1)}, u32[]{:S(2)}, u32[]{:S(2)}) collective-permute-start(bf16[192,768]{1,0:T(8,128)(2,1)S(1)} %copy-done.2), channel_id=1, source_target_pairs={{0,8},{8,0},{16,24},{24,16},{1,9},{9,1},{17,25},{25,17},{2,10},{10... | collective-permute-start | bytes 884744 | tf_op jit(solution)/shard_map/ppermute | solution.py:217
  18.4 9.9 %collective-permute-start.11 = (bf16[192,768]{1,0:T(8,128)(2,1)S(1)}, bf16[192,768]{1,0:T(8,128)(2,1)S(1)}, u32[]{:S(2)}, u32[]{:S(2)}) collective-permute-start(bf16[192,768]{1,0:T(8,128)(2,1)S(1)} %copy-done.4), channel_id=1, source_target_pairs={{0,16},{8,24},{16,0},{24,8},{1,17},{9,25},{17,1},{25,9},{2,18},{10... | collective-permute-start | bytes 884744 | tf_op jit(solution)/shard_map/ppermute | solution.py:222
  19.0 15.2 %collective-permute-start.13 = (bf16[192,768]{1,0:T(8,128)(2,1)S(1)}, bf16[192,768]{1,0:T(8,128)(2,1)S(1)}, u32[]{:S(2)}, u32[]{:S(2)}) collective-permute-start(bf16[192,768]{1,0:T(8,128)(2,1)S(1)} %copy-done.3), channel_id=1, source_target_pairs={{0,16},{8,24},{16,0},{24,8},{1,17},{9,25},{17,1},{25,9},{2,18},{10... | collective-permute-start | bytes 884744 | tf_op jit(solution)/shard_map/ppermute | solution.py:222
  28.3 11.9 %collective-permute-start.12 = (bf16[1,192,768]{2,1,0:T(8,128)(2,1)S(1)}, bf16[1,192,768]{2,1,0:T(8,128)(2,1)S(1)}, u32[]{:S(2)}, u32[]{:S(2)}) collective-permute-start(bf16[1,192,768]{2,1,0:T(8,128)(2,1)S(1)} %bitcast.14), channel_id=1, source_target_pairs={{0,8},{8,0},{16,24},{24,16},{1,9},{9,1},{17,25},{25,17},{2,10},{10... | collective-permute-start | bytes 884744 | tf_op jit(solution)/shard_map/ppermute | solution.py:217
  28.3 12.8 %collective-permute-start.14 = (bf16[1,2,192,384]{3,2,1,0:T(8,128)(2,1)S(1)}, bf16[1,2,192,384]{3,2,1,0:T(8,128)(2,1)S(1)}, u32[]{:S(2)}, u32[]{:S(2)}) collective-permute-start(bf16[1,2,192,384]{3,2,1,0:T(8,128)(2,1)S(1)} %bitcast.9), channel_id=1, source_target_pairs={{0,1},{1,0},{2,3},{3,2},{4,5},{5,4},{6,7},{7,6},{8,9},{9,8},{10,11... | collective-permute-start | bytes 884744 | tf_op jit(solution)/shard_map/ppermute | solution.py:217
  30.0 6.6 %collective-permute-start.10 = (bf16[48,768]{1,0:T(8,128)(2,1)S(1)}, bf16[48,768]{1,0:T(8,128)(2,1)S(1)}, u32[]{:S(2)}, u32[]{:S(2)}) collective-permute-start(bf16[48,768]{1,0:T(8,128)(2,1)S(1)} %pair.1), channel_id=1, source_target_pairs={{0,6},{1,7},{2,4},{3,5},{4,2},{5,3},{6,0},{7,1},{8,14},{9,15},{10,... | collective-permute-start | bytes 221192 | tf_op jit(solution)/shard_map/ppermute | solution.py:217
  32.2 7.9 %collective-permute-start.9 = (bf16[48,768]{1,0:T(8,128)(2,1)S(1)}, bf16[48,768]{1,0:T(8,128)(2,1)S(1)}, u32[]{:S(2)}, u32[]{:S(2)}) collective-permute-start(bf16[48,768]{1,0:T(8,128)(2,1)S(1)} %pair.1), channel_id=1, source_target_pairs={{0,4},{1,5},{2,6},{3,7},{4,0},{5,1},{6,2},{7,3},{8,12},{9,13},{10,... | collective-permute-start | bytes 221192 | tf_op jit(solution)/shard_map/ppermute | solution.py:217
  34.1 6.1 %collective-permute-start.8 = (bf16[48,768]{1,0:T(8,128)(2,1)S(1)}, bf16[48,768]{1,0:T(8,128)(2,1)S(1)}, u32[]{:S(2)}, u32[]{:S(2)}) collective-permute-start(bf16[48,768]{1,0:T(8,128)(2,1)S(1)} %pair.1), channel_id=1, source_target_pairs={{0,2},{1,3},{2,0},{3,1},{4,6},{5,7},{6,4},{7,5},{8,10},{9,11},{10,... | collective-permute-start | bytes 221192 | tf_op jit(solution)/shard_map/ppermute | solution.py:217
  36.6 5.7 %collective-permute-start.15 = (bf16[1,192,768]{2,1,0:T(8,128)(2,1)S(1)}, bf16[1,192,768]{2,1,0:T(8,128)(2,1)S(1)}, u32[]{:S(2)}, u32[]{:S(2)}) collective-permute-start(bf16[1,192,768]{2,1,0:T(8,128)(2,1)S(1)} %bitcast.12), channel_id=1, source_target_pairs={{0,8},{8,0},{16,24},{24,16},{1,9},{9,1},{17,25},{25,17},{2,10},{10... | collective-permute-start | bytes 884744 | tf_op jit(solution)/shard_map/ppermute | solution.py:217
  40.2 2.1 %collective-permute-start.16 = (bf16[1,2,192,384]{3,2,1,0:T(8,128)(2,1)S(1)}, bf16[1,2,192,384]{3,2,1,0:T(8,128)(2,1)S(1)}, u32[]{:S(2)}, u32[]{:S(2)}) collective-permute-start(bf16[1,2,192,384]{3,2,1,0:T(8,128)(2,1)S(1)} %bitcast.10), channel_id=1, source_target_pairs={{0,8},{8,0},{16,24},{24,16},{1,9},{9,1},{17,25},{25,17},{2,10},{10... | collective-permute-start | bytes 884744 | tf_op jit(solution)/shard_map/ppermute | solution.py:217
  40.2 2.0 %copy-start.5 = (f32[768]{0:T(1024)S(1)}, f32[768]{0:T(1024)}, u32[]{:S(2)}) copy-start(f32[768]{0:T(1024)} %param.17) | copy-start | bytes 9220
  41.0 1.8 %collective-permute-start.17 = (bf16[1,2,192,384]{3,2,1,0:T(8,128)(2,1)S(1)}, bf16[1,2,192,384]{3,2,1,0:T(8,128)(2,1)S(1)}, u32[]{:S(2)}, u32[]{:S(2)}) collective-permute-start(bf16[1,2,192,384]{3,2,1,0:T(8,128)(2,1)S(1)} %collective-permute-done.14.refs_12_), channel_id=1, source_target_pairs={{0,8},{8,0},{16,24},{24,16},{1,9},{9,1},{17,25},{25,17},{2,10},{10... | collective-permute-start | bytes 884744 | tf_op jit(solution)/shard_map/ppermute | solution.py:217

commit v5 on v4

--- a/solution.py
+++ b/solution.py
@@ -102,70 +102,39 @@
     return jnp.concatenate(out, axis=0).astype(BF16)
 
 
-def place_rows(fsdp, shard, held):
-    half_width = held.shape[2] // 2
+def first_rows(fsdp, rows):
+    me = lax.axis_index("fsdp")
     chips = fsdp // 2
-    me = lax.axis_index("fsdp")
-    cut = lax.axis_index("tile") % 2
     chip, core = me // 2, me % 2
-
-    def at(weight, owner, side):
-        rows = pl.ds(pl.multiple_of(owner * shard, shard), shard)
-        if side is None:
-            return held.at[weight, rows]
-        columns = pl.ds(pl.multiple_of(side * half_width, half_width), half_width)
-        return held.at[weight, rows, columns]
-
-    def own(weight, piece, mate):
-        return [(piece, at(weight, me, None)), (mate, at(weight, 2 * chip + 1 - core, None))]
-
-    def others(weight, near, far, side=None):
-        copies = []
-        for j in range(1, chips):
-            source = 2 * lax.rem(chip - j + chips, chips)
-            columns = None if side is None else (cut if side == 0 else 1 - cut)
-            copies.append((near(j - 1), at(weight, source + core, columns)))
-            copies.append((far(j - 1), at(weight, source + 1 - core, columns)))
-        return copies
-
-    return own, others
-
-
-def query_kernel(fsdp, tiles, piece, mate, near, far, out, held, sem):
-    own, others = place_rows(fsdp, piece.shape[0], held)
-    copies = own(0, piece, mate) + others(0, lambda j: near.at[j], lambda j: far.at[j])
-    for copy in collect(copies, sem):
+    owners = [me, 2 * chip + 1 - core]
+    for j in range(1, chips):
+        source = 2 * lax.rem(chip - j + chips, chips)
+        owners += [source + core, source + 1 - core]
+    return [pl.multiple_of(owner * rows, rows) for owner in owners]
+
+
+def place(fsdp, pieces, held):
+    rows = pieces[0].shape[0]
+    begins = first_rows(fsdp, rows)
+    return [(piece, held.at[pl.ds(begin, rows)]) for piece, begin in zip(pieces, begins)]
+
+
+def query_kernel(fsdp, tiles, *refs):
+    pieces = refs[:fsdp]
+    out, held, sem = refs[fsdp:]
+    for copy in collect(place(fsdp, pieces, held), sem):
         copy.wait()
-    out[...] = over(tiles[...], held[0], 1, 0).astype(BF16)
+    out[...] = over(tiles[...], held[...], 1, 0).astype(BF16)
 
 
 def attend_kernel(fsdp, block, *refs):
     count, sums, gain, query = refs[:4]
-    pieces, mates = refs[4:7], refs[7:10]
-    near, far = refs[10:13], refs[13:16]
-    out, held, pooled, sem = refs[16:]
+    key_pieces, value_pieces = refs[4 : 4 + fsdp], refs[4 + fsdp : 4 + 2 * fsdp]
+    out, held, pooled, sem = refs[4 + 2 * fsdp :]
     device = lax.axis_index("tile")
-    own, others = place_rows(fsdp, pieces[0].shape[0], held)
-    copies, ends = [], []
-    for weight in (1, 2, 0):
-        copies += own(weight, pieces[weight], mates[weight])
-        if weight == 0:
-            copies += others(0, lambda j: near[0].at[j], lambda j: far[0].at[j])
-        else:
-            for side in range(2):
-                copies += others(
-                    weight,
-                    lambda j: near[1 + side].at[j, weight - 1],
-                    lambda j: far[1 + side].at[j, weight - 1],
-                    side,
-                )
-        ends.append(len(copies))
-    started = collect(copies, sem)
-
-    def arrive(begin, end):
-        for copy in started[begin:end]:
-            copy.wait()
-
+    started = collect(
+        place(fsdp, key_pieces, held.at[0]) + place(fsdp, value_pieces, held.at[1]), sem
+    )
     pooled[...] = jnp.zeros_like(pooled)
     pairs = sums.shape[0] // (6 * block)
     for s in range(pairs):
@@ -180,10 +149,10 @@
     scale = lax.rsqrt(jnp.mean(mean * mean, axis=1, keepdims=True) + 1e-06)
     normed = (mean * scale * gain[...]).astype(BF16)
     ordered = sorted_rows(normed)
-    arrive(0, ends[0])
+    for copy in started:
+        copy.wait()
+    keys = over(ordered, held[0], 1, 0).astype(BF16)
     values = over(ordered, held[1], 1, 0).astype(BF16)
-    arrive(ends[1], ends[2])
-    keys = over(ordered, held[0], 1, 0).astype(BF16)
     half = keys.shape[0] // KEY_DILATION
     heads = HEADS // LANE_GROUPS
     wide = keys.shape[1] // LANE_GROUPS
@@ -197,7 +166,6 @@
     hidden = jnp.concatenate(
         [jnp.where(valid[head % KEY_DILATION], 0.0, -jnp.inf) for head in range(heads)], axis=0
     )
-    contexts = []
     for group in range(LANE_GROUPS):
         lanes = slice(group * wide, (group + 1) * wide)
         score = over(spread(keys, group, wide), query[:, lanes], 1, 1)
@@ -206,10 +174,24 @@
         share = 1.0 / jnp.sum(expo, axis=1, keepdims=True)
         weight = expo.reshape(heads * half, rows).astype(BF16)
         context = over(spread(values, group, wide), weight, 0, 0).reshape(heads, size, rows)
-        contexts.append((context * share).reshape(wide, rows).astype(BF16))
-    arrive(ends[0], ends[1])
-    context = jnp.concatenate(contexts, axis=0)
-    out[...] = over(context, held[2], 0, 0).astype(out.dtype)
+        out[lanes, :] = (context * share).reshape(wide, rows).astype(BF16)
+
+
+def near_kernel(fsdp, context, piece, mate, out):
+    rows = piece.shape[0]
+    begins = first_rows(fsdp, rows)
+    total = over(context[pl.ds(begins[0], rows), :], piece[...], 0, 0)
+    out[...] = total + over(context[pl.ds(begins[1], rows), :], mate[...], 0, 0)
+
+
+def far_kernel(fsdp, context, total, *refs):
+    pieces, out = refs[:-1], refs[-1]
+    rows = pieces[0].shape[0]
+    begins = first_rows(fsdp, rows)[2:]
+    sums = total[...]
+    for begin, piece in zip(begins, pieces):
+        sums = sums + over(context[pl.ds(begin, rows), :], piece[...], 0, 0)
+    out[...] = sums.astype(out.dtype)
 
 
 def swap(array, axis, offset):
@@ -222,22 +204,20 @@
     return lax.ppermute(array, axis, [(i, (i + 2 * step) % count) for i in range(count)])
 
 
-def halves_kernel(w_value, w_out, halves, sem):
-    cut = lax.axis_index("tile") % 2
-    width = halves.shape[2]
-    columns = pl.ds(pl.multiple_of(cut * width, width), width)
-    copies = [(w.at[:, columns], halves.at[n]) for n, w in enumerate((w_value, w_out))]
-    for copy in collect(copies, sem):
-        copy.wait()
-
-
 def behind(array, *others):
     return lax.optimization_barrier((array,) + others)[0]
 
 
 def from_chips(weight):
-    chips = lax.axis_size("fsdp") // 2
-    return jnp.stack([chip_shift(weight, "fsdp", j) for j in range(1, chips)])
+    return [chip_shift(weight, "fsdp", j) for j in range(1, lax.axis_size("fsdp") // 2)]
+
+
+def both_cores(near):
+    return [piece for mine in near for piece in (mine, swap(mine, "fsdp", 1))]
+
+
+def behind_each(arrays, *others):
+    return [behind(array, *others) for array in arrays]
 
 
 def gather_pairs(rows, axis):
@@ -272,23 +252,12 @@
     regions = nbr_tiles.shape[1]
     block = regions // REGIONS_PER_KEY
 
-    shard = w_query.shape[0]
-    halves = pl.pallas_call(
-        halves_kernel,
-        out_shape=jax.ShapeDtypeStruct((2, shard, width // 2), BF16),
-        in_specs=[anywhere()] * 2,
-        out_specs=vmem(),
-        scratch_shapes=[pltpu.SemaphoreType.DMA((2,))],
-        name="halves",
-    )(w_value, w_out)
-    near_halves = from_chips(halves)
-
+    near_query = from_chips(w_query)
+    near_key = from_chips(w_key)
     slots = jnp.where(nbr_mask[0] > 0, nbr_tiles[0] + 1, 0)
     mate = swap(slots, "tile", 1)
     inner = [(i, i + 1) for i in range(1, tile_devices - 1, 2)]
     other = lax.ppermute(slots, "tile", inner + [(b, a) for a, b in inner])
-    near_query = from_chips(behind(w_query, slots))
-    near_key = from_chips(behind(w_key, slots))
     mine = local_call(
         pool_kernel,
         jax.ShapeDtypeStruct((3 * block, width), F32),
@@ -296,45 +265,56 @@
         "pool",
     )(slots, mate, other, own_tiles)
     mates = [swap(behind(w, mine), "fsdp", 1) for w in (w_query, w_key, w_value, w_out)]
+    near_value = from_chips(behind(w_value, slots))
+    near_out = from_chips(behind(w_out, mine))
+    all_query = both_cores(near_query)
     pair = local_call(
         pair_kernel,
         jax.ShapeDtypeStruct((6 * block, width), BF16),
         [vmem()] * 2,
         "pair",
-    )(mine, behind(swap(mine, "tile", 1), near_halves, *mates))
-    near_halves = behind(near_halves, pair)
-    other_halves = swap(near_halves, "tile", 1)
-    far_halves = swap(near_halves, "fsdp", 1)
-    near_query = behind(near_query, pair)
+    )(mine, behind(swap(mine, "tile", 1), *mates, *all_query, *near_key))
+    near_key = behind_each(near_key, pair)
     query = local_call(
         functools.partial(query_kernel, fsdp),
         jax.ShapeDtypeStruct((rows, width), BF16),
-        [vmem()] + [anywhere()] * 4,
+        [vmem()] + [anywhere()] * fsdp,
         "query",
-        [pltpu.VMEM((1, width, width), BF16), pltpu.SemaphoreType.DMA((fsdp,))],
-    )(own_tiles, w_query, mates[0], near_query, swap(near_query, "fsdp", 1))
-    sums = behind(gather_pairs(pair, "tile"), query, near_key)
-    other_halves = behind(other_halves, sums)
-    attended = local_call(
+        [pltpu.VMEM((width, width), BF16), pltpu.SemaphoreType.DMA((fsdp,))],
+    )(behind(own_tiles, pair), w_query, mates[0], *all_query)
+    sums = behind(gather_pairs(pair, "tile"), query)
+    near_value = behind_each(near_value, sums)
+    context = local_call(
         functools.partial(attend_kernel, fsdp, block),
-        jax.ShapeDtypeStruct((rows, width), BF16),
-        [smem()] + [vmem()] * 3 + [anywhere()] * 12,
+        jax.ShapeDtypeStruct((width, rows), BF16),
+        [smem()] + [vmem()] * 3 + [anywhere()] * (2 * fsdp),
         "attend",
         [
-            pltpu.VMEM((3, width, width), BF16),
+            pltpu.VMEM((2, width, width), BF16),
             pltpu.VMEM(((tile_devices + 2) * block, width), F32),
-            pltpu.SemaphoreType.DMA((5 * fsdp,)),
+            pltpu.SemaphoreType.DMA((2 * fsdp,)),
         ],
     )(
         tile_count,
         sums,
         key_gain[None, :],
         query,
-        *(w_key, w_value, w_out),
-        *mates[1:],
-        *(near_key, near_halves, other_halves),
-        *(swap(near_key, "fsdp", 1), far_halves, swap(other_halves, "fsdp", 1)),
-    )
+        *(w_key, mates[1], *both_cores(near_key)),
+        *(w_value, mates[2], *both_cores(near_value)),
+    )
+    total = local_call(
+        functools.partial(near_kernel, fsdp),
+        jax.ShapeDtypeStruct((rows, width), F32),
+        [vmem()] * 3,
+        "project_near",
+    )(context, w_out, mates[3])
+    far_out = both_cores(behind_each(near_out, context))
+    attended = local_call(
+        functools.partial(far_kernel, fsdp),
+        jax.ShapeDtypeStruct((rows, width), BF16),
+        [vmem()] * fsdp,
+        "project_far",
+    )(context, total, *far_out)
     return attended[None]
 
 

time: 46.8 us -> 44.9 us (0.959)
  waiting for transfers between devices: 18 us -> 15.4 us
  Pallas kernels: 6.91 us -> 5.17 us
  local copies, waits for them, and re-layouts: 0.25 us -> 1.83 us
  starting transfers between devices: 20 us -> 20.8 us
    ppermute x3 -> x4, waiting for transfers between devices: 8.81 us -> 4.83 us  [chip_shift(): lax.ppermute(array, axis, [(i, (i + 2 * step) % count) for i in range(cou...]
    unnamed x14 -> x16, local copies, waits for them, and re-layouts: 0.03 us -> 1.61 us
    pallas_call x1, Pallas kernels: 3.82 us -> 2.3 us  [body(): local_call(functools.partial(attend_kernel, fsdp, block), jax.ShapeDtypeS...]
    ppermute x14 -> x13, waiting for transfers between devices: 9.15 us -> 10.6 us  [swap(): return lax.ppermute(array, axis, [(i, i ^ offset) for i in range(count)])]
    ppermute x3 -> x4, starting transfers between devices: 5.14 us -> 6.52 us  [chip_shift(): lax.ppermute(array, axis, [(i, (i + 2 * step) % count) for i in range(cou...]
    ppermute x14 -> x13, starting transfers between devices: 14.1 us -> 13.6 us  [swap(): return lax.ppermute(array, axis, [(i, i ^ offset) for i in range(count)])]
    pallas_call x1 -> x2, Pallas kernels: 1.8 us -> 1.58 us  [the longest x1 1.16 us: body(): local_call(functools.partial(far_kernel, fsdp), jax.ShapeDtypeStruct((row...]
  transfers between devices with their start and end apart: 18 -> 18, of which waited for: 7 -> 5; matrix products, arithmetic and copies ran while one was open for 2% -> 2% of each run, Pallas kernels for 3% -> 9%
where the time goes in v5:
time: 44.9 us; the launch traced here: 44.7 us
  starting transfers between devices  20.8 us (46%)
  waiting for transfers between devices  15.4 us (34%)
  Pallas kernels  5.17 us (12%)
  local copies, waits for them, and re-layouts  1.83 us (4%)
  between operations  0.84 us (2%)
  other arithmetic  0.72 us (2%)
    ppermute x13, starting transfers between devices, swap(): return lax.ppermute(array, axis, [(i, i ^ offset) for i in range(count)])  13.6 us
    ppermute x13, waiting for transfers between devices, swap(): return lax.ppermute(array, axis, [(i, i ^ offset) for i in range(count)])  10.6 us
    ppermute x4, starting transfers between devices, chip_shift(): lax.ppermute(array, axis, [(i, (i + 2 * step) % count) for i in range(cou...  6.52 us
    ppermute x4, waiting for transfers between devices, chip_shift(): lax.ppermute(array, axis, [(i, (i + 2 * step) % count) for i in range(cou...  4.83 us
    pallas_call x1, Pallas kernels, body(): local_call(functools.partial(attend_kernel, fsdp, block), jax.ShapeDtypeS...  2.3 us
    unnamed x16, local copies, waits for them, and re-layouts  1.61 us
    pallas_call x1, Pallas kernels, body(): local_call(functools.partial(far_kernel, fsdp), jax.ShapeDtypeStruct((row...  1.16 us
  transfers between devices with their start and end apart: 18, of which 5 were waited for; matrix products, arithmetic and copies ran while one was open for 2% of the time, Pallas kernels for 9%

profile of v5, /device:TPU:0, one launch (start us, length us, event | category | flops | bytes accessed | tf_op | source)
XLA Modules:
  0.0 44.7 jit_solution(10607468166557242284)
XLA Ops:
  0.0 3.0 %collective-permute-start.7 = (bf16[192,768]{1,0:T(8,128)(2,1)}, bf16[192,768]{1,0:T(8,128)(2,1)S(1)}, u32[]{:S(2)}, u32[]{:S(2)}) collective-permute-start(bf16[192,768]{1,0:T(8,128)(2,1)} %refs_0_.2), channel_id=1, source_target_pairs={{0,16},{8,24},{16,0},{24,8},{1,17},{9,25},{17,1},{25,9},{2,18},{10... | collective-permute-start | bytes 884744 | tf_op jit(solution)/shard_map/ppermute | solution.py:204
  3.0 0.0 collective-permute-start.9
  3.0 0.7 %broadcast_add_fusion = s32[1,64,4]{1,2,0:T(4,128)S(1)} fusion(s32[1,64,4]{1,2,0:T(4,128)} %param.10), kind=kLoop, calls=%fused_computation.3 | loop fusion | flops 256 | bytes 2048 | tf_op jit(solution)/shard_map/add | solution.py:257
  3.7 0.0 copy-start.7
  3.7 0.1 copy.16
  3.8 0.6 %copy-done.7 = s32[1,64,4]{1,2,0:T(4,128)S(1)} copy-done((s32[1,64,4]{1,2,0:T(4,128)S(1)}, s32[1,64,4]{1,2,0:T(4,128)}, u32[]{:S(2)}) %copy-start.7) | copy-done | bytes 1048
  4.4 0.1 copy.15
  4.5 2.0 %collective-permute-start = (s32[64,4]{1,0:T(8,128)S(1)}, s32[64,4]{1,0:T(8,128)S(1)}, u32[]{:S(2)}, u32[]{:S(2)}) collective-permute-start(s32[64,4]{1,0:T(8,128)S(1)} %select_bitcast_fusion.here), channel_id=1, source_target_pairs={{0,1},{1,0},{2,3},{3,2},{4,5},{5,4},{6,7},{7,6},{8,9},{9,8},{10,11... | collective-permute-start | bytes 3080 | tf_op jit(solution)/shard_map/ppermute | solution.py:199
  6.5 0.7 %collective-permute-start.1 = (s32[64,4]{1,0:T(8,128)S(1)}, s32[64,4]{1,0:T(8,128)S(1)}, u32[]{:S(2)}, u32[]{:S(2)}) collective-permute-start(s32[64,4]{1,0:T(8,128)S(1)} %select_bitcast_fusion.here), channel_id=1, source_target_pairs={{1,2},{3,4},{5,6},{2,1},{4,3},{6,5},{9,10},{11,12},{13,14},{10,9},... | collective-permute-start | bytes 3080 | tf_op jit(solution)/shard_map/ppermute | solution.py:260
  7.2 1.3 %collective-permute-done.mate = s32[64,4]{1,0:T(8,128)S(1)} collective-permute-done((s32[64,4]{1,0:T(8,128)S(1)}, s32[64,4]{1,0:T(8,128)S(1)}, u32[]{:S(2)}, u32[]{:S(2)}) %collective-permute-start) | collective-permute-done | bytes 1056 | tf_op jit(solution)/shard_map/ppermute | solution.py:199
  8.5 0.0 collective-permute-done.1.other
  8.5 0.0 copy-start
  8.5 1.0 %copy-done = bf16[1,256,768]{2,1,0:T(8,128)(2,1)S(1)} copy-done((bf16[1,256,768]{2,1,0:T(8,128)(2,1)S(1)}, bf16[1,256,768]{2,1,0:T(8,128)(2,1)}, u32[]{:S(2)}) %copy-start) | copy-done | bytes 393240
  9.5 0.0 copy-start.1
  9.5 0.0 copy-start.5
  9.5 0.5 %pool.1.mine = f32[24,768]{1,0:T(8,128)S(1)} custom-call(s32[64,4]{1,0:T(8,128)S(1)} %select_bitcast_fusion.here, s32[64,4]{1,0:T(8,128)S(1)} %collective-permute-done.mate, s32[64,4]{1,0:T(8,128)S(1)} %collective-permute-done.1.other, bf16[256,768]{1,0:T(8,128)(2,1)S(1)} %bitcast.4), custom_call_target="tpu_custom_call" | custom-call | flops 1000 | bytes 1000 | tf_op jit(solution)/shard_map/pool/pallas_call | solution.py:261
  10.0 0.1 collective-permute-start.6
  10.1 4.9 %collective-permute-start.2 = (f32[24,768]{1,0:T(8,128)S(1)}, f32[24,768]{1,0:T(8,128)S(1)}, u32[]{:S(2)}, u32[]{:S(2)}) collective-permute-start(f32[24,768]{1,0:T(8,128)S(1)} %pool.1.mine), channel_id=1, source_target_pairs={{0,1},{1,0},{2,3},{3,2},{4,5},{5,4},{6,7},{7,6},{8,9},{9,8},{10,11... | collective-permute-start | bytes 221192 | tf_op jit(solution)/shard_map/ppermute | solution.py:199
  15.0 0.2 collective-permute-start.3
  15.2 2.7 %collective-permute-done.2.theirs = f32[24,768]{1,0:T(8,128)S(1)} collective-permute-done((f32[24,768]{1,0:T(8,128)S(1)}, f32[24,768]{1,0:T(8,128)S(1)}, u32[]{:S(2)}, u32[]{:S(2)}) %collective-permute-start.2) | collective-permute-done | bytes 73760 | tf_op jit(solution)/shard_map/ppermute | solution.py:199
  17.9 0.0 collective-permute-start.4
  17.9 0.0 collective-permute-done.7.refs_2_
  17.9 0.5 %collective-permute-start.5 = (bf16[192,768]{1,0:T(8,128)(2,1)}, bf16[192,768]{1,0:T(8,128)(2,1)S(1)}, u32[]{:S(2)}, u32[]{:S(2)}) collective-permute-start(bf16[192,768]{1,0:T(8,128)(2,1)} %refs_8_.1), channel_id=1, source_target_pairs={{0,8},{8,0},{16,24},{24,16},{1,9},{9,1},{17,25},{25,17},{2,10},{10... | collective-permute-start | bytes 884744 | tf_op jit(solution)/shard_map/ppermute | solution.py:199
  18.4 0.0 collective-permute-done.9.refs_6_
  18.4 0.1 collective-permute-start.8
  18.4 0.0 collective-permute-done.6.mate
  18.4 1.9 %collective-permute-start.14 = (bf16[192,768]{1,0:T(8,128)(2,1)}, bf16[192,768]{1,0:T(8,128)(2,1)S(1)}, u32[]{:S(2)}, u32[]{:S(2)}) collective-permute-start(bf16[192,768]{1,0:T(8,128)(2,1)} %refs_8_.1), channel_id=1, source_target_pairs={{0,16},{8,24},{16,0},{24,8},{1,17},{9,25},{17,1},{25,9},{2,18},{10... | collective-permute-start | bytes 884744 | tf_op jit(solution)/shard_map/ppermute | solution.py:204
  20.4 0.0 collective-permute-done.3.refs_1_
  20.4 0.0 collective-permute-done.4.refs_5_
  20.4 0.0 collective-permute-done.5.refs_9_
  20.4 0.0 collective-permute-done.8.refs_3_
  20.4 3.1 %collective-permute-start.10 = (bf16[48,768]{1,0:T(8,128)(2,1)S(1)}, bf16[48,768]{1,0:T(8,128)(2,1)S(1)}, u32[]{:S(2)}, u32[]{:S(2)}) collective-permute-start(bf16[48,768]{1,0:T(8,128)(2,1)S(1)} %pair.1), channel_id=1, source_target_pairs={{0,2},{1,3},{2,0},{3,1},{4,6},{5,7},{6,4},{7,5},{8,10},{9,11},{10,... | collective-permute-start | bytes 221192 | tf_op jit(solution)/shard_map/ppermute | solution.py:199
  23.6 2.6 %collective-permute-start.11 = (bf16[48,768]{1,0:T(8,128)(2,1)S(1)}, bf16[48,768]{1,0:T(8,128)(2,1)S(1)}, u32[]{:S(2)}, u32[]{:S(2)}) collective-permute-start(bf16[48,768]{1,0:T(8,128)(2,1)S(1)} %pair.1), channel_id=1, source_target_pairs={{0,4},{1,5},{2,6},{3,7},{4,0},{5,1},{6,2},{7,3},{8,12},{9,13},{10,... | collective-permute-start | bytes 221192 | tf_op jit(solution)/shard_map/ppermute | solution.py:199
  26.2 0.0 collective-permute-start.12
  26.2 0.0 collective-permute-start.13
  26.2 0.0 copy-done.1
  26.2 0.0 copy-done.5
  26.2 0.0 copy-start.4
  26.2 0.0 copy-start.6
  26.2 0.8 %query.1.refs_3_ = bf16[256,768]{1,0:T(8,128)(2,1)S(1)} custom-call(bf16[256,768]{1,0:T(8,128)(2,1)S(1)} %bitcast.5, bf16[192,768]{1,0:T(8,128)(2,1)S(1)} %copy-done.5, bf16[192,768]{1,0:T(8,128)(2,1)S(1)} %collective-permute-done.3.refs_1_, bf16[192,768]{1,0:T(8,128)(2,1)S(1)} %collective-permute-done.7.refs_2_, ...), custom_call_target="tpu_custom_call" | custom-call | flops 1000 | bytes 1000 | tf_op jit(solution)/shard_map/query/pallas_call | solution.py:278
  27.0 0.0 copy-start.2
  27.0 0.0 copy-start.3
  27.0 0.0 collective-permute-done.10
  27.0 5.4 %collective-permute-done.11 = bf16[48,768]{1,0:T(8,128)(2,1)S(1)} collective-permute-done((bf16[48,768]{1,0:T(8,128)(2,1)S(1)}, bf16[48,768]{1,0:T(8,128)(2,1)S(1)}, u32[]{:S(2)}, u32[]{:S(2)}) %collective-permute-start.11) | collective-permute-done | bytes 73760 | tf_op jit(solution)/shard_map/ppermute | solution.py:199
  32.4 0.0 collective-permute-done.12
  32.5 0.0 collective-permute-done.14.refs_10_
  32.5 0.1 collective-permute-start.15
  32.5 0.0 copy-done.4
  32.6 1.6 %collective-permute-start.16 = (bf16[192,768]{1,0:T(8,128)(2,1)S(1)}, bf16[192,768]{1,0:T(8,128)(2,1)S(1)}, u32[]{:S(2)}, u32[]{:S(2)}) collective-permute-start(bf16[192,768]{1,0:T(8,128)(2,1)S(1)} %copy-done.4), channel_id=1, source_target_pairs={{0,16},{8,24},{16,0},{24,8},{1,17},{9,25},{17,1},{25,9},{2,18},{10... | collective-permute-start | bytes 884744 | tf_op jit(solution)/shard_map/ppermute | solution.py:204
  34.1 0.0 copy-done.6
  34.8 0.0 collective-permute-done.13.refs_7_
  34.8 0.0 collective-permute-done.15.refs_11_
  34.8 0.0 copy-done.2
  34.8 0.0 copy-done.3
  34.8 2.3 %attend.1.context = bf16[768,256]{1,0:T(8,128)(2,1)S(1)} custom-call(s32[1]{0:T(128)S(6)} %copy.17.refs_0_, bf16[192,768]{1,0:T(8,128)(2,1)S(1)} %pad_maximum_fusion.refs_1_, f32[1,768]{1,0:T(1,128)S(1)} %broadcast_in_dim.8.refs_2_, bf16[256,768]{1,0:T(8,128)(2,1)S(1)} %query.1.refs_3_, bf16[192,768]{1,0:T(8,128)(2,1)S(1)} %copy-done.2, ...), custom_call_target="tpu_custom_call" | custom-call | flops 1000 | bytes 1000 | tf_op jit(solution)/shard_map/attend/pallas_call | solution.py:287
  37.1 4.8 %collective-permute-done.16.refs_0_ = bf16[192,768]{1,0:T(8,128)(2,1)S(1)} collective-permute-done((bf16[192,768]{1,0:T(8,128)(2,1)S(1)}, bf16[192,768]{1,0:T(8,128)(2,1)S(1)}, u32[]{:S(2)}, u32[]{:S(2)}) %collective-permute-start.16) | collective-permute-done | bytes 294944 | tf_op jit(solution)/shard_map/ppermute | solution.py:204
  42.0 0.0 collective-permute-start.17
  42.0 0.4 project_near.1.total
  42.4 1.2 %collective-permute-done.17.refs_1_ = bf16[192,768]{1,0:T(8,128)(2,1)S(1)} collective-permute-done((bf16[192,768]{1,0:T(8,128)(2,1)S(1)}, bf16[192,768]{1,0:T(8,128)(2,1)S(1)}, u32[]{:S(2)}, u32[]{:S(2)}) %collective-permute-start.17) | collective-permute-done | bytes 294944 | tf_op jit(solution)/shard_map/ppermute | solution.py:199
  43.6 1.2 %project_far.1 = bf16[256,768]{1,0:T(8,128)(2,1)} custom-call(bf16[768,256]{1,0:T(8,128)(2,1)S(1)} %attend.1.context, f32[256,768]{1,0:T(8,128)S(1)} %project_near.1.total, bf16[192,768]{1,0:T(8,128)(2,1)S(1)} %collective-permute-done.16.refs_0_, bf16[192,768]{1,0:T(8,128)(2,1)S(1)} %collective-permute-done.17.refs_1_), custom_call_target="tpu_custom_call" | custom-call | flops 1000 | bytes 1000 | tf_op jit(solution)/shard_map/project_far/pallas_call | solution.py:312
  (5 shorter events, 0.1 us)
Async XLA Ops:
  0.0 17.9 %collective-permute-start.7 = (bf16[192,768]{1,0:T(8,128)(2,1)}, bf16[192,768]{1,0:T(8,128)(2,1)S(1)}, u32[]{:S(2)}, u32[]{:S(2)}) collective-permute-start(bf16[192,768]{1,0:T(8,128)(2,1)} %refs_0_.2), channel_id=1, source_target_pairs={{0,16},{8,24},{16,0},{24,8},{1,17},{9,25},{17,1},{25,9},{2,18},{10... | collective-permute-start | bytes 884744 | tf_op jit(solution)/shard_map/ppermute | solution.py:204
  3.0 15.4 %collective-permute-start.9 = (bf16[192,768]{1,0:T(8,128)(2,1)}, bf16[192,768]{1,0:T(8,128)(2,1)S(1)}, u32[]{:S(2)}, u32[]{:S(2)}) collective-permute-start(bf16[192,768]{1,0:T(8,128)(2,1)} %refs_4_.1), channel_id=1, source_target_pairs={{0,16},{8,24},{16,0},{24,8},{1,17},{9,25},{17,1},{25,9},{2,18},{10... | collective-permute-start | bytes 884744 | tf_op jit(solution)/shard_map/ppermute | solution.py:204
  3.7 0.7 %copy-start.7 = (s32[1,64,4]{1,2,0:T(4,128)S(1)}, s32[1,64,4]{1,2,0:T(4,128)}, u32[]{:S(2)}) copy-start(s32[1,64,4]{1,2,0:T(4,128)} %param.11) | copy-start | bytes 3076
  4.5 4.0 %collective-permute-start = (s32[64,4]{1,0:T(8,128)S(1)}, s32[64,4]{1,0:T(8,128)S(1)}, u32[]{:S(2)}, u32[]{:S(2)}) collective-permute-start(s32[64,4]{1,0:T(8,128)S(1)} %select_bitcast_fusion.here), channel_id=1, source_target_pairs={{0,1},{1,0},{2,3},{3,2},{4,5},{5,4},{6,7},{7,6},{8,9},{9,8},{10,11... | collective-permute-start | bytes 3080 | tf_op jit(solution)/shard_map/ppermute | solution.py:199
  6.5 2.0 %collective-permute-start.1 = (s32[64,4]{1,0:T(8,128)S(1)}, s32[64,4]{1,0:T(8,128)S(1)}, u32[]{:S(2)}, u32[]{:S(2)}) collective-permute-start(s32[64,4]{1,0:T(8,128)S(1)} %select_bitcast_fusion.here), channel_id=1, source_target_pairs={{1,2},{3,4},{5,6},{2,1},{4,3},{6,5},{9,10},{11,12},{13,14},{10,9},... | collective-permute-start | bytes 3080 | tf_op jit(solution)/shard_map/ppermute | solution.py:260
  8.5 1.0 %copy-start = (bf16[1,256,768]{2,1,0:T(8,128)(2,1)S(1)}, bf16[1,256,768]{2,1,0:T(8,128)(2,1)}, u32[]{:S(2)}) copy-start(bf16[1,256,768]{2,1,0:T(8,128)(2,1)} %param.9) | copy-start | bytes 1179652
  9.5 16.7 %copy-start.1 = (bf16[1,256,768]{2,1,0:T(8,128)(2,1)S(1)}, bf16[1,256,768]{2,1,0:T(8,128)(2,1)}, u32[]{:S(2)}) copy-start(bf16[1,256,768]{2,1,0:T(8,128)(2,1)} %param.9) | copy-start | bytes 1179652
  9.5 16.7 %copy-start.5 = (bf16[192,768]{1,0:T(8,128)(2,1)S(1)}, bf16[192,768]{1,0:T(8,128)(2,1)}, u32[]{:S(2)}) copy-start(bf16[192,768]{1,0:T(8,128)(2,1)} %refs_0_.2) | copy-start | bytes 884740
  10.0 8.5 %collective-permute-start.6 = (bf16[192,768]{1,0:T(8,128)(2,1)}, bf16[192,768]{1,0:T(8,128)(2,1)S(1)}, u32[]{:S(2)}, u32[]{:S(2)}) collective-permute-start(bf16[192,768]{1,0:T(8,128)(2,1)} %piece.1), channel_id=1, source_target_pairs={{0,8},{8,0},{16,24},{24,16},{1,9},{9,1},{17,25},{25,17},{2,10},{10... | collective-permute-start | bytes 884744 | tf_op jit(solution)/shard_map/ppermute | solution.py:199
  10.1 7.8 %collective-permute-start.2 = (f32[24,768]{1,0:T(8,128)S(1)}, f32[24,768]{1,0:T(8,128)S(1)}, u32[]{:S(2)}, u32[]{:S(2)}) collective-permute-start(f32[24,768]{1,0:T(8,128)S(1)} %pool.1.mine), channel_id=1, source_target_pairs={{0,1},{1,0},{2,3},{3,2},{4,5},{5,4},{6,7},{7,6},{8,9},{9,8},{10,11... | collective-permute-start | bytes 221192 | tf_op jit(solution)/shard_map/ppermute | solution.py:199
  15.0 5.4 %collective-permute-start.3 = (bf16[192,768]{1,0:T(8,128)(2,1)}, bf16[192,768]{1,0:T(8,128)(2,1)S(1)}, u32[]{:S(2)}, u32[]{:S(2)}) collective-permute-start(bf16[192,768]{1,0:T(8,128)(2,1)} %refs_0_.2), channel_id=1, source_target_pairs={{0,8},{8,0},{16,24},{24,16},{1,9},{9,1},{17,25},{25,17},{2,10},{10... | collective-permute-start | bytes 884744 | tf_op jit(solution)/shard_map/ppermute | solution.py:199
  17.9 2.5 %collective-permute-start.4 = (bf16[192,768]{1,0:T(8,128)(2,1)}, bf16[192,768]{1,0:T(8,128)(2,1)S(1)}, u32[]{:S(2)}, u32[]{:S(2)}) collective-permute-start(bf16[192,768]{1,0:T(8,128)(2,1)} %refs_4_.1), channel_id=1, source_target_pairs={{0,8},{8,0},{16,24},{24,16},{1,9},{9,1},{17,25},{25,17},{2,10},{10... | collective-permute-start | bytes 884744 | tf_op jit(solution)/shard_map/ppermute | solution.py:199
  17.9 2.5 %collective-permute-start.5 = (bf16[192,768]{1,0:T(8,128)(2,1)}, bf16[192,768]{1,0:T(8,128)(2,1)S(1)}, u32[]{:S(2)}, u32[]{:S(2)}) collective-permute-start(bf16[192,768]{1,0:T(8,128)(2,1)} %refs_8_.1), channel_id=1, source_target_pairs={{0,8},{8,0},{16,24},{24,16},{1,9},{9,1},{17,25},{25,17},{2,10},{10... | collective-permute-start | bytes 884744 | tf_op jit(solution)/shard_map/ppermute | solution.py:199
  18.4 2.0 %collective-permute-start.8 = (bf16[192,768]{1,0:T(8,128)(2,1)S(1)}, bf16[192,768]{1,0:T(8,128)(2,1)S(1)}, u32[]{:S(2)}, u32[]{:S(2)}) collective-permute-start(bf16[192,768]{1,0:T(8,128)(2,1)S(1)} %collective-permute-done.7.refs_2_), channel_id=1, source_target_pairs={{0,8},{8,0},{16,24},{24,16},{1,9},{9,1},{17,25},{25,17},{2,10},{10... | collective-permute-start | bytes 884744 | tf_op jit(solution)/shard_map/ppermute | solution.py:199
  18.4 14.0 %collective-permute-start.14 = (bf16[192,768]{1,0:T(8,128)(2,1)}, bf16[192,768]{1,0:T(8,128)(2,1)S(1)}, u32[]{:S(2)}, u32[]{:S(2)}) collective-permute-start(bf16[192,768]{1,0:T(8,128)(2,1)} %refs_8_.1), channel_id=1, source_target_pairs={{0,16},{8,24},{16,0},{24,8},{1,17},{9,25},{17,1},{25,9},{2,18},{10... | collective-permute-start | bytes 884744 | tf_op jit(solution)/shard_map/ppermute | solution.py:204
  20.4 6.6 %collective-permute-start.10 = (bf16[48,768]{1,0:T(8,128)(2,1)S(1)}, bf16[48,768]{1,0:T(8,128)(2,1)S(1)}, u32[]{:S(2)}, u32[]{:S(2)}) collective-permute-start(bf16[48,768]{1,0:T(8,128)(2,1)S(1)} %pair.1), channel_id=1, source_target_pairs={{0,2},{1,3},{2,0},{3,1},{4,6},{5,7},{6,4},{7,5},{8,10},{9,11},{10,... | collective-permute-start | bytes 221192 | tf_op jit(solution)/shard_map/ppermute | solution.py:199
  23.6 8.9 %collective-permute-start.11 = (bf16[48,768]{1,0:T(8,128)(2,1)S(1)}, bf16[48,768]{1,0:T(8,128)(2,1)S(1)}, u32[]{:S(2)}, u32[]{:S(2)}) collective-permute-start(bf16[48,768]{1,0:T(8,128)(2,1)S(1)} %pair.1), channel_id=1, source_target_pairs={{0,4},{1,5},{2,6},{3,7},{4,0},{5,1},{6,2},{7,3},{8,12},{9,13},{10,... | collective-permute-start | bytes 221192 | tf_op jit(solution)/shard_map/ppermute | solution.py:199
  26.2 6.3 %collective-permute-start.12 = (bf16[48,768]{1,0:T(8,128)(2,1)S(1)}, bf16[48,768]{1,0:T(8,128)(2,1)S(1)}, u32[]{:S(2)}, u32[]{:S(2)}) collective-permute-start(bf16[48,768]{1,0:T(8,128)(2,1)S(1)} %pair.1), channel_id=1, source_target_pairs={{0,6},{1,7},{2,4},{3,5},{4,2},{5,3},{6,0},{7,1},{8,14},{9,15},{10,... | collective-permute-start | bytes 221192 | tf_op jit(solution)/shard_map/ppermute | solution.py:199
  26.2 8.6 %collective-permute-start.13 = (bf16[192,768]{1,0:T(8,128)(2,1)S(1)}, bf16[192,768]{1,0:T(8,128)(2,1)S(1)}, u32[]{:S(2)}, u32[]{:S(2)}) collective-permute-start(bf16[192,768]{1,0:T(8,128)(2,1)S(1)} %collective-permute-done.9.refs_6_), channel_id=1, source_target_pairs={{0,8},{8,0},{16,24},{24,16},{1,9},{9,1},{17,25},{25,17},{2,10},{10... | collective-permute-start | bytes 884744 | tf_op jit(solution)/shard_map/ppermute | solution.py:199
  26.2 6.4 %copy-start.4 = (bf16[192,768]{1,0:T(8,128)(2,1)S(1)}, bf16[192,768]{1,0:T(8,128)(2,1)}, u32[]{:S(2)}) copy-start(bf16[192,768]{1,0:T(8,128)(2,1)} %piece.1) | copy-start | bytes 884740
  26.2 8.0 %copy-start.6 = (f32[768]{0:T(1024)S(1)}, f32[768]{0:T(1024)}, u32[]{:S(2)}) copy-start(f32[768]{0:T(1024)} %param.17) | copy-start | bytes 9220
  27.0 7.8 %copy-start.2 = (bf16[192,768]{1,0:T(8,128)(2,1)S(1)}, bf16[192,768]{1,0:T(8,128)(2,1)}, u32[]{:S(2)}) copy-start(bf16[192,768]{1,0:T(8,128)(2,1)} %refs_4_.1) | copy-start | bytes 884740
  27.0 7.8 %copy-start.3 = (bf16[192,768]{1,0:T(8,128)(2,1)S(1)}, bf16[192,768]{1,0:T(8,128)(2,1)}, u32[]{:S(2)}) copy-start(bf16[192,768]{1,0:T(8,128)(2,1)} %refs_8_.1) | copy-start | bytes 884740
  32.5 2.3 %collective-permute-start.15 = (bf16[192,768]{1,0:T(8,128)(2,1)S(1)}, bf16[192,768]{1,0:T(8,128)(2,1)S(1)}, u32[]{:S(2)}, u32[]{:S(2)}) collective-permute-start(bf16[192,768]{1,0:T(8,128)(2,1)S(1)} %collective-permute-done.14.refs_10_), channel_id=1, source_target_pairs={{0,8},{8,0},{16,24},{24,16},{1,9},{9,1},{17,25},{25,17},{2,10},{10... | collective-permute-start | bytes 884744 | tf_op jit(solution)/shard_map/ppermute | solution.py:199
  32.6 9.4 %collective-permute-start.16 = (bf16[192,768]{1,0:T(8,128)(2,1)S(1)}, bf16[192,768]{1,0:T(8,128)(2,1)S(1)}, u32[]{:S(2)}, u32[]{:S(2)}) collective-permute-start(bf16[192,768]{1,0:T(8,128)(2,1)S(1)} %copy-done.4), channel_id=1, source_target_pairs={{0,16},{8,24},{16,0},{24,8},{1,17},{9,25},{17,1},{25,9},{2,18},{10... | collective-permute-start | bytes 884744 | tf_op jit(solution)/shard_map/ppermute | solution.py:204
  42.0 1.6 %collective-permute-start.17 = (bf16[192,768]{1,0:T(8,128)(2,1)S(1)}, bf16[192,768]{1,0:T(8,128)(2,1)S(1)}, u32[]{:S(2)}, u32[]{:S(2)}) collective-permute-start(bf16[192,768]{1,0:T(8,128)(2,1)S(1)} %collective-permute-done.16.refs_0_), channel_id=1, source_target_pairs={{0,8},{8,0},{16,24},{24,16},{1,9},{9,1},{17,25},{25,17},{2,10},{10... | collective-permute-start | bytes 884744 | tf_op jit(solution)/shard_map/ppermute | solution.py:199

commit v6 on v4

--- a/solution.py
+++ b/solution.py
@@ -38,17 +38,25 @@
     )
 
 
-def pool_kernel(here, mate, other, tiles, out):
+def slots_kernel(nbr, mask, out, held, sem):
+    count, regions = nbr.shape
+    for copy in collect([(nbr, held.at[0]), (mask, held.at[1])], sem):
+        copy.wait()
+    out[...] = jnp.zeros_like(out)
+    out[:count, :regions] = jnp.where(held[1] > 0, held[0] + 1, 0)
+
+
+def pool_kernel(regions, here, mate, other, tiles, out):
     count = tiles.shape[0]
-    regions = here.shape[0]
     base = lax.axis_index("tile") * count + 1
     row = lax.broadcasted_iota(jnp.int32, (regions, count), 1) + base
     hits, shares = [], []
     for slots in (here, mate, other):
+        turned = slots[...].T
         hit = jnp.zeros((regions, count), F32)
         live = jnp.zeros((regions, 1), F32)
         for s in range(NB):
-            slot = slots[:, s : s + 1]
+            slot = turned[:regions, s : s + 1]
             hit += (slot == row).astype(F32)
             live += (slot > 0).astype(F32)
         hits.append(hit.astype(BF16))
@@ -273,47 +281,52 @@
     block = regions // REGIONS_PER_KEY
 
     shard = w_query.shape[0]
-    halves = pl.pallas_call(
-        halves_kernel,
-        out_shape=jax.ShapeDtypeStruct((2, shard, width // 2), BF16),
-        in_specs=[anywhere()] * 2,
-        out_specs=vmem(),
-        scratch_shapes=[pltpu.SemaphoreType.DMA((2,))],
-        name="halves",
-    )(w_value, w_out)
-    near_halves = from_chips(halves)
-
-    slots = jnp.where(nbr_mask[0] > 0, nbr_tiles[0] + 1, 0)
+    near_query = from_chips(w_query)
+    slots = local_call(
+        slots_kernel,
+        jax.ShapeDtypeStruct((8, -(-regions // 128) * 128), jnp.int32),
+        [anywhere()] * 2,
+        "slots",
+        [pltpu.VMEM((2, NB, regions), jnp.int32), pltpu.SemaphoreType.DMA((2,))],
+    )(nbr_tiles[0].T, nbr_mask[0].T)
     mate = swap(slots, "tile", 1)
     inner = [(i, i + 1) for i in range(1, tile_devices - 1, 2)]
     other = lax.ppermute(slots, "tile", inner + [(b, a) for a, b in inner])
-    near_query = from_chips(behind(w_query, slots))
-    near_key = from_chips(behind(w_key, slots))
+    halves = local_call(
+        halves_kernel,
+        jax.ShapeDtypeStruct((2, shard, width // 2), BF16),
+        [anywhere()] * 2,
+        "halves",
+        [pltpu.SemaphoreType.DMA((2,))],
+    )(w_value, w_out)
+    near_halves = from_chips(halves)
     mine = local_call(
-        pool_kernel,
+        functools.partial(pool_kernel, regions),
         jax.ShapeDtypeStruct((3 * block, width), F32),
         [vmem()] * 4,
         "pool",
-    )(slots, mate, other, own_tiles)
+    )(slots, mate, other, behind(own_tiles, near_query))
+    near_key = from_chips(behind(w_key, mine))
     mates = [swap(behind(w, mine), "fsdp", 1) for w in (w_query, w_key, w_value, w_out)]
+    far_query = swap(near_query, "fsdp", 1)
     pair = local_call(
         pair_kernel,
         jax.ShapeDtypeStruct((6 * block, width), BF16),
         [vmem()] * 2,
         "pair",
-    )(mine, behind(swap(mine, "tile", 1), near_halves, *mates))
+    )(mine, behind(swap(mine, "tile", 1), near_halves, far_query, *mates))
     near_halves = behind(near_halves, pair)
     other_halves = swap(near_halves, "tile", 1)
     far_halves = swap(near_halves, "fsdp", 1)
-    near_query = behind(near_query, pair)
     query = local_call(
         functools.partial(query_kernel, fsdp),
         jax.ShapeDtypeStruct((rows, width), BF16),
         [vmem()] + [anywhere()] * 4,
         "query",
         [pltpu.VMEM((1, width, width), BF16), pltpu.SemaphoreType.DMA((fsdp,))],
-    )(own_tiles, w_query, mates[0], near_query, swap(near_query, "fsdp", 1))
-    sums = behind(gather_pairs(pair, "tile"), query, near_key)
+    )(behind(own_tiles, pair), w_query, mates[0], near_query, far_query)
+    sums = behind(gather_pairs(pair, "tile"), query)
+    near_key = behind(near_key, sums)
     other_halves = behind(other_halves, sums)
     attended = local_call(
         functools.partial(attend_kernel, fsdp, block),

time: 46.8 us -> 38.2 us (0.82)
  waiting for transfers between devices: 18 us -> 8.43 us
  local copies, waits for them, and re-layouts: 0.25 us -> 3.38 us
  Pallas kernels: 6.91 us -> 5.23 us
  other arithmetic: 0.71 us -> 0.02 us
    ppermute x3, waiting for transfers between devices: 8.81 us -> 0.01 us  [chip_shift(): lax.ppermute(array, axis, [(i, (i + 2 * step) % count) for i in range(cou...]
    unnamed x14 -> x20, local copies, waits for them, and re-layouts: 0.03 us -> 3.38 us
    pallas_call x2 -> x3, Pallas kernels: 2.29 us -> 0.64 us  [the longest x1 0.56 us: body(): local_call(functools.partial(pool_kernel, regions), jax.ShapeDtypeStruct(...]
    ppermute x14, starting transfers between devices: 14.1 us -> 14.9 us  [swap(): return lax.ppermute(array, axis, [(i, i ^ offset) for i in range(count)])]
    ppermute x14, waiting for transfers between devices: 9.15 us -> 8.42 us  [swap(): return lax.ppermute(array, axis, [(i, i ^ offset) for i in range(count)])]
    add x1 -> x0, other arithmetic: 0.68 us -> none  [body(): slots = jnp.where(nbr_mask[0] > 0, nbr_tiles[0] + 1, 0)]
    ppermute x3, starting transfers between devices: 5.14 us -> 4.61 us  [chip_shift(): lax.ppermute(array, axis, [(i, (i + 2 * step) % count) for i in range(cou...]
  transfers between devices with their start and end apart: 18 -> 18, of which waited for: 7 -> 6; matrix products, arithmetic and copies ran while one was open for 2% -> 0% of each run, Pallas kernels for 3% -> 4%
where the time goes in v6:
time: 38.2 us; the launch traced here: 38 us
  starting transfers between devices  20.1 us (53%)
  waiting for transfers between devices  8.43 us (22%)
  Pallas kernels  5.23 us (14%)
  local copies, waits for them, and re-layouts  3.38 us (9%)
  between operations  0.79 us (2%)
    ppermute x14, starting transfers between devices, swap(): return lax.ppermute(array, axis, [(i, i ^ offset) for i in range(count)])  14.9 us
    ppermute x14, waiting for transfers between devices, swap(): return lax.ppermute(array, axis, [(i, i ^ offset) for i in range(count)])  8.42 us
    ppermute x3, starting transfers between devices, chip_shift(): lax.ppermute(array, axis, [(i, (i + 2 * step) % count) for i in range(cou...  4.61 us
    pallas_call x1, Pallas kernels, body(): local_call(functools.partial(attend_kernel, fsdp, block), jax.ShapeDtypeS...  3.82 us
    unnamed x20, local copies, waits for them, and re-layouts  3.38 us
  transfers between devices with their start and end apart: 18, of which 6 were waited for; matrix products, arithmetic and copies ran while one was open for 0% of the time, Pallas kernels for 4%

profile of v6, /device:TPU:0, one launch (start us, length us, event | category | flops | bytes accessed | tf_op | source)
XLA Modules:
  0.0 38.0 jit_solution(8090227391259347237)
XLA Ops:
  0.0 0.0 copy-start
  0.0 3.0 %collective-permute-start.2 = (bf16[192,768]{1,0:T(8,128)(2,1)}, bf16[192,768]{1,0:T(8,128)(2,1)S(1)}, u32[]{:S(2)}, u32[]{:S(2)}) collective-permute-start(bf16[192,768]{1,0:T(8,128)(2,1)} %piece.1), channel_id=1, source_target_pairs={{0,16},{8,24},{16,0},{24,8},{1,17},{9,25},{17,1},{25,9},{2,18},{10... | collective-permute-start | bytes 884744 | tf_op jit(solution)/shard_map/ppermute | solution.py:230
  3.0 0.0 copy-start.1
  3.0 1.0 %copy-done.1 = bf16[192,768]{1,0:T(8,128)(2,1)S(1)} copy-done((bf16[192,768]{1,0:T(8,128)(2,1)S(1)}, bf16[192,768]{1,0:T(8,128)(2,1)}, u32[]{:S(2)}) %copy-start.1) | copy-done | bytes 294936
  3.9 0.0 copy-start.3
  3.9 1.0 %copy-done.3 = bf16[192,768]{1,0:T(8,128)(2,1)S(1)} copy-done((bf16[192,768]{1,0:T(8,128)(2,1)S(1)}, bf16[192,768]{1,0:T(8,128)(2,1)}, u32[]{:S(2)}) %copy-start.3) | copy-done | bytes 294936
  4.9 0.0 copy-start.5
  4.9 0.0 copy-start.4
  4.9 0.1 halves.1
  5.0 0.0 copy-start.2
  5.0 0.1 collective-permute-start.4
  5.1 0.0 copy-start.7
  5.1 0.7 %copy-done.7 = s32[1,64,4]{1,2,0:T(4,128)S(1)} copy-done((s32[1,64,4]{1,2,0:T(4,128)S(1)}, s32[1,64,4]{1,2,0:T(4,128)}, u32[]{:S(2)}) %copy-start.7) | copy-done | bytes 1048
  5.8 0.0 copy-start.8
  5.8 0.7 %copy-done.8 = s32[1,64,4]{1,2,0:T(4,128)S(1)} copy-done((s32[1,64,4]{1,2,0:T(4,128)S(1)}, s32[1,64,4]{1,2,0:T(4,128)}, u32[]{:S(2)}) %copy-start.8) | copy-done | bytes 1048
  6.6 0.7 %collective-permute-start.1 = (s32[8,128]{1,0:T(8,128)S(1)}, s32[8,128]{1,0:T(8,128)S(1)}, u32[]{:S(2)}, u32[]{:S(2)}) collective-permute-start(s32[8,128]{1,0:T(8,128)S(1)} %slots.1.here), channel_id=1, source_target_pairs={{1,2},{3,4},{5,6},{2,1},{4,3},{6,5},{9,10},{11,12},{13,14},{10,9},... | collective-permute-start | bytes 12296 | tf_op jit(solution)/shard_map/ppermute | solution.py:294
  7.2 4.7 %collective-permute-start = (s32[8,128]{1,0:T(8,128)S(1)}, s32[8,128]{1,0:T(8,128)S(1)}, u32[]{:S(2)}, u32[]{:S(2)}) collective-permute-start(s32[8,128]{1,0:T(8,128)S(1)} %slots.1.here), channel_id=1, source_target_pairs={{0,1},{1,0},{2,3},{3,2},{4,5},{5,4},{6,7},{7,6},{8,9},{9,8},{10,11... | collective-permute-start | bytes 12296 | tf_op jit(solution)/shard_map/ppermute | solution.py:225
  12.0 0.0 collective-permute-done.2
  12.0 0.0 copy-start.6
  12.0 0.0 collective-permute-done.1.other
  12.0 1.6 %collective-permute-done.mate = s32[8,128]{1,0:T(8,128)S(1)} collective-permute-done((s32[8,128]{1,0:T(8,128)S(1)}, s32[8,128]{1,0:T(8,128)S(1)}, u32[]{:S(2)}, u32[]{:S(2)}) %collective-permute-start) | collective-permute-done | bytes 4128 | tf_op jit(solution)/shard_map/ppermute | solution.py:225
  13.6 0.0 copy-done
  13.6 0.6 %pool.1.mine = f32[24,768]{1,0:T(8,128)S(1)} custom-call(s32[8,128]{1,0:T(8,128)S(1)} %slots.1.here, s32[8,128]{1,0:T(8,128)S(1)} %collective-permute-done.mate, s32[8,128]{1,0:T(8,128)S(1)} %collective-permute-done.1.other, bf16[256,768]{1,0:T(8,128)(2,1)S(1)} %bitcast.11), custom_call_target="tpu_custom_call" | custom-call | flops 1000 | bytes 1000 | tf_op jit(solution)/shard_map/pool/pallas_call | solution.py:303
  14.1 2.1 %collective-permute-start.3 = (f32[24,768]{1,0:T(8,128)S(1)}, f32[24,768]{1,0:T(8,128)S(1)}, u32[]{:S(2)}, u32[]{:S(2)}) collective-permute-start(f32[24,768]{1,0:T(8,128)S(1)} %pool.1.mine), channel_id=1, source_target_pairs={{0,1},{1,0},{2,3},{3,2},{4,5},{5,4},{6,7},{7,6},{8,9},{9,8},{10,11... | collective-permute-start | bytes 221192 | tf_op jit(solution)/shard_map/ppermute | solution.py:225
  16.2 0.0 collective-permute-start.6
  16.2 0.0 copy-done.5
  16.2 0.5 %collective-permute-start.7 = (bf16[192,768]{1,0:T(8,128)(2,1)S(1)}, bf16[192,768]{1,0:T(8,128)(2,1)S(1)}, u32[]{:S(2)}, u32[]{:S(2)}) collective-permute-start(bf16[192,768]{1,0:T(8,128)(2,1)S(1)} %copy-done.5), channel_id=1, source_target_pairs={{0,8},{8,0},{16,24},{24,16},{1,9},{9,1},{17,25},{25,17},{2,10},{10... | collective-permute-start | bytes 884744 | tf_op jit(solution)/shard_map/ppermute | solution.py:225
  16.7 0.0 copy-done.2
  16.7 0.1 collective-permute-start.8
  16.8 0.0 collective-permute-done.4
  16.8 0.0 copy-done.4
  16.8 0.4 %collective-permute-start.9 = (bf16[192,768]{1,0:T(8,128)(2,1)S(1)}, bf16[192,768]{1,0:T(8,128)(2,1)S(1)}, u32[]{:S(2)}, u32[]{:S(2)}) collective-permute-start(bf16[192,768]{1,0:T(8,128)(2,1)S(1)} %copy-done.4), channel_id=1, source_target_pairs={{0,8},{8,0},{16,24},{24,16},{1,9},{9,1},{17,25},{25,17},{2,10},{10... | collective-permute-start | bytes 884744 | tf_op jit(solution)/shard_map/ppermute | solution.py:225
  17.2 1.3 %collective-permute-done.3.theirs = f32[24,768]{1,0:T(8,128)S(1)} collective-permute-done((f32[24,768]{1,0:T(8,128)S(1)}, f32[24,768]{1,0:T(8,128)S(1)}, u32[]{:S(2)}, u32[]{:S(2)}) %collective-permute-start.3) | collective-permute-done | bytes 73760 | tf_op jit(solution)/shard_map/ppermute | solution.py:225
  18.5 0.0 collective-permute-start.5
  18.5 0.0 collective-permute-done.6.mate
  18.5 1.5 %collective-permute-start.13 = (bf16[192,768]{1,0:T(8,128)(2,1)S(1)}, bf16[192,768]{1,0:T(8,128)(2,1)S(1)}, u32[]{:S(2)}, u32[]{:S(2)}) collective-permute-start(bf16[192,768]{1,0:T(8,128)(2,1)S(1)} %copy-done.5), channel_id=1, source_target_pairs={{0,16},{8,24},{16,0},{24,8},{1,17},{9,25},{17,1},{25,9},{2,18},{10... | collective-permute-start | bytes 884744 | tf_op jit(solution)/shard_map/ppermute | solution.py:230
  20.1 0.0 collective-permute-done.7.refs_7_
  20.1 0.0 collective-permute-done.8.refs_8_
  20.1 0.0 collective-permute-done.9.refs_9_
  20.1 0.0 collective-permute-done.5.far
  20.1 2.1 %collective-permute-start.14 = (bf16[1,2,192,384]{3,2,1,0:T(8,128)(2,1)S(1)}, bf16[1,2,192,384]{3,2,1,0:T(8,128)(2,1)S(1)}, u32[]{:S(2)}, u32[]{:S(2)}) collective-permute-start(bf16[1,2,192,384]{3,2,1,0:T(8,128)(2,1)S(1)} %bitcast.13), channel_id=1, source_target_pairs={{0,1},{1,0},{2,3},{3,2},{4,5},{5,4},{6,7},{7,6},{8,9},{9,8},{10,11... | collective-permute-start | bytes 884744 | tf_op jit(solution)/shard_map/ppermute | solution.py:225
  22.2 2.0 %collective-permute-start.12 = (bf16[48,768]{1,0:T(8,128)(2,1)S(1)}, bf16[48,768]{1,0:T(8,128)(2,1)S(1)}, u32[]{:S(2)}, u32[]{:S(2)}) collective-permute-start(bf16[48,768]{1,0:T(8,128)(2,1)S(1)} %pair.1), channel_id=1, source_target_pairs={{0,6},{1,7},{2,4},{3,5},{4,2},{5,3},{6,0},{7,1},{8,14},{9,15},{10,... | collective-permute-start | bytes 221192 | tf_op jit(solution)/shard_map/ppermute | solution.py:225
  24.2 1.0 %collective-permute-start.11 = (bf16[48,768]{1,0:T(8,128)(2,1)S(1)}, bf16[48,768]{1,0:T(8,128)(2,1)S(1)}, u32[]{:S(2)}, u32[]{:S(2)}) collective-permute-start(bf16[48,768]{1,0:T(8,128)(2,1)S(1)} %pair.1), channel_id=1, source_target_pairs={{0,4},{1,5},{2,6},{3,7},{4,0},{5,1},{6,2},{7,3},{8,12},{9,13},{10,... | collective-permute-start | bytes 221192 | tf_op jit(solution)/shard_map/ppermute | solution.py:225
  25.3 1.3 %collective-permute-start.10 = (bf16[48,768]{1,0:T(8,128)(2,1)S(1)}, bf16[48,768]{1,0:T(8,128)(2,1)S(1)}, u32[]{:S(2)}, u32[]{:S(2)}) collective-permute-start(bf16[48,768]{1,0:T(8,128)(2,1)S(1)} %pair.1), channel_id=1, source_target_pairs={{0,2},{1,3},{2,0},{3,1},{4,6},{5,7},{6,4},{7,5},{8,10},{9,11},{10,... | collective-permute-start | bytes 221192 | tf_op jit(solution)/shard_map/ppermute | solution.py:225
  26.6 0.0 copy-done.6
  26.6 0.8 %query.1.refs_3_ = bf16[256,768]{1,0:T(8,128)(2,1)S(1)} custom-call(bf16[256,768]{1,0:T(8,128)(2,1)S(1)} %bitcast.12, bf16[192,768]{1,0:T(8,128)(2,1)S(1)} %copy-done.6, bf16[192,768]{1,0:T(8,128)(2,1)S(1)} %collective-permute-done.6.mate, bf16[1,192,768]{2,1,0:T(8,128)(2,1)S(1)} %bitcast.19, bf16[1,192,768]{2,1,0:T(8,128)(2,1)S(1)} %collective-permute-done.5.far), custom_call_target="tpu_custom_call" | custom-call | flops 1000 | bytes 1000 | tf_op jit(solution)/shard_map/query/pallas_call | solution.py:321
  27.4 1.5 %collective-permute-done.12 = bf16[48,768]{1,0:T(8,128)(2,1)S(1)} collective-permute-done((bf16[48,768]{1,0:T(8,128)(2,1)S(1)}, bf16[48,768]{1,0:T(8,128)(2,1)S(1)}, u32[]{:S(2)}, u32[]{:S(2)}) %collective-permute-start.12) | collective-permute-done | bytes 73760 | tf_op jit(solution)/shard_map/ppermute | solution.py:225
  28.9 0.0 collective-permute-start.16
  28.9 3.2 %collective-permute-done.11 = bf16[48,768]{1,0:T(8,128)(2,1)S(1)} collective-permute-done((bf16[48,768]{1,0:T(8,128)(2,1)S(1)}, bf16[48,768]{1,0:T(8,128)(2,1)S(1)}, u32[]{:S(2)}, u32[]{:S(2)}) %collective-permute-start.11) | collective-permute-done | bytes 73760 | tf_op jit(solution)/shard_map/ppermute | solution.py:225
  32.1 0.0 collective-permute-done.10
  32.1 0.0 copy-start.9
  32.1 0.0 collective-permute-done.13
  32.1 0.1 collective-permute-start.15
  32.2 0.0 collective-permute-done.14.refs_12_
  32.2 0.5 %collective-permute-start.17 = (bf16[1,2,192,384]{3,2,1,0:T(8,128)(2,1)S(1)}, bf16[1,2,192,384]{3,2,1,0:T(8,128)(2,1)S(1)}, u32[]{:S(2)}, u32[]{:S(2)}) collective-permute-start(bf16[1,2,192,384]{3,2,1,0:T(8,128)(2,1)S(1)} %collective-permute-done.14.refs_12_), channel_id=1, source_target_pairs={{0,8},{8,0},{16,24},{24,16},{1,9},{9,1},{17,25},{25,17},{2,10},{10... | collective-permute-start | bytes 884744 | tf_op jit(solution)/shard_map/ppermute | solution.py:225
  33.3 0.0 copy-done.9
  33.4 0.0 collective-permute-done.16.refs_14_
  33.4 0.4 %collective-permute-done.15.refs_13_ = bf16[1,192,768]{2,1,0:T(8,128)(2,1)S(1)} collective-permute-done((bf16[1,192,768]{2,1,0:T(8,128)(2,1)S(1)}, bf16[1,192,768]{2,1,0:T(8,128)(2,1)S(1)}, u32[]{:S(2)}, u32[]{:S(2)}) %collective-permute-start.15) | collective-permute-done | bytes 294944 | tf_op jit(solution)/shard_map/ppermute | solution.py:225
  33.8 0.4 %collective-permute-done.17.refs_15_ = bf16[1,2,192,384]{3,2,1,0:T(8,128)(2,1)S(1)} collective-permute-done((bf16[1,2,192,384]{3,2,1,0:T(8,128)(2,1)S(1)}, bf16[1,2,192,384]{3,2,1,0:T(8,128)(2,1)S(1)}, u32[]{:S(2)}, u32[]{:S(2)}) %collective-permute-start.17) | collective-permute-done | bytes 294944 | tf_op jit(solution)/shard_map/ppermute | solution.py:225
  34.2 3.8 %attend.1 = bf16[256,768]{1,0:T(8,128)(2,1)} custom-call(s32[1]{0:T(128)S(6)} %copy.10.refs_0_, bf16[192,768]{1,0:T(8,128)(2,1)S(1)} %pad_maximum_fusion.refs_1_, f32[1,768]{1,0:T(1,128)S(1)} %broadcast_in_dim.6.refs_2_, bf16[256,768]{1,0:T(8,128)(2,1)S(1)} %query.1.refs_3_, bf16[192,768]{1,0:T(8,128)(2,1)S(1)} %copy-done.5, bf16[192,768]{1,0:T(8,128)(2,1)S(1)} %copy-done.2, ...), custom_call_target="tpu_custom_call" | custom-call | flops 1000 | bytes 1000 | tf_op jit(solution)/shard_map/attend/pallas_call | solution.py:331
  (4 shorter events, 0.1 us)
Async XLA Ops:
  0.0 13.6 %copy-start = (bf16[1,256,768]{2,1,0:T(8,128)(2,1)S(1)}, bf16[1,256,768]{2,1,0:T(8,128)(2,1)}, u32[]{:S(2)}) copy-start(bf16[1,256,768]{2,1,0:T(8,128)(2,1)} %param.9) | copy-start | bytes 1179652
  0.0 12.0 %collective-permute-start.2 = (bf16[192,768]{1,0:T(8,128)(2,1)}, bf16[192,768]{1,0:T(8,128)(2,1)S(1)}, u32[]{:S(2)}, u32[]{:S(2)}) collective-permute-start(bf16[192,768]{1,0:T(8,128)(2,1)} %piece.1), channel_id=1, source_target_pairs={{0,16},{8,24},{16,0},{24,8},{1,17},{9,25},{17,1},{25,9},{2,18},{10... | collective-permute-start | bytes 884744 | tf_op jit(solution)/shard_map/ppermute | solution.py:230
  3.0 1.0 %copy-start.1 = (bf16[192,768]{1,0:T(8,128)(2,1)S(1)}, bf16[192,768]{1,0:T(8,128)(2,1)}, u32[]{:S(2)}) copy-start(bf16[192,768]{1,0:T(8,128)(2,1)} %refs_5_.1) | copy-start | bytes 884740
  3.9 1.0 %copy-start.3 = (bf16[192,768]{1,0:T(8,128)(2,1)S(1)}, bf16[192,768]{1,0:T(8,128)(2,1)}, u32[]{:S(2)}) copy-start(bf16[192,768]{1,0:T(8,128)(2,1)} %refs_6_.1) | copy-start | bytes 884740
  4.9 11.3 %copy-start.5 = (bf16[192,768]{1,0:T(8,128)(2,1)S(1)}, bf16[192,768]{1,0:T(8,128)(2,1)}, u32[]{:S(2)}) copy-start(bf16[192,768]{1,0:T(8,128)(2,1)} %refs_4_.1) | copy-start | bytes 884740
  4.9 11.9 %copy-start.4 = (bf16[192,768]{1,0:T(8,128)(2,1)S(1)}, bf16[192,768]{1,0:T(8,128)(2,1)}, u32[]{:S(2)}) copy-start(bf16[192,768]{1,0:T(8,128)(2,1)} %refs_6_.1) | copy-start | bytes 884740
  5.0 11.8 %copy-start.2 = (bf16[192,768]{1,0:T(8,128)(2,1)S(1)}, bf16[192,768]{1,0:T(8,128)(2,1)}, u32[]{:S(2)}) copy-start(bf16[192,768]{1,0:T(8,128)(2,1)} %refs_5_.1) | copy-start | bytes 884740
  5.0 11.8 %collective-permute-start.4 = (bf16[2,192,384]{2,1,0:T(8,128)(2,1)S(1)}, bf16[2,192,384]{2,1,0:T(8,128)(2,1)S(1)}, u32[]{:S(2)}, u32[]{:S(2)}) collective-permute-start(bf16[2,192,384]{2,1,0:T(8,128)(2,1)S(1)} %halves.1), channel_id=1, source_target_pairs={{0,16},{8,24},{16,0},{24,8},{1,17},{9,25},{17,1},{25,9},{2,18},{10... | collective-permute-start | bytes 884744 | tf_op jit(solution)/shard_map/ppermute | solution.py:230
  5.1 0.8 %copy-start.7 = (s32[1,64,4]{1,2,0:T(4,128)S(1)}, s32[1,64,4]{1,2,0:T(4,128)}, u32[]{:S(2)}) copy-start(s32[1,64,4]{1,2,0:T(4,128)} %param.10) | copy-start | bytes 3076
  5.8 0.7 %copy-start.8 = (s32[1,64,4]{1,2,0:T(4,128)S(1)}, s32[1,64,4]{1,2,0:T(4,128)}, u32[]{:S(2)}) copy-start(s32[1,64,4]{1,2,0:T(4,128)} %param.11) | copy-start | bytes 3076
  6.6 5.4 %collective-permute-start.1 = (s32[8,128]{1,0:T(8,128)S(1)}, s32[8,128]{1,0:T(8,128)S(1)}, u32[]{:S(2)}, u32[]{:S(2)}) collective-permute-start(s32[8,128]{1,0:T(8,128)S(1)} %slots.1.here), channel_id=1, source_target_pairs={{1,2},{3,4},{5,6},{2,1},{4,3},{6,5},{9,10},{11,12},{13,14},{10,9},... | collective-permute-start | bytes 12296 | tf_op jit(solution)/shard_map/ppermute | solution.py:294
  7.2 6.3 %collective-permute-start = (s32[8,128]{1,0:T(8,128)S(1)}, s32[8,128]{1,0:T(8,128)S(1)}, u32[]{:S(2)}, u32[]{:S(2)}) collective-permute-start(s32[8,128]{1,0:T(8,128)S(1)} %slots.1.here), channel_id=1, source_target_pairs={{0,1},{1,0},{2,3},{3,2},{4,5},{5,4},{6,7},{7,6},{8,9},{9,8},{10,11... | collective-permute-start | bytes 12296 | tf_op jit(solution)/shard_map/ppermute | solution.py:225
  12.0 14.7 %copy-start.6 = (bf16[192,768]{1,0:T(8,128)(2,1)S(1)}, bf16[192,768]{1,0:T(8,128)(2,1)}, u32[]{:S(2)}) copy-start(bf16[192,768]{1,0:T(8,128)(2,1)} %piece.1) | copy-start | bytes 884740
  14.1 4.4 %collective-permute-start.3 = (f32[24,768]{1,0:T(8,128)S(1)}, f32[24,768]{1,0:T(8,128)S(1)}, u32[]{:S(2)}, u32[]{:S(2)}) collective-permute-start(f32[24,768]{1,0:T(8,128)S(1)} %pool.1.mine), channel_id=1, source_target_pairs={{0,1},{1,0},{2,3},{3,2},{4,5},{5,4},{6,7},{7,6},{8,9},{9,8},{10,11... | collective-permute-start | bytes 221192 | tf_op jit(solution)/shard_map/ppermute | solution.py:225
  16.2 2.3 %collective-permute-start.6 = (bf16[192,768]{1,0:T(8,128)(2,1)}, bf16[192,768]{1,0:T(8,128)(2,1)S(1)}, u32[]{:S(2)}, u32[]{:S(2)}) collective-permute-start(bf16[192,768]{1,0:T(8,128)(2,1)} %piece.1), channel_id=1, source_target_pairs={{0,8},{8,0},{16,24},{24,16},{1,9},{9,1},{17,25},{25,17},{2,10},{10... | collective-permute-start | bytes 884744 | tf_op jit(solution)/shard_map/ppermute | solution.py:225
  16.2 3.9 %collective-permute-start.7 = (bf16[192,768]{1,0:T(8,128)(2,1)S(1)}, bf16[192,768]{1,0:T(8,128)(2,1)S(1)}, u32[]{:S(2)}, u32[]{:S(2)}) collective-permute-start(bf16[192,768]{1,0:T(8,128)(2,1)S(1)} %copy-done.5), channel_id=1, source_target_pairs={{0,8},{8,0},{16,24},{24,16},{1,9},{9,1},{17,25},{25,17},{2,10},{10... | collective-permute-start | bytes 884744 | tf_op jit(solution)/shard_map/ppermute | solution.py:225
  16.7 3.4 %collective-permute-start.8 = (bf16[192,768]{1,0:T(8,128)(2,1)S(1)}, bf16[192,768]{1,0:T(8,128)(2,1)S(1)}, u32[]{:S(2)}, u32[]{:S(2)}) collective-permute-start(bf16[192,768]{1,0:T(8,128)(2,1)S(1)} %copy-done.2), channel_id=1, source_target_pairs={{0,8},{8,0},{16,24},{24,16},{1,9},{9,1},{17,25},{25,17},{2,10},{10... | collective-permute-start | bytes 884744 | tf_op jit(solution)/shard_map/ppermute | solution.py:225
  16.8 3.3 %collective-permute-start.9 = (bf16[192,768]{1,0:T(8,128)(2,1)S(1)}, bf16[192,768]{1,0:T(8,128)(2,1)S(1)}, u32[]{:S(2)}, u32[]{:S(2)}) collective-permute-start(bf16[192,768]{1,0:T(8,128)(2,1)S(1)} %copy-done.4), channel_id=1, source_target_pairs={{0,8},{8,0},{16,24},{24,16},{1,9},{9,1},{17,25},{25,17},{2,10},{10... | collective-permute-start | bytes 884744 | tf_op jit(solution)/shard_map/ppermute | solution.py:225
  18.5 1.6 %collective-permute-start.5 = (bf16[1,192,768]{2,1,0:T(8,128)(2,1)S(1)}, bf16[1,192,768]{2,1,0:T(8,128)(2,1)S(1)}, u32[]{:S(2)}, u32[]{:S(2)}) collective-permute-start(bf16[1,192,768]{2,1,0:T(8,128)(2,1)S(1)} %bitcast.18), channel_id=1, source_target_pairs={{0,8},{8,0},{16,24},{24,16},{1,9},{9,1},{17,25},{25,17},{2,10},{10... | collective-permute-start | bytes 884744 | tf_op jit(solution)/shard_map/ppermute | solution.py:225
  18.5 13.6 %collective-permute-start.13 = (bf16[192,768]{1,0:T(8,128)(2,1)S(1)}, bf16[192,768]{1,0:T(8,128)(2,1)S(1)}, u32[]{:S(2)}, u32[]{:S(2)}) collective-permute-start(bf16[192,768]{1,0:T(8,128)(2,1)S(1)} %copy-done.5), channel_id=1, source_target_pairs={{0,16},{8,24},{16,0},{24,8},{1,17},{9,25},{17,1},{25,9},{2,18},{10... | collective-permute-start | bytes 884744 | tf_op jit(solution)/shard_map/ppermute | solution.py:230
  20.1 12.1 %collective-permute-start.14 = (bf16[1,2,192,384]{3,2,1,0:T(8,128)(2,1)S(1)}, bf16[1,2,192,384]{3,2,1,0:T(8,128)(2,1)S(1)}, u32[]{:S(2)}, u32[]{:S(2)}) collective-permute-start(bf16[1,2,192,384]{3,2,1,0:T(8,128)(2,1)S(1)} %bitcast.13), channel_id=1, source_target_pairs={{0,1},{1,0},{2,3},{3,2},{4,5},{5,4},{6,7},{7,6},{8,9},{9,8},{10,11... | collective-permute-start | bytes 884744 | tf_op jit(solution)/shard_map/ppermute | solution.py:225
  22.2 6.7 %collective-permute-start.12 = (bf16[48,768]{1,0:T(8,128)(2,1)S(1)}, bf16[48,768]{1,0:T(8,128)(2,1)S(1)}, u32[]{:S(2)}, u32[]{:S(2)}) collective-permute-start(bf16[48,768]{1,0:T(8,128)(2,1)S(1)} %pair.1), channel_id=1, source_target_pairs={{0,6},{1,7},{2,4},{3,5},{4,2},{5,3},{6,0},{7,1},{8,14},{9,15},{10,... | collective-permute-start | bytes 221192 | tf_op jit(solution)/shard_map/ppermute | solution.py:225
  24.2 7.8 %collective-permute-start.11 = (bf16[48,768]{1,0:T(8,128)(2,1)S(1)}, bf16[48,768]{1,0:T(8,128)(2,1)S(1)}, u32[]{:S(2)}, u32[]{:S(2)}) collective-permute-start(bf16[48,768]{1,0:T(8,128)(2,1)S(1)} %pair.1), channel_id=1, source_target_pairs={{0,4},{1,5},{2,6},{3,7},{4,0},{5,1},{6,2},{7,3},{8,12},{9,13},{10,... | collective-permute-start | bytes 221192 | tf_op jit(solution)/shard_map/ppermute | solution.py:225
  25.3 6.8 %collective-permute-start.10 = (bf16[48,768]{1,0:T(8,128)(2,1)S(1)}, bf16[48,768]{1,0:T(8,128)(2,1)S(1)}, u32[]{:S(2)}, u32[]{:S(2)}) collective-permute-start(bf16[48,768]{1,0:T(8,128)(2,1)S(1)} %pair.1), channel_id=1, source_target_pairs={{0,2},{1,3},{2,0},{3,1},{4,6},{5,7},{6,4},{7,5},{8,10},{9,11},{10,... | collective-permute-start | bytes 221192 | tf_op jit(solution)/shard_map/ppermute | solution.py:225
  28.9 4.5 %collective-permute-start.16 = (bf16[1,2,192,384]{3,2,1,0:T(8,128)(2,1)S(1)}, bf16[1,2,192,384]{3,2,1,0:T(8,128)(2,1)S(1)}, u32[]{:S(2)}, u32[]{:S(2)}) collective-permute-start(bf16[1,2,192,384]{3,2,1,0:T(8,128)(2,1)S(1)} %bitcast.14), channel_id=1, source_target_pairs={{0,8},{8,0},{16,24},{24,16},{1,9},{9,1},{17,25},{25,17},{2,10},{10... | collective-permute-start | bytes 884744 | tf_op jit(solution)/shard_map/ppermute | solution.py:225
  32.1 1.3 %copy-start.9 = (f32[768]{0:T(1024)S(1)}, f32[768]{0:T(1024)}, u32[]{:S(2)}) copy-start(f32[768]{0:T(1024)} %param.17) | copy-start | bytes 9220
  32.1 1.6 %collective-permute-start.15 = (bf16[1,192,768]{2,1,0:T(8,128)(2,1)S(1)}, bf16[1,192,768]{2,1,0:T(8,128)(2,1)S(1)}, u32[]{:S(2)}, u32[]{:S(2)}) collective-permute-start(bf16[1,192,768]{2,1,0:T(8,128)(2,1)S(1)} %bitcast.16), channel_id=1, source_target_pairs={{0,8},{8,0},{16,24},{24,16},{1,9},{9,1},{17,25},{25,17},{2,10},{10... | collective-permute-start | bytes 884744 | tf_op jit(solution)/shard_map/ppermute | solution.py:225
  32.2 2.0 %collective-permute-start.17 = (bf16[1,2,192,384]{3,2,1,0:T(8,128)(2,1)S(1)}, bf16[1,2,192,384]{3,2,1,0:T(8,128)(2,1)S(1)}, u32[]{:S(2)}, u32[]{:S(2)}) collective-permute-start(bf16[1,2,192,384]{3,2,1,0:T(8,128)(2,1)S(1)} %collective-permute-done.14.refs_12_), channel_id=1, source_target_pairs={{0,8},{8,0},{16,24},{24,16},{1,9},{9,1},{17,25},{25,17},{2,10},{10... | collective-permute-start | bytes 884744 | tf_op jit(solution)/shard_map/ppermute | solution.py:225

commit v7 on v6

--- a/solution.py
+++ b/solution.py
@@ -28,6 +28,10 @@
     return pl.BlockSpec(memory_space=pl.ANY)
 
 
+def hbm():
+    return pl.BlockSpec(memory_space=pltpu.HBM)
+
+
 def over(left, right, left_dim, right_dim, precision=None):
     return lax.dot_general(
         left,
@@ -36,14 +40,6 @@
         precision=precision,
         preferred_element_type=F32,
     )
-
-
-def slots_kernel(nbr, mask, out, held, sem):
-    count, regions = nbr.shape
-    for copy in collect([(nbr, held.at[0]), (mask, held.at[1])], sem):
-        copy.wait()
-    out[...] = jnp.zeros_like(out)
-    out[:count, :regions] = jnp.where(held[1] > 0, held[0] + 1, 0)
 
 
 def pool_kernel(regions, here, mate, other, tiles, out):
@@ -282,24 +278,20 @@
 
     shard = w_query.shape[0]
     near_query = from_chips(w_query)
-    slots = local_call(
-        slots_kernel,
-        jax.ShapeDtypeStruct((8, -(-regions // 128) * 128), jnp.int32),
-        [anywhere()] * 2,
-        "slots",
-        [pltpu.VMEM((2, NB, regions), jnp.int32), pltpu.SemaphoreType.DMA((2,))],
-    )(nbr_tiles[0].T, nbr_mask[0].T)
+    slots = jnp.where(nbr_mask[0].T > 0, nbr_tiles[0].T + 1, 0)
+    slots = jnp.pad(slots, ((0, 8 - NB), (0, -regions % 128)))
     mate = swap(slots, "tile", 1)
-    inner = [(i, i + 1) for i in range(1, tile_devices - 1, 2)]
+    inner = [(i, (i + 1) % tile_devices) for i in range(1, tile_devices, 2)]
     other = lax.ppermute(slots, "tile", inner + [(b, a) for a, b in inner])
-    halves = local_call(
+    halves = pl.pallas_call(
         halves_kernel,
-        jax.ShapeDtypeStruct((2, shard, width // 2), BF16),
-        [anywhere()] * 2,
-        "halves",
-        [pltpu.SemaphoreType.DMA((2,))],
-    )(w_value, w_out)
-    near_halves = from_chips(halves)
+        out_shape=jax.ShapeDtypeStruct((2, shard, width // 2), BF16),
+        in_specs=[hbm()] * 2,
+        out_specs=vmem(),
+        scratch_shapes=[pltpu.SemaphoreType.DMA((2,))],
+        name="halves",
+    )(behind(w_value, slots), w_out)
+    near_halves = from_chips(behind(halves, mate, other))
     mine = local_call(
         functools.partial(pool_kernel, regions),
         jax.ShapeDtypeStruct((3 * block, width), F32),

time: 38.2 us -> 37.5 us (0.982)
  waiting for transfers between devices: 8.43 us -> 12.9 us
  starting transfers between devices: 20.1 us -> 15.9 us
  local copies, waits for them, and re-layouts: 3.38 us -> 0.04 us
  Pallas kernels: 5.23 us -> 6.93 us
  other arithmetic: 0.02 us -> 0.72 us
    ppermute x14, starting transfers between devices: 14.9 us -> 7.36 us  [swap(): return lax.ppermute(array, axis, [(i, i ^ offset) for i in range(count)])]
    ppermute x3, waiting for transfers between devices: 0.01 us -> 5.51 us  [chip_shift(): lax.ppermute(array, axis, [(i, (i + 2 * step) % count) for i in range(cou...]
    ppermute x1, starting transfers between devices: 0.66 us -> 4.59 us  [body(): other = lax.ppermute(slots, 'tile', inner + [(b, a) for a, b in inner])]
    unnamed x20 -> x12, local copies, waits for them, and re-layouts: 3.38 us -> 0.02 us
    pallas_call x2 -> x1, Pallas kernels: 0.08 us -> 1.78 us  [body(): pl.pallas_call(halves_kernel, out_shape=jax.ShapeDtypeStruct((2, shard, w...]
    ppermute x14, waiting for transfers between devices: 8.42 us -> 7.41 us  [swap(): return lax.ppermute(array, axis, [(i, i ^ offset) for i in range(count)])]
    select_n x0 -> x1, other arithmetic: none -> 0.7 us  [body(): slots = jnp.where(nbr_mask[0].T > 0, nbr_tiles[0].T + 1, 0)]
    ppermute x3, starting transfers between devices: 4.61 us -> 3.98 us  [chip_shift(): lax.ppermute(array, axis, [(i, (i + 2 * step) % count) for i in range(cou...]
  transfers between devices with their start and end apart: 18 -> 18, of which waited for: 6 -> 8; matrix products, arithmetic and copies ran while one was open for 0% -> 2% of each run, Pallas kernels for 4% -> 8%
where the time goes in v7:
time: 37.5 us; the launch traced here: 37.3 us
  starting transfers between devices  15.9 us (42%)
  waiting for transfers between devices  12.9 us (34%)
  Pallas kernels  6.93 us (18%)
  between operations  0.76 us (2%)
  other arithmetic  0.72 us (2%)
    ppermute x14, waiting for transfers between devices, swap(): return lax.ppermute(array, axis, [(i, i ^ offset) for i in range(count)])  7.41 us
    ppermute x14, starting transfers between devices, swap(): return lax.ppermute(array, axis, [(i, i ^ offset) for i in range(count)])  7.36 us
    ppermute x3, waiting for transfers between devices, chip_shift(): lax.ppermute(array, axis, [(i, (i + 2 * step) % count) for i in range(cou...  5.51 us
    ppermute x1, starting transfers between devices, body(): other = lax.ppermute(slots, 'tile', inner + [(b, a) for a, b in inner])  4.59 us
    ppermute x3, starting transfers between devices, chip_shift(): lax.ppermute(array, axis, [(i, (i + 2 * step) % count) for i in range(cou...  3.98 us
    pallas_call x1, Pallas kernels, body(): local_call(functools.partial(attend_kernel, fsdp, block), jax.ShapeDtypeS...  3.82 us
    pallas_call x1, Pallas kernels, body(): pl.pallas_call(halves_kernel, out_shape=jax.ShapeDtypeStruct((2, shard, w...  1.78 us
    pallas_call x1, Pallas kernels, body(): local_call(functools.partial(query_kernel, fsdp), jax.ShapeDtypeStruct((r...  0.76 us
  transfers between devices with their start and end apart: 18, of which 8 were waited for; matrix products, arithmetic and copies ran while one was open for 2% of the time, Pallas kernels for 8%

profile of v7, /device:TPU:0, one launch (start us, length us, event | category | flops | bytes accessed | tf_op | source)
XLA Modules:
  0.0 37.3 jit_solution(5932093185619848390)
XLA Ops:
  0.0 3.0 %collective-permute-start.2 = (bf16[192,768]{1,0:T(8,128)(2,1)}, bf16[192,768]{1,0:T(8,128)(2,1)S(1)}, u32[]{:S(2)}, u32[]{:S(2)}) collective-permute-start(bf16[192,768]{1,0:T(8,128)(2,1)} %piece.1), channel_id=1, source_target_pairs={{0,16},{8,24},{16,0},{24,8},{1,17},{9,25},{17,1},{25,9},{2,18},{10... | collective-permute-start | bytes 884744 | tf_op jit(solution)/shard_map/ppermute | solution.py:226
  3.0 0.7 %select_bitcast_fusion = s32[4,64]{1,0:T(4,128)S(1)} fusion(s32[1,64,4]{1,2,0:T(4,128)} %param.10, s32[1,64,4]{1,2,0:T(4,128)} %param.11), kind=kLoop, calls=%fused_computation.1 | loop fusion | flops 768 | bytes 3072 | tf_op jit(solution)/shard_map/jit(_where)/select_n | solution.py:281
  3.7 0.0 copy-start
  3.7 4.6 %collective-permute-start.1 = (s32[8,128]{1,0:T(8,128)S(1)}, s32[8,128]{1,0:T(8,128)S(1)}, u32[]{:S(2)}, u32[]{:S(2)}) collective-permute-start(s32[8,128]{1,0:T(8,128)S(1)} %pad.4.here), channel_id=1, source_target_pairs={{1,2},{3,4},{5,6},{7,0},{2,1},{4,3},{6,5},{0,7},{9,10},{11,12},{13... | collective-permute-start | bytes 12296 | tf_op jit(solution)/shard_map/ppermute | solution.py:285
  8.3 0.0 collective-permute-start
  8.3 0.0 copy-start.3
  8.3 0.0 copy-start.2
  8.3 1.8 %halves.1 = bf16[2,192,384]{2,1,0:T(8,128)(2,1)} custom-call(bf16[192,768]{1,0:T(8,128)(2,1)} %refs_5_.1, bf16[192,768]{1,0:T(8,128)(2,1)} %refs_6_.1), custom_call_target="tpu_custom_call" | custom-call | tf_op jit(solution)/shard_map/halves/pallas_call | solution.py:286
  10.1 0.0 copy-start.1
  10.1 0.0 collective-permute-done.1.other
  10.1 1.8 %collective-permute-done.mate = s32[8,128]{1,0:T(8,128)S(1)} collective-permute-done((s32[8,128]{1,0:T(8,128)S(1)}, s32[8,128]{1,0:T(8,128)S(1)}, u32[]{:S(2)}, u32[]{:S(2)}) %collective-permute-start) | collective-permute-done | bytes 4128 | tf_op jit(solution)/shard_map/ppermute | solution.py:221
  11.9 0.5 %collective-permute-start.4 = (bf16[2,192,384]{2,1,0:T(8,128)(2,1)}, bf16[2,192,384]{2,1,0:T(8,128)(2,1)S(1)}, u32[]{:S(2)}, u32[]{:S(2)}) collective-permute-start(bf16[2,192,384]{2,1,0:T(8,128)(2,1)} %halves.1), channel_id=1, source_target_pairs={{0,16},{8,24},{16,0},{24,8},{1,17},{9,25},{17,1},{25,9},{2,18},{10... | collective-permute-start | bytes 884744 | tf_op jit(solution)/shard_map/ppermute | solution.py:226
  12.4 0.0 collective-permute-done.2
  12.4 0.0 copy-done
  12.4 0.0 copy-start.4
  12.4 0.6 %pool.1.mine = f32[24,768]{1,0:T(8,128)S(1)} custom-call(s32[8,128]{1,0:T(8,128)S(1)} %pad.4.here, s32[8,128]{1,0:T(8,128)S(1)} %collective-permute-done.mate, s32[8,128]{1,0:T(8,128)S(1)} %collective-permute-done.1.other, bf16[256,768]{1,0:T(8,128)(2,1)S(1)} %bitcast.9), custom_call_target="tpu_custom_call" | custom-call | flops 1000 | bytes 1000 | tf_op jit(solution)/shard_map/pool/pallas_call | solution.py:295
  13.0 0.4 collective-permute-start.3
  13.3 0.0 collective-permute-start.6
  13.3 0.0 copy-done.3
  13.3 0.5 %collective-permute-start.7 = (bf16[192,768]{1,0:T(8,128)(2,1)S(1)}, bf16[192,768]{1,0:T(8,128)(2,1)S(1)}, u32[]{:S(2)}, u32[]{:S(2)}) collective-permute-start(bf16[192,768]{1,0:T(8,128)(2,1)S(1)} %copy-done.3), channel_id=1, source_target_pairs={{0,8},{8,0},{16,24},{24,16},{1,9},{9,1},{17,25},{25,17},{2,10},{10... | collective-permute-start | bytes 884744 | tf_op jit(solution)/shard_map/ppermute | solution.py:221
  13.8 0.0 copy-done.1
  13.8 0.1 collective-permute-start.8
  13.9 5.5 %collective-permute-done.4 = bf16[2,192,384]{2,1,0:T(8,128)(2,1)S(1)} collective-permute-done((bf16[2,192,384]{2,1,0:T(8,128)(2,1)}, bf16[2,192,384]{2,1,0:T(8,128)(2,1)S(1)}, u32[]{:S(2)}, u32[]{:S(2)}) %collective-permute-start.4) | collective-permute-done | bytes 294944 | tf_op jit(solution)/shard_map/ppermute | solution.py:226
  19.4 0.0 copy-done.2
  19.4 0.0 collective-permute-start.9
  19.4 0.0 collective-permute-done.3.theirs
  19.4 0.5 %collective-permute-start.5 = (bf16[1,192,768]{2,1,0:T(8,128)(2,1)S(1)}, bf16[1,192,768]{2,1,0:T(8,128)(2,1)S(1)}, u32[]{:S(2)}, u32[]{:S(2)}) collective-permute-start(bf16[1,192,768]{2,1,0:T(8,128)(2,1)S(1)} %bitcast.16), channel_id=1, source_target_pairs={{0,8},{8,0},{16,24},{24,16},{1,9},{9,1},{17,25},{25,17},{2,10},{10... | collective-permute-start | bytes 884744 | tf_op jit(solution)/shard_map/ppermute | solution.py:221
  19.9 0.0 collective-permute-done.6.mate
  19.9 0.5 %collective-permute-start.13 = (bf16[192,768]{1,0:T(8,128)(2,1)S(1)}, bf16[192,768]{1,0:T(8,128)(2,1)S(1)}, u32[]{:S(2)}, u32[]{:S(2)}) collective-permute-start(bf16[192,768]{1,0:T(8,128)(2,1)S(1)} %copy-done.3), channel_id=1, source_target_pairs={{0,16},{8,24},{16,0},{24,8},{1,17},{9,25},{17,1},{25,9},{2,18},{10... | collective-permute-start | bytes 884744 | tf_op jit(solution)/shard_map/ppermute | solution.py:226
  20.5 0.0 collective-permute-done.7.refs_7_
  20.5 0.0 collective-permute-done.8.refs_8_
  20.5 0.5 %collective-permute-done.9.refs_9_ = bf16[192,768]{1,0:T(8,128)(2,1)S(1)} collective-permute-done((bf16[192,768]{1,0:T(8,128)(2,1)S(1)}, bf16[192,768]{1,0:T(8,128)(2,1)S(1)}, u32[]{:S(2)}, u32[]{:S(2)}) %collective-permute-start.9) | collective-permute-done | bytes 294944 | tf_op jit(solution)/shard_map/ppermute | solution.py:221
  21.0 0.4 %collective-permute-done.5.far = bf16[1,192,768]{2,1,0:T(8,128)(2,1)S(1)} collective-permute-done((bf16[1,192,768]{2,1,0:T(8,128)(2,1)S(1)}, bf16[1,192,768]{2,1,0:T(8,128)(2,1)S(1)}, u32[]{:S(2)}, u32[]{:S(2)}) %collective-permute-start.5) | collective-permute-done | bytes 294944 | tf_op jit(solution)/shard_map/ppermute | solution.py:221
  21.4 0.9 %collective-permute-start.14 = (bf16[1,2,192,384]{3,2,1,0:T(8,128)(2,1)S(1)}, bf16[1,2,192,384]{3,2,1,0:T(8,128)(2,1)S(1)}, u32[]{:S(2)}, u32[]{:S(2)}) collective-permute-start(bf16[1,2,192,384]{3,2,1,0:T(8,128)(2,1)S(1)} %bitcast.11), channel_id=1, source_target_pairs={{0,1},{1,0},{2,3},{3,2},{4,5},{5,4},{6,7},{7,6},{8,9},{9,8},{10,11... | collective-permute-start | bytes 884744 | tf_op jit(solution)/shard_map/ppermute | solution.py:221
  22.4 2.4 %collective-permute-start.12 = (bf16[48,768]{1,0:T(8,128)(2,1)S(1)}, bf16[48,768]{1,0:T(8,128)(2,1)S(1)}, u32[]{:S(2)}, u32[]{:S(2)}) collective-permute-start(bf16[48,768]{1,0:T(8,128)(2,1)S(1)} %pair.1), channel_id=1, source_target_pairs={{0,6},{1,7},{2,4},{3,5},{4,2},{5,3},{6,0},{7,1},{8,14},{9,15},{10,... | collective-permute-start | bytes 221192 | tf_op jit(solution)/shard_map/ppermute | solution.py:221
  24.8 0.0 collective-permute-start.11
  24.8 2.0 %collective-permute-start.10 = (bf16[48,768]{1,0:T(8,128)(2,1)S(1)}, bf16[48,768]{1,0:T(8,128)(2,1)S(1)}, u32[]{:S(2)}, u32[]{:S(2)}) collective-permute-start(bf16[48,768]{1,0:T(8,128)(2,1)S(1)} %pair.1), channel_id=1, source_target_pairs={{0,2},{1,3},{2,0},{3,1},{4,6},{5,7},{6,4},{7,5},{8,10},{9,11},{10,... | collective-permute-start | bytes 221192 | tf_op jit(solution)/shard_map/ppermute | solution.py:221
  26.8 0.0 copy-done.4
  26.8 0.8 %query.1.refs_3_ = bf16[256,768]{1,0:T(8,128)(2,1)S(1)} custom-call(bf16[256,768]{1,0:T(8,128)(2,1)S(1)} %bitcast.10, bf16[192,768]{1,0:T(8,128)(2,1)S(1)} %copy-done.4, bf16[192,768]{1,0:T(8,128)(2,1)S(1)} %collective-permute-done.6.mate, bf16[1,192,768]{2,1,0:T(8,128)(2,1)S(1)} %bitcast.17, bf16[1,192,768]{2,1,0:T(8,128)(2,1)S(1)} %collective-permute-done.5.far), custom_call_target="tpu_custom_call" | custom-call | flops 1000 | bytes 1000 | tf_op jit(solution)/shard_map/query/pallas_call | solution.py:313
  27.6 1.6 %collective-permute-done.12 = bf16[48,768]{1,0:T(8,128)(2,1)S(1)} collective-permute-done((bf16[48,768]{1,0:T(8,128)(2,1)S(1)}, bf16[48,768]{1,0:T(8,128)(2,1)S(1)}, u32[]{:S(2)}, u32[]{:S(2)}) %collective-permute-start.12) | collective-permute-done | bytes 73760 | tf_op jit(solution)/shard_map/ppermute | solution.py:221
  29.1 0.0 collective-permute-start.16
  29.1 2.2 %collective-permute-done.11 = bf16[48,768]{1,0:T(8,128)(2,1)S(1)} collective-permute-done((bf16[48,768]{1,0:T(8,128)(2,1)S(1)}, bf16[48,768]{1,0:T(8,128)(2,1)S(1)}, u32[]{:S(2)}, u32[]{:S(2)}) %collective-permute-start.11) | collective-permute-done | bytes 73760 | tf_op jit(solution)/shard_map/ppermute | solution.py:221
  31.4 0.0 collective-permute-done.10
  31.4 0.0 copy-start.5
  31.4 0.0 collective-permute-done.13
  31.4 0.1 collective-permute-start.15
  31.5 0.0 collective-permute-done.14.refs_12_
  31.5 0.5 %collective-permute-start.17 = (bf16[1,2,192,384]{3,2,1,0:T(8,128)(2,1)S(1)}, bf16[1,2,192,384]{3,2,1,0:T(8,128)(2,1)S(1)}, u32[]{:S(2)}, u32[]{:S(2)}) collective-permute-start(bf16[1,2,192,384]{3,2,1,0:T(8,128)(2,1)S(1)} %collective-permute-done.14.refs_12_), channel_id=1, source_target_pairs={{0,8},{8,0},{16,24},{24,16},{1,9},{9,1},{17,25},{25,17},{2,10},{10... | collective-permute-start | bytes 884744 | tf_op jit(solution)/shard_map/ppermute | solution.py:221
  32.6 0.0 copy-done.5
  32.7 0.0 collective-permute-done.16.refs_14_
  32.7 0.4 %collective-permute-done.15.refs_13_ = bf16[1,192,768]{2,1,0:T(8,128)(2,1)S(1)} collective-permute-done((bf16[1,192,768]{2,1,0:T(8,128)(2,1)S(1)}, bf16[1,192,768]{2,1,0:T(8,128)(2,1)S(1)}, u32[]{:S(2)}, u32[]{:S(2)}) %collective-permute-start.15) | collective-permute-done | bytes 294944 | tf_op jit(solution)/shard_map/ppermute | solution.py:221
  33.1 0.4 %collective-permute-done.17.refs_15_ = bf16[1,2,192,384]{3,2,1,0:T(8,128)(2,1)S(1)} collective-permute-done((bf16[1,2,192,384]{3,2,1,0:T(8,128)(2,1)S(1)}, bf16[1,2,192,384]{3,2,1,0:T(8,128)(2,1)S(1)}, u32[]{:S(2)}, u32[]{:S(2)}) %collective-permute-start.17) | collective-permute-done | bytes 294944 | tf_op jit(solution)/shard_map/ppermute | solution.py:221
  33.5 3.8 %attend.1 = bf16[256,768]{1,0:T(8,128)(2,1)} custom-call(s32[1]{0:T(128)S(6)} %copy.10.refs_0_, bf16[192,768]{1,0:T(8,128)(2,1)S(1)} %pad_maximum_fusion.refs_1_, f32[1,768]{1,0:T(1,128)S(1)} %broadcast_in_dim.8.refs_2_, bf16[256,768]{1,0:T(8,128)(2,1)S(1)} %query.1.refs_3_, bf16[192,768]{1,0:T(8,128)(2,1)S(1)} %copy-done.3, bf16[192,768]{1,0:T(8,128)(2,1)S(1)} %copy-done.1, ...), custom_call_target="tpu_custom_call" | custom-call | flops 1000 | bytes 1000 | tf_op jit(solution)/shard_map/attend/pallas_call | solution.py:323
  (4 shorter events, 0.0 us)
Async XLA Ops:
  0.0 12.4 %collective-permute-start.2 = (bf16[192,768]{1,0:T(8,128)(2,1)}, bf16[192,768]{1,0:T(8,128)(2,1)S(1)}, u32[]{:S(2)}, u32[]{:S(2)}) collective-permute-start(bf16[192,768]{1,0:T(8,128)(2,1)} %piece.1), channel_id=1, source_target_pairs={{0,16},{8,24},{16,0},{24,8},{1,17},{9,25},{17,1},{25,9},{2,18},{10... | collective-permute-start | bytes 884744 | tf_op jit(solution)/shard_map/ppermute | solution.py:226
  3.7 8.7 %copy-start = (bf16[1,256,768]{2,1,0:T(8,128)(2,1)S(1)}, bf16[1,256,768]{2,1,0:T(8,128)(2,1)}, u32[]{:S(2)}) copy-start(bf16[1,256,768]{2,1,0:T(8,128)(2,1)} %param.9) | copy-start | bytes 1179652
  3.7 6.4 %collective-permute-start.1 = (s32[8,128]{1,0:T(8,128)S(1)}, s32[8,128]{1,0:T(8,128)S(1)}, u32[]{:S(2)}, u32[]{:S(2)}) collective-permute-start(s32[8,128]{1,0:T(8,128)S(1)} %pad.4.here), channel_id=1, source_target_pairs={{1,2},{3,4},{5,6},{7,0},{2,1},{4,3},{6,5},{0,7},{9,10},{11,12},{13... | collective-permute-start | bytes 12296 | tf_op jit(solution)/shard_map/ppermute | solution.py:285
  8.3 3.6 %collective-permute-start = (s32[8,128]{1,0:T(8,128)S(1)}, s32[8,128]{1,0:T(8,128)S(1)}, u32[]{:S(2)}, u32[]{:S(2)}) collective-permute-start(s32[8,128]{1,0:T(8,128)S(1)} %pad.4.here), channel_id=1, source_target_pairs={{0,1},{1,0},{2,3},{3,2},{4,5},{5,4},{6,7},{7,6},{8,9},{9,8},{10,11... | collective-permute-start | bytes 12296 | tf_op jit(solution)/shard_map/ppermute | solution.py:221
  8.3 5.1 %copy-start.3 = (bf16[192,768]{1,0:T(8,128)(2,1)S(1)}, bf16[192,768]{1,0:T(8,128)(2,1)}, u32[]{:S(2)}) copy-start(bf16[192,768]{1,0:T(8,128)(2,1)} %refs_4_.1) | copy-start | bytes 884740
  8.3 11.1 %copy-start.2 = (bf16[192,768]{1,0:T(8,128)(2,1)S(1)}, bf16[192,768]{1,0:T(8,128)(2,1)}, u32[]{:S(2)}) copy-start(bf16[192,768]{1,0:T(8,128)(2,1)} %refs_6_.1) | copy-start | bytes 884740
  10.1 3.8 %copy-start.1 = (bf16[192,768]{1,0:T(8,128)(2,1)S(1)}, bf16[192,768]{1,0:T(8,128)(2,1)}, u32[]{:S(2)}) copy-start(bf16[192,768]{1,0:T(8,128)(2,1)} %refs_5_.1) | copy-start | bytes 884740
  11.9 7.5 %collective-permute-start.4 = (bf16[2,192,384]{2,1,0:T(8,128)(2,1)}, bf16[2,192,384]{2,1,0:T(8,128)(2,1)S(1)}, u32[]{:S(2)}, u32[]{:S(2)}) collective-permute-start(bf16[2,192,384]{2,1,0:T(8,128)(2,1)} %halves.1), channel_id=1, source_target_pairs={{0,16},{8,24},{16,0},{24,8},{1,17},{9,25},{17,1},{25,9},{2,18},{10... | collective-permute-start | bytes 884744 | tf_op jit(solution)/shard_map/ppermute | solution.py:226
  12.4 14.4 %copy-start.4 = (bf16[192,768]{1,0:T(8,128)(2,1)S(1)}, bf16[192,768]{1,0:T(8,128)(2,1)}, u32[]{:S(2)}) copy-start(bf16[192,768]{1,0:T(8,128)(2,1)} %piece.1) | copy-start | bytes 884740
  13.0 6.5 %collective-permute-start.3 = (f32[24,768]{1,0:T(8,128)S(1)}, f32[24,768]{1,0:T(8,128)S(1)}, u32[]{:S(2)}, u32[]{:S(2)}) collective-permute-start(f32[24,768]{1,0:T(8,128)S(1)} %pool.1.mine), channel_id=1, source_target_pairs={{0,1},{1,0},{2,3},{3,2},{4,5},{5,4},{6,7},{7,6},{8,9},{9,8},{10,11... | collective-permute-start | bytes 221192 | tf_op jit(solution)/shard_map/ppermute | solution.py:221
  13.3 6.6 %collective-permute-start.6 = (bf16[192,768]{1,0:T(8,128)(2,1)}, bf16[192,768]{1,0:T(8,128)(2,1)S(1)}, u32[]{:S(2)}, u32[]{:S(2)}) collective-permute-start(bf16[192,768]{1,0:T(8,128)(2,1)} %piece.1), channel_id=1, source_target_pairs={{0,8},{8,0},{16,24},{24,16},{1,9},{9,1},{17,25},{25,17},{2,10},{10... | collective-permute-start | bytes 884744 | tf_op jit(solution)/shard_map/ppermute | solution.py:221
  13.3 7.1 %collective-permute-start.7 = (bf16[192,768]{1,0:T(8,128)(2,1)S(1)}, bf16[192,768]{1,0:T(8,128)(2,1)S(1)}, u32[]{:S(2)}, u32[]{:S(2)}) collective-permute-start(bf16[192,768]{1,0:T(8,128)(2,1)S(1)} %copy-done.3), channel_id=1, source_target_pairs={{0,8},{8,0},{16,24},{24,16},{1,9},{9,1},{17,25},{25,17},{2,10},{10... | collective-permute-start | bytes 884744 | tf_op jit(solution)/shard_map/ppermute | solution.py:221
  13.8 6.6 %collective-permute-start.8 = (bf16[192,768]{1,0:T(8,128)(2,1)S(1)}, bf16[192,768]{1,0:T(8,128)(2,1)S(1)}, u32[]{:S(2)}, u32[]{:S(2)}) collective-permute-start(bf16[192,768]{1,0:T(8,128)(2,1)S(1)} %copy-done.1), channel_id=1, source_target_pairs={{0,8},{8,0},{16,24},{24,16},{1,9},{9,1},{17,25},{25,17},{2,10},{10... | collective-permute-start | bytes 884744 | tf_op jit(solution)/shard_map/ppermute | solution.py:221
  19.4 1.6 %collective-permute-start.9 = (bf16[192,768]{1,0:T(8,128)(2,1)S(1)}, bf16[192,768]{1,0:T(8,128)(2,1)S(1)}, u32[]{:S(2)}, u32[]{:S(2)}) collective-permute-start(bf16[192,768]{1,0:T(8,128)(2,1)S(1)} %copy-done.2), channel_id=1, source_target_pairs={{0,8},{8,0},{16,24},{24,16},{1,9},{9,1},{17,25},{25,17},{2,10},{10... | collective-permute-start | bytes 884744 | tf_op jit(solution)/shard_map/ppermute | solution.py:221
  19.4 2.0 %collective-permute-start.5 = (bf16[1,192,768]{2,1,0:T(8,128)(2,1)S(1)}, bf16[1,192,768]{2,1,0:T(8,128)(2,1)S(1)}, u32[]{:S(2)}, u32[]{:S(2)}) collective-permute-start(bf16[1,192,768]{2,1,0:T(8,128)(2,1)S(1)} %bitcast.16), channel_id=1, source_target_pairs={{0,8},{8,0},{16,24},{24,16},{1,9},{9,1},{17,25},{25,17},{2,10},{10... | collective-permute-start | bytes 884744 | tf_op jit(solution)/shard_map/ppermute | solution.py:221
  19.9 11.5 %collective-permute-start.13 = (bf16[192,768]{1,0:T(8,128)(2,1)S(1)}, bf16[192,768]{1,0:T(8,128)(2,1)S(1)}, u32[]{:S(2)}, u32[]{:S(2)}) collective-permute-start(bf16[192,768]{1,0:T(8,128)(2,1)S(1)} %copy-done.3), channel_id=1, source_target_pairs={{0,16},{8,24},{16,0},{24,8},{1,17},{9,25},{17,1},{25,9},{2,18},{10... | collective-permute-start | bytes 884744 | tf_op jit(solution)/shard_map/ppermute | solution.py:226
  21.4 10.1 %collective-permute-start.14 = (bf16[1,2,192,384]{3,2,1,0:T(8,128)(2,1)S(1)}, bf16[1,2,192,384]{3,2,1,0:T(8,128)(2,1)S(1)}, u32[]{:S(2)}, u32[]{:S(2)}) collective-permute-start(bf16[1,2,192,384]{3,2,1,0:T(8,128)(2,1)S(1)} %bitcast.11), channel_id=1, source_target_pairs={{0,1},{1,0},{2,3},{3,2},{4,5},{5,4},{6,7},{7,6},{8,9},{9,8},{10,11... | collective-permute-start | bytes 884744 | tf_op jit(solution)/shard_map/ppermute | solution.py:221
  22.4 6.8 %collective-permute-start.12 = (bf16[48,768]{1,0:T(8,128)(2,1)S(1)}, bf16[48,768]{1,0:T(8,128)(2,1)S(1)}, u32[]{:S(2)}, u32[]{:S(2)}) collective-permute-start(bf16[48,768]{1,0:T(8,128)(2,1)S(1)} %pair.1), channel_id=1, source_target_pairs={{0,6},{1,7},{2,4},{3,5},{4,2},{5,3},{6,0},{7,1},{8,14},{9,15},{10,... | collective-permute-start | bytes 221192 | tf_op jit(solution)/shard_map/ppermute | solution.py:221
  24.8 6.6 %collective-permute-start.11 = (bf16[48,768]{1,0:T(8,128)(2,1)S(1)}, bf16[48,768]{1,0:T(8,128)(2,1)S(1)}, u32[]{:S(2)}, u32[]{:S(2)}) collective-permute-start(bf16[48,768]{1,0:T(8,128)(2,1)S(1)} %pair.1), channel_id=1, source_target_pairs={{0,4},{1,5},{2,6},{3,7},{4,0},{5,1},{6,2},{7,3},{8,12},{9,13},{10,... | collective-permute-start | bytes 221192 | tf_op jit(solution)/shard_map/ppermute | solution.py:221
  24.8 6.6 %collective-permute-start.10 = (bf16[48,768]{1,0:T(8,128)(2,1)S(1)}, bf16[48,768]{1,0:T(8,128)(2,1)S(1)}, u32[]{:S(2)}, u32[]{:S(2)}) collective-permute-start(bf16[48,768]{1,0:T(8,128)(2,1)S(1)} %pair.1), channel_id=1, source_target_pairs={{0,2},{1,3},{2,0},{3,1},{4,6},{5,7},{6,4},{7,5},{8,10},{9,11},{10,... | collective-permute-start | bytes 221192 | tf_op jit(solution)/shard_map/ppermute | solution.py:221
  29.1 3.5 %collective-permute-start.16 = (bf16[1,2,192,384]{3,2,1,0:T(8,128)(2,1)S(1)}, bf16[1,2,192,384]{3,2,1,0:T(8,128)(2,1)S(1)}, u32[]{:S(2)}, u32[]{:S(2)}) collective-permute-start(bf16[1,2,192,384]{3,2,1,0:T(8,128)(2,1)S(1)} %bitcast.12), channel_id=1, source_target_pairs={{0,8},{8,0},{16,24},{24,16},{1,9},{9,1},{17,25},{25,17},{2,10},{10... | collective-permute-start | bytes 884744 | tf_op jit(solution)/shard_map/ppermute | solution.py:221
  31.4 1.3 %copy-start.5 = (f32[768]{0:T(1024)S(1)}, f32[768]{0:T(1024)}, u32[]{:S(2)}) copy-start(f32[768]{0:T(1024)} %param.17) | copy-start | bytes 9220
  31.4 1.6 %collective-permute-start.15 = (bf16[1,192,768]{2,1,0:T(8,128)(2,1)S(1)}, bf16[1,192,768]{2,1,0:T(8,128)(2,1)S(1)}, u32[]{:S(2)}, u32[]{:S(2)}) collective-permute-start(bf16[1,192,768]{2,1,0:T(8,128)(2,1)S(1)} %bitcast.14), channel_id=1, source_target_pairs={{0,8},{8,0},{16,24},{24,16},{1,9},{9,1},{17,25},{25,17},{2,10},{10... | collective-permute-start | bytes 884744 | tf_op jit(solution)/shard_map/ppermute | solution.py:221
  31.5 2.0 %collective-permute-start.17 = (bf16[1,2,192,384]{3,2,1,0:T(8,128)(2,1)S(1)}, bf16[1,2,192,384]{3,2,1,0:T(8,128)(2,1)S(1)}, u32[]{:S(2)}, u32[]{:S(2)}) collective-permute-start(bf16[1,2,192,384]{3,2,1,0:T(8,128)(2,1)S(1)} %collective-permute-done.14.refs_12_), channel_id=1, source_target_pairs={{0,8},{8,0},{16,24},{24,16},{1,9},{9,1},{17,25},{25,17},{2,10},{10... | collective-permute-start | bytes 884744 | tf_op jit(solution)/shard_map/ppermute | solution.py:221

commit v8 on v7

--- a/solution.py
+++ b/solution.py
@@ -135,41 +135,35 @@
     return own, others
 
 
-def query_kernel(fsdp, tiles, piece, mate, near, far, out, held, sem):
-    own, others = place_rows(fsdp, piece.shape[0], held)
-    copies = own(0, piece, mate) + others(0, lambda j: near.at[j], lambda j: far.at[j])
-    for copy in collect(copies, sem):
-        copy.wait()
-    out[...] = over(tiles[...], held[0], 1, 0).astype(BF16)
-
-
 def attend_kernel(fsdp, block, *refs):
-    count, sums, gain, query = refs[:4]
-    pieces, mates = refs[4:7], refs[7:10]
-    near, far = refs[10:13], refs[13:16]
-    out, held, pooled, sem = refs[16:]
+    count, sums, gain, tiles = refs[:4]
+    pieces, mates = refs[4:8], refs[8:12]
+    near, far = refs[12:16], refs[16:20]
+    out, held, pooled, sem = refs[20:]
     device = lax.axis_index("tile")
     own, others = place_rows(fsdp, pieces[0].shape[0], held)
     copies, ends = [], []
-    for weight in (1, 2, 0):
+    for weight in range(4):
         copies += own(weight, pieces[weight], mates[weight])
-        if weight == 0:
-            copies += others(0, lambda j: near[0].at[j], lambda j: far[0].at[j])
+        if weight < 2:
+            copies += others(weight, lambda j: near[weight].at[j], lambda j: far[weight].at[j])
         else:
             for side in range(2):
                 copies += others(
                     weight,
-                    lambda j: near[1 + side].at[j, weight - 1],
-                    lambda j: far[1 + side].at[j, weight - 1],
+                    lambda j: near[2 + side].at[j, weight - 2],
+                    lambda j: far[2 + side].at[j, weight - 2],
                     side,
                 )
         ends.append(len(copies))
     started = collect(copies, sem)
 
-    def arrive(begin, end):
-        for copy in started[begin:end]:
+    def arrive(weight):
+        for copy in started[(ends[weight - 1] if weight else 0) : ends[weight]]:
             copy.wait()
 
+    arrive(0)
+    query = over(tiles[...], held[0], 1, 0).astype(BF16)
     pooled[...] = jnp.zeros_like(pooled)
     pairs = sums.shape[0] // (6 * block)
     for s in range(pairs):
@@ -184,10 +178,10 @@
     scale = lax.rsqrt(jnp.mean(mean * mean, axis=1, keepdims=True) + 1e-06)
     normed = (mean * scale * gain[...]).astype(BF16)
     ordered = sorted_rows(normed)
-    arrive(0, ends[0])
-    values = over(ordered, held[1], 1, 0).astype(BF16)
-    arrive(ends[1], ends[2])
-    keys = over(ordered, held[0], 1, 0).astype(BF16)
+    arrive(1)
+    keys = over(ordered, held[1], 1, 0).astype(BF16)
+    arrive(2)
+    values = over(ordered, held[2], 1, 0).astype(BF16)
     half = keys.shape[0] // KEY_DILATION
     heads = HEADS // LANE_GROUPS
     wide = keys.shape[1] // LANE_GROUPS
@@ -211,9 +205,9 @@
         weight = expo.reshape(heads * half, rows).astype(BF16)
         context = over(spread(values, group, wide), weight, 0, 0).reshape(heads, size, rows)
         contexts.append((context * share).reshape(wide, rows).astype(BF16))
-    arrive(ends[0], ends[1])
+    arrive(3)
     context = jnp.concatenate(contexts, axis=0)
-    out[...] = over(context, held[2], 0, 0).astype(out.dtype)
+    out[...] = over(context, held[3], 0, 0).astype(out.dtype)
 
 
 def swap(array, axis, offset):
@@ -281,8 +275,9 @@
     slots = jnp.where(nbr_mask[0].T > 0, nbr_tiles[0].T + 1, 0)
     slots = jnp.pad(slots, ((0, 8 - NB), (0, -regions % 128)))
     mate = swap(slots, "tile", 1)
-    inner = [(i, (i + 1) % tile_devices) for i in range(1, tile_devices, 2)]
-    other = lax.ppermute(slots, "tile", inner + [(b, a) for a, b in inner])
+    inner = [(i, i + 1) for i in range(1, tile_devices - 1, 2)]
+    ends = [(0, 0), (tile_devices - 1, tile_devices - 1)]
+    other = lax.ppermute(slots, "tile", inner + [(b, a) for a, b in inner] + ends)
     halves = pl.pallas_call(
         halves_kernel,
         out_shape=jax.ShapeDtypeStruct((2, shard, width // 2), BF16),
@@ -297,49 +292,36 @@
         jax.ShapeDtypeStruct((3 * block, width), F32),
         [vmem()] * 4,
         "pool",
-    )(slots, mate, other, behind(own_tiles, near_query))
+    )(slots, mate, other, behind(own_tiles, halves))
     near_key = from_chips(behind(w_key, mine))
-    mates = [swap(behind(w, mine), "fsdp", 1) for w in (w_query, w_key, w_value, w_out)]
-    far_query = swap(near_query, "fsdp", 1)
     pair = local_call(
         pair_kernel,
         jax.ShapeDtypeStruct((6 * block, width), BF16),
         [vmem()] * 2,
         "pair",
-    )(mine, behind(swap(mine, "tile", 1), near_halves, far_query, *mates))
+    )(mine, behind(swap(mine, "tile", 1), near_query))
     near_halves = behind(near_halves, pair)
     other_halves = swap(near_halves, "tile", 1)
     far_halves = swap(near_halves, "fsdp", 1)
-    query = local_call(
-        functools.partial(query_kernel, fsdp),
-        jax.ShapeDtypeStruct((rows, width), BF16),
-        [vmem()] + [anywhere()] * 4,
-        "query",
-        [pltpu.VMEM((1, width, width), BF16), pltpu.SemaphoreType.DMA((fsdp,))],
-    )(behind(own_tiles, pair), w_query, mates[0], near_query, far_query)
-    sums = behind(gather_pairs(pair, "tile"), query)
+    sums = gather_pairs(pair, "tile")
+    near_query = behind(near_query, sums)
+    weights = (w_query, w_key, w_value, w_out)
+    mates = [swap(behind(w, sums), "fsdp", 1) for w in weights]
+    far_query = swap(near_query, "fsdp", 1)
     near_key = behind(near_key, sums)
-    other_halves = behind(other_halves, sums)
+    near = (near_query, near_key, near_halves, other_halves)
+    far = (far_query, swap(near_key, "fsdp", 1), far_halves, swap(behind(other_halves, sums), "fsdp", 1))
     attended = local_call(
         functools.partial(attend_kernel, fsdp, block),
         jax.ShapeDtypeStruct((rows, width), BF16),
-        [smem()] + [vmem()] * 3 + [anywhere()] * 12,
+        [smem()] + [vmem()] * 3 + [anywhere()] * 16,
         "attend",
         [
-            pltpu.VMEM((3, width, width), BF16),
+            pltpu.VMEM((4, width, width), BF16),
             pltpu.VMEM(((tile_devices + 2) * block, width), F32),
-            pltpu.SemaphoreType.DMA((5 * fsdp,)),
+            pltpu.SemaphoreType.DMA((6 * fsdp,)),
         ],
-    )(
-        tile_count,
-        sums,
-        key_gain[None, :],
-        query,
-        *(w_key, w_value, w_out),
-        *mates[1:],
-        *(near_key, near_halves, other_halves),
-        *(swap(near_key, "fsdp", 1), far_halves, swap(other_halves, "fsdp", 1)),
-    )
+    )(tile_count, sums, key_gain[None, :], own_tiles, *weights, *mates, *near, *far)
     return attended[None]
 
 

time: 37.5 us -> 39 us (1.040)
  starting transfers between devices: 15.9 us -> 19.4 us
  waiting for transfers between devices: 12.9 us -> 11.3 us
    ppermute x14, starting transfers between devices: 7.36 us -> 13.5 us  [swap(): return lax.ppermute(array, axis, [(i, i ^ offset) for i in range(count)])]
    ppermute x3, waiting for transfers between devices: 5.51 us -> 1.51 us  [chip_shift(): lax.ppermute(array, axis, [(i, (i + 2 * step) % count) for i in range(cou...]
    ppermute x1, starting transfers between devices: 4.59 us -> 0.79 us  [body(): lax.ppermute(slots, 'tile', inner + [(b, a) for a, b in inner] + ends)]
    ppermute x14, waiting for transfers between devices: 7.41 us -> 9.79 us  [swap(): return lax.ppermute(array, axis, [(i, i ^ offset) for i in range(count)])]
    ppermute x3, starting transfers between devices: 3.98 us -> 5.06 us  [chip_shift(): lax.ppermute(array, axis, [(i, (i + 2 * step) % count) for i in range(cou...]
    pallas_call x1 -> x0, Pallas kernels: 0.76 us -> none  [body(): local_call(functools.partial(query_kernel, fsdp), jax.ShapeDtypeStruct((r...]
    pallas_call x1, Pallas kernels: 3.82 us -> 4.35 us  [body(): local_call(functools.partial(attend_kernel, fsdp, block), jax.ShapeDtypeS...]
  transfers between devices with their start and end apart: 18 -> 18, of which waited for: 8 -> 8; matrix products, arithmetic and copies ran while one was open for 2% -> 2% of each run, Pallas kernels for 8% -> 6%
where the time goes in v8:
time: 39 us; the launch traced here: 38.8 us
  starting transfers between devices  19.4 us (50%)
  waiting for transfers between devices  11.3 us (29%)
  Pallas kernels  6.63 us (17%)
  between operations  0.78 us (2%)
  other arithmetic  0.72 us (2%)
    ppermute x14, starting transfers between devices, swap(): return lax.ppermute(array, axis, [(i, i ^ offset) for i in range(count)])  13.5 us
    ppermute x14, waiting for transfers between devices, swap(): return lax.ppermute(array, axis, [(i, i ^ offset) for i in range(count)])  9.79 us
    ppermute x3, starting transfers between devices, chip_shift(): lax.ppermute(array, axis, [(i, (i + 2 * step) % count) for i in range(cou...  5.06 us
    pallas_call x1, Pallas kernels, body(): local_call(functools.partial(attend_kernel, fsdp, block), jax.ShapeDtypeS...  4.35 us
    pallas_call x1, Pallas kernels, body(): pl.pallas_call(halves_kernel, out_shape=jax.ShapeDtypeStruct((2, shard, w...  1.71 us
    ppermute x3, waiting for transfers between devices, chip_shift(): lax.ppermute(array, axis, [(i, (i + 2 * step) % count) for i in range(cou...  1.51 us
    ppermute x1, starting transfers between devices, body(): lax.ppermute(slots, 'tile', inner + [(b, a) for a, b in inner] + ends)  0.79 us
  transfers between devices with their start and end apart: 18, of which 8 were waited for; matrix products, arithmetic and copies ran while one was open for 2% of the time, Pallas kernels for 6%

profile of v8, /device:TPU:0, one launch (start us, length us, event | category | flops | bytes accessed | tf_op | source)
XLA Modules:
  0.0 38.8 jit_solution(17896481728280352217)
XLA Ops:
  0.0 3.0 %collective-permute-start.3 = (bf16[192,768]{1,0:T(8,128)(2,1)}, bf16[192,768]{1,0:T(8,128)(2,1)S(1)}, u32[]{:S(2)}, u32[]{:S(2)}) collective-permute-start(bf16[192,768]{1,0:T(8,128)(2,1)} %refs_4_.1), channel_id=1, source_target_pairs={{0,16},{8,24},{16,0},{24,8},{1,17},{9,25},{17,1},{25,9},{2,18},{10... | collective-permute-start | bytes 884744 | tf_op jit(solution)/shard_map/ppermute | solution.py:220
  3.0 0.7 %select_bitcast_fusion = s32[4,64]{1,0:T(4,128)S(1)} fusion(s32[1,64,4]{1,2,0:T(4,128)} %param.10, s32[1,64,4]{1,2,0:T(4,128)} %param.11), kind=kLoop, calls=%fused_computation.1 | loop fusion | flops 768 | bytes 3072 | tf_op jit(solution)/shard_map/jit(_where)/select_n | solution.py:275
  3.7 0.0 copy-start
  3.7 0.8 %collective-permute-start.1 = (s32[8,128]{1,0:T(8,128)S(1)}, s32[8,128]{1,0:T(8,128)S(1)}, u32[]{:S(2)}, u32[]{:S(2)}) collective-permute-start(s32[8,128]{1,0:T(8,128)S(1)} %pad.4.here), channel_id=1, source_target_pairs={{1,2},{3,4},{5,6},{2,1},{4,3},{6,5},{0,0},{7,7},{9,10},{11,12},{13... | collective-permute-start | bytes 12296 | tf_op jit(solution)/shard_map/ppermute | solution.py:280
  4.5 4.4 %collective-permute-start = (s32[8,128]{1,0:T(8,128)S(1)}, s32[8,128]{1,0:T(8,128)S(1)}, u32[]{:S(2)}, u32[]{:S(2)}) collective-permute-start(s32[8,128]{1,0:T(8,128)S(1)} %pad.4.here), channel_id=1, source_target_pairs={{0,1},{1,0},{2,3},{3,2},{4,5},{5,4},{6,7},{7,6},{8,9},{9,8},{10,11... | collective-permute-start | bytes 12296 | tf_op jit(solution)/shard_map/ppermute | solution.py:215
  8.8 1.7 %halves.1 = bf16[2,192,384]{2,1,0:T(8,128)(2,1)} custom-call(bf16[192,768]{1,0:T(8,128)(2,1)} %refs_6_.1, bf16[192,768]{1,0:T(8,128)(2,1)} %refs_7_.1), custom_call_target="tpu_custom_call" | custom-call | tf_op jit(solution)/shard_map/halves/pallas_call | solution.py:281
  10.5 0.0 collective-permute-done.1.other
  10.6 0.0 collective-permute-done.mate
  10.6 0.6 %collective-permute-start.12 = (bf16[2,192,384]{2,1,0:T(8,128)(2,1)}, bf16[2,192,384]{2,1,0:T(8,128)(2,1)S(1)}, u32[]{:S(2)}, u32[]{:S(2)}) collective-permute-start(bf16[2,192,384]{2,1,0:T(8,128)(2,1)} %halves.1), channel_id=1, source_target_pairs={{0,16},{8,24},{16,0},{24,8},{1,17},{9,25},{17,1},{25,9},{2,18},{10... | collective-permute-start | bytes 884744 | tf_op jit(solution)/shard_map/ppermute | solution.py:220
  11.1 0.0 copy-done
  11.1 0.0 copy-start.4
  11.1 0.0 copy-start.3
  11.1 0.6 %pool.1.mine = f32[24,768]{1,0:T(8,128)S(1)} custom-call(s32[8,128]{1,0:T(8,128)S(1)} %pad.4.here, s32[8,128]{1,0:T(8,128)S(1)} %collective-permute-done.mate, s32[8,128]{1,0:T(8,128)S(1)} %collective-permute-done.1.other, bf16[256,768]{1,0:T(8,128)(2,1)S(1)} %bitcast.9), custom_call_target="tpu_custom_call" | custom-call | flops 1000 | bytes 1000 | tf_op jit(solution)/shard_map/pool/pallas_call | solution.py:290
  11.7 1.9 %collective-permute-start.2 = (f32[24,768]{1,0:T(8,128)S(1)}, f32[24,768]{1,0:T(8,128)S(1)}, u32[]{:S(2)}, u32[]{:S(2)}) collective-permute-start(f32[24,768]{1,0:T(8,128)S(1)} %pool.1.mine), channel_id=1, source_target_pairs={{0,1},{1,0},{2,3},{3,2},{4,5},{5,4},{6,7},{7,6},{8,9},{9,8},{10,11... | collective-permute-start | bytes 221192 | tf_op jit(solution)/shard_map/ppermute | solution.py:215
  13.6 2.5 %collective-permute-done.2.theirs = f32[24,768]{1,0:T(8,128)S(1)} collective-permute-done((f32[24,768]{1,0:T(8,128)S(1)}, f32[24,768]{1,0:T(8,128)S(1)}, u32[]{:S(2)}, u32[]{:S(2)}) %collective-permute-start.2) | collective-permute-done | bytes 73760 | tf_op jit(solution)/shard_map/ppermute | solution.py:215
  16.1 0.0 collective-permute-done.3
  16.1 0.0 copy-start.5
  16.2 3.8 %collective-permute-start.6 = (bf16[48,768]{1,0:T(8,128)(2,1)S(1)}, bf16[48,768]{1,0:T(8,128)(2,1)S(1)}, u32[]{:S(2)}, u32[]{:S(2)}) collective-permute-start(bf16[48,768]{1,0:T(8,128)(2,1)S(1)} %pair.1), channel_id=1, source_target_pairs={{0,6},{1,7},{2,4},{3,5},{4,2},{5,3},{6,0},{7,1},{8,14},{9,15},{10,... | collective-permute-start | bytes 221192 | tf_op jit(solution)/shard_map/ppermute | solution.py:215
  20.0 0.0 collective-permute-start.5
  20.0 0.6 %collective-permute-start.4 = (bf16[48,768]{1,0:T(8,128)(2,1)S(1)}, bf16[48,768]{1,0:T(8,128)(2,1)S(1)}, u32[]{:S(2)}, u32[]{:S(2)}) collective-permute-start(bf16[48,768]{1,0:T(8,128)(2,1)S(1)} %pair.1), channel_id=1, source_target_pairs={{0,2},{1,3},{2,0},{3,1},{4,6},{5,7},{6,4},{7,5},{8,10},{9,11},{10,... | collective-permute-start | bytes 221192 | tf_op jit(solution)/shard_map/ppermute | solution.py:215
  20.6 0.0 copy-done.4
  20.6 1.5 %collective-permute-start.11 = (bf16[192,768]{1,0:T(8,128)(2,1)S(1)}, bf16[192,768]{1,0:T(8,128)(2,1)S(1)}, u32[]{:S(2)}, u32[]{:S(2)}) collective-permute-start(bf16[192,768]{1,0:T(8,128)(2,1)S(1)} %copy-done.4), channel_id=1, source_target_pairs={{0,16},{8,24},{16,0},{24,8},{1,17},{9,25},{17,1},{25,9},{2,18},{10... | collective-permute-start | bytes 884744 | tf_op jit(solution)/shard_map/ppermute | solution.py:220
  22.1 0.0 collective-permute-done.12
  22.1 0.0 copy-start.1
  22.1 0.0 copy-start.2
  22.1 0.0 collective-permute-start.16
  22.1 0.8 %collective-permute-done.6 = bf16[48,768]{1,0:T(8,128)(2,1)S(1)} collective-permute-done((bf16[48,768]{1,0:T(8,128)(2,1)S(1)}, bf16[48,768]{1,0:T(8,128)(2,1)S(1)}, u32[]{:S(2)}, u32[]{:S(2)}) %collective-permute-start.6) | collective-permute-done | bytes 73760 | tf_op jit(solution)/shard_map/ppermute | solution.py:215
  22.9 1.3 %collective-permute-start.13 = (bf16[1,2,192,384]{3,2,1,0:T(8,128)(2,1)S(1)}, bf16[1,2,192,384]{3,2,1,0:T(8,128)(2,1)S(1)}, u32[]{:S(2)}, u32[]{:S(2)}) collective-permute-start(bf16[1,2,192,384]{3,2,1,0:T(8,128)(2,1)S(1)} %bitcast.14), channel_id=1, source_target_pairs={{0,1},{1,0},{2,3},{3,2},{4,5},{5,4},{6,7},{7,6},{8,9},{9,8},{10,11... | collective-permute-start | bytes 884744 | tf_op jit(solution)/shard_map/ppermute | solution.py:215
  24.2 1.0 %collective-permute-done.5 = bf16[48,768]{1,0:T(8,128)(2,1)S(1)} collective-permute-done((bf16[48,768]{1,0:T(8,128)(2,1)S(1)}, bf16[48,768]{1,0:T(8,128)(2,1)S(1)}, u32[]{:S(2)}, u32[]{:S(2)}) %collective-permute-start.5) | collective-permute-done | bytes 73760 | tf_op jit(solution)/shard_map/ppermute | solution.py:215
  25.2 0.0 collective-permute-done.4
  25.2 0.0 copy-done.3
  25.3 0.1 collective-permute-start.7
  25.3 0.5 %collective-permute-start.8 = (bf16[192,768]{1,0:T(8,128)(2,1)S(1)}, bf16[192,768]{1,0:T(8,128)(2,1)S(1)}, u32[]{:S(2)}, u32[]{:S(2)}) collective-permute-start(bf16[192,768]{1,0:T(8,128)(2,1)S(1)} %copy-done.4), channel_id=1, source_target_pairs={{0,8},{8,0},{16,24},{24,16},{1,9},{9,1},{17,25},{25,17},{2,10},{10... | collective-permute-start | bytes 884744 | tf_op jit(solution)/shard_map/ppermute | solution.py:215
  25.8 1.5 %collective-permute-done.11 = bf16[192,768]{1,0:T(8,128)(2,1)S(1)} collective-permute-done((bf16[192,768]{1,0:T(8,128)(2,1)S(1)}, bf16[192,768]{1,0:T(8,128)(2,1)S(1)}, u32[]{:S(2)}, u32[]{:S(2)}) %collective-permute-start.11) | collective-permute-done | bytes 294944 | tf_op jit(solution)/shard_map/ppermute | solution.py:220
  27.3 0.0 copy-done.1
  27.3 0.0 collective-permute-start.9
  27.3 4.3 %collective-permute-done.13.refs_15_ = bf16[1,2,192,384]{3,2,1,0:T(8,128)(2,1)S(1)} collective-permute-done((bf16[1,2,192,384]{3,2,1,0:T(8,128)(2,1)S(1)}, bf16[1,2,192,384]{3,2,1,0:T(8,128)(2,1)S(1)}, u32[]{:S(2)}, u32[]{:S(2)}) %collective-permute-start.13) | collective-permute-done | bytes 294944 | tf_op jit(solution)/shard_map/ppermute | solution.py:215
  31.6 0.0 copy-done.2
  31.6 0.0 collective-permute-start.10
  31.6 0.0 collective-permute-done.16.refs_18_
  31.6 0.5 %collective-permute-start.14 = (bf16[1,192,768]{2,1,0:T(8,128)(2,1)S(1)}, bf16[1,192,768]{2,1,0:T(8,128)(2,1)S(1)}, u32[]{:S(2)}, u32[]{:S(2)}) collective-permute-start(bf16[1,192,768]{2,1,0:T(8,128)(2,1)S(1)} %bitcast.11), channel_id=1, source_target_pairs={{0,8},{8,0},{16,24},{24,16},{1,9},{9,1},{17,25},{25,17},{2,10},{10... | collective-permute-start | bytes 884744 | tf_op jit(solution)/shard_map/ppermute | solution.py:215
  32.1 0.0 collective-permute-done.7.refs_8_
  32.2 0.1 collective-permute-start.15
  32.2 0.0 collective-permute-done.8.refs_9_
  32.2 0.4 %collective-permute-start.17 = (bf16[1,2,192,384]{3,2,1,0:T(8,128)(2,1)S(1)}, bf16[1,2,192,384]{3,2,1,0:T(8,128)(2,1)S(1)}, u32[]{:S(2)}, u32[]{:S(2)}) collective-permute-start(bf16[1,2,192,384]{3,2,1,0:T(8,128)(2,1)S(1)} %collective-permute-done.13.refs_15_), channel_id=1, source_target_pairs={{0,8},{8,0},{16,24},{24,16},{1,9},{9,1},{17,25},{25,17},{2,10},{10... | collective-permute-start | bytes 884744 | tf_op jit(solution)/shard_map/ppermute | solution.py:215
  33.3 0.0 copy-done.5
  33.3 0.0 collective-permute-done.9.refs_10_
  33.4 0.0 collective-permute-done.10.refs_11_
  33.4 0.3 collective-permute-done.14.refs_16_
  33.6 0.4 %collective-permute-done.15.refs_17_ = bf16[1,192,768]{2,1,0:T(8,128)(2,1)S(1)} collective-permute-done((bf16[1,192,768]{2,1,0:T(8,128)(2,1)S(1)}, bf16[1,192,768]{2,1,0:T(8,128)(2,1)S(1)}, u32[]{:S(2)}, u32[]{:S(2)}) %collective-permute-start.15) | collective-permute-done | bytes 294944 | tf_op jit(solution)/shard_map/ppermute | solution.py:215
  34.1 0.4 %collective-permute-done.17.refs_19_ = bf16[1,2,192,384]{3,2,1,0:T(8,128)(2,1)S(1)} collective-permute-done((bf16[1,2,192,384]{3,2,1,0:T(8,128)(2,1)S(1)}, bf16[1,2,192,384]{3,2,1,0:T(8,128)(2,1)S(1)}, u32[]{:S(2)}, u32[]{:S(2)}) %collective-permute-start.17) | collective-permute-done | bytes 294944 | tf_op jit(solution)/shard_map/ppermute | solution.py:215
  34.5 4.3 %attend.1 = bf16[256,768]{1,0:T(8,128)(2,1)} custom-call(s32[1]{0:T(128)S(6)} %copy.10.refs_0_, bf16[192,768]{1,0:T(8,128)(2,1)S(1)} %pad_maximum_fusion.refs_1_, f32[1,768]{1,0:T(1,128)S(1)} %broadcast_in_dim.8.refs_2_, bf16[256,768]{1,0:T(8,128)(2,1)S(1)} %bitcast.10, bf16[192,768]{1,0:T(8,128)(2,1)S(1)} %copy-done.3, bf16[192,768]{1,0:T(8,128)(2,1)S(1)} %copy-done.4, ...), custom_call_target="tpu_custom_call" | custom-call | flops 1000 | bytes 1000 | tf_op jit(solution)/shard_map/attend/pallas_call | solution.py:314
  (4 shorter events, 0.0 us)
Async XLA Ops:
  0.0 16.1 %collective-permute-start.3 = (bf16[192,768]{1,0:T(8,128)(2,1)}, bf16[192,768]{1,0:T(8,128)(2,1)S(1)}, u32[]{:S(2)}, u32[]{:S(2)}) collective-permute-start(bf16[192,768]{1,0:T(8,128)(2,1)} %refs_4_.1), channel_id=1, source_target_pairs={{0,16},{8,24},{16,0},{24,8},{1,17},{9,25},{17,1},{25,9},{2,18},{10... | collective-permute-start | bytes 884744 | tf_op jit(solution)/shard_map/ppermute | solution.py:220
  3.7 7.5 %copy-start = (bf16[1,256,768]{2,1,0:T(8,128)(2,1)S(1)}, bf16[1,256,768]{2,1,0:T(8,128)(2,1)}, u32[]{:S(2)}) copy-start(bf16[1,256,768]{2,1,0:T(8,128)(2,1)} %param.9) | copy-start | bytes 1179652
  3.7 6.9 %collective-permute-start.1 = (s32[8,128]{1,0:T(8,128)S(1)}, s32[8,128]{1,0:T(8,128)S(1)}, u32[]{:S(2)}, u32[]{:S(2)}) collective-permute-start(s32[8,128]{1,0:T(8,128)S(1)} %pad.4.here), channel_id=1, source_target_pairs={{1,2},{3,4},{5,6},{2,1},{4,3},{6,5},{0,0},{7,7},{9,10},{11,12},{13... | collective-permute-start | bytes 12296 | tf_op jit(solution)/shard_map/ppermute | solution.py:280
  4.5 6.1 %collective-permute-start = (s32[8,128]{1,0:T(8,128)S(1)}, s32[8,128]{1,0:T(8,128)S(1)}, u32[]{:S(2)}, u32[]{:S(2)}) collective-permute-start(s32[8,128]{1,0:T(8,128)S(1)} %pad.4.here), channel_id=1, source_target_pairs={{0,1},{1,0},{2,3},{3,2},{4,5},{5,4},{6,7},{7,6},{8,9},{9,8},{10,11... | collective-permute-start | bytes 12296 | tf_op jit(solution)/shard_map/ppermute | solution.py:215
  10.6 11.6 %collective-permute-start.12 = (bf16[2,192,384]{2,1,0:T(8,128)(2,1)}, bf16[2,192,384]{2,1,0:T(8,128)(2,1)S(1)}, u32[]{:S(2)}, u32[]{:S(2)}) collective-permute-start(bf16[2,192,384]{2,1,0:T(8,128)(2,1)} %halves.1), channel_id=1, source_target_pairs={{0,16},{8,24},{16,0},{24,8},{1,17},{9,25},{17,1},{25,9},{2,18},{10... | collective-permute-start | bytes 884744 | tf_op jit(solution)/shard_map/ppermute | solution.py:220
  11.1 9.5 %copy-start.4 = (bf16[192,768]{1,0:T(8,128)(2,1)S(1)}, bf16[192,768]{1,0:T(8,128)(2,1)}, u32[]{:S(2)}) copy-start(bf16[192,768]{1,0:T(8,128)(2,1)} %refs_5_.1) | copy-start | bytes 884740
  11.1 14.1 %copy-start.3 = (bf16[192,768]{1,0:T(8,128)(2,1)S(1)}, bf16[192,768]{1,0:T(8,128)(2,1)}, u32[]{:S(2)}) copy-start(bf16[192,768]{1,0:T(8,128)(2,1)} %refs_4_.1) | copy-start | bytes 884740
  11.7 4.4 %collective-permute-start.2 = (f32[24,768]{1,0:T(8,128)S(1)}, f32[24,768]{1,0:T(8,128)S(1)}, u32[]{:S(2)}, u32[]{:S(2)}) collective-permute-start(f32[24,768]{1,0:T(8,128)S(1)} %pool.1.mine), channel_id=1, source_target_pairs={{0,1},{1,0},{2,3},{3,2},{4,5},{5,4},{6,7},{7,6},{8,9},{9,8},{10,11... | collective-permute-start | bytes 221192 | tf_op jit(solution)/shard_map/ppermute | solution.py:215
  16.1 17.2 %copy-start.5 = (f32[768]{0:T(1024)S(1)}, f32[768]{0:T(1024)}, u32[]{:S(2)}) copy-start(f32[768]{0:T(1024)} %param.17) | copy-start | bytes 9220
  16.2 6.8 %collective-permute-start.6 = (bf16[48,768]{1,0:T(8,128)(2,1)S(1)}, bf16[48,768]{1,0:T(8,128)(2,1)S(1)}, u32[]{:S(2)}, u32[]{:S(2)}) collective-permute-start(bf16[48,768]{1,0:T(8,128)(2,1)S(1)} %pair.1), channel_id=1, source_target_pairs={{0,6},{1,7},{2,4},{3,5},{4,2},{5,3},{6,0},{7,1},{8,14},{9,15},{10,... | collective-permute-start | bytes 221192 | tf_op jit(solution)/shard_map/ppermute | solution.py:215
  20.0 5.3 %collective-permute-start.5 = (bf16[48,768]{1,0:T(8,128)(2,1)S(1)}, bf16[48,768]{1,0:T(8,128)(2,1)S(1)}, u32[]{:S(2)}, u32[]{:S(2)}) collective-permute-start(bf16[48,768]{1,0:T(8,128)(2,1)S(1)} %pair.1), channel_id=1, source_target_pairs={{0,4},{1,5},{2,6},{3,7},{4,0},{5,1},{6,2},{7,3},{8,12},{9,13},{10,... | collective-permute-start | bytes 221192 | tf_op jit(solution)/shard_map/ppermute | solution.py:215
  20.0 5.3 %collective-permute-start.4 = (bf16[48,768]{1,0:T(8,128)(2,1)S(1)}, bf16[48,768]{1,0:T(8,128)(2,1)S(1)}, u32[]{:S(2)}, u32[]{:S(2)}) collective-permute-start(bf16[48,768]{1,0:T(8,128)(2,1)S(1)} %pair.1), channel_id=1, source_target_pairs={{0,2},{1,3},{2,0},{3,1},{4,6},{5,7},{6,4},{7,5},{8,10},{9,11},{10,... | collective-permute-start | bytes 221192 | tf_op jit(solution)/shard_map/ppermute | solution.py:215
  20.6 6.7 %collective-permute-start.11 = (bf16[192,768]{1,0:T(8,128)(2,1)S(1)}, bf16[192,768]{1,0:T(8,128)(2,1)S(1)}, u32[]{:S(2)}, u32[]{:S(2)}) collective-permute-start(bf16[192,768]{1,0:T(8,128)(2,1)S(1)} %copy-done.4), channel_id=1, source_target_pairs={{0,16},{8,24},{16,0},{24,8},{1,17},{9,25},{17,1},{25,9},{2,18},{10... | collective-permute-start | bytes 884744 | tf_op jit(solution)/shard_map/ppermute | solution.py:220
  22.1 5.2 %copy-start.1 = (bf16[192,768]{1,0:T(8,128)(2,1)S(1)}, bf16[192,768]{1,0:T(8,128)(2,1)}, u32[]{:S(2)}) copy-start(bf16[192,768]{1,0:T(8,128)(2,1)} %refs_6_.1) | copy-start | bytes 884740
  22.1 9.5 %copy-start.2 = (bf16[192,768]{1,0:T(8,128)(2,1)S(1)}, bf16[192,768]{1,0:T(8,128)(2,1)}, u32[]{:S(2)}) copy-start(bf16[192,768]{1,0:T(8,128)(2,1)} %refs_7_.1) | copy-start | bytes 884740
  22.1 9.5 %collective-permute-start.16 = (bf16[1,2,192,384]{3,2,1,0:T(8,128)(2,1)S(1)}, bf16[1,2,192,384]{3,2,1,0:T(8,128)(2,1)S(1)}, u32[]{:S(2)}, u32[]{:S(2)}) collective-permute-start(bf16[1,2,192,384]{3,2,1,0:T(8,128)(2,1)S(1)} %bitcast.13), channel_id=1, source_target_pairs={{0,8},{8,0},{16,24},{24,16},{1,9},{9,1},{17,25},{25,17},{2,10},{10... | collective-permute-start | bytes 884744 | tf_op jit(solution)/shard_map/ppermute | solution.py:215
  22.9 8.7 %collective-permute-start.13 = (bf16[1,2,192,384]{3,2,1,0:T(8,128)(2,1)S(1)}, bf16[1,2,192,384]{3,2,1,0:T(8,128)(2,1)S(1)}, u32[]{:S(2)}, u32[]{:S(2)}) collective-permute-start(bf16[1,2,192,384]{3,2,1,0:T(8,128)(2,1)S(1)} %bitcast.14), channel_id=1, source_target_pairs={{0,1},{1,0},{2,3},{3,2},{4,5},{5,4},{6,7},{7,6},{8,9},{9,8},{10,11... | collective-permute-start | bytes 884744 | tf_op jit(solution)/shard_map/ppermute | solution.py:215
  25.3 6.9 %collective-permute-start.7 = (bf16[192,768]{1,0:T(8,128)(2,1)S(1)}, bf16[192,768]{1,0:T(8,128)(2,1)S(1)}, u32[]{:S(2)}, u32[]{:S(2)}) collective-permute-start(bf16[192,768]{1,0:T(8,128)(2,1)S(1)} %copy-done.3), channel_id=1, source_target_pairs={{0,8},{8,0},{16,24},{24,16},{1,9},{9,1},{17,25},{25,17},{2,10},{10... | collective-permute-start | bytes 884744 | tf_op jit(solution)/shard_map/ppermute | solution.py:215
  25.3 6.9 %collective-permute-start.8 = (bf16[192,768]{1,0:T(8,128)(2,1)S(1)}, bf16[192,768]{1,0:T(8,128)(2,1)S(1)}, u32[]{:S(2)}, u32[]{:S(2)}) collective-permute-start(bf16[192,768]{1,0:T(8,128)(2,1)S(1)} %copy-done.4), channel_id=1, source_target_pairs={{0,8},{8,0},{16,24},{24,16},{1,9},{9,1},{17,25},{25,17},{2,10},{10... | collective-permute-start | bytes 884744 | tf_op jit(solution)/shard_map/ppermute | solution.py:215
  27.3 6.0 %collective-permute-start.9 = (bf16[192,768]{1,0:T(8,128)(2,1)S(1)}, bf16[192,768]{1,0:T(8,128)(2,1)S(1)}, u32[]{:S(2)}, u32[]{:S(2)}) collective-permute-start(bf16[192,768]{1,0:T(8,128)(2,1)S(1)} %copy-done.1), channel_id=1, source_target_pairs={{0,8},{8,0},{16,24},{24,16},{1,9},{9,1},{17,25},{25,17},{2,10},{10... | collective-permute-start | bytes 884744 | tf_op jit(solution)/shard_map/ppermute | solution.py:215
  31.6 1.7 %collective-permute-start.10 = (bf16[192,768]{1,0:T(8,128)(2,1)S(1)}, bf16[192,768]{1,0:T(8,128)(2,1)S(1)}, u32[]{:S(2)}, u32[]{:S(2)}) collective-permute-start(bf16[192,768]{1,0:T(8,128)(2,1)S(1)} %copy-done.2), channel_id=1, source_target_pairs={{0,8},{8,0},{16,24},{24,16},{1,9},{9,1},{17,25},{25,17},{2,10},{10... | collective-permute-start | bytes 884744 | tf_op jit(solution)/shard_map/ppermute | solution.py:215
  31.6 2.0 %collective-permute-start.14 = (bf16[1,192,768]{2,1,0:T(8,128)(2,1)S(1)}, bf16[1,192,768]{2,1,0:T(8,128)(2,1)S(1)}, u32[]{:S(2)}, u32[]{:S(2)}) collective-permute-start(bf16[1,192,768]{2,1,0:T(8,128)(2,1)S(1)} %bitcast.11), channel_id=1, source_target_pairs={{0,8},{8,0},{16,24},{24,16},{1,9},{9,1},{17,25},{25,17},{2,10},{10... | collective-permute-start | bytes 884744 | tf_op jit(solution)/shard_map/ppermute | solution.py:215
  32.2 1.9 %collective-permute-start.15 = (bf16[1,192,768]{2,1,0:T(8,128)(2,1)S(1)}, bf16[1,192,768]{2,1,0:T(8,128)(2,1)S(1)}, u32[]{:S(2)}, u32[]{:S(2)}) collective-permute-start(bf16[1,192,768]{2,1,0:T(8,128)(2,1)S(1)} %bitcast.16), channel_id=1, source_target_pairs={{0,8},{8,0},{16,24},{24,16},{1,9},{9,1},{17,25},{25,17},{2,10},{10... | collective-permute-start | bytes 884744 | tf_op jit(solution)/shard_map/ppermute | solution.py:215
  32.2 2.3 %collective-permute-start.17 = (bf16[1,2,192,384]{3,2,1,0:T(8,128)(2,1)S(1)}, bf16[1,2,192,384]{3,2,1,0:T(8,128)(2,1)S(1)}, u32[]{:S(2)}, u32[]{:S(2)}) collective-permute-start(bf16[1,2,192,384]{3,2,1,0:T(8,128)(2,1)S(1)} %collective-permute-done.13.refs_15_), channel_id=1, source_target_pairs={{0,8},{8,0},{16,24},{24,16},{1,9},{9,1},{17,25},{25,17},{2,10},{10... | collective-permute-start | bytes 884744 | tf_op jit(solution)/shard_map/ppermute | solution.py:215

commit v9 on v8

--- a/solution.py
+++ b/solution.py
@@ -110,7 +110,6 @@
     half_width = held.shape[2] // 2
     chips = fsdp // 2
     me = lax.axis_index("fsdp")
-    cut = lax.axis_index("tile") % 2
     chip, core = me // 2, me % 2
 
     def at(weight, owner, side):
@@ -123,11 +122,10 @@
     def own(weight, piece, mate):
         return [(piece, at(weight, me, None)), (mate, at(weight, 2 * chip + 1 - core, None))]
 
-    def others(weight, near, far, side=None):
+    def others(weight, near, far, columns=None):
         copies = []
         for j in range(1, chips):
             source = 2 * lax.rem(chip - j + chips, chips)
-            columns = None if side is None else (cut if side == 0 else 1 - cut)
             copies.append((near(j - 1), at(weight, source + core, columns)))
             copies.append((far(j - 1), at(weight, source + 1 - core, columns)))
         return copies
@@ -138,23 +136,27 @@
 def attend_kernel(fsdp, block, *refs):
     count, sums, gain, tiles = refs[:4]
     pieces, mates = refs[4:8], refs[8:12]
-    near, far = refs[12:16], refs[16:20]
-    out, held, pooled, sem = refs[20:]
+    near, far = refs[12:15], refs[15:18]
+    out, held, pooled, sem = refs[18:]
     device = lax.axis_index("tile")
+    cut = device % 2
     own, others = place_rows(fsdp, pieces[0].shape[0], held)
+
+    def from_others(weight, piece, part, columns):
+        return others(
+            weight, lambda j: near[piece].at[j, part], lambda j: far[piece].at[j, part], columns
+        )
+
     copies, ends = [], []
     for weight in range(4):
         copies += own(weight, pieces[weight], mates[weight])
-        if weight < 2:
-            copies += others(weight, lambda j: near[weight].at[j], lambda j: far[weight].at[j])
+        if weight == 0:
+            copies += from_others(0, 0, 0, 0) + from_others(0, 0, 1, 1)
+        elif weight == 1:
+            copies += others(1, lambda j: near[1].at[j], lambda j: far[1].at[j])
         else:
-            for side in range(2):
-                copies += others(
-                    weight,
-                    lambda j: near[2 + side].at[j, weight - 2],
-                    lambda j: far[2 + side].at[j, weight - 2],
-                    side,
-                )
+            copies += from_others(weight, 0, weight, cut)
+            copies += from_others(weight, 2, weight - 2, 1 - cut)
         ends.append(len(copies))
     started = collect(copies, sem)
 
@@ -220,11 +222,14 @@
     return lax.ppermute(array, axis, [(i, (i + 2 * step) % count) for i in range(count)])
 
 
-def halves_kernel(w_value, w_out, halves, sem):
+def stack_kernel(w_query, w_value, w_out, stack, sem):
     cut = lax.axis_index("tile") % 2
-    width = halves.shape[2]
-    columns = pl.ds(pl.multiple_of(cut * width, width), width)
-    copies = [(w.at[:, columns], halves.at[n]) for n, w in enumerate((w_value, w_out))]
+    width = stack.shape[2]
+    halves = ((w_query, 0), (w_query, 1), (w_value, cut), (w_out, cut))
+    copies = []
+    for n, (w, half) in enumerate(halves):
+        columns = pl.ds(pl.multiple_of(half * width, width), width)
+        copies.append((w.at[:, columns], stack.at[n]))
     for copy in collect(copies, sem):
         copy.wait()
 
@@ -271,55 +276,53 @@
     block = regions // REGIONS_PER_KEY
 
     shard = w_query.shape[0]
-    near_query = from_chips(w_query)
+    stack = pl.pallas_call(
+        stack_kernel,
+        out_shape=jax.ShapeDtypeStruct((4, shard, width // 2), BF16),
+        in_specs=[hbm()] * 3,
+        out_specs=vmem(),
+        scratch_shapes=[pltpu.SemaphoreType.DMA((4,))],
+        name="stack",
+    )(w_query, w_value, w_out)
+    near_stack = from_chips(stack)
+    near_key = from_chips(w_key)
     slots = jnp.where(nbr_mask[0].T > 0, nbr_tiles[0].T + 1, 0)
     slots = jnp.pad(slots, ((0, 8 - NB), (0, -regions % 128)))
     mate = swap(slots, "tile", 1)
     inner = [(i, i + 1) for i in range(1, tile_devices - 1, 2)]
-    ends = [(0, 0), (tile_devices - 1, tile_devices - 1)]
-    other = lax.ppermute(slots, "tile", inner + [(b, a) for a, b in inner] + ends)
-    halves = pl.pallas_call(
-        halves_kernel,
-        out_shape=jax.ShapeDtypeStruct((2, shard, width // 2), BF16),
-        in_specs=[hbm()] * 2,
-        out_specs=vmem(),
-        scratch_shapes=[pltpu.SemaphoreType.DMA((2,))],
-        name="halves",
-    )(behind(w_value, slots), w_out)
-    near_halves = from_chips(behind(halves, mate, other))
+    other = lax.ppermute(slots, "tile", inner + [(b, a) for a, b in inner])
+    mates = [swap(behind(w, slots), "fsdp", 1) for w in (w_query, w_key)]
     mine = local_call(
         functools.partial(pool_kernel, regions),
         jax.ShapeDtypeStruct((3 * block, width), F32),
         [vmem()] * 4,
         "pool",
-    )(slots, mate, other, behind(own_tiles, halves))
-    near_key = from_chips(behind(w_key, mine))
+    )(slots, mate, other, behind(own_tiles, *mates))
     pair = local_call(
         pair_kernel,
         jax.ShapeDtypeStruct((6 * block, width), BF16),
         [vmem()] * 2,
         "pair",
-    )(mine, behind(swap(mine, "tile", 1), near_query))
-    near_halves = behind(near_halves, pair)
-    other_halves = swap(near_halves, "tile", 1)
-    far_halves = swap(near_halves, "fsdp", 1)
+    )(mine, swap(mine, "tile", 1))
+    near_stack = behind(near_stack, pair)
+    other_halves = swap(near_stack[:, 2:], "tile", 1)
     sums = gather_pairs(pair, "tile")
-    near_query = behind(near_query, sums)
+    far_stack = swap(behind(near_stack, sums), "fsdp", 1)
+    mates += [swap(behind(w, sums), "fsdp", 1) for w in (w_value, w_out)]
+    near_key = behind(near_key, sums)
+    other_halves = behind(other_halves, sums)
     weights = (w_query, w_key, w_value, w_out)
-    mates = [swap(behind(w, sums), "fsdp", 1) for w in weights]
-    far_query = swap(near_query, "fsdp", 1)
-    near_key = behind(near_key, sums)
-    near = (near_query, near_key, near_halves, other_halves)
-    far = (far_query, swap(near_key, "fsdp", 1), far_halves, swap(behind(other_halves, sums), "fsdp", 1))
+    near = (near_stack, near_key, other_halves)
+    far = (far_stack, swap(near_key, "fsdp", 1), swap(other_halves, "fsdp", 1))
     attended = local_call(
         functools.partial(attend_kernel, fsdp, block),
         jax.ShapeDtypeStruct((rows, width), BF16),
-        [smem()] + [vmem()] * 3 + [anywhere()] * 16,
+        [smem()] + [vmem()] * 3 + [anywhere()] * 14,
         "attend",
         [
             pltpu.VMEM((4, width, width), BF16),
             pltpu.VMEM(((tile_devices + 2) * block, width), F32),
-            pltpu.SemaphoreType.DMA((6 * fsdp,)),
+            pltpu.SemaphoreType.DMA((7 * fsdp,)),
         ],
     )(tile_count, sums, key_gain[None, :], own_tiles, *weights, *mates, *near, *far)
     return attended[None]

time: 39 us -> 35.4 us (0.908)
  waiting for transfers between devices: 11.3 us -> 9.03 us
  starting transfers between devices: 19.4 us -> 18.4 us
  other arithmetic: 0.72 us -> 0.02 us
    ppermute x14 -> x13, waiting for transfers between devices: 9.79 us -> 7.6 us  [swap(): return lax.ppermute(array, axis, [(i, i ^ offset) for i in range(count)])]
    ppermute x3 -> x2, starting transfers between devices: 5.06 us -> 3.55 us  [chip_shift(): lax.ppermute(array, axis, [(i, (i + 2 * step) % count) for i in range(cou...]
    select_n x1, other arithmetic: 0.7 us -> 0.01 us  [body(): slots = jnp.where(nbr_mask[0].T > 0, nbr_tiles[0].T + 1, 0)]
    ppermute x14 -> x13, starting transfers between devices: 13.5 us -> 14.2 us  [swap(): return lax.ppermute(array, axis, [(i, i ^ offset) for i in range(count)])]
    ppermute x3 -> x2, waiting for transfers between devices: 1.51 us -> 1.42 us  [chip_shift(): lax.ppermute(array, axis, [(i, (i + 2 * step) % count) for i in range(cou...]
  transfers between devices with their start and end apart: 18 -> 16, of which waited for: 8 -> 7; matrix products, arithmetic and copies ran while one was open for 2% -> 0% of each run, Pallas kernels for 6% -> 2%
where the time goes in v9:
time: 35.4 us; the launch traced here: 35.3 us
  starting transfers between devices  18.4 us (52%)
  waiting for transfers between devices  9.03 us (26%)
  Pallas kernels  6.97 us (20%)
  between operations  0.81 us (2%)
    ppermute x13, starting transfers between devices, swap(): return lax.ppermute(array, axis, [(i, i ^ offset) for i in range(count)])  14.2 us
    ppermute x13, waiting for transfers between devices, swap(): return lax.ppermute(array, axis, [(i, i ^ offset) for i in range(count)])  7.6 us
    pallas_call x1, Pallas kernels, body(): local_call(functools.partial(attend_kernel, fsdp, block), jax.ShapeDtypeS...  4.32 us
    ppermute x2, starting transfers between devices, chip_shift(): lax.ppermute(array, axis, [(i, (i + 2 * step) % count) for i in range(cou...  3.55 us
    pallas_call x1, Pallas kernels, body(): pl.pallas_call(stack_kernel, out_shape=jax.ShapeDtypeStruct((4, shard, wi...  2.07 us
    ppermute x2, waiting for transfers between devices, chip_shift(): lax.ppermute(array, axis, [(i, (i + 2 * step) % count) for i in range(cou...  1.42 us
  transfers between devices with their start and end apart: 16, of which 7 were waited for; matrix products, arithmetic and copies ran while one was open for 0% of the time, Pallas kernels for 2%

profile of v9, /device:TPU:0, one launch (start us, length us, event | category | flops | bytes accessed | tf_op | source)
XLA Modules:
  0.0 35.3 jit_solution(10604947789475852005)
XLA Ops:
  0.0 0.0 copy-start.1
  0.0 0.0 copy-start.7
  0.0 0.0 copy-start.6
  0.0 0.0 copy-start.4
  0.0 0.0 copy-start
  0.0 2.1 %stack.9 = bf16[4,192,384]{2,1,0:T(8,128)(2,1)} custom-call(bf16[192,768]{1,0:T(8,128)(2,1)} %refs_4_.1, bf16[192,768]{1,0:T(8,128)(2,1)} %refs_6_.1, bf16[192,768]{1,0:T(8,128)(2,1)} %refs_7_.1), custom_call_target="tpu_custom_call" | custom-call | tf_op jit(solution)/shard_map/stack/pallas_call | solution.py:279
  2.1 3.0 %collective-permute-start.10 = (bf16[4,192,384]{2,1,0:T(8,128)(2,1)}, bf16[4,192,384]{2,1,0:T(8,128)(2,1)S(1)}, u32[]{:S(2)}, u32[]{:S(2)}) collective-permute-start(bf16[4,192,384]{2,1,0:T(8,128)(2,1)} %stack.9), channel_id=1, source_target_pairs={{0,16},{8,24},{16,0},{24,8},{1,17},{9,25},{17,1},{25,9},{2,18},{10... | collective-permute-start | bytes 1769480 | tf_op jit(solution)/shard_map/ppermute | solution.py:222
  5.1 0.0 copy-done.7
  5.1 0.0 copy-done.6
  5.2 0.0 copy-done.1
  5.2 0.1 collective-permute-start.2
  5.3 0.0 copy-done.4
  5.3 0.5 %collective-permute-start.3 = (bf16[192,768]{1,0:T(8,128)(2,1)S(1)}, bf16[192,768]{1,0:T(8,128)(2,1)S(1)}, u32[]{:S(2)}, u32[]{:S(2)}) collective-permute-start(bf16[192,768]{1,0:T(8,128)(2,1)S(1)} %copy-done.4), channel_id=1, source_target_pairs={{0,8},{8,0},{16,24},{24,16},{1,9},{9,1},{17,25},{25,17},{2,10},{10... | collective-permute-start | bytes 884744 | tf_op jit(solution)/shard_map/ppermute | solution.py:217
  5.8 0.6 %collective-permute-start.1 = (s32[8,128]{1,0:T(8,128)S(1)}, s32[8,128]{1,0:T(8,128)S(1)}, u32[]{:S(2)}, u32[]{:S(2)}) collective-permute-start(s32[8,128]{1,0:T(8,128)S(1)} %pad.4.here), channel_id=1, source_target_pairs={{1,2},{3,4},{5,6},{2,1},{4,3},{6,5},{9,10},{11,12},{13,14},{10,9},... | collective-permute-start | bytes 12296 | tf_op jit(solution)/shard_map/ppermute | solution.py:293
  6.4 4.4 %collective-permute-start = (s32[8,128]{1,0:T(8,128)S(1)}, s32[8,128]{1,0:T(8,128)S(1)}, u32[]{:S(2)}, u32[]{:S(2)}) collective-permute-start(s32[8,128]{1,0:T(8,128)S(1)} %pad.4.here), channel_id=1, source_target_pairs={{0,1},{1,0},{2,3},{3,2},{4,5},{5,4},{6,7},{7,6},{8,9},{9,8},{10,11... | collective-permute-start | bytes 12296 | tf_op jit(solution)/shard_map/ppermute | solution.py:217
  10.8 0.0 collective-permute-done.2.refs_8_
  10.8 0.0 collective-permute-done.3.refs_9_
  10.8 0.0 collective-permute-done.1.other
  10.8 1.6 %collective-permute-done.mate = s32[8,128]{1,0:T(8,128)S(1)} collective-permute-done((s32[8,128]{1,0:T(8,128)S(1)}, s32[8,128]{1,0:T(8,128)S(1)}, u32[]{:S(2)}, u32[]{:S(2)}) %collective-permute-start) | collective-permute-done | bytes 4128 | tf_op jit(solution)/shard_map/ppermute | solution.py:217
  12.3 0.0 copy-done
  12.4 0.6 %pool.1.mine = f32[24,768]{1,0:T(8,128)S(1)} custom-call(s32[8,128]{1,0:T(8,128)S(1)} %pad.4.here, s32[8,128]{1,0:T(8,128)S(1)} %collective-permute-done.mate, s32[8,128]{1,0:T(8,128)S(1)} %collective-permute-done.1.other, bf16[256,768]{1,0:T(8,128)(2,1)S(1)} %bitcast.8), custom_call_target="tpu_custom_call" | custom-call | flops 1000 | bytes 1000 | tf_op jit(solution)/shard_map/pool/pallas_call | solution.py:295
  12.9 2.1 %collective-permute-start.4 = (f32[24,768]{1,0:T(8,128)S(1)}, f32[24,768]{1,0:T(8,128)S(1)}, u32[]{:S(2)}, u32[]{:S(2)}) collective-permute-start(f32[24,768]{1,0:T(8,128)S(1)} %pool.1.mine), channel_id=1, source_target_pairs={{0,1},{1,0},{2,3},{3,2},{4,5},{5,4},{6,7},{7,6},{8,9},{9,8},{10,11... | collective-permute-start | bytes 221192 | tf_op jit(solution)/shard_map/ppermute | solution.py:217
  15.0 2.3 %collective-permute-done.4.theirs = f32[24,768]{1,0:T(8,128)S(1)} collective-permute-done((f32[24,768]{1,0:T(8,128)S(1)}, f32[24,768]{1,0:T(8,128)S(1)}, u32[]{:S(2)}, u32[]{:S(2)}) %collective-permute-start.4) | collective-permute-done | bytes 73760 | tf_op jit(solution)/shard_map/ppermute | solution.py:217
  17.4 4.0 %collective-permute-start.7 = (bf16[48,768]{1,0:T(8,128)(2,1)S(1)}, bf16[48,768]{1,0:T(8,128)(2,1)S(1)}, u32[]{:S(2)}, u32[]{:S(2)}) collective-permute-start(bf16[48,768]{1,0:T(8,128)(2,1)S(1)} %pair.1), channel_id=1, source_target_pairs={{0,6},{1,7},{2,4},{3,5},{4,2},{5,3},{6,0},{7,1},{8,14},{9,15},{10,... | collective-permute-start | bytes 221192 | tf_op jit(solution)/shard_map/ppermute | solution.py:217
  21.4 0.0 collective-permute-start.6
  21.4 0.6 %collective-permute-start.5 = (bf16[48,768]{1,0:T(8,128)(2,1)S(1)}, bf16[48,768]{1,0:T(8,128)(2,1)S(1)}, u32[]{:S(2)}, u32[]{:S(2)}) collective-permute-start(bf16[48,768]{1,0:T(8,128)(2,1)S(1)} %pair.1), channel_id=1, source_target_pairs={{0,2},{1,3},{2,0},{3,1},{4,6},{5,7},{6,4},{7,5},{8,10},{9,11},{10,... | collective-permute-start | bytes 221192 | tf_op jit(solution)/shard_map/ppermute | solution.py:217
  22.0 0.5 %collective-permute-start.11 = (bf16[192,768]{1,0:T(8,128)(2,1)S(1)}, bf16[192,768]{1,0:T(8,128)(2,1)S(1)}, u32[]{:S(2)}, u32[]{:S(2)}) collective-permute-start(bf16[192,768]{1,0:T(8,128)(2,1)S(1)} %copy-done.4), channel_id=1, source_target_pairs={{0,16},{8,24},{16,0},{24,8},{1,17},{9,25},{17,1},{25,9},{2,18},{10... | collective-permute-start | bytes 884744 | tf_op jit(solution)/shard_map/ppermute | solution.py:222
  22.5 0.0 collective-permute-done.10
  22.5 0.0 copy-start.5
  22.6 0.0 copy-start.2
  22.6 0.0 copy-start.3
  22.6 1.9 %collective-permute-start.12 = (bf16[1,2,192,384]{3,2,1,0:T(8,128)(2,1)S(1)}, bf16[1,2,192,384]{3,2,1,0:T(8,128)(2,1)S(1)}, u32[]{:S(2)}, u32[]{:S(2)}) collective-permute-start(bf16[1,2,192,384]{3,2,1,0:T(8,128)(2,1)S(1)} %slice.3), channel_id=1, source_target_pairs={{0,1},{1,0},{2,3},{3,2},{4,5},{5,4},{6,7},{7,6},{8,9},{9,8},{10,11... | collective-permute-start | bytes 884744 | tf_op jit(solution)/shard_map/ppermute | solution.py:217
  24.5 0.0 collective-permute-done.7
  24.5 2.2 %collective-permute-done.6 = bf16[48,768]{1,0:T(8,128)(2,1)S(1)} collective-permute-done((bf16[48,768]{1,0:T(8,128)(2,1)S(1)}, bf16[48,768]{1,0:T(8,128)(2,1)S(1)}, u32[]{:S(2)}, u32[]{:S(2)}) %collective-permute-start.6) | collective-permute-done | bytes 73760 | tf_op jit(solution)/shard_map/ppermute | solution.py:217
  26.6 0.0 collective-permute-done.5
  26.7 0.1 collective-permute-start.13
  26.7 0.0 copy-done.2
  26.8 0.5 %collective-permute-start.8 = (bf16[192,768]{1,0:T(8,128)(2,1)S(1)}, bf16[192,768]{1,0:T(8,128)(2,1)S(1)}, u32[]{:S(2)}, u32[]{:S(2)}) collective-permute-start(bf16[192,768]{1,0:T(8,128)(2,1)S(1)} %copy-done.2), channel_id=1, source_target_pairs={{0,8},{8,0},{16,24},{24,16},{1,9},{9,1},{17,25},{25,17},{2,10},{10... | collective-permute-start | bytes 884744 | tf_op jit(solution)/shard_map/ppermute | solution.py:217
  27.2 0.0 copy-done.3
  27.2 0.1 collective-permute-start.9
  27.3 1.4 %collective-permute-done.11 = bf16[192,768]{1,0:T(8,128)(2,1)S(1)} collective-permute-done((bf16[192,768]{1,0:T(8,128)(2,1)S(1)}, bf16[192,768]{1,0:T(8,128)(2,1)S(1)}, u32[]{:S(2)}, u32[]{:S(2)}) %collective-permute-start.11) | collective-permute-done | bytes 294944 | tf_op jit(solution)/shard_map/ppermute | solution.py:222
  28.7 0.0 collective-permute-start.14
  28.8 0.6 %collective-permute-done.12.refs_14_ = bf16[1,2,192,384]{3,2,1,0:T(8,128)(2,1)S(1)} collective-permute-done((bf16[1,2,192,384]{3,2,1,0:T(8,128)(2,1)S(1)}, bf16[1,2,192,384]{3,2,1,0:T(8,128)(2,1)S(1)}, u32[]{:S(2)}, u32[]{:S(2)}) %collective-permute-start.12) | collective-permute-done | bytes 294944 | tf_op jit(solution)/shard_map/ppermute | solution.py:217
  29.4 0.0 collective-permute-start.15
  30.0 0.0 copy-done.5
  30.1 0.0 collective-permute-done.8.refs_10_
  30.1 0.0 collective-permute-done.9.refs_11_
  30.1 0.2 collective-permute-done.14.refs_16_
  30.3 0.6 %collective-permute-done.15.refs_17_ = bf16[1,2,192,384]{3,2,1,0:T(8,128)(2,1)S(1)} collective-permute-done((bf16[1,2,192,384]{3,2,1,0:T(8,128)(2,1)S(1)}, bf16[1,2,192,384]{3,2,1,0:T(8,128)(2,1)S(1)}, u32[]{:S(2)}, u32[]{:S(2)}) %collective-permute-start.15) | collective-permute-done | bytes 294944 | tf_op jit(solution)/shard_map/ppermute | solution.py:217
  31.0 0.0 collective-permute-done.13.refs_15_
  31.0 4.3 %attend.1 = bf16[256,768]{1,0:T(8,128)(2,1)} custom-call(s32[1]{0:T(128)S(6)} %copy.10.refs_0_, bf16[192,768]{1,0:T(8,128)(2,1)S(1)} %pad_maximum_fusion.refs_1_, f32[1,768]{1,0:T(1,128)S(1)} %broadcast_in_dim.8.refs_2_, bf16[256,768]{1,0:T(8,128)(2,1)S(1)} %bitcast.9, bf16[192,768]{1,0:T(8,128)(2,1)S(1)} %copy-done.1, bf16[192,768]{1,0:T(8,128)(2,1)S(1)} %copy-done.4, ...), custom_call_target="tpu_custom_call" | custom-call | flops 1000 | bytes 1000 | tf_op jit(solution)/shard_map/attend/pallas_call | solution.py:317
  (6 shorter events, 0.1 us)
Async XLA Ops:
  0.0 5.2 %copy-start.1 = (bf16[192,768]{1,0:T(8,128)(2,1)S(1)}, bf16[192,768]{1,0:T(8,128)(2,1)}, u32[]{:S(2)}) copy-start(bf16[192,768]{1,0:T(8,128)(2,1)} %refs_4_.1) | copy-start | bytes 884740
  0.0 5.1 %copy-start.7 = (s32[1,64,4]{1,2,0:T(4,128)S(1)}, s32[1,64,4]{1,2,0:T(4,128)}, u32[]{:S(2)}) copy-start(s32[1,64,4]{1,2,0:T(4,128)} %param.11) | copy-start | bytes 3076
  0.0 5.1 %copy-start.6 = (s32[1,64,4]{1,2,0:T(4,128)S(1)}, s32[1,64,4]{1,2,0:T(4,128)}, u32[]{:S(2)}) copy-start(s32[1,64,4]{1,2,0:T(4,128)} %param.10) | copy-start | bytes 3076
  0.0 5.2 %copy-start.4 = (bf16[192,768]{1,0:T(8,128)(2,1)S(1)}, bf16[192,768]{1,0:T(8,128)(2,1)}, u32[]{:S(2)}) copy-start(bf16[192,768]{1,0:T(8,128)(2,1)} %refs_5_.1) | copy-start | bytes 884740
  0.0 12.3 %copy-start = (bf16[1,256,768]{2,1,0:T(8,128)(2,1)S(1)}, bf16[1,256,768]{2,1,0:T(8,128)(2,1)}, u32[]{:S(2)}) copy-start(bf16[1,256,768]{2,1,0:T(8,128)(2,1)} %param.9) | copy-start | bytes 1179652
  2.1 20.4 %collective-permute-start.10 = (bf16[4,192,384]{2,1,0:T(8,128)(2,1)}, bf16[4,192,384]{2,1,0:T(8,128)(2,1)S(1)}, u32[]{:S(2)}, u32[]{:S(2)}) collective-permute-start(bf16[4,192,384]{2,1,0:T(8,128)(2,1)} %stack.9), channel_id=1, source_target_pairs={{0,16},{8,24},{16,0},{24,8},{1,17},{9,25},{17,1},{25,9},{2,18},{10... | collective-permute-start | bytes 1769480 | tf_op jit(solution)/shard_map/ppermute | solution.py:222
  5.2 5.6 %collective-permute-start.2 = (bf16[192,768]{1,0:T(8,128)(2,1)S(1)}, bf16[192,768]{1,0:T(8,128)(2,1)S(1)}, u32[]{:S(2)}, u32[]{:S(2)}) collective-permute-start(bf16[192,768]{1,0:T(8,128)(2,1)S(1)} %copy-done.1), channel_id=1, source_target_pairs={{0,8},{8,0},{16,24},{24,16},{1,9},{9,1},{17,25},{25,17},{2,10},{10... | collective-permute-start | bytes 884744 | tf_op jit(solution)/shard_map/ppermute | solution.py:217
  5.3 5.5 %collective-permute-start.3 = (bf16[192,768]{1,0:T(8,128)(2,1)S(1)}, bf16[192,768]{1,0:T(8,128)(2,1)S(1)}, u32[]{:S(2)}, u32[]{:S(2)}) collective-permute-start(bf16[192,768]{1,0:T(8,128)(2,1)S(1)} %copy-done.4), channel_id=1, source_target_pairs={{0,8},{8,0},{16,24},{24,16},{1,9},{9,1},{17,25},{25,17},{2,10},{10... | collective-permute-start | bytes 884744 | tf_op jit(solution)/shard_map/ppermute | solution.py:217
  5.8 5.0 %collective-permute-start.1 = (s32[8,128]{1,0:T(8,128)S(1)}, s32[8,128]{1,0:T(8,128)S(1)}, u32[]{:S(2)}, u32[]{:S(2)}) collective-permute-start(s32[8,128]{1,0:T(8,128)S(1)} %pad.4.here), channel_id=1, source_target_pairs={{1,2},{3,4},{5,6},{2,1},{4,3},{6,5},{9,10},{11,12},{13,14},{10,9},... | collective-permute-start | bytes 12296 | tf_op jit(solution)/shard_map/ppermute | solution.py:293
  6.4 5.9 %collective-permute-start = (s32[8,128]{1,0:T(8,128)S(1)}, s32[8,128]{1,0:T(8,128)S(1)}, u32[]{:S(2)}, u32[]{:S(2)}) collective-permute-start(s32[8,128]{1,0:T(8,128)S(1)} %pad.4.here), channel_id=1, source_target_pairs={{0,1},{1,0},{2,3},{3,2},{4,5},{5,4},{6,7},{7,6},{8,9},{9,8},{10,11... | collective-permute-start | bytes 12296 | tf_op jit(solution)/shard_map/ppermute | solution.py:217
  12.9 4.4 %collective-permute-start.4 = (f32[24,768]{1,0:T(8,128)S(1)}, f32[24,768]{1,0:T(8,128)S(1)}, u32[]{:S(2)}, u32[]{:S(2)}) collective-permute-start(f32[24,768]{1,0:T(8,128)S(1)} %pool.1.mine), channel_id=1, source_target_pairs={{0,1},{1,0},{2,3},{3,2},{4,5},{5,4},{6,7},{7,6},{8,9},{9,8},{10,11... | collective-permute-start | bytes 221192 | tf_op jit(solution)/shard_map/ppermute | solution.py:217
  17.4 7.1 %collective-permute-start.7 = (bf16[48,768]{1,0:T(8,128)(2,1)S(1)}, bf16[48,768]{1,0:T(8,128)(2,1)S(1)}, u32[]{:S(2)}, u32[]{:S(2)}) collective-permute-start(bf16[48,768]{1,0:T(8,128)(2,1)S(1)} %pair.1), channel_id=1, source_target_pairs={{0,6},{1,7},{2,4},{3,5},{4,2},{5,3},{6,0},{7,1},{8,14},{9,15},{10,... | collective-permute-start | bytes 221192 | tf_op jit(solution)/shard_map/ppermute | solution.py:217
  21.4 5.3 %collective-permute-start.6 = (bf16[48,768]{1,0:T(8,128)(2,1)S(1)}, bf16[48,768]{1,0:T(8,128)(2,1)S(1)}, u32[]{:S(2)}, u32[]{:S(2)}) collective-permute-start(bf16[48,768]{1,0:T(8,128)(2,1)S(1)} %pair.1), channel_id=1, source_target_pairs={{0,4},{1,5},{2,6},{3,7},{4,0},{5,1},{6,2},{7,3},{8,12},{9,13},{10,... | collective-permute-start | bytes 221192 | tf_op jit(solution)/shard_map/ppermute | solution.py:217
  21.4 5.3 %collective-permute-start.5 = (bf16[48,768]{1,0:T(8,128)(2,1)S(1)}, bf16[48,768]{1,0:T(8,128)(2,1)S(1)}, u32[]{:S(2)}, u32[]{:S(2)}) collective-permute-start(bf16[48,768]{1,0:T(8,128)(2,1)S(1)} %pair.1), channel_id=1, source_target_pairs={{0,2},{1,3},{2,0},{3,1},{4,6},{5,7},{6,4},{7,5},{8,10},{9,11},{10,... | collective-permute-start | bytes 221192 | tf_op jit(solution)/shard_map/ppermute | solution.py:217
  22.0 6.7 %collective-permute-start.11 = (bf16[192,768]{1,0:T(8,128)(2,1)S(1)}, bf16[192,768]{1,0:T(8,128)(2,1)S(1)}, u32[]{:S(2)}, u32[]{:S(2)}) collective-permute-start(bf16[192,768]{1,0:T(8,128)(2,1)S(1)} %copy-done.4), channel_id=1, source_target_pairs={{0,16},{8,24},{16,0},{24,8},{1,17},{9,25},{17,1},{25,9},{2,18},{10... | collective-permute-start | bytes 884744 | tf_op jit(solution)/shard_map/ppermute | solution.py:222
  22.5 7.5 %copy-start.5 = (f32[768]{0:T(1024)S(1)}, f32[768]{0:T(1024)}, u32[]{:S(2)}) copy-start(f32[768]{0:T(1024)} %param.17) | copy-start | bytes 9220
  22.6 4.2 %copy-start.2 = (bf16[192,768]{1,0:T(8,128)(2,1)S(1)}, bf16[192,768]{1,0:T(8,128)(2,1)}, u32[]{:S(2)}) copy-start(bf16[192,768]{1,0:T(8,128)(2,1)} %refs_6_.1) | copy-start | bytes 884740
  22.6 4.7 %copy-start.3 = (bf16[192,768]{1,0:T(8,128)(2,1)S(1)}, bf16[192,768]{1,0:T(8,128)(2,1)}, u32[]{:S(2)}) copy-start(bf16[192,768]{1,0:T(8,128)(2,1)} %refs_7_.1) | copy-start | bytes 884740
  22.6 6.8 %collective-permute-start.12 = (bf16[1,2,192,384]{3,2,1,0:T(8,128)(2,1)S(1)}, bf16[1,2,192,384]{3,2,1,0:T(8,128)(2,1)S(1)}, u32[]{:S(2)}, u32[]{:S(2)}) collective-permute-start(bf16[1,2,192,384]{3,2,1,0:T(8,128)(2,1)S(1)} %slice.3), channel_id=1, source_target_pairs={{0,1},{1,0},{2,3},{3,2},{4,5},{5,4},{6,7},{7,6},{8,9},{9,8},{10,11... | collective-permute-start | bytes 884744 | tf_op jit(solution)/shard_map/ppermute | solution.py:217
  26.7 4.3 %collective-permute-start.13 = (bf16[1,4,192,384]{3,2,1,0:T(8,128)(2,1)S(1)}, bf16[1,4,192,384]{3,2,1,0:T(8,128)(2,1)S(1)}, u32[]{:S(2)}, u32[]{:S(2)}) collective-permute-start(bf16[1,4,192,384]{3,2,1,0:T(8,128)(2,1)S(1)} %bitcast.11), channel_id=1, source_target_pairs={{0,8},{8,0},{16,24},{24,16},{1,9},{9,1},{17,25},{25,17},{2,10},{10... | collective-permute-start | bytes 1769480 | tf_op jit(solution)/shard_map/ppermute | solution.py:217
  26.8 3.3 %collective-permute-start.8 = (bf16[192,768]{1,0:T(8,128)(2,1)S(1)}, bf16[192,768]{1,0:T(8,128)(2,1)S(1)}, u32[]{:S(2)}, u32[]{:S(2)}) collective-permute-start(bf16[192,768]{1,0:T(8,128)(2,1)S(1)} %copy-done.2), channel_id=1, source_target_pairs={{0,8},{8,0},{16,24},{24,16},{1,9},{9,1},{17,25},{25,17},{2,10},{10... | collective-permute-start | bytes 884744 | tf_op jit(solution)/shard_map/ppermute | solution.py:217
  27.2 2.8 %collective-permute-start.9 = (bf16[192,768]{1,0:T(8,128)(2,1)S(1)}, bf16[192,768]{1,0:T(8,128)(2,1)S(1)}, u32[]{:S(2)}, u32[]{:S(2)}) collective-permute-start(bf16[192,768]{1,0:T(8,128)(2,1)S(1)} %copy-done.3), channel_id=1, source_target_pairs={{0,8},{8,0},{16,24},{24,16},{1,9},{9,1},{17,25},{25,17},{2,10},{10... | collective-permute-start | bytes 884744 | tf_op jit(solution)/shard_map/ppermute | solution.py:217
  28.7 1.6 %collective-permute-start.14 = (bf16[1,192,768]{2,1,0:T(8,128)(2,1)S(1)}, bf16[1,192,768]{2,1,0:T(8,128)(2,1)S(1)}, u32[]{:S(2)}, u32[]{:S(2)}) collective-permute-start(bf16[1,192,768]{2,1,0:T(8,128)(2,1)S(1)} %bitcast.13), channel_id=1, source_target_pairs={{0,8},{8,0},{16,24},{24,16},{1,9},{9,1},{17,25},{25,17},{2,10},{10... | collective-permute-start | bytes 884744 | tf_op jit(solution)/shard_map/ppermute | solution.py:217
  29.4 1.6 %collective-permute-start.15 = (bf16[1,2,192,384]{3,2,1,0:T(8,128)(2,1)S(1)}, bf16[1,2,192,384]{3,2,1,0:T(8,128)(2,1)S(1)}, u32[]{:S(2)}, u32[]{:S(2)}) collective-permute-start(bf16[1,2,192,384]{3,2,1,0:T(8,128)(2,1)S(1)} %collective-permute-done.12.refs_14_), channel_id=1, source_target_pairs={{0,8},{8,0},{16,24},{24,16},{1,9},{9,1},{17,25},{25,17},{2,10},{10... | collective-permute-start | bytes 884744 | tf_op jit(solution)/shard_map/ppermute | solution.py:217

commit v10 on v9

--- a/solution.py
+++ b/solution.py
@@ -12,6 +12,7 @@
 REGIONS_PER_KEY = 8
 KEY_DILATION = 2
 LANE_GROUPS = 2
+STACK_ROWS = 48
 F32 = jnp.float32
 BF16 = jnp.bfloat16
 
@@ -229,7 +230,9 @@
     copies = []
     for n, (w, half) in enumerate(halves):
         columns = pl.ds(pl.multiple_of(half * width, width), width)
-        copies.append((w.at[:, columns], stack.at[n]))
+        for begin in range(0, w.shape[0], STACK_ROWS):
+            part = pl.ds(begin, STACK_ROWS)
+            copies.append((w.at[part, columns], stack.at[n, part]))
     for copy in collect(copies, sem):
         copy.wait()
 
@@ -281,7 +284,7 @@
         out_shape=jax.ShapeDtypeStruct((4, shard, width // 2), BF16),
         in_specs=[hbm()] * 3,
         out_specs=vmem(),
-        scratch_shapes=[pltpu.SemaphoreType.DMA((4,))],
+        scratch_shapes=[pltpu.SemaphoreType.DMA((4 * shard // STACK_ROWS,))],
         name="stack",
     )(w_query, w_value, w_out)
     near_stack = from_chips(stack)
@@ -289,7 +292,7 @@
     slots = jnp.where(nbr_mask[0].T > 0, nbr_tiles[0].T + 1, 0)
     slots = jnp.pad(slots, ((0, 8 - NB), (0, -regions % 128)))
     mate = swap(slots, "tile", 1)
-    inner = [(i, i + 1) for i in range(1, tile_devices - 1, 2)]
+    inner = [(i, (i + 1) % tile_devices) for i in range(1, tile_devices, 2)]
     other = lax.ppermute(slots, "tile", inner + [(b, a) for a, b in inner])
     mates = [swap(behind(w, slots), "fsdp", 1) for w in (w_query, w_key)]
     mine = local_call(

time: 35.4 us -> 36.8 us (1.040)
  waiting for transfers between devices: 9.03 us -> 14.8 us
  starting transfers between devices: 18.4 us -> 13.9 us
    ppermute x13, starting transfers between devices: 14.2 us -> 5.81 us  [swap(): return lax.ppermute(array, axis, [(i, i ^ offset) for i in range(count)])]
    ppermute x1, starting transfers between devices: 0.65 us -> 4.53 us  [body(): other = lax.ppermute(slots, 'tile', inner + [(b, a) for a, b in inner])]
    ppermute x13, waiting for transfers between devices: 7.6 us -> 10.4 us  [swap(): return lax.ppermute(array, axis, [(i, i ^ offset) for i in range(count)])]
    ppermute x1, waiting for transfers between devices: 0.01 us -> 1.76 us  [body(): other = lax.ppermute(slots, 'tile', inner + [(b, a) for a, b in inner])]
    ppermute x2, waiting for transfers between devices: 1.42 us -> 2.69 us  [chip_shift(): lax.ppermute(array, axis, [(i, (i + 2 * step) % count) for i in range(cou...]
  transfers between devices with their start and end apart: 16 -> 16, of which waited for: 7 -> 9; matrix products, arithmetic and copies ran while one was open for 0% -> 0% of each run, Pallas kernels for 2% -> 2%
where the time goes in v10:
time: 36.8 us; the launch traced here: 36.6 us
  waiting for transfers between devices  14.8 us (40%)
  starting transfers between devices  13.9 us (38%)
  Pallas kernels  6.98 us (19%)
  between operations  0.82 us (2%)
    ppermute x13, waiting for transfers between devices, swap(): return lax.ppermute(array, axis, [(i, i ^ offset) for i in range(count)])  10.4 us
    ppermute x13, starting transfers between devices, swap(): return lax.ppermute(array, axis, [(i, i ^ offset) for i in range(count)])  5.81 us
    ppermute x1, starting transfers between devices, body(): other = lax.ppermute(slots, 'tile', inner + [(b, a) for a, b in inner])  4.53 us
    pallas_call x1, Pallas kernels, body(): local_call(functools.partial(attend_kernel, fsdp, block), jax.ShapeDtypeS...  4.32 us
    ppermute x2, starting transfers between devices, chip_shift(): lax.ppermute(array, axis, [(i, (i + 2 * step) % count) for i in range(cou...  3.55 us
    ppermute x2, waiting for transfers between devices, chip_shift(): lax.ppermute(array, axis, [(i, (i + 2 * step) % count) for i in range(cou...  2.69 us
    pallas_call x1, Pallas kernels, body(): pl.pallas_call(stack_kernel, out_shape=jax.ShapeDtypeStruct((4, shard, wi...  2.09 us
    ppermute x1, waiting for transfers between devices, body(): other = lax.ppermute(slots, 'tile', inner + [(b, a) for a, b in inner])  1.76 us
  transfers between devices with their start and end apart: 16, of which 9 were waited for; matrix products, arithmetic and copies ran while one was open for 0% of the time, Pallas kernels for 2%

profile of v10, /device:TPU:0, one launch (start us, length us, event | category | flops | bytes accessed | tf_op | source)
XLA Modules:
  0.0 36.6 jit_solution(8385666212014277886)
XLA Ops:
  0.0 0.0 copy-start.1
  0.0 0.0 copy-start.7
  0.0 0.0 copy-start.6
  0.0 0.0 copy-start.4
  0.0 0.0 copy-start
  0.0 2.1 %stack.9 = bf16[4,192,384]{2,1,0:T(8,128)(2,1)} custom-call(bf16[192,768]{1,0:T(8,128)(2,1)} %refs_4_.1, bf16[192,768]{1,0:T(8,128)(2,1)} %refs_6_.1, bf16[192,768]{1,0:T(8,128)(2,1)} %refs_7_.1), custom_call_target="tpu_custom_call" | custom-call | tf_op jit(solution)/shard_map/stack/pallas_call | solution.py:282
  2.1 3.0 %collective-permute-start.10 = (bf16[4,192,384]{2,1,0:T(8,128)(2,1)}, bf16[4,192,384]{2,1,0:T(8,128)(2,1)S(1)}, u32[]{:S(2)}, u32[]{:S(2)}) collective-permute-start(bf16[4,192,384]{2,1,0:T(8,128)(2,1)} %stack.9), channel_id=1, source_target_pairs={{0,16},{8,24},{16,0},{24,8},{1,17},{9,25},{17,1},{25,9},{2,18},{10... | collective-permute-start | bytes 1769480 | tf_op jit(solution)/shard_map/ppermute | solution.py:223
  5.2 0.0 copy-done.7
  5.2 0.0 copy-done.6
  5.2 0.0 copy-done.1
  5.2 0.1 collective-permute-start.2
  5.3 0.0 copy-done.4
  5.3 0.5 %collective-permute-start.3 = (bf16[192,768]{1,0:T(8,128)(2,1)S(1)}, bf16[192,768]{1,0:T(8,128)(2,1)S(1)}, u32[]{:S(2)}, u32[]{:S(2)}) collective-permute-start(bf16[192,768]{1,0:T(8,128)(2,1)S(1)} %copy-done.4), channel_id=1, source_target_pairs={{0,8},{8,0},{16,24},{24,16},{1,9},{9,1},{17,25},{25,17},{2,10},{10... | collective-permute-start | bytes 884744 | tf_op jit(solution)/shard_map/ppermute | solution.py:218
  5.8 4.5 %collective-permute-start.1 = (s32[8,128]{1,0:T(8,128)S(1)}, s32[8,128]{1,0:T(8,128)S(1)}, u32[]{:S(2)}, u32[]{:S(2)}) collective-permute-start(s32[8,128]{1,0:T(8,128)S(1)} %pad.4.here), channel_id=1, source_target_pairs={{1,2},{3,4},{5,6},{7,0},{2,1},{4,3},{6,5},{0,7},{9,10},{11,12},{13... | collective-permute-start | bytes 12296 | tf_op jit(solution)/shard_map/ppermute | solution.py:296
  10.3 0.0 collective-permute-start
  10.3 0.0 collective-permute-done.2.refs_8_
  10.3 0.0 collective-permute-done.3.refs_9_
  10.3 1.8 %collective-permute-done.1.other = s32[8,128]{1,0:T(8,128)S(1)} collective-permute-done((s32[8,128]{1,0:T(8,128)S(1)}, s32[8,128]{1,0:T(8,128)S(1)}, u32[]{:S(2)}, u32[]{:S(2)}) %collective-permute-start.1) | collective-permute-done | bytes 4128 | tf_op jit(solution)/shard_map/ppermute | solution.py:296
  12.1 1.8 %collective-permute-done.mate = s32[8,128]{1,0:T(8,128)S(1)} collective-permute-done((s32[8,128]{1,0:T(8,128)S(1)}, s32[8,128]{1,0:T(8,128)S(1)}, u32[]{:S(2)}, u32[]{:S(2)}) %collective-permute-start) | collective-permute-done | bytes 4128 | tf_op jit(solution)/shard_map/ppermute | solution.py:218
  13.9 0.0 copy-done
  13.9 0.6 %pool.1.mine = f32[24,768]{1,0:T(8,128)S(1)} custom-call(s32[8,128]{1,0:T(8,128)S(1)} %pad.4.here, s32[8,128]{1,0:T(8,128)S(1)} %collective-permute-done.mate, s32[8,128]{1,0:T(8,128)S(1)} %collective-permute-done.1.other, bf16[256,768]{1,0:T(8,128)(2,1)S(1)} %bitcast.8), custom_call_target="tpu_custom_call" | custom-call | flops 1000 | bytes 1000 | tf_op jit(solution)/shard_map/pool/pallas_call | solution.py:298
  14.5 0.1 collective-permute-start.4
  14.6 4.3 %collective-permute-done.4.theirs = f32[24,768]{1,0:T(8,128)S(1)} collective-permute-done((f32[24,768]{1,0:T(8,128)S(1)}, f32[24,768]{1,0:T(8,128)S(1)}, u32[]{:S(2)}, u32[]{:S(2)}) %collective-permute-start.4) | collective-permute-done | bytes 73760 | tf_op jit(solution)/shard_map/ppermute | solution.py:218
  18.9 1.3 %collective-permute-start.7 = (bf16[48,768]{1,0:T(8,128)(2,1)S(1)}, bf16[48,768]{1,0:T(8,128)(2,1)S(1)}, u32[]{:S(2)}, u32[]{:S(2)}) collective-permute-start(bf16[48,768]{1,0:T(8,128)(2,1)S(1)} %pair.1), channel_id=1, source_target_pairs={{0,6},{1,7},{2,4},{3,5},{4,2},{5,3},{6,0},{7,1},{8,14},{9,15},{10,... | collective-permute-start | bytes 221192 | tf_op jit(solution)/shard_map/ppermute | solution.py:218
  20.2 0.0 collective-permute-start.6
  20.2 3.1 %collective-permute-start.5 = (bf16[48,768]{1,0:T(8,128)(2,1)S(1)}, bf16[48,768]{1,0:T(8,128)(2,1)S(1)}, u32[]{:S(2)}, u32[]{:S(2)}) collective-permute-start(bf16[48,768]{1,0:T(8,128)(2,1)S(1)} %pair.1), channel_id=1, source_target_pairs={{0,2},{1,3},{2,0},{3,1},{4,6},{5,7},{6,4},{7,5},{8,10},{9,11},{10,... | collective-permute-start | bytes 221192 | tf_op jit(solution)/shard_map/ppermute | solution.py:218
  23.4 0.5 %collective-permute-start.11 = (bf16[192,768]{1,0:T(8,128)(2,1)S(1)}, bf16[192,768]{1,0:T(8,128)(2,1)S(1)}, u32[]{:S(2)}, u32[]{:S(2)}) collective-permute-start(bf16[192,768]{1,0:T(8,128)(2,1)S(1)} %copy-done.4), channel_id=1, source_target_pairs={{0,16},{8,24},{16,0},{24,8},{1,17},{9,25},{17,1},{25,9},{2,18},{10... | collective-permute-start | bytes 884744 | tf_op jit(solution)/shard_map/ppermute | solution.py:223
  23.9 0.0 collective-permute-done.10
  23.9 0.0 copy-start.5
  23.9 0.0 copy-start.2
  23.9 0.0 copy-start.3
  23.9 0.1 collective-permute-start.12
  24.0 1.2 %collective-permute-done.7 = bf16[48,768]{1,0:T(8,128)(2,1)S(1)} collective-permute-done((bf16[48,768]{1,0:T(8,128)(2,1)S(1)}, bf16[48,768]{1,0:T(8,128)(2,1)S(1)}, u32[]{:S(2)}, u32[]{:S(2)}) %collective-permute-start.7) | collective-permute-done | bytes 73760 | tf_op jit(solution)/shard_map/ppermute | solution.py:218
  25.2 1.5 %collective-permute-done.6 = bf16[48,768]{1,0:T(8,128)(2,1)S(1)} collective-permute-done((bf16[48,768]{1,0:T(8,128)(2,1)S(1)}, bf16[48,768]{1,0:T(8,128)(2,1)S(1)}, u32[]{:S(2)}, u32[]{:S(2)}) %collective-permute-start.6) | collective-permute-done | bytes 73760 | tf_op jit(solution)/shard_map/ppermute | solution.py:218
  26.7 0.0 collective-permute-done.5
  26.7 0.1 collective-permute-start.13
  26.8 0.0 copy-done.2
  26.8 0.5 %collective-permute-start.8 = (bf16[192,768]{1,0:T(8,128)(2,1)S(1)}, bf16[192,768]{1,0:T(8,128)(2,1)S(1)}, u32[]{:S(2)}, u32[]{:S(2)}) collective-permute-start(bf16[192,768]{1,0:T(8,128)(2,1)S(1)} %copy-done.2), channel_id=1, source_target_pairs={{0,8},{8,0},{16,24},{24,16},{1,9},{9,1},{17,25},{25,17},{2,10},{10... | collective-permute-start | bytes 884744 | tf_op jit(solution)/shard_map/ppermute | solution.py:218
  27.3 0.0 copy-done.3
  27.3 0.1 collective-permute-start.9
  27.4 2.7 %collective-permute-done.11 = bf16[192,768]{1,0:T(8,128)(2,1)S(1)} collective-permute-done((bf16[192,768]{1,0:T(8,128)(2,1)S(1)}, bf16[192,768]{1,0:T(8,128)(2,1)S(1)}, u32[]{:S(2)}, u32[]{:S(2)}) %collective-permute-start.11) | collective-permute-done | bytes 294944 | tf_op jit(solution)/shard_map/ppermute | solution.py:223
  30.1 0.0 collective-permute-start.14
  30.1 0.6 %collective-permute-done.12.refs_14_ = bf16[1,2,192,384]{3,2,1,0:T(8,128)(2,1)S(1)} collective-permute-done((bf16[1,2,192,384]{3,2,1,0:T(8,128)(2,1)S(1)}, bf16[1,2,192,384]{3,2,1,0:T(8,128)(2,1)S(1)}, u32[]{:S(2)}, u32[]{:S(2)}) %collective-permute-start.12) | collective-permute-done | bytes 294944 | tf_op jit(solution)/shard_map/ppermute | solution.py:218
  30.7 0.0 collective-permute-start.15
  31.4 0.0 copy-done.5
  31.4 0.0 collective-permute-done.8.refs_10_
  31.4 0.0 collective-permute-done.9.refs_11_
  31.4 0.2 collective-permute-done.14.refs_16_
  31.7 0.6 %collective-permute-done.15.refs_17_ = bf16[1,2,192,384]{3,2,1,0:T(8,128)(2,1)S(1)} collective-permute-done((bf16[1,2,192,384]{3,2,1,0:T(8,128)(2,1)S(1)}, bf16[1,2,192,384]{3,2,1,0:T(8,128)(2,1)S(1)}, u32[]{:S(2)}, u32[]{:S(2)}) %collective-permute-start.15) | collective-permute-done | bytes 294944 | tf_op jit(solution)/shard_map/ppermute | solution.py:218
  32.3 0.0 collective-permute-done.13.refs_15_
  32.3 4.3 %attend.1 = bf16[256,768]{1,0:T(8,128)(2,1)} custom-call(s32[1]{0:T(128)S(6)} %copy.10.refs_0_, bf16[192,768]{1,0:T(8,128)(2,1)S(1)} %pad_maximum_fusion.refs_1_, f32[1,768]{1,0:T(1,128)S(1)} %broadcast_in_dim.8.refs_2_, bf16[256,768]{1,0:T(8,128)(2,1)S(1)} %bitcast.9, bf16[192,768]{1,0:T(8,128)(2,1)S(1)} %copy-done.1, bf16[192,768]{1,0:T(8,128)(2,1)S(1)} %copy-done.4, ...), custom_call_target="tpu_custom_call" | custom-call | flops 1000 | bytes 1000 | tf_op jit(solution)/shard_map/attend/pallas_call | solution.py:320
  (6 shorter events, 0.1 us)
Async XLA Ops:
  0.0 5.2 %copy-start.1 = (bf16[192,768]{1,0:T(8,128)(2,1)S(1)}, bf16[192,768]{1,0:T(8,128)(2,1)}, u32[]{:S(2)}) copy-start(bf16[192,768]{1,0:T(8,128)(2,1)} %refs_4_.1) | copy-start | bytes 884740
  0.0 5.2 %copy-start.7 = (s32[1,64,4]{1,2,0:T(4,128)S(1)}, s32[1,64,4]{1,2,0:T(4,128)}, u32[]{:S(2)}) copy-start(s32[1,64,4]{1,2,0:T(4,128)} %param.11) | copy-start | bytes 3076
  0.0 5.2 %copy-start.6 = (s32[1,64,4]{1,2,0:T(4,128)S(1)}, s32[1,64,4]{1,2,0:T(4,128)}, u32[]{:S(2)}) copy-start(s32[1,64,4]{1,2,0:T(4,128)} %param.10) | copy-start | bytes 3076
  0.0 5.3 %copy-start.4 = (bf16[192,768]{1,0:T(8,128)(2,1)S(1)}, bf16[192,768]{1,0:T(8,128)(2,1)}, u32[]{:S(2)}) copy-start(bf16[192,768]{1,0:T(8,128)(2,1)} %refs_5_.1) | copy-start | bytes 884740
  0.0 13.9 %copy-start = (bf16[1,256,768]{2,1,0:T(8,128)(2,1)S(1)}, bf16[1,256,768]{2,1,0:T(8,128)(2,1)}, u32[]{:S(2)}) copy-start(bf16[1,256,768]{2,1,0:T(8,128)(2,1)} %param.9) | copy-start | bytes 1179652
  2.1 21.8 %collective-permute-start.10 = (bf16[4,192,384]{2,1,0:T(8,128)(2,1)}, bf16[4,192,384]{2,1,0:T(8,128)(2,1)S(1)}, u32[]{:S(2)}, u32[]{:S(2)}) collective-permute-start(bf16[4,192,384]{2,1,0:T(8,128)(2,1)} %stack.9), channel_id=1, source_target_pairs={{0,16},{8,24},{16,0},{24,8},{1,17},{9,25},{17,1},{25,9},{2,18},{10... | collective-permute-start | bytes 1769480 | tf_op jit(solution)/shard_map/ppermute | solution.py:223
  5.2 5.1 %collective-permute-start.2 = (bf16[192,768]{1,0:T(8,128)(2,1)S(1)}, bf16[192,768]{1,0:T(8,128)(2,1)S(1)}, u32[]{:S(2)}, u32[]{:S(2)}) collective-permute-start(bf16[192,768]{1,0:T(8,128)(2,1)S(1)} %copy-done.1), channel_id=1, source_target_pairs={{0,8},{8,0},{16,24},{24,16},{1,9},{9,1},{17,25},{25,17},{2,10},{10... | collective-permute-start | bytes 884744 | tf_op jit(solution)/shard_map/ppermute | solution.py:218
  5.3 5.0 %collective-permute-start.3 = (bf16[192,768]{1,0:T(8,128)(2,1)S(1)}, bf16[192,768]{1,0:T(8,128)(2,1)S(1)}, u32[]{:S(2)}, u32[]{:S(2)}) collective-permute-start(bf16[192,768]{1,0:T(8,128)(2,1)S(1)} %copy-done.4), channel_id=1, source_target_pairs={{0,8},{8,0},{16,24},{24,16},{1,9},{9,1},{17,25},{25,17},{2,10},{10... | collective-permute-start | bytes 884744 | tf_op jit(solution)/shard_map/ppermute | solution.py:218
  5.8 6.3 %collective-permute-start.1 = (s32[8,128]{1,0:T(8,128)S(1)}, s32[8,128]{1,0:T(8,128)S(1)}, u32[]{:S(2)}, u32[]{:S(2)}) collective-permute-start(s32[8,128]{1,0:T(8,128)S(1)} %pad.4.here), channel_id=1, source_target_pairs={{1,2},{3,4},{5,6},{7,0},{2,1},{4,3},{6,5},{0,7},{9,10},{11,12},{13... | collective-permute-start | bytes 12296 | tf_op jit(solution)/shard_map/ppermute | solution.py:296
  10.3 3.6 %collective-permute-start = (s32[8,128]{1,0:T(8,128)S(1)}, s32[8,128]{1,0:T(8,128)S(1)}, u32[]{:S(2)}, u32[]{:S(2)}) collective-permute-start(s32[8,128]{1,0:T(8,128)S(1)} %pad.4.here), channel_id=1, source_target_pairs={{0,1},{1,0},{2,3},{3,2},{4,5},{5,4},{6,7},{7,6},{8,9},{9,8},{10,11... | collective-permute-start | bytes 12296 | tf_op jit(solution)/shard_map/ppermute | solution.py:218
  14.5 4.4 %collective-permute-start.4 = (f32[24,768]{1,0:T(8,128)S(1)}, f32[24,768]{1,0:T(8,128)S(1)}, u32[]{:S(2)}, u32[]{:S(2)}) collective-permute-start(f32[24,768]{1,0:T(8,128)S(1)} %pool.1.mine), channel_id=1, source_target_pairs={{0,1},{1,0},{2,3},{3,2},{4,5},{5,4},{6,7},{7,6},{8,9},{9,8},{10,11... | collective-permute-start | bytes 221192 | tf_op jit(solution)/shard_map/ppermute | solution.py:218
  18.9 6.3 %collective-permute-start.7 = (bf16[48,768]{1,0:T(8,128)(2,1)S(1)}, bf16[48,768]{1,0:T(8,128)(2,1)S(1)}, u32[]{:S(2)}, u32[]{:S(2)}) collective-permute-start(bf16[48,768]{1,0:T(8,128)(2,1)S(1)} %pair.1), channel_id=1, source_target_pairs={{0,6},{1,7},{2,4},{3,5},{4,2},{5,3},{6,0},{7,1},{8,14},{9,15},{10,... | collective-permute-start | bytes 221192 | tf_op jit(solution)/shard_map/ppermute | solution.py:218
  20.2 6.5 %collective-permute-start.6 = (bf16[48,768]{1,0:T(8,128)(2,1)S(1)}, bf16[48,768]{1,0:T(8,128)(2,1)S(1)}, u32[]{:S(2)}, u32[]{:S(2)}) collective-permute-start(bf16[48,768]{1,0:T(8,128)(2,1)S(1)} %pair.1), channel_id=1, source_target_pairs={{0,4},{1,5},{2,6},{3,7},{4,0},{5,1},{6,2},{7,3},{8,12},{9,13},{10,... | collective-permute-start | bytes 221192 | tf_op jit(solution)/shard_map/ppermute | solution.py:218
  20.2 6.5 %collective-permute-start.5 = (bf16[48,768]{1,0:T(8,128)(2,1)S(1)}, bf16[48,768]{1,0:T(8,128)(2,1)S(1)}, u32[]{:S(2)}, u32[]{:S(2)}) collective-permute-start(bf16[48,768]{1,0:T(8,128)(2,1)S(1)} %pair.1), channel_id=1, source_target_pairs={{0,2},{1,3},{2,0},{3,1},{4,6},{5,7},{6,4},{7,5},{8,10},{9,11},{10,... | collective-permute-start | bytes 221192 | tf_op jit(solution)/shard_map/ppermute | solution.py:218
  23.4 6.7 %collective-permute-start.11 = (bf16[192,768]{1,0:T(8,128)(2,1)S(1)}, bf16[192,768]{1,0:T(8,128)(2,1)S(1)}, u32[]{:S(2)}, u32[]{:S(2)}) collective-permute-start(bf16[192,768]{1,0:T(8,128)(2,1)S(1)} %copy-done.4), channel_id=1, source_target_pairs={{0,16},{8,24},{16,0},{24,8},{1,17},{9,25},{17,1},{25,9},{2,18},{10... | collective-permute-start | bytes 884744 | tf_op jit(solution)/shard_map/ppermute | solution.py:223
  23.9 7.5 %copy-start.5 = (f32[768]{0:T(1024)S(1)}, f32[768]{0:T(1024)}, u32[]{:S(2)}) copy-start(f32[768]{0:T(1024)} %param.17) | copy-start | bytes 9220
  23.9 2.9 %copy-start.2 = (bf16[192,768]{1,0:T(8,128)(2,1)S(1)}, bf16[192,768]{1,0:T(8,128)(2,1)}, u32[]{:S(2)}) copy-start(bf16[192,768]{1,0:T(8,128)(2,1)} %refs_6_.1) | copy-start | bytes 884740
  23.9 3.4 %copy-start.3 = (bf16[192,768]{1,0:T(8,128)(2,1)S(1)}, bf16[192,768]{1,0:T(8,128)(2,1)}, u32[]{:S(2)}) copy-start(bf16[192,768]{1,0:T(8,128)(2,1)} %refs_7_.1) | copy-start | bytes 884740
  23.9 6.8 %collective-permute-start.12 = (bf16[1,2,192,384]{3,2,1,0:T(8,128)(2,1)S(1)}, bf16[1,2,192,384]{3,2,1,0:T(8,128)(2,1)S(1)}, u32[]{:S(2)}, u32[]{:S(2)}) collective-permute-start(bf16[1,2,192,384]{3,2,1,0:T(8,128)(2,1)S(1)} %slice.3), channel_id=1, source_target_pairs={{0,1},{1,0},{2,3},{3,2},{4,5},{5,4},{6,7},{7,6},{8,9},{9,8},{10,11... | collective-permute-start | bytes 884744 | tf_op jit(solution)/shard_map/ppermute | solution.py:218
  26.7 5.6 %collective-permute-start.13 = (bf16[1,4,192,384]{3,2,1,0:T(8,128)(2,1)S(1)}, bf16[1,4,192,384]{3,2,1,0:T(8,128)(2,1)S(1)}, u32[]{:S(2)}, u32[]{:S(2)}) collective-permute-start(bf16[1,4,192,384]{3,2,1,0:T(8,128)(2,1)S(1)} %bitcast.11), channel_id=1, source_target_pairs={{0,8},{8,0},{16,24},{24,16},{1,9},{9,1},{17,25},{25,17},{2,10},{10... | collective-permute-start | bytes 1769480 | tf_op jit(solution)/shard_map/ppermute | solution.py:218
  26.8 4.6 %collective-permute-start.8 = (bf16[192,768]{1,0:T(8,128)(2,1)S(1)}, bf16[192,768]{1,0:T(8,128)(2,1)S(1)}, u32[]{:S(2)}, u32[]{:S(2)}) collective-permute-start(bf16[192,768]{1,0:T(8,128)(2,1)S(1)} %copy-done.2), channel_id=1, source_target_pairs={{0,8},{8,0},{16,24},{24,16},{1,9},{9,1},{17,25},{25,17},{2,10},{10... | collective-permute-start | bytes 884744 | tf_op jit(solution)/shard_map/ppermute | solution.py:218
  27.3 4.1 %collective-permute-start.9 = (bf16[192,768]{1,0:T(8,128)(2,1)S(1)}, bf16[192,768]{1,0:T(8,128)(2,1)S(1)}, u32[]{:S(2)}, u32[]{:S(2)}) collective-permute-start(bf16[192,768]{1,0:T(8,128)(2,1)S(1)} %copy-done.3), channel_id=1, source_target_pairs={{0,8},{8,0},{16,24},{24,16},{1,9},{9,1},{17,25},{25,17},{2,10},{10... | collective-permute-start | bytes 884744 | tf_op jit(solution)/shard_map/ppermute | solution.py:218
  30.1 1.6 %collective-permute-start.14 = (bf16[1,192,768]{2,1,0:T(8,128)(2,1)S(1)}, bf16[1,192,768]{2,1,0:T(8,128)(2,1)S(1)}, u32[]{:S(2)}, u32[]{:S(2)}) collective-permute-start(bf16[1,192,768]{2,1,0:T(8,128)(2,1)S(1)} %bitcast.13), channel_id=1, source_target_pairs={{0,8},{8,0},{16,24},{24,16},{1,9},{9,1},{17,25},{25,17},{2,10},{10... | collective-permute-start | bytes 884744 | tf_op jit(solution)/shard_map/ppermute | solution.py:218
  30.7 1.6 %collective-permute-start.15 = (bf16[1,2,192,384]{3,2,1,0:T(8,128)(2,1)S(1)}, bf16[1,2,192,384]{3,2,1,0:T(8,128)(2,1)S(1)}, u32[]{:S(2)}, u32[]{:S(2)}) collective-permute-start(bf16[1,2,192,384]{3,2,1,0:T(8,128)(2,1)S(1)} %collective-permute-done.12.refs_14_), channel_id=1, source_target_pairs={{0,8},{8,0},{16,24},{24,16},{1,9},{9,1},{17,25},{25,17},{2,10},{10... | collective-permute-start | bytes 884744 | tf_op jit(solution)/shard_map/ppermute | solution.py:218

commit v11 on v9

--- a/solution.py
+++ b/solution.py
@@ -12,6 +12,7 @@
 REGIONS_PER_KEY = 8
 KEY_DILATION = 2
 LANE_GROUPS = 2
+OUT_PARTS = 2
 F32 = jnp.float32
 BF16 = jnp.bfloat16
 
@@ -137,7 +138,7 @@
     count, sums, gain, tiles = refs[:4]
     pieces, mates = refs[4:8], refs[8:12]
     near, far = refs[12:15], refs[15:18]
-    out, held, pooled, sem = refs[18:]
+    out, held, pooled, made, sem, out_sem = refs[18:]
     device = lax.axis_index("tile")
     cut = device % 2
     own, others = place_rows(fsdp, pieces[0].shape[0], held)
@@ -180,9 +181,9 @@
     scale = lax.rsqrt(jnp.mean(mean * mean, axis=1, keepdims=True) + 1e-06)
     normed = (mean * scale * gain[...]).astype(BF16)
     ordered = sorted_rows(normed)
-    arrive(1)
+    for weight in range(1, 4):
+        arrive(weight)
     keys = over(ordered, held[1], 1, 0).astype(BF16)
-    arrive(2)
     values = over(ordered, held[2], 1, 0).astype(BF16)
     half = keys.shape[0] // KEY_DILATION
     heads = HEADS // LANE_GROUPS
@@ -207,9 +208,17 @@
         weight = expo.reshape(heads * half, rows).astype(BF16)
         context = over(spread(values, group, wide), weight, 0, 0).reshape(heads, size, rows)
         contexts.append((context * share).reshape(wide, rows).astype(BF16))
-    arrive(3)
     context = jnp.concatenate(contexts, axis=0)
-    out[...] = over(context, held[3], 0, 0).astype(out.dtype)
+    leaving = []
+    for part in range(OUT_PARTS):
+        piece = pl.ds(part * rows // OUT_PARTS, rows // OUT_PARTS)
+        lanes = slice(part * rows // OUT_PARTS, (part + 1) * rows // OUT_PARTS)
+        made[piece, :] = over(context[:, lanes], held[3], 0, 0).astype(made.dtype)
+        copy = pltpu.make_async_copy(made.at[piece], out.at[piece], out_sem.at[part])
+        copy.start()
+        leaving.append(copy)
+    for copy in leaving:
+        copy.wait()
 
 
 def swap(array, axis, offset):
@@ -254,12 +263,12 @@
     return rows
 
 
-def local_call(kernel, out_shape, in_specs, name, scratch=()):
+def local_call(kernel, out_shape, in_specs, name, scratch=(), out_spec=None):
     return pl.pallas_call(
         kernel,
         out_shape=out_shape,
         in_specs=in_specs,
-        out_specs=vmem(),
+        out_specs=vmem() if out_spec is None else out_spec,
         scratch_shapes=list(scratch),
         compiler_params=pltpu.CompilerParams(vmem_limit_bytes=40 * 1024 * 1024),
         cost_estimate=pl.CostEstimate(flops=1000, bytes_accessed=1000, transcendentals=0),
@@ -322,8 +331,11 @@
         [
             pltpu.VMEM((4, width, width), BF16),
             pltpu.VMEM(((tile_devices + 2) * block, width), F32),
+            pltpu.VMEM((rows, width), BF16),
             pltpu.SemaphoreType.DMA((7 * fsdp,)),
+            pltpu.SemaphoreType.DMA((OUT_PARTS,)),
         ],
+        hbm(),
     )(tile_count, sums, key_gain[None, :], own_tiles, *weights, *mates, *near, *far)
     return attended[None]
 

time: 35.4 us -> 35 us (0.989)
  Pallas kernels: 6.97 us -> 6.5 us
    pallas_call x1, Pallas kernels: 4.32 us -> 3.85 us  [body(): local_call(functools.partial(attend_kernel, fsdp, block), jax.ShapeDtypeS...]
where the time goes in v11:
time: 35 us; the launch traced here: 34.8 us
  starting transfers between devices  18.4 us (53%)
  waiting for transfers between devices  9.03 us (26%)
  Pallas kernels  6.5 us (19%)
  between operations  0.81 us (2%)
    ppermute x13, starting transfers between devices, swap(): return lax.ppermute(array, axis, [(i, i ^ offset) for i in range(count)])  14.2 us
    ppermute x13, waiting for transfers between devices, swap(): return lax.ppermute(array, axis, [(i, i ^ offset) for i in range(count)])  7.6 us
    pallas_call x1, Pallas kernels, body(): local_call(functools.partial(attend_kernel, fsdp, block), jax.ShapeDtypeS...  3.85 us
    ppermute x2, starting transfers between devices, chip_shift(): lax.ppermute(array, axis, [(i, (i + 2 * step) % count) for i in range(cou...  3.55 us
    pallas_call x1, Pallas kernels, body(): pl.pallas_call(stack_kernel, out_shape=jax.ShapeDtypeStruct((4, shard, wi...  2.07 us
    ppermute x2, waiting for transfers between devices, chip_shift(): lax.ppermute(array, axis, [(i, (i + 2 * step) % count) for i in range(cou...  1.42 us
  transfers between devices with their start and end apart: 16, of which 7 were waited for; matrix products, arithmetic and copies ran while one was open for 0% of the time, Pallas kernels for 2%

profile of v11, /device:TPU:0, one launch (start us, length us, event | category | flops | bytes accessed | tf_op | source)
XLA Modules:
  0.0 34.8 jit_solution(10048013945493767240)
XLA Ops:
  0.0 0.0 copy-start.1
  0.0 0.0 copy-start.7
  0.0 0.0 copy-start.6
  0.0 0.0 copy-start.4
  0.0 0.0 copy-start
  0.0 2.1 %stack.9 = bf16[4,192,384]{2,1,0:T(8,128)(2,1)} custom-call(bf16[192,768]{1,0:T(8,128)(2,1)} %refs_4_.1, bf16[192,768]{1,0:T(8,128)(2,1)} %refs_6_.1, bf16[192,768]{1,0:T(8,128)(2,1)} %refs_7_.1), custom_call_target="tpu_custom_call" | custom-call | tf_op jit(solution)/shard_map/stack/pallas_call | solution.py:288
  2.1 3.0 %collective-permute-start.10 = (bf16[4,192,384]{2,1,0:T(8,128)(2,1)}, bf16[4,192,384]{2,1,0:T(8,128)(2,1)S(1)}, u32[]{:S(2)}, u32[]{:S(2)}) collective-permute-start(bf16[4,192,384]{2,1,0:T(8,128)(2,1)} %stack.9), channel_id=1, source_target_pairs={{0,16},{8,24},{16,0},{24,8},{1,17},{9,25},{17,1},{25,9},{2,18},{10... | collective-permute-start | bytes 1769480 | tf_op jit(solution)/shard_map/ppermute | solution.py:231
  5.1 0.0 copy-done.7
  5.1 0.0 copy-done.6
  5.2 0.0 copy-done.1
  5.2 0.1 collective-permute-start.2
  5.3 0.0 copy-done.4
  5.3 0.5 %collective-permute-start.3 = (bf16[192,768]{1,0:T(8,128)(2,1)S(1)}, bf16[192,768]{1,0:T(8,128)(2,1)S(1)}, u32[]{:S(2)}, u32[]{:S(2)}) collective-permute-start(bf16[192,768]{1,0:T(8,128)(2,1)S(1)} %copy-done.4), channel_id=1, source_target_pairs={{0,8},{8,0},{16,24},{24,16},{1,9},{9,1},{17,25},{25,17},{2,10},{10... | collective-permute-start | bytes 884744 | tf_op jit(solution)/shard_map/ppermute | solution.py:226
  5.8 0.6 %collective-permute-start.1 = (s32[8,128]{1,0:T(8,128)S(1)}, s32[8,128]{1,0:T(8,128)S(1)}, u32[]{:S(2)}, u32[]{:S(2)}) collective-permute-start(s32[8,128]{1,0:T(8,128)S(1)} %pad.4.here), channel_id=1, source_target_pairs={{1,2},{3,4},{5,6},{2,1},{4,3},{6,5},{9,10},{11,12},{13,14},{10,9},... | collective-permute-start | bytes 12296 | tf_op jit(solution)/shard_map/ppermute | solution.py:302
  6.4 4.4 %collective-permute-start = (s32[8,128]{1,0:T(8,128)S(1)}, s32[8,128]{1,0:T(8,128)S(1)}, u32[]{:S(2)}, u32[]{:S(2)}) collective-permute-start(s32[8,128]{1,0:T(8,128)S(1)} %pad.4.here), channel_id=1, source_target_pairs={{0,1},{1,0},{2,3},{3,2},{4,5},{5,4},{6,7},{7,6},{8,9},{9,8},{10,11... | collective-permute-start | bytes 12296 | tf_op jit(solution)/shard_map/ppermute | solution.py:226
  10.8 0.0 collective-permute-done.2.refs_8_
  10.8 0.0 collective-permute-done.3.refs_9_
  10.8 0.0 collective-permute-done.1.other
  10.8 1.6 %collective-permute-done.mate = s32[8,128]{1,0:T(8,128)S(1)} collective-permute-done((s32[8,128]{1,0:T(8,128)S(1)}, s32[8,128]{1,0:T(8,128)S(1)}, u32[]{:S(2)}, u32[]{:S(2)}) %collective-permute-start) | collective-permute-done | bytes 4128 | tf_op jit(solution)/shard_map/ppermute | solution.py:226
  12.3 0.0 copy-done
  12.4 0.6 %pool.1.mine = f32[24,768]{1,0:T(8,128)S(1)} custom-call(s32[8,128]{1,0:T(8,128)S(1)} %pad.4.here, s32[8,128]{1,0:T(8,128)S(1)} %collective-permute-done.mate, s32[8,128]{1,0:T(8,128)S(1)} %collective-permute-done.1.other, bf16[256,768]{1,0:T(8,128)(2,1)S(1)} %bitcast.8), custom_call_target="tpu_custom_call" | custom-call | flops 1000 | bytes 1000 | tf_op jit(solution)/shard_map/pool/pallas_call | solution.py:304
  12.9 2.1 %collective-permute-start.4 = (f32[24,768]{1,0:T(8,128)S(1)}, f32[24,768]{1,0:T(8,128)S(1)}, u32[]{:S(2)}, u32[]{:S(2)}) collective-permute-start(f32[24,768]{1,0:T(8,128)S(1)} %pool.1.mine), channel_id=1, source_target_pairs={{0,1},{1,0},{2,3},{3,2},{4,5},{5,4},{6,7},{7,6},{8,9},{9,8},{10,11... | collective-permute-start | bytes 221192 | tf_op jit(solution)/shard_map/ppermute | solution.py:226
  15.0 2.3 %collective-permute-done.4.theirs = f32[24,768]{1,0:T(8,128)S(1)} collective-permute-done((f32[24,768]{1,0:T(8,128)S(1)}, f32[24,768]{1,0:T(8,128)S(1)}, u32[]{:S(2)}, u32[]{:S(2)}) %collective-permute-start.4) | collective-permute-done | bytes 73760 | tf_op jit(solution)/shard_map/ppermute | solution.py:226
  17.4 4.0 %collective-permute-start.7 = (bf16[48,768]{1,0:T(8,128)(2,1)S(1)}, bf16[48,768]{1,0:T(8,128)(2,1)S(1)}, u32[]{:S(2)}, u32[]{:S(2)}) collective-permute-start(bf16[48,768]{1,0:T(8,128)(2,1)S(1)} %pair.1), channel_id=1, source_target_pairs={{0,6},{1,7},{2,4},{3,5},{4,2},{5,3},{6,0},{7,1},{8,14},{9,15},{10,... | collective-permute-start | bytes 221192 | tf_op jit(solution)/shard_map/ppermute | solution.py:226
  21.4 0.0 collective-permute-start.6
  21.4 0.6 %collective-permute-start.5 = (bf16[48,768]{1,0:T(8,128)(2,1)S(1)}, bf16[48,768]{1,0:T(8,128)(2,1)S(1)}, u32[]{:S(2)}, u32[]{:S(2)}) collective-permute-start(bf16[48,768]{1,0:T(8,128)(2,1)S(1)} %pair.1), channel_id=1, source_target_pairs={{0,2},{1,3},{2,0},{3,1},{4,6},{5,7},{6,4},{7,5},{8,10},{9,11},{10,... | collective-permute-start | bytes 221192 | tf_op jit(solution)/shard_map/ppermute | solution.py:226
  22.0 0.5 %collective-permute-start.11 = (bf16[192,768]{1,0:T(8,128)(2,1)S(1)}, bf16[192,768]{1,0:T(8,128)(2,1)S(1)}, u32[]{:S(2)}, u32[]{:S(2)}) collective-permute-start(bf16[192,768]{1,0:T(8,128)(2,1)S(1)} %copy-done.4), channel_id=1, source_target_pairs={{0,16},{8,24},{16,0},{24,8},{1,17},{9,25},{17,1},{25,9},{2,18},{10... | collective-permute-start | bytes 884744 | tf_op jit(solution)/shard_map/ppermute | solution.py:231
  22.5 0.0 collective-permute-done.10
  22.5 0.0 copy-start.5
  22.6 0.0 copy-start.2
  22.6 0.0 copy-start.3
  22.6 1.9 %collective-permute-start.12 = (bf16[1,2,192,384]{3,2,1,0:T(8,128)(2,1)S(1)}, bf16[1,2,192,384]{3,2,1,0:T(8,128)(2,1)S(1)}, u32[]{:S(2)}, u32[]{:S(2)}) collective-permute-start(bf16[1,2,192,384]{3,2,1,0:T(8,128)(2,1)S(1)} %slice.3), channel_id=1, source_target_pairs={{0,1},{1,0},{2,3},{3,2},{4,5},{5,4},{6,7},{7,6},{8,9},{9,8},{10,11... | collective-permute-start | bytes 884744 | tf_op jit(solution)/shard_map/ppermute | solution.py:226
  24.5 0.0 collective-permute-done.7
  24.5 2.2 %collective-permute-done.6 = bf16[48,768]{1,0:T(8,128)(2,1)S(1)} collective-permute-done((bf16[48,768]{1,0:T(8,128)(2,1)S(1)}, bf16[48,768]{1,0:T(8,128)(2,1)S(1)}, u32[]{:S(2)}, u32[]{:S(2)}) %collective-permute-start.6) | collective-permute-done | bytes 73760 | tf_op jit(solution)/shard_map/ppermute | solution.py:226
  26.6 0.0 collective-permute-done.5
  26.7 0.1 collective-permute-start.13
  26.7 0.0 copy-done.2
  26.8 0.5 %collective-permute-start.8 = (bf16[192,768]{1,0:T(8,128)(2,1)S(1)}, bf16[192,768]{1,0:T(8,128)(2,1)S(1)}, u32[]{:S(2)}, u32[]{:S(2)}) collective-permute-start(bf16[192,768]{1,0:T(8,128)(2,1)S(1)} %copy-done.2), channel_id=1, source_target_pairs={{0,8},{8,0},{16,24},{24,16},{1,9},{9,1},{17,25},{25,17},{2,10},{10... | collective-permute-start | bytes 884744 | tf_op jit(solution)/shard_map/ppermute | solution.py:226
  27.2 0.0 copy-done.3
  27.2 0.1 collective-permute-start.9
  27.3 1.4 %collective-permute-done.11 = bf16[192,768]{1,0:T(8,128)(2,1)S(1)} collective-permute-done((bf16[192,768]{1,0:T(8,128)(2,1)S(1)}, bf16[192,768]{1,0:T(8,128)(2,1)S(1)}, u32[]{:S(2)}, u32[]{:S(2)}) %collective-permute-start.11) | collective-permute-done | bytes 294944 | tf_op jit(solution)/shard_map/ppermute | solution.py:231
  28.7 0.0 collective-permute-start.14
  28.8 0.6 %collective-permute-done.12.refs_14_ = bf16[1,2,192,384]{3,2,1,0:T(8,128)(2,1)S(1)} collective-permute-done((bf16[1,2,192,384]{3,2,1,0:T(8,128)(2,1)S(1)}, bf16[1,2,192,384]{3,2,1,0:T(8,128)(2,1)S(1)}, u32[]{:S(2)}, u32[]{:S(2)}) %collective-permute-start.12) | collective-permute-done | bytes 294944 | tf_op jit(solution)/shard_map/ppermute | solution.py:226
  29.4 0.0 collective-permute-start.15
  30.0 0.0 copy-done.5
  30.1 0.0 collective-permute-done.8.refs_10_
  30.1 0.0 collective-permute-done.9.refs_11_
  30.1 0.2 collective-permute-done.14.refs_16_
  30.3 0.6 %collective-permute-done.15.refs_17_ = bf16[1,2,192,384]{3,2,1,0:T(8,128)(2,1)S(1)} collective-permute-done((bf16[1,2,192,384]{3,2,1,0:T(8,128)(2,1)S(1)}, bf16[1,2,192,384]{3,2,1,0:T(8,128)(2,1)S(1)}, u32[]{:S(2)}, u32[]{:S(2)}) %collective-permute-start.15) | collective-permute-done | bytes 294944 | tf_op jit(solution)/shard_map/ppermute | solution.py:226
  31.0 0.0 collective-permute-done.13.refs_15_
  31.0 3.8 %attend.1 = bf16[256,768]{1,0:T(8,128)(2,1)} custom-call(s32[1]{0:T(128)S(6)} %copy.10.refs_0_, bf16[192,768]{1,0:T(8,128)(2,1)S(1)} %pad_maximum_fusion.refs_1_, f32[1,768]{1,0:T(1,128)S(1)} %broadcast_in_dim.8.refs_2_, bf16[256,768]{1,0:T(8,128)(2,1)S(1)} %bitcast.9, bf16[192,768]{1,0:T(8,128)(2,1)S(1)} %copy-done.1, bf16[192,768]{1,0:T(8,128)(2,1)S(1)} %copy-done.4, ...), custom_call_target="tpu_custom_call" | custom-call | flops 1000 | bytes 1000 | tf_op jit(solution)/shard_map/attend/pallas_call | solution.py:326
  (6 shorter events, 0.1 us)
Async XLA Ops:
  0.0 5.2 %copy-start.1 = (bf16[192,768]{1,0:T(8,128)(2,1)S(1)}, bf16[192,768]{1,0:T(8,128)(2,1)}, u32[]{:S(2)}) copy-start(bf16[192,768]{1,0:T(8,128)(2,1)} %refs_4_.1) | copy-start | bytes 884740
  0.0 5.1 %copy-start.7 = (s32[1,64,4]{1,2,0:T(4,128)S(1)}, s32[1,64,4]{1,2,0:T(4,128)}, u32[]{:S(2)}) copy-start(s32[1,64,4]{1,2,0:T(4,128)} %param.11) | copy-start | bytes 3076
  0.0 5.1 %copy-start.6 = (s32[1,64,4]{1,2,0:T(4,128)S(1)}, s32[1,64,4]{1,2,0:T(4,128)}, u32[]{:S(2)}) copy-start(s32[1,64,4]{1,2,0:T(4,128)} %param.10) | copy-start | bytes 3076
  0.0 5.2 %copy-start.4 = (bf16[192,768]{1,0:T(8,128)(2,1)S(1)}, bf16[192,768]{1,0:T(8,128)(2,1)}, u32[]{:S(2)}) copy-start(bf16[192,768]{1,0:T(8,128)(2,1)} %refs_5_.1) | copy-start | bytes 884740
  0.0 12.3 %copy-start = (bf16[1,256,768]{2,1,0:T(8,128)(2,1)S(1)}, bf16[1,256,768]{2,1,0:T(8,128)(2,1)}, u32[]{:S(2)}) copy-start(bf16[1,256,768]{2,1,0:T(8,128)(2,1)} %param.9) | copy-start | bytes 1179652
  2.1 20.4 %collective-permute-start.10 = (bf16[4,192,384]{2,1,0:T(8,128)(2,1)}, bf16[4,192,384]{2,1,0:T(8,128)(2,1)S(1)}, u32[]{:S(2)}, u32[]{:S(2)}) collective-permute-start(bf16[4,192,384]{2,1,0:T(8,128)(2,1)} %stack.9), channel_id=1, source_target_pairs={{0,16},{8,24},{16,0},{24,8},{1,17},{9,25},{17,1},{25,9},{2,18},{10... | collective-permute-start | bytes 1769480 | tf_op jit(solution)/shard_map/ppermute | solution.py:231
  5.2 5.6 %collective-permute-start.2 = (bf16[192,768]{1,0:T(8,128)(2,1)S(1)}, bf16[192,768]{1,0:T(8,128)(2,1)S(1)}, u32[]{:S(2)}, u32[]{:S(2)}) collective-permute-start(bf16[192,768]{1,0:T(8,128)(2,1)S(1)} %copy-done.1), channel_id=1, source_target_pairs={{0,8},{8,0},{16,24},{24,16},{1,9},{9,1},{17,25},{25,17},{2,10},{10... | collective-permute-start | bytes 884744 | tf_op jit(solution)/shard_map/ppermute | solution.py:226
  5.3 5.5 %collective-permute-start.3 = (bf16[192,768]{1,0:T(8,128)(2,1)S(1)}, bf16[192,768]{1,0:T(8,128)(2,1)S(1)}, u32[]{:S(2)}, u32[]{:S(2)}) collective-permute-start(bf16[192,768]{1,0:T(8,128)(2,1)S(1)} %copy-done.4), channel_id=1, source_target_pairs={{0,8},{8,0},{16,24},{24,16},{1,9},{9,1},{17,25},{25,17},{2,10},{10... | collective-permute-start | bytes 884744 | tf_op jit(solution)/shard_map/ppermute | solution.py:226
  5.8 5.0 %collective-permute-start.1 = (s32[8,128]{1,0:T(8,128)S(1)}, s32[8,128]{1,0:T(8,128)S(1)}, u32[]{:S(2)}, u32[]{:S(2)}) collective-permute-start(s32[8,128]{1,0:T(8,128)S(1)} %pad.4.here), channel_id=1, source_target_pairs={{1,2},{3,4},{5,6},{2,1},{4,3},{6,5},{9,10},{11,12},{13,14},{10,9},... | collective-permute-start | bytes 12296 | tf_op jit(solution)/shard_map/ppermute | solution.py:302
  6.4 5.9 %collective-permute-start = (s32[8,128]{1,0:T(8,128)S(1)}, s32[8,128]{1,0:T(8,128)S(1)}, u32[]{:S(2)}, u32[]{:S(2)}) collective-permute-start(s32[8,128]{1,0:T(8,128)S(1)} %pad.4.here), channel_id=1, source_target_pairs={{0,1},{1,0},{2,3},{3,2},{4,5},{5,4},{6,7},{7,6},{8,9},{9,8},{10,11... | collective-permute-start | bytes 12296 | tf_op jit(solution)/shard_map/ppermute | solution.py:226
  12.9 4.4 %collective-permute-start.4 = (f32[24,768]{1,0:T(8,128)S(1)}, f32[24,768]{1,0:T(8,128)S(1)}, u32[]{:S(2)}, u32[]{:S(2)}) collective-permute-start(f32[24,768]{1,0:T(8,128)S(1)} %pool.1.mine), channel_id=1, source_target_pairs={{0,1},{1,0},{2,3},{3,2},{4,5},{5,4},{6,7},{7,6},{8,9},{9,8},{10,11... | collective-permute-start | bytes 221192 | tf_op jit(solution)/shard_map/ppermute | solution.py:226
  17.4 7.1 %collective-permute-start.7 = (bf16[48,768]{1,0:T(8,128)(2,1)S(1)}, bf16[48,768]{1,0:T(8,128)(2,1)S(1)}, u32[]{:S(2)}, u32[]{:S(2)}) collective-permute-start(bf16[48,768]{1,0:T(8,128)(2,1)S(1)} %pair.1), channel_id=1, source_target_pairs={{0,6},{1,7},{2,4},{3,5},{4,2},{5,3},{6,0},{7,1},{8,14},{9,15},{10,... | collective-permute-start | bytes 221192 | tf_op jit(solution)/shard_map/ppermute | solution.py:226
  21.4 5.3 %collective-permute-start.6 = (bf16[48,768]{1,0:T(8,128)(2,1)S(1)}, bf16[48,768]{1,0:T(8,128)(2,1)S(1)}, u32[]{:S(2)}, u32[]{:S(2)}) collective-permute-start(bf16[48,768]{1,0:T(8,128)(2,1)S(1)} %pair.1), channel_id=1, source_target_pairs={{0,4},{1,5},{2,6},{3,7},{4,0},{5,1},{6,2},{7,3},{8,12},{9,13},{10,... | collective-permute-start | bytes 221192 | tf_op jit(solution)/shard_map/ppermute | solution.py:226
  21.4 5.3 %collective-permute-start.5 = (bf16[48,768]{1,0:T(8,128)(2,1)S(1)}, bf16[48,768]{1,0:T(8,128)(2,1)S(1)}, u32[]{:S(2)}, u32[]{:S(2)}) collective-permute-start(bf16[48,768]{1,0:T(8,128)(2,1)S(1)} %pair.1), channel_id=1, source_target_pairs={{0,2},{1,3},{2,0},{3,1},{4,6},{5,7},{6,4},{7,5},{8,10},{9,11},{10,... | collective-permute-start | bytes 221192 | tf_op jit(solution)/shard_map/ppermute | solution.py:226
  22.0 6.7 %collective-permute-start.11 = (bf16[192,768]{1,0:T(8,128)(2,1)S(1)}, bf16[192,768]{1,0:T(8,128)(2,1)S(1)}, u32[]{:S(2)}, u32[]{:S(2)}) collective-permute-start(bf16[192,768]{1,0:T(8,128)(2,1)S(1)} %copy-done.4), channel_id=1, source_target_pairs={{0,16},{8,24},{16,0},{24,8},{1,17},{9,25},{17,1},{25,9},{2,18},{10... | collective-permute-start | bytes 884744 | tf_op jit(solution)/shard_map/ppermute | solution.py:231
  22.5 7.5 %copy-start.5 = (f32[768]{0:T(1024)S(1)}, f32[768]{0:T(1024)}, u32[]{:S(2)}) copy-start(f32[768]{0:T(1024)} %param.17) | copy-start | bytes 9220
  22.6 4.2 %copy-start.2 = (bf16[192,768]{1,0:T(8,128)(2,1)S(1)}, bf16[192,768]{1,0:T(8,128)(2,1)}, u32[]{:S(2)}) copy-start(bf16[192,768]{1,0:T(8,128)(2,1)} %refs_6_.1) | copy-start | bytes 884740
  22.6 4.7 %copy-start.3 = (bf16[192,768]{1,0:T(8,128)(2,1)S(1)}, bf16[192,768]{1,0:T(8,128)(2,1)}, u32[]{:S(2)}) copy-start(bf16[192,768]{1,0:T(8,128)(2,1)} %refs_7_.1) | copy-start | bytes 884740
  22.6 6.8 %collective-permute-start.12 = (bf16[1,2,192,384]{3,2,1,0:T(8,128)(2,1)S(1)}, bf16[1,2,192,384]{3,2,1,0:T(8,128)(2,1)S(1)}, u32[]{:S(2)}, u32[]{:S(2)}) collective-permute-start(bf16[1,2,192,384]{3,2,1,0:T(8,128)(2,1)S(1)} %slice.3), channel_id=1, source_target_pairs={{0,1},{1,0},{2,3},{3,2},{4,5},{5,4},{6,7},{7,6},{8,9},{9,8},{10,11... | collective-permute-start | bytes 884744 | tf_op jit(solution)/shard_map/ppermute | solution.py:226
  26.7 4.3 %collective-permute-start.13 = (bf16[1,4,192,384]{3,2,1,0:T(8,128)(2,1)S(1)}, bf16[1,4,192,384]{3,2,1,0:T(8,128)(2,1)S(1)}, u32[]{:S(2)}, u32[]{:S(2)}) collective-permute-start(bf16[1,4,192,384]{3,2,1,0:T(8,128)(2,1)S(1)} %bitcast.11), channel_id=1, source_target_pairs={{0,8},{8,0},{16,24},{24,16},{1,9},{9,1},{17,25},{25,17},{2,10},{10... | collective-permute-start | bytes 1769480 | tf_op jit(solution)/shard_map/ppermute | solution.py:226
  26.8 3.3 %collective-permute-start.8 = (bf16[192,768]{1,0:T(8,128)(2,1)S(1)}, bf16[192,768]{1,0:T(8,128)(2,1)S(1)}, u32[]{:S(2)}, u32[]{:S(2)}) collective-permute-start(bf16[192,768]{1,0:T(8,128)(2,1)S(1)} %copy-done.2), channel_id=1, source_target_pairs={{0,8},{8,0},{16,24},{24,16},{1,9},{9,1},{17,25},{25,17},{2,10},{10... | collective-permute-start | bytes 884744 | tf_op jit(solution)/shard_map/ppermute | solution.py:226
  27.2 2.8 %collective-permute-start.9 = (bf16[192,768]{1,0:T(8,128)(2,1)S(1)}, bf16[192,768]{1,0:T(8,128)(2,1)S(1)}, u32[]{:S(2)}, u32[]{:S(2)}) collective-permute-start(bf16[192,768]{1,0:T(8,128)(2,1)S(1)} %copy-done.3), channel_id=1, source_target_pairs={{0,8},{8,0},{16,24},{24,16},{1,9},{9,1},{17,25},{25,17},{2,10},{10... | collective-permute-start | bytes 884744 | tf_op jit(solution)/shard_map/ppermute | solution.py:226
  28.7 1.6 %collective-permute-start.14 = (bf16[1,192,768]{2,1,0:T(8,128)(2,1)S(1)}, bf16[1,192,768]{2,1,0:T(8,128)(2,1)S(1)}, u32[]{:S(2)}, u32[]{:S(2)}) collective-permute-start(bf16[1,192,768]{2,1,0:T(8,128)(2,1)S(1)} %bitcast.13), channel_id=1, source_target_pairs={{0,8},{8,0},{16,24},{24,16},{1,9},{9,1},{17,25},{25,17},{2,10},{10... | collective-permute-start | bytes 884744 | tf_op jit(solution)/shard_map/ppermute | solution.py:226
  29.4 1.6 %collective-permute-start.15 = (bf16[1,2,192,384]{3,2,1,0:T(8,128)(2,1)S(1)}, bf16[1,2,192,384]{3,2,1,0:T(8,128)(2,1)S(1)}, u32[]{:S(2)}, u32[]{:S(2)}) collective-permute-start(bf16[1,2,192,384]{3,2,1,0:T(8,128)(2,1)S(1)} %collective-permute-done.12.refs_14_), channel_id=1, source_target_pairs={{0,8},{8,0},{16,24},{24,16},{1,9},{9,1},{17,25},{25,17},{2,10},{10... | collective-permute-start | bytes 884744 | tf_op jit(solution)/shard_map/ppermute | solution.py:226

commit v12 on v11

--- a/solution.py
+++ b/solution.py
@@ -165,8 +165,6 @@
         for copy in started[(ends[weight - 1] if weight else 0) : ends[weight]]:
             copy.wait()
 
-    arrive(0)
-    query = over(tiles[...], held[0], 1, 0).astype(BF16)
     pooled[...] = jnp.zeros_like(pooled)
     pairs = sums.shape[0] // (6 * block)
     for s in range(pairs):
@@ -181,8 +179,9 @@
     scale = lax.rsqrt(jnp.mean(mean * mean, axis=1, keepdims=True) + 1e-06)
     normed = (mean * scale * gain[...]).astype(BF16)
     ordered = sorted_rows(normed)
-    for weight in range(1, 4):
+    for weight in range(4):
         arrive(weight)
+    query = over(tiles[...], held[0], 1, 0).astype(BF16)
     keys = over(ordered, held[1], 1, 0).astype(BF16)
     values = over(ordered, held[2], 1, 0).astype(BF16)
     half = keys.shape[0] // KEY_DILATION

time: 35 us -> 35.4 us (1.011)
  Pallas kernels: 6.5 us -> 6.94 us
    pallas_call x1, Pallas kernels: 3.85 us -> 4.3 us  [body(): local_call(functools.partial(attend_kernel, fsdp, block), jax.ShapeDtypeS...]
where the time goes in v12:
time: 35.4 us; the launch traced here: 35.3 us
  starting transfers between devices  18.4 us (52%)
  waiting for transfers between devices  9.03 us (26%)
  Pallas kernels  6.94 us (20%)
  between operations  0.81 us (2%)
    ppermute x13, starting transfers between devices, swap(): return lax.ppermute(array, axis, [(i, i ^ offset) for i in range(count)])  14.2 us
    ppermute x13, waiting for transfers between devices, swap(): return lax.ppermute(array, axis, [(i, i ^ offset) for i in range(count)])  7.6 us
    pallas_call x1, Pallas kernels, body(): local_call(functools.partial(attend_kernel, fsdp, block), jax.ShapeDtypeS...  4.3 us
    ppermute x2, starting transfers between devices, chip_shift(): lax.ppermute(array, axis, [(i, (i + 2 * step) % count) for i in range(cou...  3.55 us
    pallas_call x1, Pallas kernels, body(): pl.pallas_call(stack_kernel, out_shape=jax.ShapeDtypeStruct((4, shard, wi...  2.07 us
    ppermute x2, waiting for transfers between devices, chip_shift(): lax.ppermute(array, axis, [(i, (i + 2 * step) % count) for i in range(cou...  1.42 us
  transfers between devices with their start and end apart: 16, of which 7 were waited for; matrix products, arithmetic and copies ran while one was open for 0% of the time, Pallas kernels for 2%

profile of v12, /device:TPU:0, one launch (start us, length us, event | category | flops | bytes accessed | tf_op | source)
XLA Modules:
  0.0 35.3 jit_solution(994105046917789196)
XLA Ops:
  0.0 0.0 copy-start.1
  0.0 0.0 copy-start.7
  0.0 0.0 copy-start.6
  0.0 0.0 copy-start.4
  0.0 0.0 copy-start
  0.0 2.1 %stack.9 = bf16[4,192,384]{2,1,0:T(8,128)(2,1)} custom-call(bf16[192,768]{1,0:T(8,128)(2,1)} %refs_4_.1, bf16[192,768]{1,0:T(8,128)(2,1)} %refs_6_.1, bf16[192,768]{1,0:T(8,128)(2,1)} %refs_7_.1), custom_call_target="tpu_custom_call" | custom-call | tf_op jit(solution)/shard_map/stack/pallas_call | solution.py:287
  2.1 3.0 %collective-permute-start.10 = (bf16[4,192,384]{2,1,0:T(8,128)(2,1)}, bf16[4,192,384]{2,1,0:T(8,128)(2,1)S(1)}, u32[]{:S(2)}, u32[]{:S(2)}) collective-permute-start(bf16[4,192,384]{2,1,0:T(8,128)(2,1)} %stack.9), channel_id=1, source_target_pairs={{0,16},{8,24},{16,0},{24,8},{1,17},{9,25},{17,1},{25,9},{2,18},{10... | collective-permute-start | bytes 1769480 | tf_op jit(solution)/shard_map/ppermute | solution.py:230
  5.1 0.0 copy-done.7
  5.1 0.0 copy-done.6
  5.2 0.0 copy-done.1
  5.2 0.1 collective-permute-start.2
  5.3 0.0 copy-done.4
  5.3 0.5 %collective-permute-start.3 = (bf16[192,768]{1,0:T(8,128)(2,1)S(1)}, bf16[192,768]{1,0:T(8,128)(2,1)S(1)}, u32[]{:S(2)}, u32[]{:S(2)}) collective-permute-start(bf16[192,768]{1,0:T(8,128)(2,1)S(1)} %copy-done.4), channel_id=1, source_target_pairs={{0,8},{8,0},{16,24},{24,16},{1,9},{9,1},{17,25},{25,17},{2,10},{10... | collective-permute-start | bytes 884744 | tf_op jit(solution)/shard_map/ppermute | solution.py:225
  5.8 0.6 %collective-permute-start.1 = (s32[8,128]{1,0:T(8,128)S(1)}, s32[8,128]{1,0:T(8,128)S(1)}, u32[]{:S(2)}, u32[]{:S(2)}) collective-permute-start(s32[8,128]{1,0:T(8,128)S(1)} %pad.4.here), channel_id=1, source_target_pairs={{1,2},{3,4},{5,6},{2,1},{4,3},{6,5},{9,10},{11,12},{13,14},{10,9},... | collective-permute-start | bytes 12296 | tf_op jit(solution)/shard_map/ppermute | solution.py:301
  6.4 4.4 %collective-permute-start = (s32[8,128]{1,0:T(8,128)S(1)}, s32[8,128]{1,0:T(8,128)S(1)}, u32[]{:S(2)}, u32[]{:S(2)}) collective-permute-start(s32[8,128]{1,0:T(8,128)S(1)} %pad.4.here), channel_id=1, source_target_pairs={{0,1},{1,0},{2,3},{3,2},{4,5},{5,4},{6,7},{7,6},{8,9},{9,8},{10,11... | collective-permute-start | bytes 12296 | tf_op jit(solution)/shard_map/ppermute | solution.py:225
  10.8 0.0 collective-permute-done.2.refs_8_
  10.8 0.0 collective-permute-done.3.refs_9_
  10.8 0.0 collective-permute-done.1.other
  10.8 1.6 %collective-permute-done.mate = s32[8,128]{1,0:T(8,128)S(1)} collective-permute-done((s32[8,128]{1,0:T(8,128)S(1)}, s32[8,128]{1,0:T(8,128)S(1)}, u32[]{:S(2)}, u32[]{:S(2)}) %collective-permute-start) | collective-permute-done | bytes 4128 | tf_op jit(solution)/shard_map/ppermute | solution.py:225
  12.3 0.0 copy-done
  12.4 0.6 %pool.1.mine = f32[24,768]{1,0:T(8,128)S(1)} custom-call(s32[8,128]{1,0:T(8,128)S(1)} %pad.4.here, s32[8,128]{1,0:T(8,128)S(1)} %collective-permute-done.mate, s32[8,128]{1,0:T(8,128)S(1)} %collective-permute-done.1.other, bf16[256,768]{1,0:T(8,128)(2,1)S(1)} %bitcast.8), custom_call_target="tpu_custom_call" | custom-call | flops 1000 | bytes 1000 | tf_op jit(solution)/shard_map/pool/pallas_call | solution.py:303
  12.9 2.1 %collective-permute-start.4 = (f32[24,768]{1,0:T(8,128)S(1)}, f32[24,768]{1,0:T(8,128)S(1)}, u32[]{:S(2)}, u32[]{:S(2)}) collective-permute-start(f32[24,768]{1,0:T(8,128)S(1)} %pool.1.mine), channel_id=1, source_target_pairs={{0,1},{1,0},{2,3},{3,2},{4,5},{5,4},{6,7},{7,6},{8,9},{9,8},{10,11... | collective-permute-start | bytes 221192 | tf_op jit(solution)/shard_map/ppermute | solution.py:225
  15.0 2.3 %collective-permute-done.4.theirs = f32[24,768]{1,0:T(8,128)S(1)} collective-permute-done((f32[24,768]{1,0:T(8,128)S(1)}, f32[24,768]{1,0:T(8,128)S(1)}, u32[]{:S(2)}, u32[]{:S(2)}) %collective-permute-start.4) | collective-permute-done | bytes 73760 | tf_op jit(solution)/shard_map/ppermute | solution.py:225
  17.4 4.0 %collective-permute-start.7 = (bf16[48,768]{1,0:T(8,128)(2,1)S(1)}, bf16[48,768]{1,0:T(8,128)(2,1)S(1)}, u32[]{:S(2)}, u32[]{:S(2)}) collective-permute-start(bf16[48,768]{1,0:T(8,128)(2,1)S(1)} %pair.1), channel_id=1, source_target_pairs={{0,6},{1,7},{2,4},{3,5},{4,2},{5,3},{6,0},{7,1},{8,14},{9,15},{10,... | collective-permute-start | bytes 221192 | tf_op jit(solution)/shard_map/ppermute | solution.py:225
  21.4 0.0 collective-permute-start.6
  21.4 0.6 %collective-permute-start.5 = (bf16[48,768]{1,0:T(8,128)(2,1)S(1)}, bf16[48,768]{1,0:T(8,128)(2,1)S(1)}, u32[]{:S(2)}, u32[]{:S(2)}) collective-permute-start(bf16[48,768]{1,0:T(8,128)(2,1)S(1)} %pair.1), channel_id=1, source_target_pairs={{0,2},{1,3},{2,0},{3,1},{4,6},{5,7},{6,4},{7,5},{8,10},{9,11},{10,... | collective-permute-start | bytes 221192 | tf_op jit(solution)/shard_map/ppermute | solution.py:225
  22.0 0.5 %collective-permute-start.11 = (bf16[192,768]{1,0:T(8,128)(2,1)S(1)}, bf16[192,768]{1,0:T(8,128)(2,1)S(1)}, u32[]{:S(2)}, u32[]{:S(2)}) collective-permute-start(bf16[192,768]{1,0:T(8,128)(2,1)S(1)} %copy-done.4), channel_id=1, source_target_pairs={{0,16},{8,24},{16,0},{24,8},{1,17},{9,25},{17,1},{25,9},{2,18},{10... | collective-permute-start | bytes 884744 | tf_op jit(solution)/shard_map/ppermute | solution.py:230
  22.5 0.0 collective-permute-done.10
  22.5 0.0 copy-start.5
  22.6 0.0 copy-start.2
  22.6 0.0 copy-start.3
  22.6 1.9 %collective-permute-start.12 = (bf16[1,2,192,384]{3,2,1,0:T(8,128)(2,1)S(1)}, bf16[1,2,192,384]{3,2,1,0:T(8,128)(2,1)S(1)}, u32[]{:S(2)}, u32[]{:S(2)}) collective-permute-start(bf16[1,2,192,384]{3,2,1,0:T(8,128)(2,1)S(1)} %slice.3), channel_id=1, source_target_pairs={{0,1},{1,0},{2,3},{3,2},{4,5},{5,4},{6,7},{7,6},{8,9},{9,8},{10,11... | collective-permute-start | bytes 884744 | tf_op jit(solution)/shard_map/ppermute | solution.py:225
  24.5 0.0 collective-permute-done.7
  24.5 2.2 %collective-permute-done.6 = bf16[48,768]{1,0:T(8,128)(2,1)S(1)} collective-permute-done((bf16[48,768]{1,0:T(8,128)(2,1)S(1)}, bf16[48,768]{1,0:T(8,128)(2,1)S(1)}, u32[]{:S(2)}, u32[]{:S(2)}) %collective-permute-start.6) | collective-permute-done | bytes 73760 | tf_op jit(solution)/shard_map/ppermute | solution.py:225
  26.6 0.0 collective-permute-done.5
  26.7 0.1 collective-permute-start.13
  26.7 0.0 copy-done.2
  26.8 0.5 %collective-permute-start.8 = (bf16[192,768]{1,0:T(8,128)(2,1)S(1)}, bf16[192,768]{1,0:T(8,128)(2,1)S(1)}, u32[]{:S(2)}, u32[]{:S(2)}) collective-permute-start(bf16[192,768]{1,0:T(8,128)(2,1)S(1)} %copy-done.2), channel_id=1, source_target_pairs={{0,8},{8,0},{16,24},{24,16},{1,9},{9,1},{17,25},{25,17},{2,10},{10... | collective-permute-start | bytes 884744 | tf_op jit(solution)/shard_map/ppermute | solution.py:225
  27.2 0.0 copy-done.3
  27.2 0.1 collective-permute-start.9
  27.3 1.4 %collective-permute-done.11 = bf16[192,768]{1,0:T(8,128)(2,1)S(1)} collective-permute-done((bf16[192,768]{1,0:T(8,128)(2,1)S(1)}, bf16[192,768]{1,0:T(8,128)(2,1)S(1)}, u32[]{:S(2)}, u32[]{:S(2)}) %collective-permute-start.11) | collective-permute-done | bytes 294944 | tf_op jit(solution)/shard_map/ppermute | solution.py:230
  28.7 0.0 collective-permute-start.14
  28.8 0.6 %collective-permute-done.12.refs_14_ = bf16[1,2,192,384]{3,2,1,0:T(8,128)(2,1)S(1)} collective-permute-done((bf16[1,2,192,384]{3,2,1,0:T(8,128)(2,1)S(1)}, bf16[1,2,192,384]{3,2,1,0:T(8,128)(2,1)S(1)}, u32[]{:S(2)}, u32[]{:S(2)}) %collective-permute-start.12) | collective-permute-done | bytes 294944 | tf_op jit(solution)/shard_map/ppermute | solution.py:225
  29.4 0.0 collective-permute-start.15
  30.0 0.0 copy-done.5
  30.1 0.0 collective-permute-done.8.refs_10_
  30.1 0.0 collective-permute-done.9.refs_11_
  30.1 0.2 collective-permute-done.14.refs_16_
  30.3 0.6 %collective-permute-done.15.refs_17_ = bf16[1,2,192,384]{3,2,1,0:T(8,128)(2,1)S(1)} collective-permute-done((bf16[1,2,192,384]{3,2,1,0:T(8,128)(2,1)S(1)}, bf16[1,2,192,384]{3,2,1,0:T(8,128)(2,1)S(1)}, u32[]{:S(2)}, u32[]{:S(2)}) %collective-permute-start.15) | collective-permute-done | bytes 294944 | tf_op jit(solution)/shard_map/ppermute | solution.py:225
  31.0 0.0 collective-permute-done.13.refs_15_
  31.0 4.3 %attend.1 = bf16[256,768]{1,0:T(8,128)(2,1)} custom-call(s32[1]{0:T(128)S(6)} %copy.10.refs_0_, bf16[192,768]{1,0:T(8,128)(2,1)S(1)} %pad_maximum_fusion.refs_1_, f32[1,768]{1,0:T(1,128)S(1)} %broadcast_in_dim.8.refs_2_, bf16[256,768]{1,0:T(8,128)(2,1)S(1)} %bitcast.9, bf16[192,768]{1,0:T(8,128)(2,1)S(1)} %copy-done.1, bf16[192,768]{1,0:T(8,128)(2,1)S(1)} %copy-done.4, ...), custom_call_target="tpu_custom_call" | custom-call | flops 1000 | bytes 1000 | tf_op jit(solution)/shard_map/attend/pallas_call | solution.py:325
  (6 shorter events, 0.1 us)
Async XLA Ops:
  0.0 5.2 %copy-start.1 = (bf16[192,768]{1,0:T(8,128)(2,1)S(1)}, bf16[192,768]{1,0:T(8,128)(2,1)}, u32[]{:S(2)}) copy-start(bf16[192,768]{1,0:T(8,128)(2,1)} %refs_4_.1) | copy-start | bytes 884740
  0.0 5.1 %copy-start.7 = (s32[1,64,4]{1,2,0:T(4,128)S(1)}, s32[1,64,4]{1,2,0:T(4,128)}, u32[]{:S(2)}) copy-start(s32[1,64,4]{1,2,0:T(4,128)} %param.11) | copy-start | bytes 3076
  0.0 5.1 %copy-start.6 = (s32[1,64,4]{1,2,0:T(4,128)S(1)}, s32[1,64,4]{1,2,0:T(4,128)}, u32[]{:S(2)}) copy-start(s32[1,64,4]{1,2,0:T(4,128)} %param.10) | copy-start | bytes 3076
  0.0 5.2 %copy-start.4 = (bf16[192,768]{1,0:T(8,128)(2,1)S(1)}, bf16[192,768]{1,0:T(8,128)(2,1)}, u32[]{:S(2)}) copy-start(bf16[192,768]{1,0:T(8,128)(2,1)} %refs_5_.1) | copy-start | bytes 884740
  0.0 12.3 %copy-start = (bf16[1,256,768]{2,1,0:T(8,128)(2,1)S(1)}, bf16[1,256,768]{2,1,0:T(8,128)(2,1)}, u32[]{:S(2)}) copy-start(bf16[1,256,768]{2,1,0:T(8,128)(2,1)} %param.9) | copy-start | bytes 1179652
  2.1 20.4 %collective-permute-start.10 = (bf16[4,192,384]{2,1,0:T(8,128)(2,1)}, bf16[4,192,384]{2,1,0:T(8,128)(2,1)S(1)}, u32[]{:S(2)}, u32[]{:S(2)}) collective-permute-start(bf16[4,192,384]{2,1,0:T(8,128)(2,1)} %stack.9), channel_id=1, source_target_pairs={{0,16},{8,24},{16,0},{24,8},{1,17},{9,25},{17,1},{25,9},{2,18},{10... | collective-permute-start | bytes 1769480 | tf_op jit(solution)/shard_map/ppermute | solution.py:230
  5.2 5.6 %collective-permute-start.2 = (bf16[192,768]{1,0:T(8,128)(2,1)S(1)}, bf16[192,768]{1,0:T(8,128)(2,1)S(1)}, u32[]{:S(2)}, u32[]{:S(2)}) collective-permute-start(bf16[192,768]{1,0:T(8,128)(2,1)S(1)} %copy-done.1), channel_id=1, source_target_pairs={{0,8},{8,0},{16,24},{24,16},{1,9},{9,1},{17,25},{25,17},{2,10},{10... | collective-permute-start | bytes 884744 | tf_op jit(solution)/shard_map/ppermute | solution.py:225
  5.3 5.5 %collective-permute-start.3 = (bf16[192,768]{1,0:T(8,128)(2,1)S(1)}, bf16[192,768]{1,0:T(8,128)(2,1)S(1)}, u32[]{:S(2)}, u32[]{:S(2)}) collective-permute-start(bf16[192,768]{1,0:T(8,128)(2,1)S(1)} %copy-done.4), channel_id=1, source_target_pairs={{0,8},{8,0},{16,24},{24,16},{1,9},{9,1},{17,25},{25,17},{2,10},{10... | collective-permute-start | bytes 884744 | tf_op jit(solution)/shard_map/ppermute | solution.py:225
  5.8 5.0 %collective-permute-start.1 = (s32[8,128]{1,0:T(8,128)S(1)}, s32[8,128]{1,0:T(8,128)S(1)}, u32[]{:S(2)}, u32[]{:S(2)}) collective-permute-start(s32[8,128]{1,0:T(8,128)S(1)} %pad.4.here), channel_id=1, source_target_pairs={{1,2},{3,4},{5,6},{2,1},{4,3},{6,5},{9,10},{11,12},{13,14},{10,9},... | collective-permute-start | bytes 12296 | tf_op jit(solution)/shard_map/ppermute | solution.py:301
  6.4 5.9 %collective-permute-start = (s32[8,128]{1,0:T(8,128)S(1)}, s32[8,128]{1,0:T(8,128)S(1)}, u32[]{:S(2)}, u32[]{:S(2)}) collective-permute-start(s32[8,128]{1,0:T(8,128)S(1)} %pad.4.here), channel_id=1, source_target_pairs={{0,1},{1,0},{2,3},{3,2},{4,5},{5,4},{6,7},{7,6},{8,9},{9,8},{10,11... | collective-permute-start | bytes 12296 | tf_op jit(solution)/shard_map/ppermute | solution.py:225
  12.9 4.4 %collective-permute-start.4 = (f32[24,768]{1,0:T(8,128)S(1)}, f32[24,768]{1,0:T(8,128)S(1)}, u32[]{:S(2)}, u32[]{:S(2)}) collective-permute-start(f32[24,768]{1,0:T(8,128)S(1)} %pool.1.mine), channel_id=1, source_target_pairs={{0,1},{1,0},{2,3},{3,2},{4,5},{5,4},{6,7},{7,6},{8,9},{9,8},{10,11... | collective-permute-start | bytes 221192 | tf_op jit(solution)/shard_map/ppermute | solution.py:225
  17.4 7.1 %collective-permute-start.7 = (bf16[48,768]{1,0:T(8,128)(2,1)S(1)}, bf16[48,768]{1,0:T(8,128)(2,1)S(1)}, u32[]{:S(2)}, u32[]{:S(2)}) collective-permute-start(bf16[48,768]{1,0:T(8,128)(2,1)S(1)} %pair.1), channel_id=1, source_target_pairs={{0,6},{1,7},{2,4},{3,5},{4,2},{5,3},{6,0},{7,1},{8,14},{9,15},{10,... | collective-permute-start | bytes 221192 | tf_op jit(solution)/shard_map/ppermute | solution.py:225
  21.4 5.3 %collective-permute-start.6 = (bf16[48,768]{1,0:T(8,128)(2,1)S(1)}, bf16[48,768]{1,0:T(8,128)(2,1)S(1)}, u32[]{:S(2)}, u32[]{:S(2)}) collective-permute-start(bf16[48,768]{1,0:T(8,128)(2,1)S(1)} %pair.1), channel_id=1, source_target_pairs={{0,4},{1,5},{2,6},{3,7},{4,0},{5,1},{6,2},{7,3},{8,12},{9,13},{10,... | collective-permute-start | bytes 221192 | tf_op jit(solution)/shard_map/ppermute | solution.py:225
  21.4 5.3 %collective-permute-start.5 = (bf16[48,768]{1,0:T(8,128)(2,1)S(1)}, bf16[48,768]{1,0:T(8,128)(2,1)S(1)}, u32[]{:S(2)}, u32[]{:S(2)}) collective-permute-start(bf16[48,768]{1,0:T(8,128)(2,1)S(1)} %pair.1), channel_id=1, source_target_pairs={{0,2},{1,3},{2,0},{3,1},{4,6},{5,7},{6,4},{7,5},{8,10},{9,11},{10,... | collective-permute-start | bytes 221192 | tf_op jit(solution)/shard_map/ppermute | solution.py:225
  22.0 6.7 %collective-permute-start.11 = (bf16[192,768]{1,0:T(8,128)(2,1)S(1)}, bf16[192,768]{1,0:T(8,128)(2,1)S(1)}, u32[]{:S(2)}, u32[]{:S(2)}) collective-permute-start(bf16[192,768]{1,0:T(8,128)(2,1)S(1)} %copy-done.4), channel_id=1, source_target_pairs={{0,16},{8,24},{16,0},{24,8},{1,17},{9,25},{17,1},{25,9},{2,18},{10... | collective-permute-start | bytes 884744 | tf_op jit(solution)/shard_map/ppermute | solution.py:230
  22.5 7.5 %copy-start.5 = (f32[768]{0:T(1024)S(1)}, f32[768]{0:T(1024)}, u32[]{:S(2)}) copy-start(f32[768]{0:T(1024)} %param.17) | copy-start | bytes 9220
  22.6 4.2 %copy-start.2 = (bf16[192,768]{1,0:T(8,128)(2,1)S(1)}, bf16[192,768]{1,0:T(8,128)(2,1)}, u32[]{:S(2)}) copy-start(bf16[192,768]{1,0:T(8,128)(2,1)} %refs_6_.1) | copy-start | bytes 884740
  22.6 4.7 %copy-start.3 = (bf16[192,768]{1,0:T(8,128)(2,1)S(1)}, bf16[192,768]{1,0:T(8,128)(2,1)}, u32[]{:S(2)}) copy-start(bf16[192,768]{1,0:T(8,128)(2,1)} %refs_7_.1) | copy-start | bytes 884740
  22.6 6.8 %collective-permute-start.12 = (bf16[1,2,192,384]{3,2,1,0:T(8,128)(2,1)S(1)}, bf16[1,2,192,384]{3,2,1,0:T(8,128)(2,1)S(1)}, u32[]{:S(2)}, u32[]{:S(2)}) collective-permute-start(bf16[1,2,192,384]{3,2,1,0:T(8,128)(2,1)S(1)} %slice.3), channel_id=1, source_target_pairs={{0,1},{1,0},{2,3},{3,2},{4,5},{5,4},{6,7},{7,6},{8,9},{9,8},{10,11... | collective-permute-start | bytes 884744 | tf_op jit(solution)/shard_map/ppermute | solution.py:225
  26.7 4.3 %collective-permute-start.13 = (bf16[1,4,192,384]{3,2,1,0:T(8,128)(2,1)S(1)}, bf16[1,4,192,384]{3,2,1,0:T(8,128)(2,1)S(1)}, u32[]{:S(2)}, u32[]{:S(2)}) collective-permute-start(bf16[1,4,192,384]{3,2,1,0:T(8,128)(2,1)S(1)} %bitcast.11), channel_id=1, source_target_pairs={{0,8},{8,0},{16,24},{24,16},{1,9},{9,1},{17,25},{25,17},{2,10},{10... | collective-permute-start | bytes 1769480 | tf_op jit(solution)/shard_map/ppermute | solution.py:225
  26.8 3.3 %collective-permute-start.8 = (bf16[192,768]{1,0:T(8,128)(2,1)S(1)}, bf16[192,768]{1,0:T(8,128)(2,1)S(1)}, u32[]{:S(2)}, u32[]{:S(2)}) collective-permute-start(bf16[192,768]{1,0:T(8,128)(2,1)S(1)} %copy-done.2), channel_id=1, source_target_pairs={{0,8},{8,0},{16,24},{24,16},{1,9},{9,1},{17,25},{25,17},{2,10},{10... | collective-permute-start | bytes 884744 | tf_op jit(solution)/shard_map/ppermute | solution.py:225
  27.2 2.8 %collective-permute-start.9 = (bf16[192,768]{1,0:T(8,128)(2,1)S(1)}, bf16[192,768]{1,0:T(8,128)(2,1)S(1)}, u32[]{:S(2)}, u32[]{:S(2)}) collective-permute-start(bf16[192,768]{1,0:T(8,128)(2,1)S(1)} %copy-done.3), channel_id=1, source_target_pairs={{0,8},{8,0},{16,24},{24,16},{1,9},{9,1},{17,25},{25,17},{2,10},{10... | collective-permute-start | bytes 884744 | tf_op jit(solution)/shard_map/ppermute | solution.py:225
  28.7 1.6 %collective-permute-start.14 = (bf16[1,192,768]{2,1,0:T(8,128)(2,1)S(1)}, bf16[1,192,768]{2,1,0:T(8,128)(2,1)S(1)}, u32[]{:S(2)}, u32[]{:S(2)}) collective-permute-start(bf16[1,192,768]{2,1,0:T(8,128)(2,1)S(1)} %bitcast.13), channel_id=1, source_target_pairs={{0,8},{8,0},{16,24},{24,16},{1,9},{9,1},{17,25},{25,17},{2,10},{10... | collective-permute-start | bytes 884744 | tf_op jit(solution)/shard_map/ppermute | solution.py:225
  29.4 1.6 %collective-permute-start.15 = (bf16[1,2,192,384]{3,2,1,0:T(8,128)(2,1)S(1)}, bf16[1,2,192,384]{3,2,1,0:T(8,128)(2,1)S(1)}, u32[]{:S(2)}, u32[]{:S(2)}) collective-permute-start(bf16[1,2,192,384]{3,2,1,0:T(8,128)(2,1)S(1)} %collective-permute-done.12.refs_14_), channel_id=1, source_target_pairs={{0,8},{8,0},{16,24},{24,16},{1,9},{9,1},{17,25},{25,17},{2,10},{10... | collective-permute-start | bytes 884744 | tf_op jit(solution)/shard_map/ppermute | solution.py:225
